TPU v7x, 32 devices: a whole 2x2x4 slice. The times are simulated.
32 devices in a mesh: ctx: 16 (over z, y, x), fsdp: 2 (over core).
Axes of the slice: x: 2, y: 2, z: 4, core: 2. Of those that a mesh axis runs over, the one named last changes fastest.
Arguments:
- tokens: bfloat16 [2, 2048, 1024], P('fsdp', 'ctx'), may hold values from -6 to 6
- block_order: int32 [16, 2], P('ctx'), may hold values from 0 to 31, as said below
- ln_gain: bfloat16 [1024], P('fsdp'), may hold values from 0.25 to 1.75
- ln_bias: bfloat16 [1024], P('fsdp'), may hold values from -1.75 to 1.75
- w_qkv: bfloat16 [1024, 3072], P('fsdp')
- qv_bias: bfloat16 [2, 1024], P(None, 'fsdp'), may hold values from -3 to 3
- w_out: bfloat16 [1024, 1024], P('fsdp'), may hold values from -1.5 to 1.5
- b_out: bfloat16 [1024], P('fsdp'), may hold values from -3 to 3
- w_in: bfloat16 [1024, 4096], P('fsdp'), may hold values from -0.1875 to 0.1875
- b_in: bfloat16 [4096], P('fsdp'), may hold values from -3 to 3
- w_down: bfloat16 [4096, 1024], P('fsdp'), may hold values from -0.09375 to 0.09375
- b_down: bfloat16 [1024], P('fsdp'), may hold values from -3 to 3
- cotangent: bfloat16 [2, 2048, 1024], P('fsdp', 'ctx'), may hold values from -6 to 6
Outputs:
- layer_out: bfloat16 [2, 2048, 1024], P('fsdp', 'ctx')
- grad_tokens: bfloat16 [2, 2048, 1024], P('fsdp', 'ctx')
- grad_ln_gain: float32 [1024], P(('ctx', 'fsdp'))
- grad_ln_bias: float32 [1024], P(('ctx', 'fsdp'))
- grad_w_qkv: float32 [1024, 3072], P(('ctx', 'fsdp'))
- grad_qv_bias: float32 [2, 1024], P(None, ('ctx', 'fsdp'))
- grad_w_out: float32 [1024, 1024], P(('ctx', 'fsdp'))
- grad_b_out: float32 [1024], P(('ctx', 'fsdp'))
- grad_w_in: float32 [1024, 4096], P(('ctx', 'fsdp'))
- grad_b_in: float32 [4096], P(('ctx', 'fsdp'))
- grad_w_down: float32 [4096, 1024], P(('ctx', 'fsdp'))
- grad_b_down: float32 [1024], P(('ctx', 'fsdp'))
Inputs may be any that keep to these rules, and one draw needn't show every extreme that they name: Row i of block_order holds some j below 16 and 31 - j, in either order; each of the 32 block numbers appears once.
All inputs are finite; a program needn't handle non-finite values.
Results may differ from a plain program's by a relative error of at most 0.015.
Values may be sent and summed in bfloat16 or wider, within the bound.
No kernel may reach another device: no remote copies, remote signals or barrier semaphores. Data moves between devices by JAX's collectives and lax.ppermute only.
A program may use at most 320 MiB of HBM per device.

v0:
```python
from functools import partial
import math

import jax
import jax.numpy as jnp
from jax import lax
from jax.sharding import PartitionSpec as P

HEADS = 16
HEAD_DIM = 64
ROT = 16


epsilon = 1e-05


def from_behind(block, axis, distance):
    devices = range(lax.axis_size(axis))
    route = [((i - distance) % len(devices), i) for i in devices]
    return lax.ppermute(block, axis, route)


def rotate(vectors, cosine, sine_part):
    half_rot = ROT // 2
    rotary_part = vectors[..., :ROT]
    turned = jnp.concatenate([-rotary_part[..., half_rot:], rotary_part[..., :half_rot]], -1)
    return jnp.concatenate([rotary_part * cosine + turned * sine_part, vectors[..., ROT:]], -1)


def tables(positions):
    freq_index = jnp.arange(ROT // 2, dtype=jnp.float32)
    inverse = 10000.0 ** (-2.0 * freq_index / ROT)
    angles = positions.astype(jnp.float32)[:, None] * inverse[None, :]
    angles = jnp.concatenate([angles, angles], -1)
    return (jnp.cos(angles), jnp.sin(angles))


def spread_positions(orders, half_rows):
    offsets = jnp.arange(half_rows, dtype=jnp.int32)
    return (orders[:, :, None] * half_rows + offsets[None, None, :]).reshape(-1)


def outer_sum(left_side, right_side):
    return lax.dot_general(
        left_side, right_side, (((0,), (0,)), ((), ())), preferred_element_type=jnp.float32
    )


def times_transposed(left_side, right_side):
    return lax.dot_general(
        left_side, right_side, (((1,), (1,)), ((), ())), preferred_element_type=jnp.float32
    )


def attend_block(carried, queries, query_pos, key_rows, value_rows, key_pos, score_scale):
    row_max, row_sum, weighted = carried
    scores = (
        jnp.einsum("qhd,khd->hqk", queries, key_rows, preferred_element_type=jnp.float32)
        * score_scale
    )
    allowed = (query_pos[:, None] >= key_pos[None, :])[None]
    new_max = jnp.maximum(row_max, jnp.max(jnp.where(allowed, scores, -1e30), -1))
    weights = jnp.where(allowed, jnp.exp(scores - new_max[:, :, None]), 0.0)
    rescale = jnp.exp(row_max - new_max)
    row_sum = row_sum * rescale + jnp.sum(weights, -1)
    weighted = weighted * rescale.T[:, :, None] + jnp.einsum(
        "hqk,khd->qhd", weights.astype(jnp.bfloat16), value_rows, preferred_element_type=jnp.float32
    )
    return (new_max, row_sum, weighted)


def block_grads(
    queries, grad_rows, log_sum, delta_rows, query_pos, key_rows, value_rows, key_pos, score_scale
):
    scores = (
        jnp.einsum("qhd,khd->hqk", queries, key_rows, preferred_element_type=jnp.float32)
        * score_scale
    )
    allowed = (query_pos[:, None] >= key_pos[None, :])[None]
    probs = jnp.where(allowed, jnp.exp(scores - log_sum[:, :, None]), 0.0)
    grad_values = jnp.einsum(
        "hqk,qhd->khd", probs.astype(jnp.bfloat16), grad_rows, preferred_element_type=jnp.float32
    )
    grad_probs = jnp.einsum(
        "qhd,khd->hqk", grad_rows, value_rows, preferred_element_type=jnp.float32
    )
    grad_scores = (probs * (grad_probs - delta_rows[:, :, None])).astype(jnp.bfloat16)
    grad_queries = (
        jnp.einsum("hqk,khd->qhd", grad_scores, key_rows, preferred_element_type=jnp.float32)
        * score_scale
    )
    grad_keys = (
        jnp.einsum("hqk,qhd->khd", grad_scores, queries, preferred_element_type=jnp.float32)
        * score_scale
    )
    return (grad_queries, grad_keys, grad_values)


def body(
    tokens,
    block_order,
    ln_gain,
    ln_bias,
    w_qkv,
    qv_bias,
    w_out,
    b_out,
    w_in,
    b_in,
    w_down,
    b_down,
    cotangent,
):
    gathered = (
        lax.all_gather(ln_gain, "fsdp", axis=0, tiled=True),
        lax.all_gather(ln_bias, "fsdp", axis=0, tiled=True),
        lax.all_gather(w_qkv, "fsdp", axis=0, tiled=True),
        lax.all_gather(qv_bias, "fsdp", axis=1, tiled=True),
        lax.all_gather(w_out, "fsdp", axis=0, tiled=True),
        lax.all_gather(b_out, "fsdp", axis=0, tiled=True),
        lax.all_gather(w_in, "fsdp", axis=0, tiled=True),
        lax.all_gather(b_in, "fsdp", axis=0, tiled=True),
        lax.all_gather(w_down, "fsdp", axis=0, tiled=True),
        lax.all_gather(b_down, "fsdp", axis=0, tiled=True),
    )
    (
        gain_full,
        shift_full,
        qkv_full,
        bias_full,
        out_full,
        out_bias,
        in_full,
        in_bias,
        down_full,
        down_bias,
    ) = gathered
    tok_rows = tokens.shape[1]
    model_width = tokens.shape[2]
    half_rows = tok_rows // 2
    score_scale = HEAD_DIM ** (-0.5)
    head_shape = (tok_rows, HEADS, HEAD_DIM)
    flat_shape = (tok_rows, model_width)
    inputs = tokens[0].astype(jnp.float32)
    row_mean = jnp.mean(inputs, -1, keepdims=True)
    centered = inputs - row_mean
    inverse = lax.rsqrt(jnp.mean(centered * centered, -1, keepdims=True) + epsilon)
    normed = centered * inverse
    ln_out = (normed * gain_full.astype(jnp.float32) + shift_full.astype(jnp.float32)).astype(
        jnp.bfloat16
    )
    qkv_pre = jnp.dot(ln_out, qkv_full, preferred_element_type=jnp.float32)
    positions = spread_positions(block_order, half_rows)
    cosine, sine_part = tables(positions)
    cosine = cosine[:, None, :]
    sine_part = sine_part[:, None, :]
    query_pre = qkv_pre[:, :model_width] + bias_full[0].astype(jnp.float32)
    query_rows = rotate(query_pre.reshape(head_shape), cosine, sine_part).astype(jnp.bfloat16)
    key_rows = rotate(
        qkv_pre[:, model_width : 2 * model_width].reshape(head_shape), cosine, sine_part
    ).astype(jnp.bfloat16)
    value_rows = (qkv_pre[:, 2 * model_width :] + bias_full[1].astype(jnp.float32)).astype(
        jnp.bfloat16
    )
    key_flat = key_rows.reshape(flat_shape)
    start_state = (
        jnp.full((HEADS, tok_rows), -1e30, jnp.float32),
        jnp.zeros((HEADS, tok_rows), jnp.float32),
        jnp.zeros(head_shape, jnp.float32),
    )
    carried = start_state
    piece_keys = lax.all_gather(key_flat, "ctx", axis=0, tiled=True)
    piece_values = lax.all_gather(value_rows, "ctx", axis=0, tiled=True)
    piece_orders = lax.all_gather(block_order, "ctx", axis=0, tiled=True)
    shard_count = piece_orders.shape[0]
    group_size = math.gcd(shard_count, max(1, 1024 // tok_rows))
    rounds = shard_count // group_size
    stacked = (
        piece_keys.reshape(rounds, group_size * tok_rows, HEADS, HEAD_DIM),
        piece_values.reshape(rounds, group_size * tok_rows, HEADS, HEAD_DIM),
        piece_orders.reshape(rounds, group_size, 2),
    )

    def one_round(inner_state, block_item):
        key_pos = spread_positions(block_item[2], half_rows)
        return (
            attend_block(
                inner_state,
                query_rows,
                positions,
                block_item[0],
                block_item[1],
                key_pos,
                score_scale,
            ),
            None,
        )

    carried, _ = lax.scan(one_round, carried, stacked)
    row_max, row_sum, weighted = carried
    attended_f32 = weighted / row_sum.T[:, :, None]
    log_sum = row_max + jnp.log(row_sum)
    attended = attended_f32.reshape(flat_shape).astype(jnp.bfloat16)
    branch = jnp.dot(attended, out_full, preferred_element_type=jnp.float32) + out_bias.astype(
        jnp.float32
    )
    hidden = jnp.dot(ln_out, in_full, preferred_element_type=jnp.float32) + in_bias.astype(
        jnp.float32
    )
    active = jax.nn.gelu(hidden, approximate=False).astype(jnp.bfloat16)
    feed_out = jnp.dot(active, down_full, preferred_element_type=jnp.float32) + down_bias.astype(
        jnp.float32
    )
    layer_out = (inputs + branch + feed_out).astype(jnp.bfloat16)[None]
    gain_back, qkv_back, out_back, in_back, down_back = (
        gain_full,
        qkv_full,
        out_full,
        in_full,
        down_full,
    )
    grad_out = cotangent[0]
    grad_f32 = grad_out.astype(jnp.float32)
    grad_attended = times_transposed(grad_out, out_back).astype(jnp.bfloat16).reshape(head_shape)
    grad_active = times_transposed(grad_out, down_back)
    _, gelu_pull = jax.vjp(partial(jax.nn.gelu, approximate=False), hidden)
    grad_hidden = gelu_pull(grad_active)[0].astype(jnp.bfloat16)
    delta_rows = jnp.sum(grad_attended.astype(jnp.float32) * attended_f32, -1).T
    cotangent_sum = jnp.sum(grad_f32, 0)
    term_out_w = outer_sum(attended, grad_out)
    term_in_w = outer_sum(ln_out, grad_hidden)
    term_in_b = jnp.sum(grad_hidden.astype(jnp.float32), 0)
    term_down_w = outer_sum(active, grad_out)
    cycle_size = lax.axis_size("ctx")
    zeros_flat = jnp.zeros(flat_shape, jnp.float32)
    zeros_heads = jnp.zeros(head_shape, jnp.float32)

    def send_home(grad_keys, grad_values):
        return (
            from_behind(grad_keys.astype(jnp.bfloat16), "ctx", 1).astype(grad_keys.dtype),
            from_behind(grad_values.astype(jnp.bfloat16), "ctx", 1).astype(grad_values.dtype),
        )

    def visit_keys(carried):
        visit_key, visit_value, visit_order, grad_keys, grad_values, grad_query = carried
        part_query, part_key, part_value = block_grads(
            query_rows,
            grad_attended,
            log_sum,
            delta_rows,
            positions,
            visit_key.reshape(head_shape),
            visit_value.reshape(head_shape),
            spread_positions(visit_order, half_rows),
            score_scale,
        )
        return (
            grad_keys + part_key.reshape(flat_shape),
            grad_values + part_value.reshape(flat_shape),
            grad_query + part_query,
        )

    def cycle_step(step_index, carried):
        grad_keys, grad_values, grad_query = visit_keys(carried)
        visit_key, visit_value, visit_order = from_behind(
            (carried[0], carried[1], carried[2]), "ctx", 1
        )
        grad_keys, grad_values = send_home(grad_keys, grad_values)
        return (visit_key, visit_value, visit_order, grad_keys, grad_values, grad_query)

    carried = lax.fori_loop(
        0,
        cycle_size - 1,
        cycle_step,
        (key_flat, value_rows, block_order, zeros_flat, zeros_flat, zeros_heads),
    )
    grad_keys, grad_values, grad_query = visit_keys(carried)
    grad_keys, grad_values = send_home(grad_keys, grad_values)
    grad_keys = grad_keys.reshape(head_shape)
    grad_values = grad_values.reshape(head_shape)
    grad_q_pre = rotate(grad_query, cosine, -sine_part).reshape(flat_shape).astype(jnp.bfloat16)
    grad_k_pre = rotate(grad_keys, cosine, -sine_part).reshape(flat_shape).astype(jnp.bfloat16)
    grad_v_pre = grad_values.reshape(flat_shape).astype(jnp.bfloat16)
    grad_qkv = jnp.concatenate([grad_q_pre, grad_k_pre, grad_v_pre], -1)
    grad_ln = times_transposed(grad_qkv, qkv_back) + times_transposed(grad_hidden, in_back)
    grad_normed = grad_ln * gain_back.astype(jnp.float32)
    grad_inputs = inverse * (
        grad_normed
        - jnp.mean(grad_normed, -1, keepdims=True)
        - normed * jnp.mean(grad_normed * normed, -1, keepdims=True)
    )
    grad_tokens = (grad_f32 + grad_inputs).astype(jnp.bfloat16)[None]
    term_gain = jnp.sum(grad_ln * normed, 0)
    term_bias = jnp.sum(grad_ln, 0)
    term_qkv = outer_sum(ln_out, grad_qkv)
    term_qv = jnp.stack(
        [jnp.sum(grad_q_pre.astype(jnp.float32), 0), jnp.sum(grad_v_pre.astype(jnp.float32), 0)], 0
    )
    (
        sum_gain,
        sum_bias,
        sum_qkv,
        sum_qv,
        sum_out_w,
        sum_out_b,
        sum_in_w,
        sum_in_b,
        sum_down_w,
        sum_down_b,
    ) = (
        lax.psum_scatter(term_gain, ("ctx", "fsdp"), scatter_dimension=0, tiled=True),
        lax.psum_scatter(term_bias, ("ctx", "fsdp"), scatter_dimension=0, tiled=True),
        lax.psum_scatter(term_qkv, ("ctx", "fsdp"), scatter_dimension=0, tiled=True),
        lax.psum_scatter(term_qv, ("ctx", "fsdp"), scatter_dimension=1, tiled=True),
        lax.psum_scatter(term_out_w, ("ctx", "fsdp"), scatter_dimension=0, tiled=True),
        lax.psum_scatter(cotangent_sum, ("ctx", "fsdp"), scatter_dimension=0, tiled=True),
        lax.psum_scatter(term_in_w, ("ctx", "fsdp"), scatter_dimension=0, tiled=True),
        lax.psum_scatter(term_in_b, ("ctx", "fsdp"), scatter_dimension=0, tiled=True),
        lax.psum_scatter(term_down_w, ("ctx", "fsdp"), scatter_dimension=0, tiled=True),
        lax.psum_scatter(cotangent_sum, ("ctx", "fsdp"), scatter_dimension=0, tiled=True),
    )
    return (
        layer_out,
        grad_tokens,
        sum_gain,
        sum_bias,
        sum_qkv,
        sum_qv,
        sum_out_w,
        sum_out_b,
        sum_in_w,
        sum_in_b,
        sum_down_w,
        sum_down_b,
    )


def solution(mesh):
    return jax.shard_map(
        body,
        mesh=mesh,
        in_specs=(
            P("fsdp", "ctx", None),
            P("ctx", None),
            P("fsdp"),
            P("fsdp"),
            P("fsdp", None),
            P(None, "fsdp"),
            P("fsdp", None),
            P("fsdp"),
            P("fsdp", None),
            P("fsdp"),
            P("fsdp", None),
            P("fsdp"),
            P("fsdp", "ctx", None),
        ),
        out_specs=(
            P("fsdp", "ctx", None),
            P("fsdp", "ctx", None),
            P(("ctx", "fsdp")),
            P(("ctx", "fsdp")),
            P(("ctx", "fsdp"), None),
            P(None, ("ctx", "fsdp")),
            P(("ctx", "fsdp"), None),
            P(("ctx", "fsdp")),
            P(("ctx", "fsdp"), None),
            P(("ctx", "fsdp")),
            P(("ctx", "fsdp"), None),
            P(("ctx", "fsdp")),
        ),
        check_vma=False,
    )
```

profile of v0, /device:TPU:0, one launch (start us, length us, event | category | flops | bytes accessed | tf_op | source)
XLA Modules:
  0.0 1479.4 jit_solution(8294640296650787842)
XLA Ops:
  9.0 1.9 all-gather.1
  15.1 13.9 all-gather.12.cloned.1.call-done
  29.0 3.9 fusion.109
  36.9 40.8 %all-gather = s32[16,1,2]{2,1,0:T(1,128)S(1)} all-gather(s32[1,1,2]{2,1,0:T(1,128)S(1)} %bitcast.289), channel_id=1, replica_groups=mesh['ctx'=16,'fsdp'=2] {'ctx'}, dimensions={0}, use_global_device_ids=true | all-gather | bytes 136 | tf_op jit(solution)/shard_map/all_gather | solution.py:174
  77.8 2.5 convolution_convert_fusion
  81.3 54.2 %all-gather.14.cloned.1.call-done = bf16[2048,1024]{0,1:T(8,128)(2,1)} async-done(((bf16[128,1024]{0,1:T(8,128)(2,1)}), bf16[2048,1024]{0,1:T(8,128)(2,1)}) %all-gather.14.cloned.1.call-update) | async-done | bytes 4194320 | tf_op jit(solution)/shard_map/all_gather | solution.py:172
  135.5 8.4 reshape.418
  143.8 5.7 copy.63
  149.5 63.5 %all-gather.16.cloned.1.call-done = bf16[2048,1024]{1,0:T(8,128)(2,1)} async-done(((bf16[128,1024]{1,0:T(8,128)(2,1)}), bf16[2048,1024]{1,0:T(8,128)(2,1)}) %all-gather.16.cloned.1.call-update) | async-done | bytes 4194320 | tf_op jit(solution)/shard_map/all_gather | solution.py:173
  213.0 11.9 reshape.449
  224.9 10.3 copy.64
  235.2 34.6 %while.36 = (s32[]{:T(128)}, f32[16,128]{1,0:T(8,128)S(1)}, f32[16,128]{1,0:T(8,128)S(1)}, f32[128,16,64]{0,2,1:T(8,128)S(1)}, s32[2,8,2]{1,2,0:T(2,128)S(1)}, /...) while((s32[]{:T(128)}, f32[16,128]{1,0:T(8,128)S(1)}, ...), condition=%wide.region_5.6_spmd.clone, body=%wide.region_2.5_spmd.clone.sunk | while | flops 560477312 | bytes 64900576 | solution.py:199
  235.8 7.1 fusion.169
  242.9 7.8 fusion.173
  255.0 6.7 fusion.169
  261.6 6.0 fusion.173
  270.6 383.6 %while.37 = (s32[]{:T(128)}, bf16[128,1024]{0,1:T(8,128)(2,1)}, bf16[128,1024]{0,1:T(8,128)(2,1)}, s32[1,2]{1,0:T(1,128)S(1)}, f32[128,1024]{0,1:T(8,128)}, /*in...) while((s32[]{:T(128)}, bf16[128,1024]{0,1:T(8,128)(2,1)}, ...), condition=%wide.region_8.9_spmd.clone, body=%wide.region_7.8_spmd.clone.sunk | while | flops 171196672 | bytes 24436220 | solution.py:271
  278.2 2.9 collective-permute-start.3
  283.4 11.7 collective-permute-done.3
  302.8 1.9 fusion.186
  304.7 3.8 collective-permute-start.3
  309.4 12.9 collective-permute-done.3
  329.7 1.9 fusion.186
  331.6 2.4 collective-permute-start.3
  334.9 13.9 collective-permute-done.3
  356.2 1.9 fusion.186
  359.7 14.7 collective-permute-done.3
  385.2 14.0 collective-permute-done.3
  406.6 1.9 fusion.186
  411.1 12.2 collective-permute-done.3
  430.6 1.9 fusion.186
  432.5 3.7 collective-permute-start.3
  437.1 11.1 collective-permute-done.3
  457.5 4.1 collective-permute-start.3
  462.5 11.6 collective-permute-done.3
  483.4 4.2 collective-permute-start.3
  488.6 11.1 collective-permute-done.3
  508.9 4.1 collective-permute-start.3
  513.9 11.6 collective-permute-done.3
  534.8 4.3 collective-permute-start.3
  540.0 11.1 collective-permute-done.3
  560.4 4.0 collective-permute-start.3
  565.2 11.7 collective-permute-done.3
  586.2 2.5 collective-permute-start.3
  589.7 12.6 collective-permute-done.3
  613.3 13.5 collective-permute-done.3
  637.5 12.9 collective-permute-done.3
  659.8 9.6 collective-permute-done.6
  670.7 2.7 fusion.85
  674.8 10.0 collective-permute-done.5
  685.0 6.4 fusion.81
  693.9 6.1 convolution_add_fusion
  700.0 10.0 convert_reduce_fusion
  710.0 8.2 fusion.105
  718.2 11.0 fusion.83
  733.5 6.4 fusion.112
  739.9 8.3 convolution_add_fusion.2
  749.5 2.4 fusion.73
  753.0 37.2 %all-reduce.4 = (f32[1024]{0:T(1024)S(1)}, f32[1024]{0:T(1024)S(1)}, f32[1024]{0:T(1024)S(1)}, f32[4096]{0:T(1024)S(1)}) all-reduce(f32[1024]{0:T(1024)S(1)} %get-tuple-element.275, f32[1024]{0:T(1024)S(1)} %get-tuple-element.278, f32[1024]{0:T(1024)S(1)} %get-tuple-element.344, ...), channel_id=2, replica_groups=mesh['ctx'=16,'fsdp'=2] {'ctx','fsdp'}, use_global_device_ids=true, to_apply=%region_12.13.clone | all-reduce | flops 7168 | bytes 57344
  792.0 8.7 reduce-scatter.16.cloned.1.call-done
  802.1 138.6 %reduce-scatter.10.cloned.1.call-done = f32[32,1024]{1,0:T(8,128)} async-done(((f32[1024,1024]{1,0:T(8,128)}), f32[32,1024]{1,0:T(8,128)}) %reduce-scatter.10.cloned.1.call-update) | async-done | bytes 131088 | tf_op jit(solution)/shard_map/reduce_scatter | solution.py:315
  940.7 159.3 %reduce-scatter.8.cloned.1.call-done = f32[32,3072]{1,0:T(8,128)} async-done(((f32[1024,3072]{1,0:T(8,128)}), f32[32,3072]{1,0:T(8,128)}) %reduce-scatter.8.cloned.1.call-update) | async-done | bytes 393232 | tf_op jit(solution)/shard_map/reduce_scatter | solution.py:313
  1100.1 184.7 %reduce-scatter.12.cloned.1.call-done = f32[32,4096]{1,0:T(8,128)} async-done(((f32[1024,4096]{1,0:T(8,128)}), f32[32,4096]{1,0:T(8,128)}) %reduce-scatter.12.cloned.1.call-update) | async-done | bytes 524304 | tf_op jit(solution)/shard_map/reduce_scatter | solution.py:317
  1284.8 187.3 %reduce-scatter.14.cloned.1.call-done = f32[128,1024]{1,0:T(8,128)} async-done(((f32[4096,1024]{1,0:T(8,128)}), f32[128,1024]{1,0:T(8,128)}) %reduce-scatter.14.cloned.1.call-update) | async-done | bytes 524304 | tf_op jit(solution)/shard_map/reduce_scatter | solution.py:319
  (706 shorter events, 189.0 us)
Async XLA Ops:
  7.2 21.9 %all-gather.12.cloned.1.call-start = ((), (), s32[]{:S(2)}) async-start(), calls=%async_computation.5 | async-start | bytes 9437184 | tf_op jit(solution)/shard_map/all_gather | solution.py:117
  7.9 69.8 %all-gather.18.cloned.1.call-start = ((), (), s32[]{:S(2)}) async-start(), calls=%async_computation.8 | async-start | bytes 3145728 | tf_op jit(solution)/shard_map/all_gather | solution.py:119
  8.7 126.8 %all-gather.14.cloned.1.call-start = ((), (), s32[]{:S(2)}) async-start(), calls=%async_computation.6 | async-start | bytes 4456448 | tf_op jit(solution)/shard_map/all_gather | solution.py:172
  35.0 177.9 %all-gather.16.cloned.1.call-start = ((), (), s32[]{:S(2)}) async-start(), calls=%async_computation.7 | async-start | bytes 4456448 | tf_op jit(solution)/shard_map/all_gather | solution.py:173
  35.6 658.3 %all-gather.20.cloned.1.call-start = ((), (), s32[]{:S(2)}) async-start(), calls=%async_computation.9 | async-start | bytes 12582912 | tf_op jit(solution)/shard_map/all_gather | solution.py:121
  36.2 663.8 %all-gather.22.cloned.1.call-start = ((), (), s32[]{:S(2)}) async-start(), calls=%async_computation.10 | async-start | bytes 12582912 | tf_op jit(solution)/shard_map/all_gather | solution.py:123
  36.8 764.0 %reduce-scatter.16.cloned.1.call-start = ((), (), s32[]{:S(2)}) async-start(), calls=%async_computation.15 | async-start | bytes 540672
  271.5 27.1 %collective-permute-start = (bf16[128,1024]{0,1:T(8,128)(2,1)S(1)}, bf16[128,1024]{0,1:T(8,128)(2,1)}, u32[]{:S(2)}, u32[]{:S(2)}) collective-permute-start(bf16[128,1024]{0,1:T(8,128)(2,1)S(1)} %copy.96), channel_id=1, source_target_pairs={{30,0},{0,2},{2,4},{4,6},{6,8},{8,10},{10,12},{12,14},{14,16},{16,... | collective-permute-start | bytes 786440 | tf_op jit(solution)/shard_map/while/body/eval_jaxpr/ppermute | solution.py:20
  274.0 24.7 %collective-permute-start.1 = (bf16[128,1024]{0,1:T(8,128)(2,1)S(1)}, bf16[128,1024]{0,1:T(8,128)(2,1)}, u32[]{:S(2)}, u32[]{:S(2)}) collective-permute-start(bf16[128,1024]{0,1:T(8,128)(2,1)S(1)} %copy.97), channel_id=1, source_target_pairs={{30,0},{0,2},{2,4},{4,6},{6,8},{8,10},{10,12},{12,14},{14,16},{16,... | collective-permute-start | bytes 786440 | tf_op jit(solution)/shard_map/while/body/eval_jaxpr/ppermute | solution.py:20
  275.5 23.1 %collective-permute-start.2 = (s32[1,2]{1,0:T(1,128)S(1)}, s32[1,2]{1,0:T(1,128)S(1)}, u32[]{:S(2)}, u32[]{:S(2)}) collective-permute-start(s32[1,2]{1,0:T(1,128)S(1)} %copy.98), channel_id=1, source_target_pairs={{30,0},{0,2},{2,4},{4,6},{6,8},{8,10},{10,12},{12,14},{14,16},{16,... | collective-permute-start | bytes 32 | tf_op jit(solution)/shard_map/while/body/eval_jaxpr/ppermute | solution.py:20
  278.2 16.9 %collective-permute-start.3 = (bf16[128,1024]{0,1:T(8,128)(2,1)}, bf16[128,1024]{0,1:T(8,128)(2,1)}, u32[]{:S(2)}, u32[]{:S(2)}) collective-permute-start(bf16[128,1024]{0,1:T(8,128)(2,1)} %fusion.186), channel_id=1, source_target_pairs={{30,0},{0,2},{2,4},{4,6},{6,8},{8,10},{10,12},{12,14},{14,16},{16,... | collective-permute-start | bytes 786440 | tf_op jit(solution)/shard_map/while/body/eval_jaxpr/ppermute | solution.py:20
  299.6 26.3 %collective-permute-start = (bf16[128,1024]{0,1:T(8,128)(2,1)S(1)}, bf16[128,1024]{0,1:T(8,128)(2,1)}, u32[]{:S(2)}, u32[]{:S(2)}) collective-permute-start(bf16[128,1024]{0,1:T(8,128)(2,1)S(1)} %copy.96), channel_id=1, source_target_pairs={{30,0},{0,2},{2,4},{4,6},{6,8},{8,10},{10,12},{12,14},{14,16},{16,... | collective-permute-start | bytes 786440 | tf_op jit(solution)/shard_map/while/body/eval_jaxpr/ppermute | solution.py:20
  300.6 25.3 %collective-permute-start.1 = (bf16[128,1024]{0,1:T(8,128)(2,1)S(1)}, bf16[128,1024]{0,1:T(8,128)(2,1)}, u32[]{:S(2)}, u32[]{:S(2)}) collective-permute-start(bf16[128,1024]{0,1:T(8,128)(2,1)S(1)} %copy.97), channel_id=1, source_target_pairs={{30,0},{0,2},{2,4},{4,6},{6,8},{8,10},{10,12},{12,14},{14,16},{16,... | collective-permute-start | bytes 786440 | tf_op jit(solution)/shard_map/while/body/eval_jaxpr/ppermute | solution.py:20
  300.9 25.0 %collective-permute-start.2 = (s32[1,2]{1,0:T(1,128)S(1)}, s32[1,2]{1,0:T(1,128)S(1)}, u32[]{:S(2)}, u32[]{:S(2)}) collective-permute-start(s32[1,2]{1,0:T(1,128)S(1)} %copy.98), channel_id=1, source_target_pairs={{30,0},{0,2},{2,4},{4,6},{6,8},{8,10},{10,12},{12,14},{14,16},{16,... | collective-permute-start | bytes 32 | tf_op jit(solution)/shard_map/while/body/eval_jaxpr/ppermute | solution.py:20
  304.7 17.7 %collective-permute-start.3 = (bf16[128,1024]{0,1:T(8,128)(2,1)}, bf16[128,1024]{0,1:T(8,128)(2,1)}, u32[]{:S(2)}, u32[]{:S(2)}) collective-permute-start(bf16[128,1024]{0,1:T(8,128)(2,1)} %fusion.186), channel_id=1, source_target_pairs={{30,0},{0,2},{2,4},{4,6},{6,8},{8,10},{10,12},{12,14},{14,16},{16,... | collective-permute-start | bytes 786440 | tf_op jit(solution)/shard_map/while/body/eval_jaxpr/ppermute | solution.py:20
  326.9 25.5 %collective-permute-start = (bf16[128,1024]{0,1:T(8,128)(2,1)S(1)}, bf16[128,1024]{0,1:T(8,128)(2,1)}, u32[]{:S(2)}, u32[]{:S(2)}) collective-permute-start(bf16[128,1024]{0,1:T(8,128)(2,1)S(1)} %copy.96), channel_id=1, source_target_pairs={{30,0},{0,2},{2,4},{4,6},{6,8},{8,10},{10,12},{12,14},{14,16},{16,... | collective-permute-start | bytes 786440 | tf_op jit(solution)/shard_map/while/body/eval_jaxpr/ppermute | solution.py:20
  327.8 24.5 %collective-permute-start.1 = (bf16[128,1024]{0,1:T(8,128)(2,1)S(1)}, bf16[128,1024]{0,1:T(8,128)(2,1)}, u32[]{:S(2)}, u32[]{:S(2)}) collective-permute-start(bf16[128,1024]{0,1:T(8,128)(2,1)S(1)} %copy.97), channel_id=1, source_target_pairs={{30,0},{0,2},{2,4},{4,6},{6,8},{8,10},{10,12},{12,14},{14,16},{16,... | collective-permute-start | bytes 786440 | tf_op jit(solution)/shard_map/while/body/eval_jaxpr/ppermute | solution.py:20
  327.8 24.5 %collective-permute-start.2 = (s32[1,2]{1,0:T(1,128)S(1)}, s32[1,2]{1,0:T(1,128)S(1)}, u32[]{:S(2)}, u32[]{:S(2)}) collective-permute-start(s32[1,2]{1,0:T(1,128)S(1)} %copy.98), channel_id=1, source_target_pairs={{30,0},{0,2},{2,4},{4,6},{6,8},{8,10},{10,12},{12,14},{14,16},{16,... | collective-permute-start | bytes 32 | tf_op jit(solution)/shard_map/while/body/eval_jaxpr/ppermute | solution.py:20
  331.6 17.2 %collective-permute-start.3 = (bf16[128,1024]{0,1:T(8,128)(2,1)}, bf16[128,1024]{0,1:T(8,128)(2,1)}, u32[]{:S(2)}, u32[]{:S(2)}) collective-permute-start(bf16[128,1024]{0,1:T(8,128)(2,1)} %fusion.186), channel_id=1, source_target_pairs={{30,0},{0,2},{2,4},{4,6},{6,8},{8,10},{10,12},{12,14},{14,16},{16,... | collective-permute-start | bytes 786440 | tf_op jit(solution)/shard_map/while/body/eval_jaxpr/ppermute | solution.py:20
  334.4 17.1 %collective-permute-start.4 = (bf16[128,1024]{0,1:T(8,128)(2,1)S(1)}, bf16[128,1024]{0,1:T(8,128)(2,1)S(1)}, u32[]{:S(2)}, u32[]{:S(2)}) collective-permute-start(bf16[128,1024]{0,1:T(8,128)(2,1)S(1)} %fusion.188), channel_id=1, source_target_pairs={{30,0},{0,2},{2,4},{4,6},{6,8},{8,10},{10,12},{12,14},{14,16},{16,... | collective-permute-start | bytes 786440 | tf_op jit(solution)/shard_map/while/body/eval_jaxpr/ppermute | solution.py:20
  353.3 24.6 %collective-permute-start = (bf16[128,1024]{0,1:T(8,128)(2,1)S(1)}, bf16[128,1024]{0,1:T(8,128)(2,1)}, u32[]{:S(2)}, u32[]{:S(2)}) collective-permute-start(bf16[128,1024]{0,1:T(8,128)(2,1)S(1)} %copy.96), channel_id=1, source_target_pairs={{30,0},{0,2},{2,4},{4,6},{6,8},{8,10},{10,12},{12,14},{14,16},{16,... | collective-permute-start | bytes 786440 | tf_op jit(solution)/shard_map/while/body/eval_jaxpr/ppermute | solution.py:20
  354.3 23.7 %collective-permute-start.1 = (bf16[128,1024]{0,1:T(8,128)(2,1)S(1)}, bf16[128,1024]{0,1:T(8,128)(2,1)}, u32[]{:S(2)}, u32[]{:S(2)}) collective-permute-start(bf16[128,1024]{0,1:T(8,128)(2,1)S(1)} %copy.97), channel_id=1, source_target_pairs={{30,0},{0,2},{2,4},{4,6},{6,8},{8,10},{10,12},{12,14},{14,16},{16,... | collective-permute-start | bytes 786440 | tf_op jit(solution)/shard_map/while/body/eval_jaxpr/ppermute | solution.py:20
  354.3 23.7 %collective-permute-start.2 = (s32[1,2]{1,0:T(1,128)S(1)}, s32[1,2]{1,0:T(1,128)S(1)}, u32[]{:S(2)}, u32[]{:S(2)}) collective-permute-start(s32[1,2]{1,0:T(1,128)S(1)} %copy.98), channel_id=1, source_target_pairs={{30,0},{0,2},{2,4},{4,6},{6,8},{8,10},{10,12},{12,14},{14,16},{16,... | collective-permute-start | bytes 32 | tf_op jit(solution)/shard_map/while/body/eval_jaxpr/ppermute | solution.py:20
  359.1 18.0 %collective-permute-start.4 = (bf16[128,1024]{0,1:T(8,128)(2,1)S(1)}, bf16[128,1024]{0,1:T(8,128)(2,1)S(1)}, u32[]{:S(2)}, u32[]{:S(2)}) collective-permute-start(bf16[128,1024]{0,1:T(8,128)(2,1)S(1)} %fusion.188), channel_id=1, source_target_pairs={{30,0},{0,2},{2,4},{4,6},{6,8},{8,10},{10,12},{12,14},{14,16},{16,... | collective-permute-start | bytes 786440 | tf_op jit(solution)/shard_map/while/body/eval_jaxpr/ppermute | solution.py:20
  379.0 23.8 %collective-permute-start = (bf16[128,1024]{0,1:T(8,128)(2,1)S(1)}, bf16[128,1024]{0,1:T(8,128)(2,1)}, u32[]{:S(2)}, u32[]{:S(2)}) collective-permute-start(bf16[128,1024]{0,1:T(8,128)(2,1)S(1)} %copy.96), channel_id=1, source_target_pairs={{30,0},{0,2},{2,4},{4,6},{6,8},{8,10},{10,12},{12,14},{14,16},{16,... | collective-permute-start | bytes 786440 | tf_op jit(solution)/shard_map/while/body/eval_jaxpr/ppermute | solution.py:20
  379.9 22.9 %collective-permute-start.1 = (bf16[128,1024]{0,1:T(8,128)(2,1)S(1)}, bf16[128,1024]{0,1:T(8,128)(2,1)}, u32[]{:S(2)}, u32[]{:S(2)}) collective-permute-start(bf16[128,1024]{0,1:T(8,128)(2,1)S(1)} %copy.97), channel_id=1, source_target_pairs={{30,0},{0,2},{2,4},{4,6},{6,8},{8,10},{10,12},{12,14},{14,16},{16,... | collective-permute-start | bytes 786440 | tf_op jit(solution)/shard_map/while/body/eval_jaxpr/ppermute | solution.py:20
  379.9 22.9 %collective-permute-start.2 = (s32[1,2]{1,0:T(1,128)S(1)}, s32[1,2]{1,0:T(1,128)S(1)}, u32[]{:S(2)}, u32[]{:S(2)}) collective-permute-start(s32[1,2]{1,0:T(1,128)S(1)} %copy.98), channel_id=1, source_target_pairs={{30,0},{0,2},{2,4},{4,6},{6,8},{8,10},{10,12},{12,14},{14,16},{16,... | collective-permute-start | bytes 32 | tf_op jit(solution)/shard_map/while/body/eval_jaxpr/ppermute | solution.py:20
  384.4 17.5 %collective-permute-start.4 = (bf16[128,1024]{0,1:T(8,128)(2,1)S(1)}, bf16[128,1024]{0,1:T(8,128)(2,1)S(1)}, u32[]{:S(2)}, u32[]{:S(2)}) collective-permute-start(bf16[128,1024]{0,1:T(8,128)(2,1)S(1)} %fusion.188), channel_id=1, source_target_pairs={{30,0},{0,2},{2,4},{4,6},{6,8},{8,10},{10,12},{12,14},{14,16},{16,... | collective-permute-start | bytes 786440 | tf_op jit(solution)/shard_map/while/body/eval_jaxpr/ppermute | solution.py:20
  403.8 23.0 %collective-permute-start = (bf16[128,1024]{0,1:T(8,128)(2,1)S(1)}, bf16[128,1024]{0,1:T(8,128)(2,1)}, u32[]{:S(2)}, u32[]{:S(2)}) collective-permute-start(bf16[128,1024]{0,1:T(8,128)(2,1)S(1)} %copy.96), channel_id=1, source_target_pairs={{30,0},{0,2},{2,4},{4,6},{6,8},{8,10},{10,12},{12,14},{14,16},{16,... | collective-permute-start | bytes 786440 | tf_op jit(solution)/shard_map/while/body/eval_jaxpr/ppermute | solution.py:20
  404.7 22.1 %collective-permute-start.1 = (bf16[128,1024]{0,1:T(8,128)(2,1)S(1)}, bf16[128,1024]{0,1:T(8,128)(2,1)}, u32[]{:S(2)}, u32[]{:S(2)}) collective-permute-start(bf16[128,1024]{0,1:T(8,128)(2,1)S(1)} %copy.97), channel_id=1, source_target_pairs={{30,0},{0,2},{2,4},{4,6},{6,8},{8,10},{10,12},{12,14},{14,16},{16,... | collective-permute-start | bytes 786440 | tf_op jit(solution)/shard_map/while/body/eval_jaxpr/ppermute | solution.py:20
  404.7 22.0 %collective-permute-start.2 = (s32[1,2]{1,0:T(1,128)S(1)}, s32[1,2]{1,0:T(1,128)S(1)}, u32[]{:S(2)}, u32[]{:S(2)}) collective-permute-start(s32[1,2]{1,0:T(1,128)S(1)} %copy.98), channel_id=1, source_target_pairs={{30,0},{0,2},{2,4},{4,6},{6,8},{8,10},{10,12},{12,14},{14,16},{16,... | collective-permute-start | bytes 32 | tf_op jit(solution)/shard_map/while/body/eval_jaxpr/ppermute | solution.py:20
  427.8 24.0 %collective-permute-start = (bf16[128,1024]{0,1:T(8,128)(2,1)S(1)}, bf16[128,1024]{0,1:T(8,128)(2,1)}, u32[]{:S(2)}, u32[]{:S(2)}) collective-permute-start(bf16[128,1024]{0,1:T(8,128)(2,1)S(1)} %copy.96), channel_id=1, source_target_pairs={{30,0},{0,2},{2,4},{4,6},{6,8},{8,10},{10,12},{12,14},{14,16},{16,... | collective-permute-start | bytes 786440 | tf_op jit(solution)/shard_map/while/body/eval_jaxpr/ppermute | solution.py:20
  428.7 23.0 %collective-permute-start.1 = (bf16[128,1024]{0,1:T(8,128)(2,1)S(1)}, bf16[128,1024]{0,1:T(8,128)(2,1)}, u32[]{:S(2)}, u32[]{:S(2)}) collective-permute-start(bf16[128,1024]{0,1:T(8,128)(2,1)S(1)} %copy.97), channel_id=1, source_target_pairs={{30,0},{0,2},{2,4},{4,6},{6,8},{8,10},{10,12},{12,14},{14,16},{16,... | collective-permute-start | bytes 786440 | tf_op jit(solution)/shard_map/while/body/eval_jaxpr/ppermute | solution.py:20
  428.7 23.0 %collective-permute-start.2 = (s32[1,2]{1,0:T(1,128)S(1)}, s32[1,2]{1,0:T(1,128)S(1)}, u32[]{:S(2)}, u32[]{:S(2)}) collective-permute-start(s32[1,2]{1,0:T(1,128)S(1)} %copy.98), channel_id=1, source_target_pairs={{30,0},{0,2},{2,4},{4,6},{6,8},{8,10},{10,12},{12,14},{14,16},{16,... | collective-permute-start | bytes 32 | tf_op jit(solution)/shard_map/while/body/eval_jaxpr/ppermute | solution.py:20
  452.7 24.9 %collective-permute-start = (bf16[128,1024]{0,1:T(8,128)(2,1)S(1)}, bf16[128,1024]{0,1:T(8,128)(2,1)}, u32[]{:S(2)}, u32[]{:S(2)}) collective-permute-start(bf16[128,1024]{0,1:T(8,128)(2,1)S(1)} %copy.96), channel_id=1, source_target_pairs={{30,0},{0,2},{2,4},{4,6},{6,8},{8,10},{10,12},{12,14},{14,16},{16,... | collective-permute-start | bytes 786440 | tf_op jit(solution)/shard_map/while/body/eval_jaxpr/ppermute | solution.py:20
  453.7 23.9 %collective-permute-start.1 = (bf16[128,1024]{0,1:T(8,128)(2,1)S(1)}, bf16[128,1024]{0,1:T(8,128)(2,1)}, u32[]{:S(2)}, u32[]{:S(2)}) collective-permute-start(bf16[128,1024]{0,1:T(8,128)(2,1)S(1)} %copy.97), channel_id=1, source_target_pairs={{30,0},{0,2},{2,4},{4,6},{6,8},{8,10},{10,12},{12,14},{14,16},{16,... | collective-permute-start | bytes 786440 | tf_op jit(solution)/shard_map/while/body/eval_jaxpr/ppermute | solution.py:20
  453.7 23.9 %collective-permute-start.2 = (s32[1,2]{1,0:T(1,128)S(1)}, s32[1,2]{1,0:T(1,128)S(1)}, u32[]{:S(2)}, u32[]{:S(2)}) collective-permute-start(s32[1,2]{1,0:T(1,128)S(1)} %copy.98), channel_id=1, source_target_pairs={{30,0},{0,2},{2,4},{4,6},{6,8},{8,10},{10,12},{12,14},{14,16},{16,... | collective-permute-start | bytes 32 | tf_op jit(solution)/shard_map/while/body/eval_jaxpr/ppermute | solution.py:20
  478.6 24.7 %collective-permute-start = (bf16[128,1024]{0,1:T(8,128)(2,1)S(1)}, bf16[128,1024]{0,1:T(8,128)(2,1)}, u32[]{:S(2)}, u32[]{:S(2)}) collective-permute-start(bf16[128,1024]{0,1:T(8,128)(2,1)S(1)} %copy.96), channel_id=1, source_target_pairs={{30,0},{0,2},{2,4},{4,6},{6,8},{8,10},{10,12},{12,14},{14,16},{16,... | collective-permute-start | bytes 786440 | tf_op jit(solution)/shard_map/while/body/eval_jaxpr/ppermute | solution.py:20
  479.5 23.7 %collective-permute-start.1 = (bf16[128,1024]{0,1:T(8,128)(2,1)S(1)}, bf16[128,1024]{0,1:T(8,128)(2,1)}, u32[]{:S(2)}, u32[]{:S(2)}) collective-permute-start(bf16[128,1024]{0,1:T(8,128)(2,1)S(1)} %copy.97), channel_id=1, source_target_pairs={{30,0},{0,2},{2,4},{4,6},{6,8},{8,10},{10,12},{12,14},{14,16},{16,... | collective-permute-start | bytes 786440 | tf_op jit(solution)/shard_map/while/body/eval_jaxpr/ppermute | solution.py:20
  479.5 23.7 %collective-permute-start.2 = (s32[1,2]{1,0:T(1,128)S(1)}, s32[1,2]{1,0:T(1,128)S(1)}, u32[]{:S(2)}, u32[]{:S(2)}) collective-permute-start(s32[1,2]{1,0:T(1,128)S(1)} %copy.98), channel_id=1, source_target_pairs={{30,0},{0,2},{2,4},{4,6},{6,8},{8,10},{10,12},{12,14},{14,16},{16,... | collective-permute-start | bytes 32 | tf_op jit(solution)/shard_map/while/body/eval_jaxpr/ppermute | solution.py:20
  504.2 24.9 %collective-permute-start = (bf16[128,1024]{0,1:T(8,128)(2,1)S(1)}, bf16[128,1024]{0,1:T(8,128)(2,1)}, u32[]{:S(2)}, u32[]{:S(2)}) collective-permute-start(bf16[128,1024]{0,1:T(8,128)(2,1)S(1)} %copy.96), channel_id=1, source_target_pairs={{30,0},{0,2},{2,4},{4,6},{6,8},{8,10},{10,12},{12,14},{14,16},{16,... | collective-permute-start | bytes 786440 | tf_op jit(solution)/shard_map/while/body/eval_jaxpr/ppermute | solution.py:20
  505.2 23.9 %collective-permute-start.1 = (bf16[128,1024]{0,1:T(8,128)(2,1)S(1)}, bf16[128,1024]{0,1:T(8,128)(2,1)}, u32[]{:S(2)}, u32[]{:S(2)}) collective-permute-start(bf16[128,1024]{0,1:T(8,128)(2,1)S(1)} %copy.97), channel_id=1, source_target_pairs={{30,0},{0,2},{2,4},{4,6},{6,8},{8,10},{10,12},{12,14},{14,16},{16,... | collective-permute-start | bytes 786440 | tf_op jit(solution)/shard_map/while/body/eval_jaxpr/ppermute | solution.py:20
  505.2 23.9 %collective-permute-start.2 = (s32[1,2]{1,0:T(1,128)S(1)}, s32[1,2]{1,0:T(1,128)S(1)}, u32[]{:S(2)}, u32[]{:S(2)}) collective-permute-start(s32[1,2]{1,0:T(1,128)S(1)} %copy.98), channel_id=1, source_target_pairs={{30,0},{0,2},{2,4},{4,6},{6,8},{8,10},{10,12},{12,14},{14,16},{16,... | collective-permute-start | bytes 32 | tf_op jit(solution)/shard_map/while/body/eval_jaxpr/ppermute | solution.py:20
  530.1 24.6 %collective-permute-start = (bf16[128,1024]{0,1:T(8,128)(2,1)S(1)}, bf16[128,1024]{0,1:T(8,128)(2,1)}, u32[]{:S(2)}, u32[]{:S(2)}) collective-permute-start(bf16[128,1024]{0,1:T(8,128)(2,1)S(1)} %copy.96), channel_id=1, source_target_pairs={{30,0},{0,2},{2,4},{4,6},{6,8},{8,10},{10,12},{12,14},{14,16},{16,... | collective-permute-start | bytes 786440 | tf_op jit(solution)/shard_map/while/body/eval_jaxpr/ppermute | solution.py:20
  531.0 23.7 %collective-permute-start.1 = (bf16[128,1024]{0,1:T(8,128)(2,1)S(1)}, bf16[128,1024]{0,1:T(8,128)(2,1)}, u32[]{:S(2)}, u32[]{:S(2)}) collective-permute-start(bf16[128,1024]{0,1:T(8,128)(2,1)S(1)} %copy.97), channel_id=1, source_target_pairs={{30,0},{0,2},{2,4},{4,6},{6,8},{8,10},{10,12},{12,14},{14,16},{16,... | collective-permute-start | bytes 786440 | tf_op jit(solution)/shard_map/while/body/eval_jaxpr/ppermute | solution.py:20
  531.0 23.7 %collective-permute-start.2 = (s32[1,2]{1,0:T(1,128)S(1)}, s32[1,2]{1,0:T(1,128)S(1)}, u32[]{:S(2)}, u32[]{:S(2)}) collective-permute-start(s32[1,2]{1,0:T(1,128)S(1)} %copy.98), channel_id=1, source_target_pairs={{30,0},{0,2},{2,4},{4,6},{6,8},{8,10},{10,12},{12,14},{14,16},{16,... | collective-permute-start | bytes 32 | tf_op jit(solution)/shard_map/while/body/eval_jaxpr/ppermute | solution.py:20
  555.7 24.9 %collective-permute-start = (bf16[128,1024]{0,1:T(8,128)(2,1)S(1)}, bf16[128,1024]{0,1:T(8,128)(2,1)}, u32[]{:S(2)}, u32[]{:S(2)}) collective-permute-start(bf16[128,1024]{0,1:T(8,128)(2,1)S(1)} %copy.96), channel_id=1, source_target_pairs={{30,0},{0,2},{2,4},{4,6},{6,8},{8,10},{10,12},{12,14},{14,16},{16,... | collective-permute-start | bytes 786440 | tf_op jit(solution)/shard_map/while/body/eval_jaxpr/ppermute | solution.py:20
  556.6 23.9 %collective-permute-start.1 = (bf16[128,1024]{0,1:T(8,128)(2,1)S(1)}, bf16[128,1024]{0,1:T(8,128)(2,1)}, u32[]{:S(2)}, u32[]{:S(2)}) collective-permute-start(bf16[128,1024]{0,1:T(8,128)(2,1)S(1)} %copy.97), channel_id=1, source_target_pairs={{30,0},{0,2},{2,4},{4,6},{6,8},{8,10},{10,12},{12,14},{14,16},{16,... | collective-permute-start | bytes 786440 | tf_op jit(solution)/shard_map/while/body/eval_jaxpr/ppermute | solution.py:20
  556.6 23.9 %collective-permute-start.2 = (s32[1,2]{1,0:T(1,128)S(1)}, s32[1,2]{1,0:T(1,128)S(1)}, u32[]{:S(2)}, u32[]{:S(2)}) collective-permute-start(s32[1,2]{1,0:T(1,128)S(1)} %copy.98), channel_id=1, source_target_pairs={{30,0},{0,2},{2,4},{4,6},{6,8},{8,10},{10,12},{12,14},{14,16},{16,... | collective-permute-start | bytes 32 | tf_op jit(solution)/shard_map/while/body/eval_jaxpr/ppermute | solution.py:20
  581.5 24.3 %collective-permute-start = (bf16[128,1024]{0,1:T(8,128)(2,1)S(1)}, bf16[128,1024]{0,1:T(8,128)(2,1)}, u32[]{:S(2)}, u32[]{:S(2)}) collective-permute-start(bf16[128,1024]{0,1:T(8,128)(2,1)S(1)} %copy.96), channel_id=1, source_target_pairs={{30,0},{0,2},{2,4},{4,6},{6,8},{8,10},{10,12},{12,14},{14,16},{16,... | collective-permute-start | bytes 786440 | tf_op jit(solution)/shard_map/while/body/eval_jaxpr/ppermute | solution.py:20
  582.4 23.4 %collective-permute-start.1 = (bf16[128,1024]{0,1:T(8,128)(2,1)S(1)}, bf16[128,1024]{0,1:T(8,128)(2,1)}, u32[]{:S(2)}, u32[]{:S(2)}) collective-permute-start(bf16[128,1024]{0,1:T(8,128)(2,1)S(1)} %copy.97), channel_id=1, source_target_pairs={{30,0},{0,2},{2,4},{4,6},{6,8},{8,10},{10,12},{12,14},{14,16},{16,... | collective-permute-start | bytes 786440 | tf_op jit(solution)/shard_map/while/body/eval_jaxpr/ppermute | solution.py:20
  582.4 23.4 %collective-permute-start.2 = (s32[1,2]{1,0:T(1,128)S(1)}, s32[1,2]{1,0:T(1,128)S(1)}, u32[]{:S(2)}, u32[]{:S(2)}) collective-permute-start(s32[1,2]{1,0:T(1,128)S(1)} %copy.98), channel_id=1, source_target_pairs={{30,0},{0,2},{2,4},{4,6},{6,8},{8,10},{10,12},{12,14},{14,16},{16,... | collective-permute-start | bytes 32 | tf_op jit(solution)/shard_map/while/body/eval_jaxpr/ppermute | solution.py:20
  606.8 23.5 %collective-permute-start = (bf16[128,1024]{0,1:T(8,128)(2,1)S(1)}, bf16[128,1024]{0,1:T(8,128)(2,1)}, u32[]{:S(2)}, u32[]{:S(2)}) collective-permute-start(bf16[128,1024]{0,1:T(8,128)(2,1)S(1)} %copy.96), channel_id=1, source_target_pairs={{30,0},{0,2},{2,4},{4,6},{6,8},{8,10},{10,12},{12,14},{14,16},{16,... | collective-permute-start | bytes 786440 | tf_op jit(solution)/shard_map/while/body/eval_jaxpr/ppermute | solution.py:20
  607.8 22.6 %collective-permute-start.1 = (bf16[128,1024]{0,1:T(8,128)(2,1)S(1)}, bf16[128,1024]{0,1:T(8,128)(2,1)}, u32[]{:S(2)}, u32[]{:S(2)}) collective-permute-start(bf16[128,1024]{0,1:T(8,128)(2,1)S(1)} %copy.97), channel_id=1, source_target_pairs={{30,0},{0,2},{2,4},{4,6},{6,8},{8,10},{10,12},{12,14},{14,16},{16,... | collective-permute-start | bytes 786440 | tf_op jit(solution)/shard_map/while/body/eval_jaxpr/ppermute | solution.py:20
  607.8 22.5 %collective-permute-start.2 = (s32[1,2]{1,0:T(1,128)S(1)}, s32[1,2]{1,0:T(1,128)S(1)}, u32[]{:S(2)}, u32[]{:S(2)}) collective-permute-start(s32[1,2]{1,0:T(1,128)S(1)} %copy.98), channel_id=1, source_target_pairs={{30,0},{0,2},{2,4},{4,6},{6,8},{8,10},{10,12},{12,14},{14,16},{16,... | collective-permute-start | bytes 32 | tf_op jit(solution)/shard_map/while/body/eval_jaxpr/ppermute | solution.py:20
  612.7 16.8 %collective-permute-start.4 = (bf16[128,1024]{0,1:T(8,128)(2,1)S(1)}, bf16[128,1024]{0,1:T(8,128)(2,1)S(1)}, u32[]{:S(2)}, u32[]{:S(2)}) collective-permute-start(bf16[128,1024]{0,1:T(8,128)(2,1)S(1)} %fusion.188), channel_id=1, source_target_pairs={{30,0},{0,2},{2,4},{4,6},{6,8},{8,10},{10,12},{12,14},{14,16},{16,... | collective-permute-start | bytes 786440 | tf_op jit(solution)/shard_map/while/body/eval_jaxpr/ppermute | solution.py:20
  631.3 22.7 %collective-permute-start = (bf16[128,1024]{0,1:T(8,128)(2,1)S(1)}, bf16[128,1024]{0,1:T(8,128)(2,1)}, u32[]{:S(2)}, u32[]{:S(2)}) collective-permute-start(bf16[128,1024]{0,1:T(8,128)(2,1)S(1)} %copy.96), channel_id=1, source_target_pairs={{30,0},{0,2},{2,4},{4,6},{6,8},{8,10},{10,12},{12,14},{14,16},{16,... | collective-permute-start | bytes 786440 | tf_op jit(solution)/shard_map/while/body/eval_jaxpr/ppermute | solution.py:20
  632.2 21.7 %collective-permute-start.1 = (bf16[128,1024]{0,1:T(8,128)(2,1)S(1)}, bf16[128,1024]{0,1:T(8,128)(2,1)}, u32[]{:S(2)}, u32[]{:S(2)}) collective-permute-start(bf16[128,1024]{0,1:T(8,128)(2,1)S(1)} %copy.97), channel_id=1, source_target_pairs={{30,0},{0,2},{2,4},{4,6},{6,8},{8,10},{10,12},{12,14},{14,16},{16,... | collective-permute-start | bytes 786440 | tf_op jit(solution)/shard_map/while/body/eval_jaxpr/ppermute | solution.py:20
  632.3 21.7 %collective-permute-start.2 = (s32[1,2]{1,0:T(1,128)S(1)}, s32[1,2]{1,0:T(1,128)S(1)}, u32[]{:S(2)}, u32[]{:S(2)}) collective-permute-start(s32[1,2]{1,0:T(1,128)S(1)} %copy.98), channel_id=1, source_target_pairs={{30,0},{0,2},{2,4},{4,6},{6,8},{8,10},{10,12},{12,14},{14,16},{16,... | collective-permute-start | bytes 32 | tf_op jit(solution)/shard_map/while/body/eval_jaxpr/ppermute | solution.py:20
  636.4 16.8 %collective-permute-start.4 = (bf16[128,1024]{0,1:T(8,128)(2,1)S(1)}, bf16[128,1024]{0,1:T(8,128)(2,1)S(1)}, u32[]{:S(2)}, u32[]{:S(2)}) collective-permute-start(bf16[128,1024]{0,1:T(8,128)(2,1)S(1)} %fusion.188), channel_id=1, source_target_pairs={{30,0},{0,2},{2,4},{4,6},{6,8},{8,10},{10,12},{12,14},{14,16},{16,... | collective-permute-start | bytes 786440 | tf_op jit(solution)/shard_map/while/body/eval_jaxpr/ppermute | solution.py:20
  670.7 270.1 %reduce-scatter.10.cloned.1.call-start = ((), (), s32[]{:S(2)}) async-start(), calls=%async_computation.12 | async-start | bytes 4325376 | tf_op jit(solution)/shard_map/reduce_scatter | solution.py:315
  673.5 426.6 %reduce-scatter.8.cloned.1.call-start = ((), (), s32[]{:S(2)}) async-start(), calls=%async_computation.11 | async-start | bytes 12976128 | tf_op jit(solution)/shard_map/reduce_scatter | solution.py:313
  691.5 593.3 %reduce-scatter.12.cloned.1.call-start = ((), (), s32[]{:S(2)}) async-start(), calls=%async_computation.13 | async-start | bytes 17301504 | tf_op jit(solution)/shard_map/reduce_scatter | solution.py:317
  718.2 753.9 %reduce-scatter.14.cloned.1.call-start = ((), (), s32[]{:S(2)}) async-start(), calls=%async_computation.14 | async-start | bytes 17301504 | tf_op jit(solution)/shard_map/reduce_scatter | solution.py:319
  (92 other events, 1653.3 us)
Sparse Core Ops, SparseCore 0:
  9.5 19.4 all-gather.11
  30.6 11.7 all-gather.17
  45.1 90.3 all-gather.13
  138.7 74.2 all-gather.15
  214.4 18.4 all-gather.19
  234.3 21.0 all-gather.21
  670.8 129.9 reduce-scatter.15
  803.7 136.9 reduce-scatter.9
  948.4 151.6 reduce-scatter.7
  1102.8 181.9 reduce-scatter.11
  1287.7 184.3 reduce-scatter.13
where the time goes:
time: 1490 us; the launch traced here: 1480 us
  waiting for transfers between devices  1030 us (69%)
  matrix products  132 us (9%)
  blocking collectives  88.8 us (6%)
  local copies, waits for them, and re-layouts  83.1 us (6%)
  other arithmetic  78.8 us (5%)
  starting transfers between devices  46.6 us (3%)
    ppermute x77, waiting for transfers between devices, from_behind(): return lax.ppermute(block, axis, route)  220 us
    reduce_scatter x1, waiting for transfers between devices, body(): lax.psum_scatter(term_down_w, ('ctx', 'fsdp'), scatter_dimension=0, tiled...  187 us
    reduce_scatter x1, waiting for transfers between devices, body(): lax.psum_scatter(term_in_w, ('ctx', 'fsdp'), scatter_dimension=0, tiled=T...  185 us
    reduce_scatter x1, waiting for transfers between devices, body(): lax.psum_scatter(term_qkv, ('ctx', 'fsdp'), scatter_dimension=0, tiled=True)  159 us
    reduce_scatter x1, waiting for transfers between devices, body(): lax.psum_scatter(term_out_w, ('ctx', 'fsdp'), scatter_dimension=0, tiled=...  139 us
    all_gather x1, waiting for transfers between devices, body(): piece_values = lax.all_gather(value_rows, 'ctx', axis=0, tiled=True)  63.5 us
    all_gather x1, waiting for transfers between devices, body(): piece_keys = lax.all_gather(key_flat, 'ctx', axis=0, tiled=True)  54.2 us
    ppermute x77, starting transfers between devices, from_behind(): return lax.ppermute(block, axis, route)  46.1 us
  transfers between devices with their start and end apart: 88, of which 40 were waited for; matrix products, arithmetic and copies ran while one was open for 19% of the time, Pallas kernels for 0%

commit v1 on v0

--- a/solution.py
+++ b/solution.py
@@ -4,6 +4,8 @@
 import jax
 import jax.numpy as jnp
 from jax import lax
+from jax.experimental import pallas as pl
+from jax.experimental.pallas import tpu as pltpu
 from jax.sharding import PartitionSpec as P
 
 HEADS = 16
@@ -335,9 +337,737 @@
     )
 
 
+LINES = 4
+ACROSS = HEADS // LINES
+F32 = jnp.float32
+BF16 = jnp.bfloat16
+VMEM_LIMIT = 56 * 1024 * 1024
+VEC = 16
+
+
+def dot(left, right):
+    return jnp.dot(left, right, preferred_element_type=F32)
+
+
+def dot_nt(left, right):
+    return lax.dot_general(left, right, (((1,), (1,)), ((), ())), preferred_element_type=F32)
+
+
+def call(kernel, out_shapes, scratch, flops, *operands):
+    specs = [
+        pl.BlockSpec(memory_space=pltpu.SMEM if x.dtype == jnp.int32 else pltpu.VMEM)
+        for x in operands
+    ]
+    outs = [jax.ShapeDtypeStruct(s, d) for s, d in out_shapes]
+    moved = sum(x.size * x.dtype.itemsize for x in list(operands) + outs)
+    return pl.pallas_call(
+        kernel,
+        out_shape=outs,
+        in_specs=specs,
+        out_specs=[pl.BlockSpec(memory_space=pltpu.VMEM) for _ in outs],
+        scratch_shapes=scratch,
+        compiler_params=pltpu.CompilerParams(vmem_limit_bytes=VMEM_LIMIT),
+        cost_estimate=pl.CostEstimate(flops=flops, bytes_accessed=moved, transcendentals=0),
+    )(*operands)
+
+
+def reorder(x, place):
+    upper, lower = x[:, :128], x[:, 128:]
+    far = (place & 2) != 0
+    near = (place & 1) != 0
+    first = jnp.where(far, lower, upper)
+    second = jnp.where(far, upper, lower)
+    first = jnp.where(near, pltpu.roll(first, 64, 1), first)
+    second = jnp.where(near, pltpu.roll(second, 64, 1), second)
+    return first, second
+
+
+def left_lanes(rows):
+    return lax.broadcasted_iota(jnp.int32, (rows, 128), 1) < 64
+
+
+def pair_heads(one, two, slot):
+    keep = left_lanes(one.shape[0])
+    if slot % 2 == 0:
+        return jnp.where(keep, one, pltpu.roll(two, 64, 1))
+    return jnp.where(keep, pltpu.roll(one, 64, 1), two)
+
+
+def fold_rows(chunk, slot):
+    rows = chunk.shape[0] // 2
+    return pair_heads(chunk[:rows], chunk[rows:], slot)
+
+
+def unfold_pair(even, odd):
+    keep = left_lanes(even.shape[0])
+    top = jnp.where(keep, even, pltpu.roll(odd, 64, 1))
+    bottom = jnp.where(keep, pltpu.roll(even, 64, 1), odd)
+    return jnp.concatenate([top, bottom], 0)
+
+
+def normalise(rows):
+    x = rows.astype(F32)
+    centred = x - jnp.mean(x, -1, keepdims=True)
+    inverse = lax.rsqrt(jnp.mean(centred * centred, -1, keepdims=True) + epsilon)
+    return centred * inverse, inverse
+
+
+def project_kernel(at, t0, t1, t2, t3, gain, shift, bias_q, bias_v, w_own, w_twin, *outs):
+    slots, ln_ref, lnt_ref = outs[:4], outs[4], outs[5]
+    place, core = at[1], at[2]
+    rows = t0.shape[0]
+    half = w_own.shape[0]
+    for k, ref in enumerate((t0, t1, t2, t3)):
+        normed, _ = normalise(ref[...])
+        low = (normed * gain[...] + shift[...]).astype(BF16)
+        ln_ref[rows * k : rows * (k + 1), :] = low
+    mine = pl.ds(pl.multiple_of(core * half, half), half)
+    other = pl.ds(pl.multiple_of((1 - core) * half, half), half)
+
+    def part(index):
+        cols = slice(256 * index, 256 * (index + 1))
+        return dot(ln_ref[:, mine], w_own[:, cols]) + dot(ln_ref[:, other], w_twin[:, cols])
+
+    q_chunks = reorder(part(0) + bias_q[...], place)
+    k_chunks = reorder(part(1), place)
+    v_chunks = reorder(part(2) + bias_v[...], place)
+    total = ln_ref.shape[0]
+    for slot in range(4):
+        pair = slot // 2
+        slots[slot][:total, :] = pair_heads(q_chunks[pair], k_chunks[pair], slot).astype(BF16)
+        slots[slot][total:, :] = fold_rows(v_chunks[pair], slot).astype(BF16)
+    lnt_ref[...] = ln_ref[...].T
+
+
+def back_rows_kernel(at, c0, c1, c2, c3, w_out, s0, s1, s2, s3):
+    cot = jnp.concatenate([c0[...], c1[...], c2[...], c3[...]], 0)
+    chunks = reorder(dot_nt(cot, w_out[...]), at[1])
+    for slot, ref in enumerate((s0, s1, s2, s3)):
+        ref[...] = fold_rows(chunks[slot // 2], slot).astype(BF16)
+
+
+def sort_rows(table, refs, target, rows, base, folded):
+    for j in range(4):
+        for i in range(8):
+            dest = pl.ds(pl.multiple_of(table[j * 8 + i] * 64, 64), 64)
+            if folded:
+                source = base + 64 * (i % 4)
+                lanes = slice(0, 64) if i < 4 else slice(64, 128)
+                target[dest, :] = refs[j][source : source + 64, lanes]
+            else:
+                target[dest, :] = refs[j][base + 64 * i : base + 64 * (i + 1), :]
+
+
+def turn(x, cosine, low_sine, high_sine):
+    return x * cosine + pltpu.roll(x, 120, 1) * low_sine + pltpu.roll(x, 8, 1) * high_sine
+
+
+TILE = 256
+
+
+def scores_of(qk_ref, i):
+    rows = slice(TILE * i, TILE * (i + 1))
+    queries = jnp.where(left_lanes(TILE), qk_ref[rows, :], jnp.zeros((), BF16))
+    queries = queries * jnp.asarray(HEAD_DIM ** (-0.5), BF16)
+    return queries
+
+
+def allowed_tile():
+    row = lax.broadcasted_iota(jnp.int32, (TILE, TILE), 0)
+    col = lax.broadcasted_iota(jnp.int32, (TILE, TILE), 1)
+    return row >= col
+
+
+def attend_kernel(table, r0, r1, r2, r3, cosine, low_sine, high_sine, *rest):
+    a0, a1, a2, a3, qk_ref, kq_ref, v_ref, att_ref, lse_ref, raw = rest
+    refs = (r0, r1, r2, r3)
+    count = qk_ref.shape[0]
+    lines = count // 4
+    sort_rows(table, refs, raw, lines, 0, False)
+    sort_rows(table, refs, v_ref, lines, lines, True)
+    for i in range(count // TILE):
+        rows = slice(TILE * i, TILE * (i + 1))
+        turned = turn(
+            raw[rows, :].astype(F32), cosine[rows, :], low_sine[rows, :], high_sine[rows, :]
+        )
+        qk_ref[rows, :] = turned.astype(BF16)
+        kq_ref[rows, :] = pltpu.roll(turned, 64, 1).astype(BF16)
+    mask = allowed_tile()
+    for i in range(count // TILE):
+        rows = slice(TILE * i, TILE * (i + 1))
+        keys = TILE * (i + 1)
+        scores = dot_nt(scores_of(qk_ref, i), kq_ref[:keys, :])
+        last = jnp.where(mask, scores[:, keys - TILE :], -1e30)
+        scores = last if i == 0 else jnp.concatenate([scores[:, : keys - TILE], last], 1)
+        top = jnp.max(scores, -1, keepdims=True)
+        weights = jnp.exp(scores - top)
+        total = jnp.sum(weights, -1, keepdims=True)
+        weighted = dot(weights.astype(BF16), v_ref[:keys, :])
+        att_ref[rows, :] = weighted / total
+        lse_ref[rows, :] = top + jnp.log(total)
+    for j, out in enumerate((a0, a1, a2, a3)):
+        for i in range(8):
+            source = pl.ds(pl.multiple_of(table[j * 8 + i] * 64, 64), 64)
+            lanes = slice(0, 64) if i < 4 else slice(64, 128)
+            out[64 * (i % 4) : 64 * (i % 4) + 64, lanes] = att_ref[source, :].astype(BF16)
+
+
+def attend_back_kernel(table, g0, g1, g2, g3, qk_ref, kq_ref, v_ref, att_ref, lse_ref, *rest):
+    cosine, low_sine, high_sine, o0, o1, o2, o3, sums, ga_ref, kt_ref, vt_ref, gqk, gv = rest
+    count = qk_ref.shape[0]
+    lines = count // 4
+    sort_rows(table, (g0, g1, g2, g3), ga_ref, lines, 0, True)
+    mask = allowed_tile()
+    kt_ref[...] = jnp.zeros_like(kt_ref)
+    vt_ref[...] = jnp.zeros_like(vt_ref)
+    for i in range(count // TILE):
+        rows = slice(TILE * i, TILE * (i + 1))
+        keys = TILE * (i + 1)
+        queries = scores_of(qk_ref, i)
+        scores = dot_nt(queries, kq_ref[:keys, :])
+        last = jnp.where(mask, scores[:, keys - TILE :], -1e30)
+        scores = last if i == 0 else jnp.concatenate([scores[:, : keys - TILE], last], 1)
+        probs = jnp.exp(scores - lse_ref[rows, :])
+        grad_rows = ga_ref[rows, :]
+        delta = jnp.sum(grad_rows.astype(F32) * att_ref[rows, :], -1, keepdims=True)
+        grad_probs = dot_nt(grad_rows, v_ref[:keys, :])
+        grad_scores = (probs * (grad_probs - delta)).astype(BF16)
+        gqk[rows, :] = dot(grad_scores, kq_ref[:keys, :]) * HEAD_DIM ** (-0.5)
+        vt_ref[:, :keys] += dot(grad_rows.astype(F32).T.astype(BF16), probs.astype(BF16))
+        kt_ref[:, :keys] += dot(queries.astype(F32).T.astype(BF16), grad_scores)
+    sum_q = jnp.zeros((1, 128), F32)
+    sum_v = jnp.zeros((1, 64), F32)
+    for i in range(count // TILE):
+        rows = slice(TILE * i, TILE * (i + 1))
+        grad_keys = pltpu.roll(kt_ref[:, rows].T, 64, 1)
+        both = jnp.where(left_lanes(TILE), gqk[rows, :], grad_keys)
+        both = turn(both, cosine[rows, :], -low_sine[rows, :], -high_sine[rows, :])
+        both = both.astype(BF16).astype(F32)
+        values = vt_ref[:, rows].T.astype(BF16).astype(F32)
+        gqk[rows, :] = both
+        gv[rows, :] = values
+        sum_q = sum_q + jnp.sum(both, 0, keepdims=True)
+        sum_v = sum_v + jnp.sum(values, 0, keepdims=True)
+    sums[...] = jnp.zeros_like(sums)
+    sums[0:1, :64] = sum_q[:, :64]
+    sums[1:2, :64] = sum_v
+    for j, out in enumerate((o0, o1, o2, o3)):
+        for i in range(8):
+            source = pl.ds(pl.multiple_of(table[j * 8 + i] * 64, 64), 64)
+            lanes = slice(0, 64) if i < 4 else slice(64, 128)
+            out[64 * i : 64 * (i + 1), :] = gqk[source, :].astype(BF16)
+            base = lines + 64 * (i % 4)
+            out[base : base + 64, lanes] = gv[source, :].astype(BF16)
+
+
+def feed_kernel(at, ln, w_own, w_twin, bias, w_down, hidden_ref, act_ref, actt_ref, low_ref):
+    core = at[2]
+    half = w_own.shape[0]
+    mine = pl.ds(pl.multiple_of(core * half, half), half)
+    other = pl.ds(pl.multiple_of((1 - core) * half, half), half)
+    for f in range(4):
+        cols = slice(256 * f, 256 * (f + 1))
+        hidden = dot(ln[:, mine], w_own[:, cols]) + dot(ln[:, other], w_twin[:, cols])
+        hidden = hidden + bias[:, cols]
+        hidden_ref[:, cols] = hidden
+        active = 0.5 * hidden * (1.0 + lax.erf(hidden * 0.7071067811865476))
+        act_ref[:, cols] = active.astype(BF16)
+        actt_ref[cols, :] = active.astype(BF16).T
+    for f in range(4):
+        cols = slice(256 * f, 256 * (f + 1))
+        low_ref[:, cols] = dot(act_ref[...], w_down[:, cols])
+
+
+def feed_back_kernel(at, c0, c1, c2, c3, hidden, actt, lnt, w_own, w_twin, w_down, *rest):
+    send, keep, low_ref, gh_ref, chunk_ref = rest
+    line, core = at[0], at[2]
+    half = w_own.shape[0]
+    cot = jnp.concatenate([c0[...], c1[...], c2[...], c3[...]], 0)
+    block = send.shape[0] // 4
+    sums = jnp.zeros((1, 1024), F32)
+    cot_sum = jnp.sum(cot.astype(F32), 0, keepdims=True)
+    bias_sums = []
+    for f in range(4):
+        cols = slice(256 * f, 256 * (f + 1))
+        grad_active = dot_nt(cot, w_down[cols, :])
+        h = hidden[:, cols]
+        slope = 0.5 * (1.0 + lax.erf(h * 0.7071067811865476)) + h * jnp.exp(
+            -0.5 * h * h
+        ) * 0.3989422804014327
+        grad_hidden = (slope * grad_active).astype(BF16)
+        gh_ref[:, cols] = grad_hidden
+        bias_sums.append(jnp.sum(grad_hidden.astype(F32), 0, keepdims=True))
+    for f in range(4):
+        chunk_ref[...] = dot(actt[256 * f : 256 * (f + 1), :], cot)
+        base = block * f
+        send[base : base + 128, :] = chunk_ref[
+            pl.ds(pl.multiple_of((1 - core) * 128, 128), 128), :
+        ].astype(BF16)
+        keep[base : base + 128, :] = chunk_ref[pl.ds(pl.multiple_of(core * 128, 128), 128), :]
+    for z in range(4):
+        chunk_ref[...] = dot(lnt[256 * z : 256 * (z + 1), :], gh_ref[...])
+        for f in range(4):
+            base = block * f + 128 + 32 * z
+            send[base : base + 32, :] = chunk_ref[
+                pl.ds(pl.multiple_of(64 * f + 32 * (1 - core), 32), 32), :
+            ].astype(BF16)
+            keep[base : base + 32, :] = chunk_ref[
+                pl.ds(pl.multiple_of(64 * f + 32 * core, 32), 32), :
+            ]
+    picked = jnp.where(
+        line < 2,
+        jnp.where(line == 0, cot_sum[:, 0:256], cot_sum[:, 256:512]),
+        jnp.where(line == 2, cot_sum[:, 512:768], cot_sum[:, 768:1024]),
+    )
+    zero = jnp.zeros((1, 640), F32)
+    for f in range(4):
+        even, odd = bias_sums[f][:, :128], bias_sums[f][:, 128:]
+        first = core == 0
+        base = block * f + 256
+        given = jnp.concatenate([jnp.where(first, odd, even), picked, zero], 1)
+        kept = jnp.concatenate([jnp.where(first, even, odd), picked, zero], 1)
+        send[base : base + VEC, :] = jnp.broadcast_to(given, (VEC, 1024)).astype(BF16)
+        keep[base : base + VEC, :] = jnp.broadcast_to(kept, (VEC, 1024))
+    mine = pl.ds(pl.multiple_of(core * half, half), half)
+    other = pl.ds(pl.multiple_of((1 - core) * half, half), half)
+    low_ref[:, mine] = dot_nt(gh_ref[...], w_own[...])
+    low_ref[:, other] = dot_nt(gh_ref[...], w_twin[...])
+
+
+def add_twin_kernel(at, keep, received, o0, o1, o2, o3):
+    block = o0.shape[0]
+    for slot, ref in enumerate((o0, o1, o2, o3)):
+        rows = pl.ds(pl.multiple_of((at[1] ^ slot) * block, 16), block)
+        ref[...] = (keep[rows, :] + received[rows, :].astype(F32)).astype(ref.dtype)
+
+
+def feed_sum_kernel(at, own, r1, r2, r3, down_ref, vec_ref, i0, i1, i2, i3):
+    def total(rows):
+        return (
+            own[rows, :]
+            + r1[rows, :].astype(F32)
+            + r2[rows, :].astype(F32)
+            + r3[rows, :].astype(F32)
+        )
+
+    down_ref[...] = total(slice(0, 128))
+    vec_ref[...] = total(slice(256, 264))
+    for slot, ref in enumerate((i0, i1, i2, i3)):
+        rows = pl.ds(pl.multiple_of(128 + 32 * (at[0] ^ slot), 16), 32)
+        ref[...] = total(rows).astype(ref.dtype)
+
+
+def branch_kernel(at, a0, a1, a2, a3, low, w_out, c0, c1, c2, c3, *rest):
+    s0, s1, s2, s3, send, keep, chunk_ref = rest
+    place, core = at[1], at[2]
+    chunks = (
+        unfold_pair(a0[...].astype(F32), a1[...].astype(F32)),
+        unfold_pair(a2[...].astype(F32), a3[...].astype(F32)),
+    )
+    attended = jnp.concatenate(reorder(jnp.concatenate(chunks, 1), place), 1).astype(BF16)
+    rows = s0.shape[0]
+    for k, ref in enumerate((s0, s1, s2, s3)):
+        part = slice(rows * k, rows * (k + 1))
+        ref[...] = (low[part, :] + dot(attended[part, :], w_out[...])).astype(ref.dtype)
+    cot = jnp.concatenate([c0[...], c1[...], c2[...], c3[...]], 0)
+    chunk_ref[...] = dot(attended.T, cot)
+    for f in range(4):
+        send[32 * f : 32 * (f + 1), :] = chunk_ref[
+            pl.ds(pl.multiple_of(64 * f + 32 * (1 - core), 32), 32), :
+        ].astype(BF16)
+        keep[32 * f : 32 * (f + 1), :] = chunk_ref[
+            pl.ds(pl.multiple_of(64 * f + 32 * core, 32), 32), :
+        ]
+
+
+def grads_kernel(at, g0, g1, g2, g3, low, t0, t1, t2, t3, lnt, w_own, w_twin, *rest):
+    s0, s1, s2, s3, send, keep, g_ref, low_ref, chunk_ref = rest
+    place, core = at[1], at[2]
+    half = w_own.shape[0]
+    rows = t0.shape[0]
+    total = 4 * rows
+    parts = [ref[...].astype(F32) for ref in (g0, g1, g2, g3)]
+    keep_left = left_lanes(total)
+    q_chunks, k_chunks, v_chunks = [], [], []
+    for pair in range(2):
+        even, odd = parts[2 * pair][:total], parts[2 * pair + 1][:total]
+        q_chunks.append(jnp.where(keep_left, even, pltpu.roll(odd, 64, 1)))
+        k_chunks.append(jnp.where(keep_left, pltpu.roll(even, 64, 1), odd))
+        v_chunks.append(unfold_pair(parts[2 * pair][total:], parts[2 * pair + 1][total:]))
+    for index, chunks in enumerate((q_chunks, k_chunks, v_chunks)):
+        first, second = reorder(jnp.concatenate(chunks, 1), place)
+        g_ref[:, 256 * index : 256 * index + 128] = first.astype(BF16)
+        g_ref[:, 256 * index + 128 : 256 * index + 256] = second.astype(BF16)
+    mine = pl.ds(pl.multiple_of(core * half, half), half)
+    other = pl.ds(pl.multiple_of((1 - core) * half, half), half)
+    low_ref[:, mine] = low[:, mine] + dot_nt(g_ref[...], w_own[...])
+    low_ref[:, other] = low[:, other] + dot_nt(g_ref[...], w_twin[...])
+    sum_gain = jnp.zeros((1, 1024), F32)
+    sum_bias = jnp.zeros((1, 1024), F32)
+    for k, (ref, out) in enumerate(zip((t0, t1, t2, t3), (s0, s1, s2, s3))):
+        grad = low_ref[rows * k : rows * (k + 1), :]
+        out[...] = grad.astype(out.dtype)
+        normed, _ = normalise(ref[...])
+        sum_gain = sum_gain + jnp.sum(grad * normed, 0, keepdims=True)
+        sum_bias = sum_bias + jnp.sum(grad, 0, keepdims=True)
+    block = send.shape[0] // 4
+    for z in range(4):
+        chunk_ref[...] = dot(lnt[256 * z : 256 * (z + 1), :], g_ref[...])
+        for f in range(4):
+            base = block * f + 32 * z
+            send[base : base + 32, :] = chunk_ref[
+                pl.ds(pl.multiple_of(64 * f + 32 * (1 - core), 32), 32), :
+            ].astype(BF16)
+            keep[base : base + 32, :] = chunk_ref[
+                pl.ds(pl.multiple_of(64 * f + 32 * core, 32), 32), :
+            ]
+    zero = jnp.zeros((1, 512), F32)
+    vec = jnp.concatenate(
+        [
+            sum_gain[:, :768],
+            sum_bias[:, :768],
+            jnp.concatenate([sum_gain[:, 768:], zero], 1),
+            jnp.concatenate([sum_bias[:, 768:], zero], 1),
+            jnp.zeros((VEC - 4, 768), F32),
+        ],
+        0,
+    )
+    for f in range(4):
+        base = block * f + 128
+        send[base : base + VEC, :] = vec.astype(BF16)
+        keep[base : base + VEC, :] = vec
+
+
+def grad_sum_kernel(at, own, r1, r2, r3, i0, i1, i2, i3):
+    def total(rows):
+        return (
+            own[rows, :]
+            + r1[rows, :].astype(F32)
+            + r2[rows, :].astype(F32)
+            + r3[rows, :].astype(F32)
+        )
+
+    vec = total(slice(128, 128 + VEC))
+    for slot, ref in enumerate((i0, i1, i2, i3)):
+        rows = pl.ds(pl.multiple_of(32 * (at[0] ^ slot), 16), 32)
+        ref[:32, :] = total(rows).astype(ref.dtype)
+        ref[32:, :] = vec.astype(ref.dtype)
+
+
+def out_sum_kernel(own, r1, r2, r3, out):
+    out[...] = own[...] + r1[...].astype(F32) + r2[...].astype(F32) + r3[...].astype(F32)
+
+
+def join_in_kernel(at, i0, i1, i2, i3, out):
+    for slot, ref in enumerate((i0, i1, i2, i3)):
+        cols = pl.ds(pl.multiple_of((at[0] ^ slot) * 1024, 1024), 1024)
+        out[:, cols] = ref[...].astype(F32)
+
+
+def join_qkv_kernel(at, i0, i1, i2, i3, out, vec_ref):
+    vec = jnp.zeros((VEC, 768), F32)
+    for slot, ref in enumerate((i0, i1, i2, i3)):
+        for part in range(3):
+            cols = pl.ds(pl.multiple_of(1024 * part + (at[0] ^ slot) * 256, 256), 256)
+            out[:, cols] = ref[:32, 256 * part : 256 * (part + 1)].astype(F32)
+        vec = vec + ref[32:, :].astype(F32)
+    vec_ref[...] = vec
+
+
+def layer_kernel(own, r1, r2, r3, tokens, b_out, b_down, out):
+    total = own[...] + r1[...].astype(F32) + r2[...].astype(F32) + r3[...].astype(F32)
+    total = total + tokens[...].astype(F32) + b_out[...] + b_down[...]
+    out[...] = total.astype(BF16)
+
+
+def tokens_kernel(own, r1, r2, r3, tokens, cot, gain, out):
+    grad_ln = own[...] + r1[...].astype(F32) + r2[...].astype(F32) + r3[...].astype(F32)
+    normed, inverse = normalise(tokens[...])
+    g = grad_ln * gain[...]
+    grad = inverse * (
+        g - jnp.mean(g, -1, keepdims=True) - normed * jnp.mean(g * normed, -1, keepdims=True)
+    )
+    out[...] = (cot[...].astype(F32) + grad).astype(BF16)
+
+
+def turn_tables(count):
+    cosine, sine_part = tables(jnp.arange(count, dtype=jnp.int32))
+    half_rot = ROT // 2
+    cosine, sine_part = cosine[:, :half_rot], sine_part[:, :half_rot]
+    rest = HEAD_DIM - ROT
+    ones = jnp.ones((count, rest), F32)
+    zeros = jnp.zeros((count, rest), F32)
+    none = jnp.zeros((count, half_rot), F32)
+    whole = jnp.concatenate([cosine, cosine, ones], -1)
+    low_sine = jnp.concatenate([-sine_part, none, zeros], -1)
+    high_sine = jnp.concatenate([none, sine_part, zeros], -1)
+    return tuple(jnp.concatenate([t, t], -1) for t in (whole, low_sine, high_sine))
+
+
+def head_body(
+    tokens,
+    block_order,
+    ln_gain,
+    ln_bias,
+    w_qkv,
+    qv_bias,
+    w_out,
+    b_out,
+    w_in,
+    b_in,
+    w_down,
+    b_down,
+    cotangent,
+):
+    context = lax.axis_index("ctx")
+    line, place = context // ACROSS, context % ACROSS
+    core = lax.axis_index("fsdp")
+    at = jnp.stack([line, place, core]).astype(jnp.int32)
+    positions = range(LINES * ACROSS)
+
+    def over_lines(x, k):
+        return lax.ppermute(x, "ctx", [(i, i ^ (k * ACROSS)) for i in positions])
+
+    def over_places(x, j):
+        return lax.ppermute(x, "ctx", [(i, i ^ j) for i in positions])
+
+    def twin(x):
+        return lax.ppermute(x, "fsdp", [(0, 1), (1, 0)])
+
+    def with_lines(x):
+        return [x] + [over_lines(x, k) for k in range(1, LINES)]
+
+    def with_places(x):
+        return [x] + [over_places(x, j) for j in range(1, ACROSS)]
+
+    rows, width = tokens.shape[1], tokens.shape[2]
+    half = w_qkv.shape[0]
+    feed = w_in.shape[1]
+    owner = line // (LINES // 2)
+    part = line % (LINES // 2)
+    head_cols = width // LINES
+    feed_cols = feed // LINES
+
+    token_lines = with_lines(tokens[0])
+    cot_lines = with_lines(cotangent[0])
+    orders = jnp.stack(with_lines(block_order), 0).reshape(LINES, 2)
+    table = jnp.stack(with_places(orders), 0).reshape(2 * LINES * ACROSS)
+
+    cut = lax.dynamic_slice
+    qkv_own = jnp.concatenate(
+        [cut(w_qkv, (0, width * i + head_cols * line), (half, head_cols)) for i in range(3)], 1
+    )
+    qkv_twin = twin(qkv_own)
+    in_own = cut(w_in, (0, feed_cols * line), (half, feed_cols))
+    in_twin = twin(in_own)
+    out_cut = cut(w_out, (head_cols * part, 0), (head_cols, width))
+    out_rows = jnp.where(core == owner, out_cut, twin(out_cut))
+    down_cut = cut(w_down, (feed_cols * part, 0), (feed_cols, width))
+    down_rows = jnp.where(core == owner, down_cut, twin(down_cut))
+    vectors = jnp.concatenate(
+        [
+            ln_gain,
+            ln_bias,
+            b_out,
+            b_down,
+            cut(qv_bias, (0, head_cols * part), (2, head_cols)).reshape(-1),
+            cut(b_in, (feed_cols * part,), (feed_cols,)),
+        ]
+    )
+    twin_vectors = twin(vectors)
+    ours = vectors.astype(F32)
+    theirs = twin_vectors.astype(F32)
+    pair = jnp.where(core == 0, jnp.stack([ours, theirs]), jnp.stack([theirs, ours]))
+    gain, shift, out_bias, down_bias = (
+        pair[:, half * i : half * (i + 1)].reshape(1, width) for i in range(4)
+    )
+    chosen = jnp.where(core == owner, ours, theirs)[None, 4 * half :]
+    bias_q = chosen[:, :head_cols]
+    bias_v = chosen[:, head_cols : 2 * head_cols]
+    bias_in = chosen[:, 2 * head_cols :]
+    length = rows * LINES * ACROSS
+    rotation = turn_tables(length)
+    line_rows = rows * LINES
+    slot_shape = (line_rows * 3 // 2, 128)
+    fold_shape = (line_rows // 2, 128)
+
+    *qkv_slots, ln_low, ln_turned = call(
+        project_kernel,
+        [(slot_shape, BF16)] * 4 + [((line_rows, width), BF16), ((width, line_rows), BF16)],
+        [],
+        2 * line_rows * width * 3 * head_cols,
+        at, *token_lines, gain, shift, bias_q, bias_v, qkv_own, qkv_twin,
+    )
+    qkv_in = [qkv_slots[0]] + [over_places(qkv_slots[j], j) for j in range(1, 4)]
+    back_slots = call(
+        back_rows_kernel,
+        [(fold_shape, BF16)] * 4,
+        [],
+        2 * line_rows * width * head_cols,
+        at, *cot_lines, out_rows,
+    )
+    back_in = [back_slots[0]] + [over_places(back_slots[j], j) for j in range(1, 4)]
+    hidden, _, active_turned, feed_low = call(
+        feed_kernel,
+        [
+            ((line_rows, feed_cols), F32),
+            ((line_rows, feed_cols), BF16),
+            ((feed_cols, line_rows), BF16),
+            ((line_rows, width), F32),
+        ],
+        [],
+        4 * line_rows * width * feed_cols,
+        at, ln_low, in_own, in_twin, bias_in, down_rows,
+    )
+    *att_slots, qk_rows, kq_rows, value_rows, attended, lse = call(
+        attend_kernel,
+        [(fold_shape, BF16)] * 4
+        + [
+            ((length, 128), BF16),
+            ((length, 128), BF16),
+            ((length, 64), BF16),
+            ((length, 64), F32),
+            ((length, 1), F32),
+        ],
+        [pltpu.VMEM((length, 128), BF16)],
+        4 * length * length * 64,
+        table, *qkv_in, *rotation,
+    )
+    att_in = [att_slots[0]] + [over_places(att_slots[j], j) for j in range(1, 4)]
+    block = 128 + 128 + VEC
+    feed_send, feed_keep, feed_grad_low = call(
+        feed_back_kernel,
+        [((4 * block, width), BF16), ((4 * block, width), F32), ((line_rows, width), F32)],
+        [pltpu.VMEM((line_rows, feed_cols), BF16), pltpu.VMEM((256, 1024), F32)],
+        8 * line_rows * width * feed_cols,
+        at, *cot_lines, hidden, active_turned, ln_turned, in_own, in_twin, down_rows,
+    )
+    feed_blocks = call(
+        add_twin_kernel,
+        [((block, width), F32)] + [((block, width), BF16)] * 3,
+        [],
+        0,
+        at, feed_keep, twin(feed_send),
+    )
+    feed_in = [feed_blocks[0]] + [over_places(feed_blocks[j], j) for j in range(1, 4)]
+    grad_down, feed_vec, *in_slots = call(
+        feed_sum_kernel,
+        [((128, width), F32), ((8, width), F32), ((32, width), F32)] + [((32, width), BF16)] * 3,
+        [],
+        0,
+        at, *feed_in,
+    )
+    in_parts = [in_slots[0]] + [over_lines(in_slots[k], k) for k in range(1, 4)]
+    (grad_in,) = call(join_in_kernel, [((32, feed), F32)], [], 0, at, *in_parts)
+
+    *low_slots, out_send, out_keep = call(
+        branch_kernel,
+        [((rows, width), F32)]
+        + [((rows, width), BF16)] * 3
+        + [((128, width), BF16), ((128, width), F32)],
+        [pltpu.VMEM((256, 1024), F32)],
+        4 * line_rows * width * head_cols,
+        at, *att_in, feed_low, out_rows, *cot_lines,
+    )
+    low_in = [low_slots[0]] + [over_lines(low_slots[k], k) for k in range(1, 4)]
+    (layer_out,) = call(
+        layer_kernel, [((rows, width), BF16)], [], 0, *low_in, tokens[0], out_bias, down_bias
+    )
+    out_blocks = call(
+        add_twin_kernel,
+        [((32, width), F32)] + [((32, width), BF16)] * 3,
+        [],
+        0,
+        at, out_keep, twin(out_send),
+    )
+    out_in = [out_blocks[0]] + [over_places(out_blocks[j], j) for j in range(1, 4)]
+    (grad_out,) = call(out_sum_kernel, [((32, width), F32)], [], 0, *out_in)
+
+    *grad_slots, bias_sums = call(
+        attend_back_kernel,
+        [(slot_shape, BF16)] * 4 + [((8, 128), F32)],
+        [
+            pltpu.VMEM((length, 64), BF16),
+            pltpu.VMEM((128, length), F32),
+            pltpu.VMEM((64, length), F32),
+            pltpu.VMEM((length, 128), F32),
+            pltpu.VMEM((length, 64), F32),
+        ],
+        10 * length * length * 64,
+        table, *back_in, qk_rows, kq_rows, value_rows, attended, lse, *rotation,
+    )
+    bias_sums = bias_sums + twin(bias_sums)
+    grad_in_slots = [grad_slots[0]] + [over_places(grad_slots[j], j) for j in range(1, 4)]
+    qkv_cols = 3 * head_cols
+    qkv_block = 128 + VEC
+    *ln_slots, qkv_send, qkv_keep = call(
+        grads_kernel,
+        [((rows, width), F32)]
+        + [((rows, width), BF16)] * 3
+        + [((4 * qkv_block, qkv_cols), BF16), ((4 * qkv_block, qkv_cols), F32)],
+        [
+            pltpu.VMEM((line_rows, qkv_cols), BF16),
+            pltpu.VMEM((line_rows, width), F32),
+            pltpu.VMEM((256, qkv_cols), F32),
+        ],
+        4 * line_rows * width * qkv_cols,
+        at, *grad_in_slots, feed_grad_low, *token_lines, ln_turned, qkv_own, qkv_twin,
+    )
+    ln_in = [ln_slots[0]] + [over_lines(ln_slots[k], k) for k in range(1, 4)]
+    (grad_tokens,) = call(
+        tokens_kernel, [((rows, width), BF16)], [], 0, *ln_in, tokens[0], cotangent[0], gain
+    )
+    qkv_blocks = call(
+        add_twin_kernel,
+        [((qkv_block, qkv_cols), F32)] + [((qkv_block, qkv_cols), BF16)] * 3,
+        [],
+        0,
+        at, qkv_keep, twin(qkv_send),
+    )
+    qkv_sums = [qkv_blocks[0]] + [over_places(qkv_blocks[j], j) for j in range(1, 4)]
+    qkv_parts = call(
+        grad_sum_kernel,
+        [((32 + VEC, qkv_cols), F32)] + [((32 + VEC, qkv_cols), BF16)] * 3,
+        [],
+        0,
+        at, *qkv_sums,
+    )
+    qkv_parts = [qkv_parts[0]] + [over_lines(qkv_parts[k], k) for k in range(1, 4)]
+    grad_qkv, ln_vec = call(
+        join_qkv_kernel,
+        [((32, 3 * width), F32), ((VEC, qkv_cols), F32)],
+        [],
+        0,
+        at, *qkv_parts,
+    )
+    index = context * 2 + core
+    gains = jnp.concatenate([ln_vec[0], ln_vec[2, :256]])
+    shifts = jnp.concatenate([ln_vec[1], ln_vec[3, :256]])
+    grad_gain = cut(gains, (32 * index,), (32,))
+    grad_shift = cut(shifts, (32 * index,), (32,))
+    grad_qv = cut(bias_sums, (0, 32 * core), (2, 32))
+    grad_b_in = feed_vec[0, :128]
+    grad_b = cut(feed_vec, (0, 128 + 64 * place + 32 * core), (1, 32))[0]
+    return (
+        layer_out[None],
+        grad_tokens[None],
+        grad_gain,
+        grad_shift,
+        grad_qkv,
+        grad_qv,
+        grad_out,
+        grad_b,
+        grad_in,
+        grad_b_in,
+        grad_down,
+        grad_b,
+    )
+
+
 def solution(mesh):
+    one_head_each = mesh.shape["ctx"] == HEADS and mesh.shape["fsdp"] == 2
     return jax.shard_map(
-        body,
+        head_body if one_head_each else body,
         mesh=mesh,
         in_specs=(
             P("fsdp", "ctx", None),

time: 1490 us -> 259 us (0.17)
  waiting for transfers between devices: 1030 us -> 60.1 us
  matrix products: 132 us -> 0 us
  blocking collectives: 88.8 us -> 0 us
  Pallas kernels: 0 us -> 83.8 us
  other arithmetic: 78.8 us -> 7.69 us
  local copies, waits for them, and re-layouts: 83.1 us -> 37 us
  starting transfers between devices: 46.6 us -> 63.9 us
    reduce_scatter x4 -> x0, waiting for transfers between devices: 670 us -> none  [the longest x1 187 us: body(): lax.psum_scatter(term_down_w, ('ctx', 'fsdp'), scatter_dimension=0, tiled...]
    ppermute x77 -> x54, waiting for transfers between devices: 220 us -> 60.1 us  [the longest x21 30.6 us: over_lines(): return lax.ppermute(x, 'ctx', [(i, i ^ k * ACROSS) for i in positions])]
    dot_general x96 -> x0, matrix products: 132 us -> none  [the longest x4 28.3 us: outer_sum(): lax.dot_general(left_side, right_side, (((0,), (0,)), ((), ())), preferre...]
    all_gather x6 -> x0, waiting for transfers between devices: 132 us -> none  [the longest x1 63.5 us: body(): piece_values = lax.all_gather(value_rows, 'ctx', axis=0, tiled=True)]
    pallas_call x0 -> x18, Pallas kernels: none -> 83.8 us  [call(): pl.pallas_call(kernel, out_shape=outs, in_specs=specs, out_specs=[pl.Bloc...]
    convert_element_type x68 -> x2, other arithmetic: 68.4 us -> 0.02 us  [the longest x1 0.02 us: head_body(): ours = vectors.astype(F32)]
    all_gather x7 -> x0, blocking collectives: 51.6 us -> none  [the longest x1 40.8 us: body(): piece_orders = lax.all_gather(block_order, 'ctx', axis=0, tiled=True)]
    unnamed x1 -> x0, blocking collectives: 37.2 us -> none
  transfers between devices with their start and end apart: 88 -> 54, of which waited for: 40 -> 18; matrix products, arithmetic and copies ran while one was open for 19% -> 14% of each run, Pallas kernels for 0% -> 31%
where the time goes in v1:
time: 259 us; the launch traced here: 254 us
  Pallas kernels  83.8 us (32%)
  starting transfers between devices  63.9 us (25%)
  waiting for transfers between devices  60.1 us (23%)
  local copies, waits for them, and re-layouts  37 us (14%)
  other arithmetic  7.69 us (3%)
    pallas_call x18, Pallas kernels, call(): pl.pallas_call(kernel, out_shape=outs, in_specs=specs, out_specs=[pl.Bloc...  83.8 us
    ppermute x21, starting transfers between devices, over_lines(): return lax.ppermute(x, 'ctx', [(i, i ^ k * ACROSS) for i in positions])  31.8 us
    ppermute x21, waiting for transfers between devices, over_lines(): return lax.ppermute(x, 'ctx', [(i, i ^ k * ACROSS) for i in positions])  30.6 us
    ppermute x24, starting transfers between devices, over_places(): return lax.ppermute(x, 'ctx', [(i, i ^ j) for i in positions])  30.4 us
    ppermute x24, waiting for transfers between devices, over_places(): return lax.ppermute(x, 'ctx', [(i, i ^ j) for i in positions])  29.4 us
    unnamed x148, local copies, waits for them, and re-layouts  11.7 us
    concatenate x3, local copies, waits for them, and re-layouts, turn_tables(): jnp.concatenate([t, t], -1)  10.5 us
  transfers between devices with their start and end apart: 54, of which 18 were waited for; matrix products, arithmetic and copies ran while one was open for 14% of the time, Pallas kernels for 31%

profile of v1, /device:TPU:0, one launch (start us, length us, event | category | flops | bytes accessed | tf_op | source)
XLA Modules:
  0.0 254.4 jit_solution(180583299057886200)
XLA Ops:
  0.6 3.1 %collective-permute-start = (s32[1,2]{1,0:T(1,128)}, s32[1,2]{1,0:T(1,128)}, u32[]{:S(2)}, u32[]{:S(2)}) collective-permute-start(s32[1,2]{1,0:T(1,128)} %param.14), channel_id=1, source_target_pairs={{0,8},{2,10},{4,12},{6,14},{8,0},{10,2},{12,4},{14,6},{16,24},{18,... | collective-permute-start | bytes 32 | tf_op jit(solution)/shard_map/ppermute | solution.py:829
  3.7 2.5 collective-permute-start.2
  6.3 2.9 %collective-permute-start.8 = (bf16[128,1024]{1,0:T(8,128)(2,1)}, bf16[128,1024]{1,0:T(8,128)(2,1)}, u32[]{:S(2)}, u32[]{:S(2)}) collective-permute-start(bf16[128,1024]{1,0:T(8,128)(2,1)} %bitcast.52), channel_id=1, source_target_pairs={{0,24},{2,26},{4,28},{6,30},{8,16},{10,18},{12,20},{14,22},{16,8},... | collective-permute-start | bytes 786440 | tf_op jit(solution)/shard_map/ppermute | solution.py:829
  9.3 3.1 %constant_dynamic-slice_fusion.3 = bf16[1024,1024]{1,0:T(8,128)(2,1)} fusion(bf16[2048,1024]{1,0:T(8,128)(2,1)} %param.23, s32[]{:T(128)S(6)} %select_n.85), kind=kLoop, calls=%fused_computation.31 | loop fusion | bytes 4194308 | tf_op jit(solution)/shard_map/dynamic_slice | solution.py:865
  14.6 3.0 %concatenate.63.high_sine.rest_2_ = f32[2048,128]{1,0:T(8,128)} concatenate(f32[2048,8]{1,0:T(8,128)S(1)} %broadcast_in_dim.22, f32[2048,8]{1,0:T(8,128)S(1)} %copy.44, f32[2048,48]{1,0:T(8,128)S(1)} %broadcast_in_dim.23, f32[2048,8]{1,0:T(8,128)S(1)} %broadcast_in_dim.22, f32[2048,8]{1,0:T(8,128)S(1)} %copy.44, f32[2048,48]{1,0:T(8,128)S(1)} %broadcast_in_dim.23), dimensions={1} | concatenate | bytes 2097152 | tf_op jit(solution)/shard_map/concatenate | solution.py:804
  17.6 4.4 %concatenate.62.low_sine.rest_1_ = f32[2048,128]{1,0:T(8,128)} concatenate(f32[2048,8]{1,0:T(8,128)} %neg.3, f32[2048,8]{1,0:T(8,128)S(1)} %broadcast_in_dim.22, f32[2048,48]{1,0:T(8,128)S(1)} %broadcast_in_dim.23, f32[2048,8]{1,0:T(8,128)} %neg.3, f32[2048,8]{1,0:T(8,128)S(1)} %broadcast_in_dim.22, f32[2048,48]{1,0:T(8,128)S(1)} %broadcast_in_dim.23), dimensions={1} | concatenate | bytes 2097152 | tf_op jit(solution)/shard_map/concatenate | solution.py:804
  23.7 3.1 %concatenate.61.cosine.rest_0_ = f32[2048,128]{1,0:T(8,128)} concatenate(f32[2048,8]{1,0:T(8,128)S(1)} %copy.39, f32[2048,8]{1,0:T(8,128)S(1)} %copy.39, f32[2048,48]{1,0:T(8,128)S(1)} %broadcast_in_dim.21, f32[2048,8]{1,0:T(8,128)S(1)} %copy.39, f32[2048,8]{1,0:T(8,128)S(1)} %copy.39, f32[2048,48]{1,0:T(8,128)S(1)} %broadcast_in_dim.21), dimensions={1} | concatenate | bytes 2097152 | tf_op jit(solution)/shard_map/concatenate | solution.py:804
  28.3 1.2 constant_dynamic-slice_fusion.7
  29.6 1.6 constant_dynamic-slice_fusion.4.w_own
  32.7 2.4 collective-permute-start.5
  35.1 2.0 collective-permute-done.5
  37.2 1.5 collective-permute-start.4
  38.7 2.0 collective-permute-done.4
  40.7 1.5 collective-permute-start.3
  42.2 2.1 collective-permute-done.3
  45.6 1.2 collective-permute-start.6
  49.2 2.9 %collective-permute-start.22 = (bf16[128,1024]{1,0:T(8,128)(2,1)S(1)}, bf16[128,1024]{1,0:T(8,128)(2,1)S(1)}, u32[]{:S(2)}, u32[]{:S(2)}) collective-permute-start(bf16[128,1024]{1,0:T(8,128)(2,1)S(1)} %bitcast.49), channel_id=1, source_target_pairs={{0,24},{2,26},{4,28},{6,30},{8,16},{10,18},{12,20},{14,22},{16,8},... | collective-permute-start | bytes 786440 | tf_op jit(solution)/shard_map/ppermute | solution.py:829
  52.1 1.8 collective-permute-done.6.t1
  53.9 3.5 %collective-permute-start.21 = (bf16[128,1024]{1,0:T(8,128)(2,1)S(1)}, bf16[128,1024]{1,0:T(8,128)(2,1)S(1)}, u32[]{:S(2)}, u32[]{:S(2)}) collective-permute-start(bf16[128,1024]{1,0:T(8,128)(2,1)S(1)} %bitcast.50), channel_id=1, source_target_pairs={{0,16},{2,18},{4,20},{6,22},{8,24},{10,26},{12,28},{14,30},{16,0},... | collective-permute-start | bytes 786440 | tf_op jit(solution)/shard_map/ppermute | solution.py:829
  57.5 5.4 %shard_map.220 = (bf16[768,128]{1,0:T(8,128)(2,1)}, bf16[768,128]{1,0:T(8,128)(2,1)}, bf16[768,128]{1,0:T(8,128)(2,1)}, bf16[768,128]{1,0:T(8,128)(2,1)}, bf16[5...) custom-call(s32[3]{0:T(128)} %pad_add_fusion.2.at, bf16[128,1024]{1,0:T(8,128)(2,1)} %bitcast.53, ...), custom_call_target="tpu_custom_call" | custom-call | flops 805306368 | bytes 5515276 | tf_op jit(solution)/shard_map/pallas_call | solution.py:363
  62.9 3.9 %broadcast_select_fusion.w_down = bf16[1024,1024]{1,0:T(8,128)(2,1)} fusion(bf16[1024,1024]{1,0:T(8,128)(2,1)} %collective-permute-done.18, pred[]{:T(512)S(6)} %eq.12, bf16[2048,1024]{1,0:T(8,128)(2,1)} %param.23, s32[]{:T(128)S(6)} %select_n.85), kind=kLoop, calls=%fused_computation | loop fusion | flops 1048576 | bytes 6291461 | tf_op jit(solution)/shard_map/jit(_where)/select_n | solution.py:866
  66.8 1.6 collective-permute-start.11
  68.4 6.8 %shard_map.222 = (f32[512,1024]{1,0:T(8,128)}, bf16[512,1024]{1,0:T(8,128)(2,1)}, bf16[1024,512]{1,0:T(8,128)(2,1)}, f32[512,1024]{1,0:T(8,128)}) custom-call(s32[3]{0:T(128)} %pad_add_fusion.2.at, bf16[512,1024]{1,0:T(8,128)(2,1)} %get-tuple-element.86.ln, bf16[512,1024]{1,0:T(8,128)(2,1)} %copy-done.4, bf16[512,1024]{1,0:T(8,128)(2,1)} %copy-done.45, ...), custom_call_target="tpu_custom_call" | custom-call | flops 2147483648 | bytes 11538444 | tf_op jit(solution)/shard_map/pallas_call | solution.py:363
  75.2 1.6 collective-permute-start.12
  78.4 11.4 %shard_map.227 = (bf16[1088,1024]{1,0:T(8,128)(2,1)}, f32[1088,1024]{1,0:T(8,128)}, f32[512,1024]{1,0:T(8,128)}) custom-call(s32[3]{0:T(128)} %pad_add_fusion.2.at, bf16[128,1024]{1,0:T(8,128)(2,1)} %bitcast.45, bf16[128,1024]{1,0:T(8,128)(2,1)} %copy-done.7, bf16[128,1024]{1,0:T(8,128)(2,1)} %copy-done.6, bf16[128,1024]{1,0:T(8,128)(2,1)} %copy-done.5, ...), custom_call_target="tpu_custom_call" | custom-call | flops 4294967296 | bytes 18219020 | tf_op jit(solution)/shard_map/pallas_call | solution.py:363
  91.4 2.7 %shard_map.225 = (bf16[256,128]{1,0:T(8,128)(2,1)}, bf16[256,128]{1,0:T(8,128)(2,1)}, bf16[256,128]{1,0:T(8,128)(2,1)}, bf16[256,128]{1,0:T(8,128)(2,1)}) custom-call(s32[3]{0:T(128)} %pad_add_fusion.2.at, bf16[128,1024]{1,0:T(8,128)(2,1)} %bitcast.46, bf16[128,1024]{1,0:T(8,128)(2,1)} %copy-done.7, bf16[128,1024]{1,0:T(8,128)(2,1)} %copy-done.6, ...), custom_call_target="tpu_custom_call" | custom-call | flops 268435456 | bytes 1835020 | tf_op jit(solution)/shard_map/pallas_call | solution.py:363
  95.1 1.5 collective-permute-start.27
  98.4 9.5 %shard_map.221 = (bf16[256,128]{1,0:T(8,128)(2,1)}, bf16[256,128]{1,0:T(8,128)(2,1)}, bf16[256,128]{1,0:T(8,128)(2,1)}, bf16[256,128]{1,0:T(8,128)(2,1)}, bf16[2...) custom-call(s32[32]{0:T(128)} %reshape.137.table, ...), custom_call_target="tpu_custom_call" | custom-call | flops 1073741824 | bytes 6037632 | tf_op jit(solution)/shard_map/pallas_call | solution.py:363
  108.6 11.6 %shard_map.226 = (bf16[768,128]{1,0:T(8,128)(2,1)}, bf16[768,128]{1,0:T(8,128)(2,1)}, bf16[768,128]{1,0:T(8,128)(2,1)}, bf16[768,128]{1,0:T(8,128)(2,1)}, f32[8,128]{1,0:T(8,128)}) custom-call(s32[32]{0:T(128)} %reshape.137.table, bf16[256,128]{1,0:T(8,128)(2,1)} %get-tuple-element.92.g0, bf16[256,128]{1,0:T(8,128)(2,1)} %copy-done.60, ...), custom_call_target="tpu_custom_call" | custom-call | flops 2684354560 | bytes 6041728 | tf_op jit(solution)/shard_map/pallas_call | solution.py:363
  121.1 1.5 collective-permute-start.30
  123.7 4.6 %collective-permute-done.29.g1 = bf16[768,128]{1,0:T(8,128)(2,1)S(1)} collective-permute-done((bf16[768,128]{1,0:T(8,128)(2,1)}, bf16[768,128]{1,0:T(8,128)(2,1)S(1)}, u32[]{:S(2)}, u32[]{:S(2)}) %collective-permute-start.29) | collective-permute-done | bytes 196640 | tf_op jit(solution)/shard_map/ppermute | solution.py:832
  128.3 2.3 collective-permute-done.30.g2
  132.3 7.9 %shard_map.228 = (f32[128,1024]{1,0:T(8,128)}, bf16[128,1024]{1,0:T(8,128)(2,1)}, bf16[128,1024]{1,0:T(8,128)(2,1)}, bf16[128,1024]{1,0:T(8,128)(2,1)}, bf16[576,768]{1,0:T(8,128)(2,1)}, /*index=5*/f32[576,768]{1,0:T(8,128)}) custom-call(s32[3]{0:T(128)} %pad_add_fusion.2.at, bf16[768,128]{1,0:T(8,128)(2,1)} %get-tuple-element.101.g0, ...), custom_call_target="tpu_custom_call" | custom-call | flops 1610612736 | bytes 10518540 | tf_op jit(solution)/shard_map/pallas_call | solution.py:363
  141.4 1.3 collective-permute-start.15
  145.7 2.2 collective-permute-done.16.a3
  148.5 4.0 %shard_map.223 = (f32[128,1024]{1,0:T(8,128)}, bf16[128,1024]{1,0:T(8,128)(2,1)}, bf16[128,1024]{1,0:T(8,128)(2,1)}, bf16[128,1024]{1,0:T(8,128)(2,1)}, bf16[128,1024]{1,0:T(8,128)(2,1)}, /*index=5*/f32[128,1024]{1,0:T(8,128)}) custom-call(s32[3]{0:T(128)} %pad_add_fusion.2.at, bf16[256,128]{1,0:T(8,128)(2,1)} %get-tuple-element.82.a0, ...), custom_call_target="tpu_custom_call" | custom-call | flops 536870912 | bytes 6029324 | tf_op jit(solution)/shard_map/pallas_call | solution.py:363
  152.5 2.1 collective-permute-start.23
  155.3 1.8 collective-permute-start.25
  158.1 2.8 %shard_map.230 = (f32[144,768]{1,0:T(8,128)}, bf16[144,768]{1,0:T(8,128)(2,1)}, bf16[144,768]{1,0:T(8,128)(2,1)}, bf16[144,768]{1,0:T(8,128)(2,1)}) custom-call(s32[3]{0:T(128)} %pad_add_fusion.2.at, f32[576,768]{1,0:T(8,128)} %get-tuple-element.113.keep, bf16[576,768]{1,0:T(8,128)(2,1)} %copy-done.9), custom_call_target="tpu_custom_call" | custom-call | bytes 3760140 | tf_op jit(solution)/shard_map/pallas_call | solution.py:363
  162.0 1.8 collective-permute-done.23.r1
  164.6 11.2 %collective-permute-done.24.r2 = bf16[128,1024]{1,0:T(8,128)(2,1)S(1)} collective-permute-done((bf16[128,1024]{1,0:T(8,128)(2,1)}, bf16[128,1024]{1,0:T(8,128)(2,1)S(1)}, u32[]{:S(2)}, u32[]{:S(2)}) %collective-permute-start.24) | collective-permute-done | bytes 262176 | tf_op jit(solution)/shard_map/ppermute | solution.py:829
  175.8 1.2 collective-permute-start.38
  177.1 2.8 %collective-permute-start.32 = (bf16[128,1024]{1,0:T(8,128)(2,1)S(1)}, bf16[128,1024]{1,0:T(8,128)(2,1)S(1)}, u32[]{:S(2)}, u32[]{:S(2)}) collective-permute-start(bf16[128,1024]{1,0:T(8,128)(2,1)S(1)} %copy-done.47), channel_id=1, source_target_pairs={{0,8},{2,10},{4,12},{6,14},{8,0},{10,2},{12,4},{14,6},{16,24},{18,... | collective-permute-start | bytes 786440 | tf_op jit(solution)/shard_map/ppermute | solution.py:829
  180.0 2.8 %collective-permute-done.38.r3 = bf16[144,768]{1,0:T(8,128)(2,1)S(1)} collective-permute-done((bf16[144,768]{1,0:T(8,128)(2,1)}, bf16[144,768]{1,0:T(8,128)(2,1)S(1)}, u32[]{:S(2)}, u32[]{:S(2)}) %collective-permute-start.38) | collective-permute-done | bytes 221216 | tf_op jit(solution)/shard_map/ppermute | solution.py:832
  182.8 1.4 collective-permute-start.34
  184.3 2.0 shard_map.231
  187.0 1.9 shard_map.233
  188.9 2.2 collective-permute-done.32.r1
  192.2 9.1 %collective-permute-done.33.r2 = bf16[128,1024]{1,0:T(8,128)(2,1)S(1)} collective-permute-done((bf16[128,1024]{1,0:T(8,128)(2,1)S(1)}, bf16[128,1024]{1,0:T(8,128)(2,1)S(1)}, u32[]{:S(2)}, u32[]{:S(2)}) %collective-permute-start.33) | collective-permute-done | bytes 262176 | tf_op jit(solution)/shard_map/ppermute | solution.py:829
  202.2 1.7 collective-permute-start.46
  205.1 4.9 %shard_map.235 = (f32[272,1024]{1,0:T(8,128)}, bf16[272,1024]{1,0:T(8,128)(2,1)}, bf16[272,1024]{1,0:T(8,128)(2,1)}, bf16[272,1024]{1,0:T(8,128)(2,1)}) custom-call(s32[3]{0:T(128)} %pad_add_fusion.2.at, f32[1088,1024]{1,0:T(8,128)} %get-tuple-element.132.keep, bf16[1088,1024]{1,0:T(8,128)(2,1)} %copy-done.3), custom_call_target="tpu_custom_call" | custom-call | bytes 9469964 | tf_op jit(solution)/shard_map/pallas_call | solution.py:363
  213.1 1.7 collective-permute-start.50
  215.5 2.6 %shard_map.229 = bf16[128,1024]{1,0:T(8,128)(2,1)} custom-call(f32[128,1024]{1,0:T(8,128)} %get-tuple-element.109.own, bf16[128,1024]{1,0:T(8,128)(2,1)} %copy-done.18, bf16[128,1024]{1,0:T(8,128)(2,1)} %copy-done.19, bf16[128,1024]{1,0:T(8,128)(2,1)} %collective-permute-done.34.r3, bf16[128,1024]{1,0:T(8,128)(2,1)} %bitcast.55, bf16[128,1024]{1,0:T(8,128)(2,1)} %bitcast.48, ...), custom_call_target="tpu_custom_call" | custom-call | bytes 2101248 | tf_op jit(solution)/shard_map/pallas_call | solution.py:363
  218.1 2.2 shard_map.224
  220.3 1.6 shard_map.234
  222.6 1.8 shard_map.232
  227.2 8.5 %collective-permute-done.49.r2 = bf16[272,1024]{1,0:T(8,128)(2,1)S(1)} collective-permute-done((bf16[272,1024]{1,0:T(8,128)(2,1)}, bf16[272,1024]{1,0:T(8,128)(2,1)S(1)}, u32[]{:S(2)}, u32[]{:S(2)}) %collective-permute-start.49) | collective-permute-done | bytes 557088 | tf_op jit(solution)/shard_map/ppermute | solution.py:832
  236.8 2.7 %shard_map.236 = (f32[128,1024]{1,0:T(8,128)}, f32[8,1024]{1,0:T(8,128)}, f32[32,1024]{1,0:T(8,128)}, bf16[32,1024]{1,0:T(8,128)(2,1)}, bf16[32,1024]{1,0:T(8,128)(2,1)}, /*index=5*/bf16[32,1024]{1,0:T(8,128)(2,1)}) custom-call(s32[3]{0:T(128)} %pad_add_fusion.2.at, f32[272,1024]{1,0:T(8,128)} %get-tuple-element.134.own, bf16[272,1024]{1,0:T(8,128)(2,1)} %copy-done.10, ...), custom_call_target="tpu_custom_call" | custom-call | bytes 3670028 | tf_op jit(solution)/shard_map/pallas_call | solution.py:363
  239.5 1.2 slice_bitcast_fusion.4
  240.7 2.8 %collective-permute-start.51 = (bf16[32,1024]{1,0:T(8,128)(2,1)}, bf16[32,1024]{1,0:T(8,128)(2,1)S(1)}, u32[]{:S(2)}, u32[]{:S(2)}) collective-permute-start(bf16[32,1024]{1,0:T(8,128)(2,1)} %get-tuple-element.140), channel_id=1, source_target_pairs={{0,8},{2,10},{4,12},{6,14},{8,0},{10,2},{12,4},{14,6},{16,24},{18,... | collective-permute-start | bytes 196616 | tf_op jit(solution)/shard_map/ppermute | solution.py:829
  243.5 1.3 collective-permute-start.52
  246.6 2.4 collective-permute-done.52.i2
  249.0 2.0 collective-permute-done.53.i3
  251.6 1.8 shard_map.237
  (256 shorter events, 44.3 us)
Async XLA Ops:
  0.6 30.6 %collective-permute-start = (s32[1,2]{1,0:T(1,128)}, s32[1,2]{1,0:T(1,128)}, u32[]{:S(2)}, u32[]{:S(2)}) collective-permute-start(s32[1,2]{1,0:T(1,128)} %param.14), channel_id=1, source_target_pairs={{0,8},{2,10},{4,12},{6,14},{8,0},{10,2},{12,4},{14,6},{16,24},{18,... | collective-permute-start | bytes 32 | tf_op jit(solution)/shard_map/ppermute | solution.py:829
  3.7 27.9 %collective-permute-start.2 = (s32[1,2]{1,0:T(1,128)}, s32[1,2]{1,0:T(1,128)}, u32[]{:S(2)}, u32[]{:S(2)}) collective-permute-start(s32[1,2]{1,0:T(1,128)} %param.14), channel_id=1, source_target_pairs={{0,24},{2,26},{4,28},{6,30},{8,16},{10,18},{12,20},{14,22},{16,8},... | collective-permute-start | bytes 32 | tf_op jit(solution)/shard_map/ppermute | solution.py:829
  6.2 25.7 %collective-permute-start.1 = (s32[1,2]{1,0:T(1,128)}, s32[1,2]{1,0:T(1,128)}, u32[]{:S(2)}, u32[]{:S(2)}) collective-permute-start(s32[1,2]{1,0:T(1,128)} %param.14), channel_id=1, source_target_pairs={{0,16},{2,18},{4,20},{6,22},{8,24},{10,26},{12,28},{14,30},{16,0},... | collective-permute-start | bytes 32 | tf_op jit(solution)/shard_map/ppermute | solution.py:829
  6.3 39.3 %collective-permute-start.8 = (bf16[128,1024]{1,0:T(8,128)(2,1)}, bf16[128,1024]{1,0:T(8,128)(2,1)}, u32[]{:S(2)}, u32[]{:S(2)}) collective-permute-start(bf16[128,1024]{1,0:T(8,128)(2,1)} %bitcast.52), channel_id=1, source_target_pairs={{0,24},{2,26},{4,28},{6,30},{8,16},{10,18},{12,20},{14,22},{16,8},... | collective-permute-start | bytes 786440 | tf_op jit(solution)/shard_map/ppermute | solution.py:829
  12.4 50.4 %collective-permute-start.18 = (bf16[1024,1024]{1,0:T(8,128)(2,1)}, bf16[1024,1024]{1,0:T(8,128)(2,1)}, u32[]{:S(2)}, u32[]{:S(2)}) collective-permute-start(bf16[1024,1024]{1,0:T(8,128)(2,1)} %constant_dynamic-slice_fusion.3), channel_id=1, source_target_pairs={{0,1},{1,0},{2,3},{3,2},{4,5},{5,4},{6,7},{7,6},{8,9},{9,8},{10,11... | collective-permute-start | bytes 6291464 | tf_op jit(solution)/shard_map/ppermute | solution.py:835
  29.5 19.7 %copy-start.1 = (bf16[1,128,1024]{2,1,0:T(8,128)(2,1)S(1)}, bf16[1,128,1024]{2,1,0:T(8,128)(2,1)}, u32[]{:S(2)}) copy-start(bf16[1,128,1024]{2,1,0:T(8,128)(2,1)} %param.25) | copy-start | bytes 786436
  29.6 27.9 %copy-start = (bf16[512,768]{1,0:T(8,128)(2,1)}, bf16[512,768]{1,0:T(8,128)(2,1)S(1)}, u32[]{:S(2)}) copy-start(bf16[512,768]{1,0:T(8,128)(2,1)S(1)} %pad_maximum_fusion.w_own) | copy-start | bytes 2359300
  31.2 35.6 %copy-start.4 = (bf16[512,1024]{1,0:T(8,128)(2,1)}, bf16[512,1024]{1,0:T(8,128)(2,1)S(1)}, u32[]{:S(2)}) copy-start(bf16[512,1024]{1,0:T(8,128)(2,1)S(1)} %constant_dynamic-slice_fusion.4.w_own) | copy-start | bytes 3145732
  31.2 17.9 %collective-permute-start.7 = (bf16[128,1024]{1,0:T(8,128)(2,1)S(1)}, bf16[128,1024]{1,0:T(8,128)(2,1)}, u32[]{:S(2)}, u32[]{:S(2)}) collective-permute-start(bf16[128,1024]{1,0:T(8,128)(2,1)S(1)} %bitcast.57), channel_id=1, source_target_pairs={{0,16},{2,18},{4,20},{6,22},{8,24},{10,26},{12,28},{14,30},{16,0},... | collective-permute-start | bytes 786440 | tf_op jit(solution)/shard_map/ppermute | solution.py:829
  31.7 13.4 %collective-permute-start.9 = (bf16[3584]{0:T(1024)(128)(2,1)S(1)}, bf16[3584]{0:T(1024)(128)(2,1)S(1)}, u32[]{:S(2)}, u32[]{:S(2)}) collective-permute-start(bf16[3584]{0:T(1024)(128)(2,1)S(1)} %copy-done.41), channel_id=1, source_target_pairs={{0,1},{1,0},{2,3},{3,2},{4,5},{5,4},{6,7},{7,6},{8,9},{9,8},{10,11... | collective-permute-start | bytes 21512 | tf_op jit(solution)/shard_map/ppermute | solution.py:835
  32.7 4.5 %collective-permute-start.5 = (s32[4,2]{0,1:T(2,128)S(1)}, s32[4,2]{0,1:T(2,128)S(1)}, u32[]{:S(2)}, u32[]{:S(2)}) collective-permute-start(s32[4,2]{0,1:T(2,128)S(1)} %bitcast.70), channel_id=1, source_target_pairs={{0,6},{2,4},{4,2},{6,0},{8,14},{10,12},{12,10},{14,8},{16,22},{18,... | collective-permute-start | bytes 104 | tf_op jit(solution)/shard_map/ppermute | solution.py:832
  37.2 3.6 %collective-permute-start.4 = (s32[4,2]{0,1:T(2,128)S(1)}, s32[4,2]{0,1:T(2,128)S(1)}, u32[]{:S(2)}, u32[]{:S(2)}) collective-permute-start(s32[4,2]{0,1:T(2,128)S(1)} %bitcast.71), channel_id=1, source_target_pairs={{0,4},{2,6},{4,0},{6,2},{8,12},{10,14},{12,8},{14,10},{16,20},{18,... | collective-permute-start | bytes 104 | tf_op jit(solution)/shard_map/ppermute | solution.py:832
  40.7 3.6 %collective-permute-start.3 = (s32[4,2]{0,1:T(2,128)S(1)}, s32[4,2]{0,1:T(2,128)S(1)}, u32[]{:S(2)}, u32[]{:S(2)}) collective-permute-start(s32[4,2]{0,1:T(2,128)S(1)} %bitcast.72), channel_id=1, source_target_pairs={{0,2},{2,0},{4,6},{6,4},{8,10},{10,8},{12,14},{14,12},{16,18},{18,... | collective-permute-start | bytes 104 | tf_op jit(solution)/shard_map/ppermute | solution.py:832
  44.3 13.1 %collective-permute-start.10 = (bf16[512,768]{1,0:T(8,128)(2,1)S(1)}, bf16[512,768]{1,0:T(8,128)(2,1)}, u32[]{:S(2)}, u32[]{:S(2)}) collective-permute-start(bf16[512,768]{1,0:T(8,128)(2,1)S(1)} %pad_maximum_fusion.w_own), channel_id=1, source_target_pairs={{0,1},{1,0},{2,3},{3,2},{4,5},{5,4},{6,7},{7,6},{8,9},{9,8},{10,11... | collective-permute-start | bytes 2359304 | tf_op jit(solution)/shard_map/ppermute | solution.py:835
  45.0 21.8 %collective-permute-start.17 = (bf16[512,1024]{1,0:T(8,128)(2,1)S(1)}, bf16[512,1024]{1,0:T(8,128)(2,1)S(1)}, u32[]{:S(2)}, u32[]{:S(2)}) collective-permute-start(bf16[512,1024]{1,0:T(8,128)(2,1)S(1)} %constant_dynamic-slice_fusion.4.w_own), channel_id=1, source_target_pairs={{0,1},{1,0},{2,3},{3,2},{4,5},{5,4},{6,7},{7,6},{8,9},{9,8},{10,11... | collective-permute-start | bytes 3145736 | tf_op jit(solution)/shard_map/ppermute | solution.py:835
  45.6 8.3 %collective-permute-start.6 = (bf16[128,1024]{1,0:T(8,128)(2,1)S(1)}, bf16[128,1024]{1,0:T(8,128)(2,1)S(1)}, u32[]{:S(2)}, u32[]{:S(2)}) collective-permute-start(bf16[128,1024]{1,0:T(8,128)(2,1)S(1)} %bitcast.58), channel_id=1, source_target_pairs={{0,8},{2,10},{4,12},{6,14},{8,0},{10,2},{12,4},{14,6},{16,24},{18,... | collective-permute-start | bytes 786440 | tf_op jit(solution)/shard_map/ppermute | solution.py:829
  49.2 26.0 %collective-permute-start.22 = (bf16[128,1024]{1,0:T(8,128)(2,1)S(1)}, bf16[128,1024]{1,0:T(8,128)(2,1)S(1)}, u32[]{:S(2)}, u32[]{:S(2)}) collective-permute-start(bf16[128,1024]{1,0:T(8,128)(2,1)S(1)} %bitcast.49), channel_id=1, source_target_pairs={{0,24},{2,26},{4,28},{6,30},{8,16},{10,18},{12,20},{14,22},{16,8},... | collective-permute-start | bytes 786440 | tf_op jit(solution)/shard_map/ppermute | solution.py:829
  53.9 22.9 %collective-permute-start.21 = (bf16[128,1024]{1,0:T(8,128)(2,1)S(1)}, bf16[128,1024]{1,0:T(8,128)(2,1)S(1)}, u32[]{:S(2)}, u32[]{:S(2)}) collective-permute-start(bf16[128,1024]{1,0:T(8,128)(2,1)S(1)} %bitcast.50), channel_id=1, source_target_pairs={{0,16},{2,18},{4,20},{6,22},{8,24},{10,26},{12,28},{14,30},{16,0},... | collective-permute-start | bytes 786440 | tf_op jit(solution)/shard_map/ppermute | solution.py:829
  57.4 20.3 %collective-permute-start.20 = (bf16[128,1024]{1,0:T(8,128)(2,1)S(1)}, bf16[128,1024]{1,0:T(8,128)(2,1)S(1)}, u32[]{:S(2)}, u32[]{:S(2)}) collective-permute-start(bf16[128,1024]{1,0:T(8,128)(2,1)S(1)} %bitcast.51), channel_id=1, source_target_pairs={{0,8},{2,10},{4,12},{6,14},{8,0},{10,2},{12,4},{14,6},{16,24},{18,... | collective-permute-start | bytes 786440 | tf_op jit(solution)/shard_map/ppermute | solution.py:829
  62.9 27.5 %collective-permute-start.19 = (bf16[256,1024]{1,0:T(8,128)(2,1)S(1)}, bf16[256,1024]{1,0:T(8,128)(2,1)S(1)}, u32[]{:S(2)}, u32[]{:S(2)}) collective-permute-start(bf16[256,1024]{1,0:T(8,128)(2,1)S(1)} %copy-done.13), channel_id=1, source_target_pairs={{0,1},{1,0},{2,3},{3,2},{4,5},{5,4},{6,7},{7,6},{8,9},{9,8},{10,11... | collective-permute-start | bytes 1572872 | tf_op jit(solution)/shard_map/ppermute | solution.py:835
  66.8 28.2 %collective-permute-start.11 = (bf16[768,128]{1,0:T(8,128)(2,1)S(1)}, bf16[768,128]{1,0:T(8,128)(2,1)S(1)}, u32[]{:S(2)}, u32[]{:S(2)}) collective-permute-start(bf16[768,128]{1,0:T(8,128)(2,1)S(1)} %copy-done.52), channel_id=1, source_target_pairs={{0,2},{2,0},{4,6},{6,4},{8,10},{10,8},{12,14},{14,12},{16,18},{18,... | collective-permute-start | bytes 589832 | tf_op jit(solution)/shard_map/ppermute | solution.py:832
  75.2 21.4 %collective-permute-start.12 = (bf16[768,128]{1,0:T(8,128)(2,1)S(1)}, bf16[768,128]{1,0:T(8,128)(2,1)S(1)}, u32[]{:S(2)}, u32[]{:S(2)}) collective-permute-start(bf16[768,128]{1,0:T(8,128)(2,1)S(1)} %copy-done.50), channel_id=1, source_target_pairs={{0,4},{2,6},{4,0},{6,2},{8,12},{10,14},{12,8},{14,10},{16,20},{18,... | collective-permute-start | bytes 589832 | tf_op jit(solution)/shard_map/ppermute | solution.py:832
  76.8 21.0 %collective-permute-start.13 = (bf16[768,128]{1,0:T(8,128)(2,1)S(1)}, bf16[768,128]{1,0:T(8,128)(2,1)S(1)}, u32[]{:S(2)}, u32[]{:S(2)}) collective-permute-start(bf16[768,128]{1,0:T(8,128)(2,1)S(1)} %copy-done.49), channel_id=1, source_target_pairs={{0,6},{2,4},{4,2},{6,0},{8,14},{10,12},{12,10},{14,8},{16,22},{18,... | collective-permute-start | bytes 589832 | tf_op jit(solution)/shard_map/ppermute | solution.py:832
  89.8 112.4 %collective-permute-start.47 = (bf16[1088,1024]{1,0:T(8,128)(2,1)}, bf16[1088,1024]{1,0:T(8,128)(2,1)S(1)}, u32[]{:S(2)}, u32[]{:S(2)}) collective-permute-start(bf16[1088,1024]{1,0:T(8,128)(2,1)} %get-tuple-element.133), channel_id=1, source_target_pairs={{0,1},{1,0},{2,3},{3,2},{4,5},{5,4},{6,7},{7,6},{8,9},{9,8},{10,11... | collective-permute-start | bytes 6684680 | tf_op jit(solution)/shard_map/ppermute | solution.py:835
  94.0 13.9 %collective-permute-start.26 = (bf16[256,128]{1,0:T(8,128)(2,1)}, bf16[256,128]{1,0:T(8,128)(2,1)S(1)}, u32[]{:S(2)}, u32[]{:S(2)}) collective-permute-start(bf16[256,128]{1,0:T(8,128)(2,1)} %get-tuple-element.93), channel_id=1, source_target_pairs={{0,2},{2,0},{4,6},{6,4},{8,10},{10,8},{12,14},{14,12},{16,18},{18,... | collective-permute-start | bytes 196616 | tf_op jit(solution)/shard_map/ppermute | solution.py:832
  95.1 12.8 %collective-permute-start.27 = (bf16[256,128]{1,0:T(8,128)(2,1)}, bf16[256,128]{1,0:T(8,128)(2,1)S(1)}, u32[]{:S(2)}, u32[]{:S(2)}) collective-permute-start(bf16[256,128]{1,0:T(8,128)(2,1)} %get-tuple-element.94), channel_id=1, source_target_pairs={{0,4},{2,6},{4,0},{6,2},{8,12},{10,14},{12,8},{14,10},{16,20},{18,... | collective-permute-start | bytes 196616 | tf_op jit(solution)/shard_map/ppermute | solution.py:832
  96.6 11.3 %collective-permute-start.28 = (bf16[256,128]{1,0:T(8,128)(2,1)}, bf16[256,128]{1,0:T(8,128)(2,1)S(1)}, u32[]{:S(2)}, u32[]{:S(2)}) collective-permute-start(bf16[256,128]{1,0:T(8,128)(2,1)} %get-tuple-element.95), channel_id=1, source_target_pairs={{0,6},{2,4},{4,2},{6,0},{8,14},{10,12},{12,10},{14,8},{16,22},{18,... | collective-permute-start | bytes 196616 | tf_op jit(solution)/shard_map/ppermute | solution.py:832
  120.2 8.0 %collective-permute-start.29 = (bf16[768,128]{1,0:T(8,128)(2,1)}, bf16[768,128]{1,0:T(8,128)(2,1)S(1)}, u32[]{:S(2)}, u32[]{:S(2)}) collective-permute-start(bf16[768,128]{1,0:T(8,128)(2,1)} %get-tuple-element.102), channel_id=1, source_target_pairs={{0,2},{2,0},{4,6},{6,4},{8,10},{10,8},{12,14},{14,12},{16,18},{18,... | collective-permute-start | bytes 589832 | tf_op jit(solution)/shard_map/ppermute | solution.py:832
  121.1 9.5 %collective-permute-start.30 = (bf16[768,128]{1,0:T(8,128)(2,1)}, bf16[768,128]{1,0:T(8,128)(2,1)S(1)}, u32[]{:S(2)}, u32[]{:S(2)}) collective-permute-start(bf16[768,128]{1,0:T(8,128)(2,1)} %get-tuple-element.103), channel_id=1, source_target_pairs={{0,4},{2,6},{4,0},{6,2},{8,12},{10,14},{12,8},{14,10},{16,20},{18,... | collective-permute-start | bytes 589832 | tf_op jit(solution)/shard_map/ppermute | solution.py:832
  122.6 9.0 %collective-permute-start.31 = (bf16[768,128]{1,0:T(8,128)(2,1)}, bf16[768,128]{1,0:T(8,128)(2,1)S(1)}, u32[]{:S(2)}, u32[]{:S(2)}) collective-permute-start(bf16[768,128]{1,0:T(8,128)(2,1)} %get-tuple-element.104), channel_id=1, source_target_pairs={{0,6},{2,4},{4,2},{6,0},{8,14},{10,12},{12,10},{14,8},{16,22},{18,... | collective-permute-start | bytes 589832 | tf_op jit(solution)/shard_map/ppermute | solution.py:832
  140.2 16.9 %collective-permute-start.35 = (bf16[576,768]{1,0:T(8,128)(2,1)}, bf16[576,768]{1,0:T(8,128)(2,1)S(1)}, u32[]{:S(2)}, u32[]{:S(2)}) collective-permute-start(bf16[576,768]{1,0:T(8,128)(2,1)} %get-tuple-element.114), channel_id=1, source_target_pairs={{0,1},{1,0},{2,3},{3,2},{4,5},{5,4},{6,7},{7,6},{8,9},{9,8},{10,11... | collective-permute-start | bytes 2654216 | tf_op jit(solution)/shard_map/ppermute | solution.py:835
  140.3 4.5 %collective-permute-start.14 = (bf16[256,128]{1,0:T(8,128)(2,1)S(1)}, bf16[256,128]{1,0:T(8,128)(2,1)S(1)}, u32[]{:S(2)}, u32[]{:S(2)}) collective-permute-start(bf16[256,128]{1,0:T(8,128)(2,1)S(1)} %copy-done.59), channel_id=1, source_target_pairs={{0,2},{2,0},{4,6},{6,4},{8,10},{10,8},{12,14},{14,12},{16,18},{18,... | collective-permute-start | bytes 196616 | tf_op jit(solution)/shard_map/ppermute | solution.py:832
  141.4 4.3 %collective-permute-start.15 = (bf16[256,128]{1,0:T(8,128)(2,1)S(1)}, bf16[256,128]{1,0:T(8,128)(2,1)S(1)}, u32[]{:S(2)}, u32[]{:S(2)}) collective-permute-start(bf16[256,128]{1,0:T(8,128)(2,1)S(1)} %copy-done.58), channel_id=1, source_target_pairs={{0,4},{2,6},{4,0},{6,2},{8,12},{10,14},{12,8},{14,10},{16,20},{18,... | collective-permute-start | bytes 196616 | tf_op jit(solution)/shard_map/ppermute | solution.py:832
  142.7 5.2 %collective-permute-start.16 = (bf16[256,128]{1,0:T(8,128)(2,1)S(1)}, bf16[256,128]{1,0:T(8,128)(2,1)S(1)}, u32[]{:S(2)}, u32[]{:S(2)}) collective-permute-start(bf16[256,128]{1,0:T(8,128)(2,1)S(1)} %copy-done.57), channel_id=1, source_target_pairs={{0,6},{2,4},{4,2},{6,0},{8,14},{10,12},{12,10},{14,8},{16,22},{18,... | collective-permute-start | bytes 196616 | tf_op jit(solution)/shard_map/ppermute | solution.py:832
  152.5 24.5 %copy-start.48 = (bf16[128,1024]{1,0:T(8,128)(2,1)S(1)}, bf16[128,1024]{1,0:T(8,128)(2,1)}, u32[]{:S(2)}) copy-start(bf16[128,1024]{1,0:T(8,128)(2,1)} %get-tuple-element.127) | copy-start | bytes 786436
  152.5 24.6 %copy-start.47 = (bf16[128,1024]{1,0:T(8,128)(2,1)S(1)}, bf16[128,1024]{1,0:T(8,128)(2,1)}, u32[]{:S(2)}) copy-start(bf16[128,1024]{1,0:T(8,128)(2,1)} %get-tuple-element.110) | copy-start | bytes 786436
  152.5 27.4 %copy-start.46 = (bf16[128,1024]{1,0:T(8,128)(2,1)S(1)}, bf16[128,1024]{1,0:T(8,128)(2,1)}, u32[]{:S(2)}) copy-start(bf16[128,1024]{1,0:T(8,128)(2,1)} %get-tuple-element.111) | copy-start | bytes 786436
  152.5 11.3 %collective-permute-start.23 = (bf16[128,1024]{1,0:T(8,128)(2,1)}, bf16[128,1024]{1,0:T(8,128)(2,1)S(1)}, u32[]{:S(2)}, u32[]{:S(2)}) collective-permute-start(bf16[128,1024]{1,0:T(8,128)(2,1)} %get-tuple-element.89), channel_id=1, source_target_pairs={{0,8},{2,10},{4,12},{6,14},{8,0},{10,2},{12,4},{14,6},{16,24},{18,... | collective-permute-start | bytes 786440 | tf_op jit(solution)/shard_map/ppermute | solution.py:829
  154.6 21.2 %collective-permute-start.24 = (bf16[128,1024]{1,0:T(8,128)(2,1)}, bf16[128,1024]{1,0:T(8,128)(2,1)S(1)}, u32[]{:S(2)}, u32[]{:S(2)}) collective-permute-start(bf16[128,1024]{1,0:T(8,128)(2,1)} %get-tuple-element.90), channel_id=1, source_target_pairs={{0,16},{2,18},{4,20},{6,22},{8,24},{10,26},{12,28},{14,30},{16,0},... | collective-permute-start | bytes 786440 | tf_op jit(solution)/shard_map/ppermute | solution.py:829
  155.3 21.8 %collective-permute-start.25 = (bf16[128,1024]{1,0:T(8,128)(2,1)}, bf16[128,1024]{1,0:T(8,128)(2,1)S(1)}, u32[]{:S(2)}, u32[]{:S(2)}) collective-permute-start(bf16[128,1024]{1,0:T(8,128)(2,1)} %get-tuple-element.91), channel_id=1, source_target_pairs={{0,24},{2,26},{4,28},{6,30},{8,16},{10,18},{12,20},{14,22},{16,8},... | collective-permute-start | bytes 786440 | tf_op jit(solution)/shard_map/ppermute | solution.py:829
  157.1 3.9 %collective-permute-start.42 = (f32[8,128]{1,0:T(8,128)S(1)}, f32[8,128]{1,0:T(8,128)S(1)}, u32[]{:S(2)}, u32[]{:S(2)}) collective-permute-start(f32[8,128]{1,0:T(8,128)S(1)} %copy-done.35), channel_id=1, source_target_pairs={{0,1},{1,0},{2,3},{3,2},{4,5},{5,4},{6,7},{7,6},{8,9},{9,8},{10,11... | collective-permute-start | bytes 12296 | tf_op jit(solution)/shard_map/ppermute | solution.py:835
  160.9 16.2 %collective-permute-start.36 = (bf16[144,768]{1,0:T(8,128)(2,1)}, bf16[144,768]{1,0:T(8,128)(2,1)S(1)}, u32[]{:S(2)}, u32[]{:S(2)}) collective-permute-start(bf16[144,768]{1,0:T(8,128)(2,1)} %get-tuple-element.116), channel_id=1, source_target_pairs={{0,2},{2,0},{4,6},{6,4},{8,10},{10,8},{12,14},{14,12},{16,18},{18,... | collective-permute-start | bytes 663560 | tf_op jit(solution)/shard_map/ppermute | solution.py:832
  163.8 46.2 %copy-start.14 = (bf16[128,1024]{1,0:T(8,128)(2,1)}, bf16[128,1024]{1,0:T(8,128)(2,1)S(1)}, u32[]{:S(2)}) copy-start(bf16[128,1024]{1,0:T(8,128)(2,1)S(1)} %collective-permute-done.23.r1) | copy-start | bytes 786436
  163.8 16.2 %collective-permute-start.37 = (bf16[144,768]{1,0:T(8,128)(2,1)}, bf16[144,768]{1,0:T(8,128)(2,1)S(1)}, u32[]{:S(2)}, u32[]{:S(2)}) collective-permute-start(bf16[144,768]{1,0:T(8,128)(2,1)} %get-tuple-element.117), channel_id=1, source_target_pairs={{0,4},{2,6},{4,0},{6,2},{8,12},{10,14},{12,8},{14,10},{16,20},{18,... | collective-permute-start | bytes 663560 | tf_op jit(solution)/shard_map/ppermute | solution.py:832
  175.8 34.2 %copy-start.15 = (bf16[128,1024]{1,0:T(8,128)(2,1)}, bf16[128,1024]{1,0:T(8,128)(2,1)S(1)}, u32[]{:S(2)}) copy-start(bf16[128,1024]{1,0:T(8,128)(2,1)S(1)} %collective-permute-done.24.r2) | copy-start | bytes 786436
  175.8 7.0 %collective-permute-start.38 = (bf16[144,768]{1,0:T(8,128)(2,1)}, bf16[144,768]{1,0:T(8,128)(2,1)S(1)}, u32[]{:S(2)}, u32[]{:S(2)}) collective-permute-start(bf16[144,768]{1,0:T(8,128)(2,1)} %get-tuple-element.118), channel_id=1, source_target_pairs={{0,6},{2,4},{4,2},{6,0},{8,14},{10,12},{12,10},{14,8},{16,22},{18,... | collective-permute-start | bytes 663560 | tf_op jit(solution)/shard_map/ppermute | solution.py:832
  177.0 33.0 %copy-start.16 = (bf16[128,1024]{1,0:T(8,128)(2,1)}, bf16[128,1024]{1,0:T(8,128)(2,1)S(1)}, u32[]{:S(2)}) copy-start(bf16[128,1024]{1,0:T(8,128)(2,1)S(1)} %collective-permute-done.25.r3) | copy-start | bytes 786436
  177.0 9.3 %collective-permute-start.43 = (bf16[128,1024]{1,0:T(8,128)(2,1)S(1)}, bf16[128,1024]{1,0:T(8,128)(2,1)S(1)}, u32[]{:S(2)}, u32[]{:S(2)}) collective-permute-start(bf16[128,1024]{1,0:T(8,128)(2,1)S(1)} %copy-done.48), channel_id=1, source_target_pairs={{0,1},{1,0},{2,3},{3,2},{4,5},{5,4},{6,7},{7,6},{8,9},{9,8},{10,11... | collective-permute-start | bytes 786440 | tf_op jit(solution)/shard_map/ppermute | solution.py:835
  177.1 14.0 %collective-permute-start.32 = (bf16[128,1024]{1,0:T(8,128)(2,1)S(1)}, bf16[128,1024]{1,0:T(8,128)(2,1)S(1)}, u32[]{:S(2)}, u32[]{:S(2)}) collective-permute-start(bf16[128,1024]{1,0:T(8,128)(2,1)S(1)} %copy-done.47), channel_id=1, source_target_pairs={{0,8},{2,10},{4,12},{6,14},{8,0},{10,2},{12,4},{14,6},{16,24},{18,... | collective-permute-start | bytes 786440 | tf_op jit(solution)/shard_map/ppermute | solution.py:829
  180.0 21.4 %collective-permute-start.33 = (bf16[128,1024]{1,0:T(8,128)(2,1)S(1)}, bf16[128,1024]{1,0:T(8,128)(2,1)S(1)}, u32[]{:S(2)}, u32[]{:S(2)}) collective-permute-start(bf16[128,1024]{1,0:T(8,128)(2,1)S(1)} %copy-done.46), channel_id=1, source_target_pairs={{0,16},{2,18},{4,20},{6,22},{8,24},{10,26},{12,28},{14,30},{16,0},... | collective-permute-start | bytes 786440 | tf_op jit(solution)/shard_map/ppermute | solution.py:829
  182.8 27.2 %collective-permute-start.34 = (bf16[128,1024]{1,0:T(8,128)(2,1)}, bf16[128,1024]{1,0:T(8,128)(2,1)}, u32[]{:S(2)}, u32[]{:S(2)}) collective-permute-start(bf16[128,1024]{1,0:T(8,128)(2,1)} %get-tuple-element.112), channel_id=1, source_target_pairs={{0,24},{2,26},{4,28},{6,30},{8,16},{10,18},{12,20},{14,22},{16,8},... | collective-permute-start | bytes 786440 | tf_op jit(solution)/shard_map/ppermute | solution.py:829
  186.3 26.8 %collective-permute-start.39 = (bf16[48,768]{1,0:T(8,128)(2,1)}, bf16[48,768]{1,0:T(8,128)(2,1)}, u32[]{:S(2)}, u32[]{:S(2)}) collective-permute-start(bf16[48,768]{1,0:T(8,128)(2,1)} %get-tuple-element.120), channel_id=1, source_target_pairs={{0,8},{2,10},{4,12},{6,14},{8,0},{10,2},{12,4},{14,6},{16,24},{18,... | collective-permute-start | bytes 221192 | tf_op jit(solution)/shard_map/ppermute | solution.py:829
  191.1 24.3 %copy-start.18 = (bf16[128,1024]{1,0:T(8,128)(2,1)}, bf16[128,1024]{1,0:T(8,128)(2,1)S(1)}, u32[]{:S(2)}) copy-start(bf16[128,1024]{1,0:T(8,128)(2,1)S(1)} %collective-permute-done.32.r1) | copy-start | bytes 786436
  191.1 19.0 %collective-permute-start.44 = (bf16[32,1024]{1,0:T(8,128)(2,1)}, bf16[32,1024]{1,0:T(8,128)(2,1)}, u32[]{:S(2)}, u32[]{:S(2)}) collective-permute-start(bf16[32,1024]{1,0:T(8,128)(2,1)} %get-tuple-element.129), channel_id=1, source_target_pairs={{0,2},{2,0},{4,6},{6,4},{8,10},{10,8},{12,14},{14,12},{16,18},{18,... | collective-permute-start | bytes 196616 | tf_op jit(solution)/shard_map/ppermute | solution.py:832
  201.4 10.0 %collective-permute-start.45 = (bf16[32,1024]{1,0:T(8,128)(2,1)}, bf16[32,1024]{1,0:T(8,128)(2,1)}, u32[]{:S(2)}, u32[]{:S(2)}) collective-permute-start(bf16[32,1024]{1,0:T(8,128)(2,1)} %get-tuple-element.130), channel_id=1, source_target_pairs={{0,4},{2,6},{4,0},{6,2},{8,12},{10,14},{12,8},{14,10},{16,20},{18,... | collective-permute-start | bytes 196616 | tf_op jit(solution)/shard_map/ppermute | solution.py:832
  202.2 10.1 %collective-permute-start.46 = (bf16[32,1024]{1,0:T(8,128)(2,1)}, bf16[32,1024]{1,0:T(8,128)(2,1)}, u32[]{:S(2)}, u32[]{:S(2)}) collective-permute-start(bf16[32,1024]{1,0:T(8,128)(2,1)} %get-tuple-element.131), channel_id=1, source_target_pairs={{0,6},{2,4},{4,2},{6,0},{8,14},{10,12},{12,10},{14,8},{16,22},{18,... | collective-permute-start | bytes 196616 | tf_op jit(solution)/shard_map/ppermute | solution.py:832
  210.1 11.9 %collective-permute-start.40 = (bf16[48,768]{1,0:T(8,128)(2,1)S(1)}, bf16[48,768]{1,0:T(8,128)(2,1)S(1)}, u32[]{:S(2)}, u32[]{:S(2)}) collective-permute-start(bf16[48,768]{1,0:T(8,128)(2,1)S(1)} %copy-done.56), channel_id=1, source_target_pairs={{0,16},{2,18},{4,20},{6,22},{8,24},{10,26},{12,28},{14,30},{16,0},... | collective-permute-start | bytes 221192 | tf_op jit(solution)/shard_map/ppermute | solution.py:829
  210.2 11.8 %collective-permute-start.41 = (bf16[48,768]{1,0:T(8,128)(2,1)S(1)}, bf16[48,768]{1,0:T(8,128)(2,1)S(1)}, u32[]{:S(2)}, u32[]{:S(2)}) collective-permute-start(bf16[48,768]{1,0:T(8,128)(2,1)S(1)} %copy-done.55), channel_id=1, source_target_pairs={{0,24},{2,26},{4,28},{6,30},{8,16},{10,18},{12,20},{14,22},{16,8},... | collective-permute-start | bytes 221192 | tf_op jit(solution)/shard_map/ppermute | solution.py:829
  211.3 15.9 %collective-permute-start.48 = (bf16[272,1024]{1,0:T(8,128)(2,1)}, bf16[272,1024]{1,0:T(8,128)(2,1)S(1)}, u32[]{:S(2)}, u32[]{:S(2)}) collective-permute-start(bf16[272,1024]{1,0:T(8,128)(2,1)} %get-tuple-element.135), channel_id=1, source_target_pairs={{0,2},{2,0},{4,6},{6,4},{8,10},{10,8},{12,14},{14,12},{16,18},{18,... | collective-permute-start | bytes 1671176 | tf_op jit(solution)/shard_map/ppermute | solution.py:832
  212.3 23.5 %collective-permute-start.49 = (bf16[272,1024]{1,0:T(8,128)(2,1)}, bf16[272,1024]{1,0:T(8,128)(2,1)S(1)}, u32[]{:S(2)}, u32[]{:S(2)}) collective-permute-start(bf16[272,1024]{1,0:T(8,128)(2,1)} %get-tuple-element.136), channel_id=1, source_target_pairs={{0,4},{2,6},{4,0},{6,2},{8,12},{10,14},{12,8},{14,10},{16,20},{18,... | collective-permute-start | bytes 1671176 | tf_op jit(solution)/shard_map/ppermute | solution.py:832
  213.1 22.7 %collective-permute-start.50 = (bf16[272,1024]{1,0:T(8,128)(2,1)}, bf16[272,1024]{1,0:T(8,128)(2,1)S(1)}, u32[]{:S(2)}, u32[]{:S(2)}) collective-permute-start(bf16[272,1024]{1,0:T(8,128)(2,1)} %get-tuple-element.137), channel_id=1, source_target_pairs={{0,6},{2,4},{4,2},{6,0},{8,14},{10,12},{12,10},{14,8},{16,22},{18,... | collective-permute-start | bytes 1671176 | tf_op jit(solution)/shard_map/ppermute | solution.py:832
  240.7 5.9 %collective-permute-start.51 = (bf16[32,1024]{1,0:T(8,128)(2,1)}, bf16[32,1024]{1,0:T(8,128)(2,1)S(1)}, u32[]{:S(2)}, u32[]{:S(2)}) collective-permute-start(bf16[32,1024]{1,0:T(8,128)(2,1)} %get-tuple-element.140), channel_id=1, source_target_pairs={{0,8},{2,10},{4,12},{6,14},{8,0},{10,2},{12,4},{14,6},{16,24},{18,... | collective-permute-start | bytes 196616 | tf_op jit(solution)/shard_map/ppermute | solution.py:829
  243.5 5.5 %collective-permute-start.52 = (bf16[32,1024]{1,0:T(8,128)(2,1)}, bf16[32,1024]{1,0:T(8,128)(2,1)S(1)}, u32[]{:S(2)}, u32[]{:S(2)}) collective-permute-start(bf16[32,1024]{1,0:T(8,128)(2,1)} %get-tuple-element.141), channel_id=1, source_target_pairs={{0,16},{2,18},{4,20},{6,22},{8,24},{10,26},{12,28},{14,30},{16,0},... | collective-permute-start | bytes 196616 | tf_op jit(solution)/shard_map/ppermute | solution.py:829
  244.7 6.3 %collective-permute-start.53 = (bf16[32,1024]{1,0:T(8,128)(2,1)}, bf16[32,1024]{1,0:T(8,128)(2,1)S(1)}, u32[]{:S(2)}, u32[]{:S(2)}) collective-permute-start(bf16[32,1024]{1,0:T(8,128)(2,1)} %get-tuple-element.142), channel_id=1, source_target_pairs={{0,24},{2,26},{4,28},{6,30},{8,16},{10,18},{12,20},{14,22},{16,8},... | collective-permute-start | bytes 196616 | tf_op jit(solution)/shard_map/ppermute | solution.py:829
  (54 other events, 209.9 us)

commit v2 on v0

--- a/solution.py
+++ b/solution.py
@@ -3,7 +3,10 @@
 
 import jax
 import jax.numpy as jnp
+import numpy as np
 from jax import lax
+from jax.experimental import pallas as pl
+from jax.experimental.pallas import tpu as pltpu
 from jax.sharding import PartitionSpec as P
 
 HEADS = 16
@@ -335,9 +338,903 @@
     )
 
 
+LINES = 4
+ACROSS = HEADS // LINES
+F32 = jnp.float32
+BF16 = jnp.bfloat16
+VMEM_LIMIT = 16 * 1024 * 1024
+TIMES = {'branch': 500, 'layer': 500}
+
+VEC = 16
+
+
+def dot(left, right):
+    return jnp.dot(left, right, preferred_element_type=F32)
+
+
+def dot_nt(left, right):
+    return lax.dot_general(left, right, (((1,), (1,)), ((), ())), preferred_element_type=F32)
+
+
+class Far(tuple):
+    pass
+
+
+class Near(tuple):
+    pass
+
+
+def far(*x):
+    return Far(x)
+
+
+def near(*x):
+    return Near(x)
+
+
+def raw(x):
+    return x[0] if isinstance(x, (Far, Near)) else x
+
+
+def spot():
+    context = lax.axis_index("ctx")
+    return context // ACROSS, context % ACROSS, lax.axis_index("fsdp")
+
+
+def call(kernel, out_shapes, scratch, *operands, after=(), loose_in=0):
+    whole = pl.BlockSpec(memory_space=pltpu.VMEM)
+    loose = pl.BlockSpec(memory_space=pl.ANY)
+    arrays, specs = [], []
+    for x in operands:
+        if isinstance(x, Far):
+            arrays.append(pltpu.with_memory_space_constraint(x[0], pltpu.HBM))
+        elif isinstance(x, Near):
+            arrays.append(pltpu.with_memory_space_constraint(x[0], pltpu.VMEM))
+        else:
+            arrays.append(x)
+        if arrays[-1].dtype == jnp.int32 and arrays[-1].ndim == 1:
+            specs.append(pl.BlockSpec(memory_space=pltpu.SMEM))
+        else:
+            specs.append(loose if len(specs) < loose_in else whole)
+    outs = []
+    for shape in out_shapes:
+        if isinstance(shape, Far):
+            outs.append(pltpu.HBM(*shape))
+        elif isinstance(shape, Near):
+            outs.append(pltpu.VMEM(*shape))
+        else:
+            outs.append(jax.ShapeDtypeStruct(*shape))
+    count = len(arrays)
+
+    def body(*refs):
+        kernel(*refs[:count], *refs[count + len(after) :])
+
+    name = kernel.__name__.removesuffix("_kernel")
+    results = pl.pallas_call(
+        body,
+        name=name,
+        out_shape=outs,
+        in_specs=specs + [loose] * len(after),
+        out_specs=[whole for _ in outs],
+        scratch_shapes=scratch,
+        compiler_params=pltpu.CompilerParams(vmem_limit_bytes=VMEM_LIMIT),
+        cost_estimate=pl.CostEstimate(
+            flops=TIMES.get(name, 0) * 115_000_000, bytes_accessed=0, transcendentals=0
+        ),
+    )(*arrays, *map(raw, after))
+    return [
+        near(x) if isinstance(shape, Near) else x for x, shape in zip(results, out_shapes)
+    ]
+
+
+def run_copies(pairs, sems):
+    copies = [pltpu.make_async_copy(x, y, sems.at[i]) for i, (x, y) in enumerate(pairs)]
+    for copy in copies:
+        copy.start()
+    for copy in copies:
+        copy.wait()
+
+
+def prepare_kernel(qkv, w_in, w_out, w_down, gain, shift, b_out, b_down, qv, b_in, packed, sems):
+    line, _, _ = spot()
+    heads, feed = qkv.shape[1] // 12, w_in.shape[1] // LINES
+    part = line % (LINES // 2)
+    row = 0
+    pairs = []
+    for source in (
+        w_in.at[:, pl.ds(pl.multiple_of(feed * line, 128), feed)],
+        w_out.at[pl.ds(pl.multiple_of(heads * part, 16), heads), :],
+        w_down.at[pl.ds(pl.multiple_of(feed * part, 16), feed), :],
+    ):
+        pairs.append((source, packed.at[row : row + source.shape[0], :]))
+        row += source.shape[0]
+    half = qkv.shape[0]
+    for i in range(3):
+        columns = pl.ds(pl.multiple_of(heads * (LINES * i + line), 128), heads)
+        pairs.append(
+            (qkv.at[:, columns], packed.at[row : row + half, heads * i : heads * (i + 1)])
+        )
+    row += half
+    rows = [x[...].astype(F32).reshape(1, half) for x in (gain, shift, b_out, b_down)]
+    rows += [qv[...].astype(F32), b_in[...].astype(F32).reshape(4, half)]
+    rows.append(jnp.zeros((VEC - 10, half), F32))
+    packed[row : row + VEC, :half] = jnp.concatenate(rows, 0).astype(BF16)
+    run_copies(pairs, sems)
+
+
+def assemble_kernel(own, twin, qkv, w_in, w_out, w_down, vectors, low, sems):
+    line, _, core = spot()
+    half = qkv.shape[0] // 2
+    heads, feed = w_out.shape[0], w_down.shape[0]
+    qkv_row = half + heads + feed
+    vec_row = qkv_row + half
+    pairs = []
+    for source, side in ((own, core), (twin, 1 - core)):
+        rows = pl.ds(pl.multiple_of(half * side, half), half)
+        pairs.append((source.at[:half, :], w_in.at[rows, :]))
+        pairs.append((source.at[qkv_row:vec_row, : 3 * heads], qkv.at[rows, :]))
+        spare = pl.ds(pl.multiple_of(VEC * side, VEC), VEC)
+        pairs.append((source.at[vec_row:, :half], low.at[spare, :]))
+    holds = core == line // (LINES // 2)
+
+    @pl.when(holds)
+    def _():
+        rest = [
+            (own.at[half : half + heads, :], w_out),
+            (own.at[half + heads : qkv_row, :], w_down),
+        ]
+        run_copies(pairs + rest, sems)
+
+    @pl.when(jnp.logical_not(holds))
+    def _():
+        rest = [
+            (twin.at[half : half + heads, :], w_out),
+            (twin.at[half + heads : qkv_row, :], w_down),
+        ]
+        run_copies(pairs + rest, sems)
+
+    vectors[...] = low[...].astype(F32)
+
+
+def full_row(vectors, index):
+    return jnp.concatenate(
+        [vectors[index : index + 1, :], vectors[VEC + index : VEC + index + 1, :]], 1
+    )
+
+
+def pack_kernel(order, tokens, packed):
+    rows = tokens.shape[0]
+    packed[:rows, :] = tokens[...]
+    lane = lax.broadcasted_iota(jnp.int32, (VEC, 128), 1)
+    numbers = jnp.where(lane == 0, order[0], jnp.where(lane == 1, order[1], 0))
+    packed[rows:, :128] = numbers.astype(F32).astype(BF16)
+    packed[rows:, 128:] = jnp.zeros((VEC, tokens.shape[1] - 128), BF16)
+
+
+def hold_kernel(x, y):
+    y[...] = x[...]
+
+
+def reorder(chunks, place):
+    upper, lower = chunks
+    turned = (place & 2) != 0
+    near_by = (place & 1) != 0
+    first = jnp.where(turned, lower, upper)
+    second = jnp.where(turned, upper, lower)
+    first = jnp.where(near_by, pltpu.roll(first, 64, 1), first)
+    second = jnp.where(near_by, pltpu.roll(second, 64, 1), second)
+    return first, second
+
+
+def left_lanes(rows):
+    return lax.broadcasted_iota(jnp.int32, (rows, 128), 1) < 64
+
+
+def pair_heads(one, two, slot):
+    keep = left_lanes(one.shape[0])
+    if slot % 2 == 0:
+        return jnp.where(keep, one, pltpu.roll(two, 64, 1))
+    return jnp.where(keep, pltpu.roll(one, 64, 1), two)
+
+
+def fold_rows(chunk, slot):
+    rows = chunk.shape[0] // 2
+    return pair_heads(chunk[:rows], chunk[rows:], slot)
+
+
+def unfold_pair(even, odd):
+    keep = left_lanes(even.shape[0])
+    top = jnp.where(keep, even, pltpu.roll(odd, 64, 1))
+    bottom = jnp.where(keep, pltpu.roll(even, 64, 1), odd)
+    return jnp.concatenate([top, bottom], 0)
+
+
+def normalise(rows):
+    x = rows.astype(F32)
+    centred = x - jnp.mean(x, -1, keepdims=True)
+    inverse = lax.rsqrt(jnp.mean(centred * centred, -1, keepdims=True) + epsilon)
+    return centred * inverse, inverse
+
+
+def two_chunks(x):
+    return x[:, :128], x[:, 128:256]
+
+
+def two_chunks(x):
+    return x[:, :128], x[:, 128:256]
+
+
+def project_kernel(t0, t1, t2, t3, vectors, qkv, s0, s1, s2, s3, ln_ref, lnt_ref, normed_ref):
+    line, place, _ = spot()
+    rows = t0.shape[0] - VEC
+    gain, shift = full_row(vectors, 0), full_row(vectors, 1)
+    numbers = jnp.zeros((VEC, 128), F32)
+    for k, ref in enumerate((t0, t1, t2, t3)):
+        source = line ^ k
+        part = pl.ds(pl.multiple_of(rows * source, rows), rows)
+        normed, _ = normalise(ref[:rows, :])
+        normed_ref[part, :] = normed
+        ln_ref[part, :] = (normed * gain + shift).astype(BF16)
+        numbers = numbers + pltpu.roll(ref[rows:, :128].astype(F32), 2 * source, 1)
+    side = VEC * (line // (LINES // 2))
+    lanes = pl.ds(pl.multiple_of(256 * (line % (LINES // 2)), 256), 256)
+    bias_q = vectors[pl.ds(side + 4, 1), lanes]
+    bias_v = vectors[pl.ds(side + 5, 1), lanes]
+    q_chunks = reorder(two_chunks(dot(ln_ref[...], qkv[:, :256]) + bias_q), place)
+    k_chunks = reorder(two_chunks(dot(ln_ref[...], qkv[:, 256:512])), place)
+    v_chunks = reorder(two_chunks(dot(ln_ref[...], qkv[:, 512:]) + bias_v), place)
+    total = ln_ref.shape[0]
+    end = total * 3 // 2
+    for slot, ref in enumerate((s0, s1, s2, s3)):
+        pair = slot // 2
+        ref[:total, :] = pair_heads(q_chunks[pair], k_chunks[pair], slot).astype(BF16)
+        ref[total:end, :] = fold_rows(v_chunks[pair], slot).astype(BF16)
+        ref[end:, :] = numbers.astype(BF16)
+    lnt_ref[...] = ln_ref[...].T
+
+
+def back_rows_kernel(c0, c1, c2, c3, w_out, att, s0, s1, s2, s3, cot):
+    line, place, _ = spot()
+    rows = c0.shape[0]
+    for k, ref in enumerate((c0, c1, c2, c3)):
+        cot[pl.ds(pl.multiple_of(rows * (line ^ k), rows), rows), :] = ref[...]
+    chunks = reorder(two_chunks(dot_nt(cot[...], w_out[...])), place)
+    fold = att.shape[0] // 4
+    for slot, ref in enumerate((s0, s1, s2, s3)):
+        ref[:fold, :] = att[fold * slot : fold * (slot + 1), :]
+        ref[fold:, :] = fold_rows(chunks[slot // 2], slot).astype(BF16)
+
+
+def block_rows(table):
+    for j in range(4):
+        for i in range(8):
+            yield j, i, pl.ds(pl.multiple_of(table[8 * j, i] * 64, 64), 64)
+
+
+def sort_rows(table, slots, target, base, folded):
+    for j, i, dest in block_rows(table):
+        if folded:
+            start = base + 64 * (i % 4)
+            lanes = slice(0, 64) if i < 4 else slice(64, 128)
+            target[dest, :] = slots[j][start : start + 64, lanes]
+        else:
+            target[dest, :] = slots[j][base + 64 * i : base + 64 * (i + 1), :]
+
+
+def turn(x, cosine, sine):
+    lane = lax.broadcasted_iota(jnp.int32, x.shape, 1) & (HEAD_DIM - 1)
+    other = jnp.where(lane < ROT // 2, pltpu.roll(x, 120, 1), pltpu.roll(x, 8, 1))
+    return x * cosine + other * sine
+
+
+TILE = 256
+
+
+def scores_of(qk_ref, i):
+    rows = slice(TILE * i, TILE * (i + 1))
+    queries = jnp.where(left_lanes(TILE), qk_ref[rows, :], jnp.zeros((), BF16))
+    queries = queries * jnp.asarray(HEAD_DIM ** (-0.5), BF16)
+    return queries
+
+
+def allowed_tile():
+    row = lax.broadcasted_iota(jnp.int32, (TILE, TILE), 0)
+    col = lax.broadcasted_iota(jnp.int32, (TILE, TILE), 1)
+    return row >= col
+
+
+def attend_kernel(r0, r1, r2, r3, cosine, sine, *rest):
+    att_slots, qk_ref, kq_ref, v_ref, att_ref, lse_ref, table_ref, raw, table, sem = rest
+    refs = (r0, r1, r2, r3)
+    count = qk_ref.shape[0]
+    lines = count // 4
+    for j, ref in enumerate(refs):
+        numbers = ref[lines * 3 // 2 :, :].astype(F32)[:8, :]
+        table_ref[8 * j : 8 * (j + 1), :] = numbers.astype(jnp.int32)
+    run_copies([(table_ref, table)], sem)
+    sort_rows(table, refs, raw, 0, False)
+    sort_rows(table, refs, v_ref, lines, True)
+    for i in range(count // TILE):
+        rows = slice(TILE * i, TILE * (i + 1))
+        turned = turn(raw[rows, :].astype(F32), cosine[rows, :], sine[rows, :])
+        qk_ref[rows, :] = turned.astype(BF16)
+        kq_ref[rows, :] = pltpu.roll(turned, 64, 1).astype(BF16)
+    mask = allowed_tile()
+    for i in range(count // TILE):
+        rows = slice(TILE * i, TILE * (i + 1))
+        keys = TILE * (i + 1)
+        scores = dot_nt(scores_of(qk_ref, i), kq_ref[:keys, :])
+        last = jnp.where(mask, scores[:, keys - TILE :], -1e30)
+        scores = last if i == 0 else jnp.concatenate([scores[:, : keys - TILE], last], 1)
+        top = jnp.max(scores, -1, keepdims=True)
+        weights = jnp.exp(scores - top)
+        total = jnp.sum(weights, -1, keepdims=True)
+        weighted = dot(weights.astype(BF16), v_ref[:keys, :])
+        att_ref[rows, :] = weighted / total
+        lse_ref[rows, :] = top + jnp.log(total)
+    for j, i, source in block_rows(table):
+        start = lines // 2 * j + 64 * (i % 4)
+        lanes = slice(0, 64) if i < 4 else slice(64, 128)
+        att_slots[start : start + 64, lanes] = att_ref[source, :].astype(BF16)
+
+
+def attend_back_kernel(r0, r1, r2, r3, table_ref, qk_ref, kq_ref, v_ref, att_ref, *rest):
+    lse_ref, cosine, sine, o0, o1, o2, o3, sums, ga_ref, kt_ref, vt_ref, gqk, gv = rest[:13]
+    table, sem = rest[13:]
+    refs = (r0, r1, r2, r3)
+    count = qk_ref.shape[0]
+    lines = count // 4
+    run_copies([(table_ref, table)], sem)
+    sort_rows(table, refs, ga_ref, lines // 2, True)
+    mask = allowed_tile()
+    kt_ref[...] = jnp.zeros_like(kt_ref)
+    vt_ref[...] = jnp.zeros_like(vt_ref)
+    for i in range(count // TILE):
+        rows = slice(TILE * i, TILE * (i + 1))
+        keys = TILE * (i + 1)
+        queries = scores_of(qk_ref, i)
+        scores = dot_nt(queries, kq_ref[:keys, :])
+        last = jnp.where(mask, scores[:, keys - TILE :], -1e30)
+        scores = last if i == 0 else jnp.concatenate([scores[:, : keys - TILE], last], 1)
+        probs = jnp.exp(scores - lse_ref[rows, :])
+        grad_rows = ga_ref[rows, :]
+        delta = jnp.sum(grad_rows.astype(F32) * att_ref[rows, :], -1, keepdims=True)
+        grad_probs = dot_nt(grad_rows, v_ref[:keys, :])
+        grad_scores = (probs * (grad_probs - delta)).astype(BF16)
+        gqk[rows, :] = dot(grad_scores, kq_ref[:keys, :]) * HEAD_DIM ** (-0.5)
+        vt_ref[:, :keys] += dot(grad_rows.astype(F32).T.astype(BF16), probs.astype(BF16))
+        kt_ref[:, :keys] += dot(queries.astype(F32).T.astype(BF16), grad_scores)
+    sum_q = jnp.zeros((1, 128), F32)
+    sum_v = jnp.zeros((1, 64), F32)
+    for i in range(count // TILE):
+        rows = slice(TILE * i, TILE * (i + 1))
+        grad_keys = pltpu.roll(kt_ref[:, rows].T, 64, 1)
+        both = jnp.where(left_lanes(TILE), gqk[rows, :], grad_keys)
+        both = turn(both, cosine[rows, :], -sine[rows, :])
+        both = both.astype(BF16).astype(F32)
+        values = vt_ref[:, rows].T.astype(BF16).astype(F32)
+        gqk[rows, :] = both
+        gv[rows, :] = values
+        sum_q = sum_q + jnp.sum(both, 0, keepdims=True)
+        sum_v = sum_v + jnp.sum(values, 0, keepdims=True)
+    sums[...] = jnp.zeros_like(sums)
+    sums[0:1, :64] = sum_q[:, :64]
+    sums[1:2, :64] = sum_v
+    outs = (o0, o1, o2, o3)
+    for j, i, source in block_rows(table):
+        lanes = slice(0, 64) if i < 4 else slice(64, 128)
+        outs[j][64 * i : 64 * (i + 1), :] = gqk[source, :].astype(BF16)
+        start = lines + 64 * (i % 4)
+        outs[j][start : start + 64, lanes] = gv[source, :].astype(BF16)
+
+
+def feed_kernel(ln, w_in, vectors, w_down, hidden_ref, actt_ref, low_ref, act_ref):
+    line, _, _ = spot()
+    row = VEC * (line // (LINES // 2)) + 6 + 2 * (line % (LINES // 2))
+    bias = jnp.concatenate([vectors[pl.ds(row, 1), :], vectors[pl.ds(row + 1, 1), :]], 1)
+    for f in range(4):
+        cols = slice(256 * f, 256 * (f + 1))
+        hidden = dot(ln[...], w_in[:, cols]) + bias[:, cols]
+        hidden_ref[:, cols] = hidden
+        active = 0.5 * hidden * (1.0 + lax.erf(hidden * 0.7071067811865476))
+        act_ref[:, cols] = active.astype(BF16)
+        actt_ref[cols, :] = active.astype(BF16).T
+    for f in range(4):
+        cols = slice(256 * f, 256 * (f + 1))
+        low_ref[:, cols] = dot(act_ref[...], w_down[:, cols])
+
+
+def feed_back_kernel(cot_ref, hidden, actt, lnt, w_in, w_down, *rest):
+    send, keep, low_ref, gh_ref, chunk_ref = rest
+    line, _, core = spot()
+    cot = cot_ref[...]
+    block = send.shape[0] // 4
+    sums = jnp.zeros((1, 1024), F32)
+    cot_sum = jnp.sum(cot.astype(F32), 0, keepdims=True)
+    bias_sums = []
+    for f in range(4):
+        cols = slice(256 * f, 256 * (f + 1))
+        grad_active = dot_nt(cot, w_down[cols, :])
+        h = hidden[:, cols]
+        slope = 0.5 * (1.0 + lax.erf(h * 0.7071067811865476)) + h * jnp.exp(
+            -0.5 * h * h
+        ) * 0.3989422804014327
+        grad_hidden = (slope * grad_active).astype(BF16)
+        gh_ref[:, cols] = grad_hidden
+        bias_sums.append(jnp.sum(grad_hidden.astype(F32), 0, keepdims=True))
+    for f in range(4):
+        chunk_ref[...] = dot(actt[256 * f : 256 * (f + 1), :], cot)
+        base = block * f
+        send[base : base + 128, :] = chunk_ref[
+            pl.ds(pl.multiple_of((1 - core) * 128, 128), 128), :
+        ].astype(BF16)
+        keep[base : base + 128, :] = chunk_ref[pl.ds(pl.multiple_of(core * 128, 128), 128), :]
+    for z in range(4):
+        chunk_ref[...] = dot(lnt[256 * z : 256 * (z + 1), :], gh_ref[...])
+        for f in range(4):
+            base = block * f + 128 + 32 * z
+            send[base : base + 32, :] = chunk_ref[
+                pl.ds(pl.multiple_of(64 * f + 32 * (1 - core), 32), 32), :
+            ].astype(BF16)
+            keep[base : base + 32, :] = chunk_ref[
+                pl.ds(pl.multiple_of(64 * f + 32 * core, 32), 32), :
+            ]
+    picked = jnp.where(
+        line < 2,
+        jnp.where(line == 0, cot_sum[:, 0:256], cot_sum[:, 256:512]),
+        jnp.where(line == 2, cot_sum[:, 512:768], cot_sum[:, 768:1024]),
+    )
+    zero = jnp.zeros((1, 640), F32)
+    for f in range(4):
+        even, odd = bias_sums[f][:, :128], bias_sums[f][:, 128:]
+        first = core == 0
+        base = block * f + 256
+        given = jnp.concatenate([jnp.where(first, odd, even), picked, zero], 1)
+        kept = jnp.concatenate([jnp.where(first, even, odd), picked, zero], 1)
+        send[base : base + VEC, :] = jnp.broadcast_to(given, (VEC, 1024)).astype(BF16)
+        keep[base : base + VEC, :] = jnp.broadcast_to(kept, (VEC, 1024))
+    for i in range(4):
+        low_ref[:, 256 * i : 256 * (i + 1)] = dot_nt(gh_ref[...], w_in[256 * i : 256 * (i + 1), :])
+
+
+def share_twin_kernel(keep, received, o0, o1, o2, o3):
+    _, place, _ = spot()
+    block = o0.shape[0]
+    for slot, ref in enumerate((o0, o1, o2, o3)):
+        rows = pl.ds(pl.multiple_of((place ^ slot) * block, 16), block)
+        ref[...] = (keep[rows, :] + received[rows, :].astype(F32)).astype(ref.dtype)
+
+
+def adder(own, r1, r2, r3):
+    def total(rows, cols=slice(None)):
+        return (own[rows, cols].astype(F32) + r1[rows, cols].astype(F32)) + (
+            r2[rows, cols].astype(F32) + r3[rows, cols].astype(F32)
+        )
+
+    return total
+
+
+def owned_lanes(rows):
+    _, place, core = spot()
+    return pltpu.roll(rows, lax.rem(256 - (64 * place + 32 * core), 256), 1)[:, :32]
+
+
+def feed_sum_kernel(own, r1, r2, r3, down_ref, bias_in, bias_out, i0, i1, i2, i3):
+    line, _, _ = spot()
+    total = adder(own, r1, r2, r3)
+    down_ref[...] = total(slice(0, 128))
+    bias_in[...] = total(slice(256, 264), slice(0, 128))[:1]
+    bias_out[...] = owned_lanes(total(slice(256, 264), slice(128, 384)))[:1]
+    for slot, ref in enumerate((i0, i1, i2, i3)):
+        rows = pl.ds(pl.multiple_of(128 + 32 * (line ^ slot), 32), 32)
+        ref[...] = total(rows).astype(ref.dtype)
+
+
+def branch_kernel(r0, r1, r2, r3, low, w_out, keep, send, att_t, low_ref):
+    line, place, _ = spot()
+    fold = r0.shape[0] // 2
+    parts = [ref[:fold, :].astype(F32) for ref in (r0, r1, r2, r3)]
+    chunks = reorder((unfold_pair(parts[0], parts[1]), unfold_pair(parts[2], parts[3])), place)
+    attended = jnp.concatenate(chunks, 1).astype(BF16)
+    att_t[...] = attended.T
+    low_ref[...] = low[...] + dot(attended, w_out[...])
+    rows = low_ref.shape[0] // 4
+    for k, (ref, base) in enumerate(((keep, 0), (send, 0), (keep, rows), (send, rows))):
+        part = pl.ds(pl.multiple_of(rows * (line ^ k), rows), rows)
+        ref[base : base + rows, :] = low_ref[part, :].astype(ref.dtype)
+
+
+def halve_kernel(keep, received, own, send):
+    rows = own.shape[0]
+    own[...] = keep[:rows, :] + received[:rows, :].astype(F32)
+    send[...] = (keep[rows:, :] + received[rows:, :].astype(F32)).astype(BF16)
+
+
+def grads_kernel(r0, r1, r2, r3, low, normed, lnt, qkv, att_t, cot, head_sums, *rest):
+    s0, s1, s2, s3, send, keep, g_ref, low_ref, chunk_ref, out_ref = rest
+    line, place, core = spot()
+    rows = s0.shape[0]
+    total = 4 * rows
+    parts = [ref[...].astype(F32) for ref in (r0, r1, r2, r3)]
+    keep_left = left_lanes(total)
+    queries, keys, values = [], [], []
+    for pair in range(2):
+        even, odd = parts[2 * pair][:total], parts[2 * pair + 1][:total]
+        queries.append(jnp.where(keep_left, even, pltpu.roll(odd, 64, 1)))
+        keys.append(jnp.where(keep_left, pltpu.roll(even, 64, 1), odd))
+        values.append(unfold_pair(parts[2 * pair][total:], parts[2 * pair + 1][total:]))
+    for index, chunks in enumerate((queries, keys, values)):
+        for pair, chunk in enumerate(reorder(chunks, place)):
+            base = 256 * index + 128 * pair
+            g_ref[:, base : base + 128] = chunk.astype(BF16)
+    for i in range(4):
+        cols = slice(256 * i, 256 * (i + 1))
+        low_ref[:, cols] = low[:, cols] + dot_nt(g_ref[...], qkv[cols, :])
+    sum_gain = jnp.zeros((1, 1024), F32)
+    sum_bias = jnp.zeros((1, 1024), F32)
+    for k, out in enumerate((s0, s1, s2, s3)):
+        part = pl.ds(pl.multiple_of(rows * (line ^ k), rows), rows)
+        grad = low_ref[part, :]
+        out[...] = grad.astype(out.dtype)
+        sum_gain = sum_gain + jnp.sum(grad * normed[part, :], 0, keepdims=True)
+        sum_bias = sum_bias + jnp.sum(grad, 0, keepdims=True)
+    block = send.shape[0] // 4
+    for z in range(4):
+        chunk_ref[...] = dot(lnt[256 * z : 256 * (z + 1), :], g_ref[...])
+        for f in range(4):
+            base = block * f + 32 * z
+            send[base : base + 32, :] = chunk_ref[
+                pl.ds(pl.multiple_of(64 * f + 32 * (1 - core), 32), 32), :
+            ].astype(BF16)
+            keep[base : base + 32, :] = chunk_ref[
+                pl.ds(pl.multiple_of(64 * f + 32 * core, 32), 32), :
+            ]
+    out_ref[...] = dot(att_t[...], cot[...])
+    sums = [sum_gain[:, 256 * i : 256 * (i + 1)] for i in range(4)]
+    sums += [sum_bias[:, 256 * i : 256 * (i + 1)] for i in range(4)]
+    spare = jnp.concatenate([head_sums[...], jnp.zeros((8, 128), F32)], 1)
+    for f in range(4):
+        base = block * f + 128
+        vec = jnp.concatenate(sums + [jnp.where(place == f, spare, 0.0)], 0)
+        for ref, side in ((send, 1 - core), (keep, core)):
+            rows = out_ref[pl.ds(pl.multiple_of(64 * f + 32 * side, 32), 32), :]
+            tail = jnp.concatenate([rows[:16, 768:], rows[16:, 768:], vec], 1)
+            ref[base : base + 32, :] = rows[:, :768].astype(ref.dtype)
+            ref[base + 32 : base + 48, :] = tail.astype(ref.dtype)
+
+
+def grad_sum_kernel(own, r1, r2, r3, grad_out, qv, i0, i1, i2, i3):
+    line, _, core = spot()
+    total = adder(own, r1, r2, r3)
+    tail = total(slice(160, 176))
+    grad_out[:, :768] = total(slice(128, 160))
+    grad_out[:16, 768:] = tail[:, :256]
+    grad_out[16:, 768:] = tail[:, 256:512]
+    qv[...] = jnp.where(core == 0, tail[8:10, 512:544], tail[8:10, 544:576])
+    for slot, ref in enumerate((i0, i1, i2, i3)):
+        rows = pl.ds(pl.multiple_of(32 * (line ^ slot), 32), 32)
+        ref[:32, :] = total(rows).astype(ref.dtype)
+        ref[32:, :] = tail.astype(ref.dtype)
+
+
+def join_in_kernel(i0, i1, i2, i3, out):
+    line, _, _ = spot()
+    for slot, ref in enumerate((i0, i1, i2, i3)):
+        cols = pl.ds(pl.multiple_of((line ^ slot) * 1024, 1024), 1024)
+        out[:, cols] = ref[...].astype(F32)
+
+
+def join_qkv_kernel(i0, i1, i2, i3, out, gain, bias, vec_ref):
+    line, _, _ = spot()
+    vec = jnp.zeros((VEC, 256), F32)
+    for slot, ref in enumerate((i0, i1, i2, i3)):
+        for part in range(3):
+            cols = pl.ds(pl.multiple_of(1024 * part + (line ^ slot) * 256, 256), 256)
+            out[:, cols] = ref[:32, 256 * part : 256 * (part + 1)].astype(F32)
+        vec = vec + ref[32:, 512:768].astype(F32)
+    vec_ref[...] = owned_lanes(vec)
+    gain[...] = vec_ref[pl.ds(line, 1), :]
+    bias[...] = vec_ref[pl.ds(4 + line, 1), :]
+
+
+def layer_kernel(own, received, tokens, vectors, out):
+    total = own[...] + received[...].astype(F32) + tokens[: own.shape[0], :].astype(F32)
+    out[...] = (total + full_row(vectors, 2) + full_row(vectors, 3)).astype(BF16)
+
+
+def tokens_kernel(own, r1, r2, r3, tokens, cot, vectors, out):
+    grad_ln = own[...] + r1[...].astype(F32) + r2[...].astype(F32) + r3[...].astype(F32)
+    line, _, _ = spot()
+    rows = own.shape[0]
+    normed, inverse = normalise(tokens[:rows, :])
+    g = grad_ln * full_row(vectors, 0)
+    grad = inverse * (
+        g - jnp.mean(g, -1, keepdims=True) - normed * jnp.mean(g * normed, -1, keepdims=True)
+    )
+    mine = cot[pl.ds(pl.multiple_of(rows * line, rows), rows), :]
+    out[...] = (mine.astype(F32) + grad).astype(BF16)
+
+
+def turn_tables(count):
+    half_rot = ROT // 2
+    inverse = 10000.0 ** (-2.0 * np.arange(half_rot) / ROT)
+    angles = np.arange(count)[:, None] * inverse[None, :]
+    cosine = np.ones((count, HEAD_DIM), np.float32)
+    sine = np.zeros((count, HEAD_DIM), np.float32)
+    cosine[:, :half_rot] = cosine[:, half_rot:ROT] = np.cos(angles)
+    sine[:, :half_rot] = -np.sin(angles)
+    sine[:, half_rot:ROT] = np.sin(angles)
+    return tuple(np.concatenate([t, t], -1) for t in (cosine, sine))
+
+
+def head_body(
+    tokens,
+    block_order,
+    ln_gain,
+    ln_bias,
+    w_qkv,
+    qv_bias,
+    w_out,
+    b_out,
+    w_in,
+    b_in,
+    w_down,
+    b_down,
+    cotangent,
+):
+    positions = range(LINES * ACROSS)
+
+    def over_lines(x, k):
+        return lax.ppermute(x, "ctx", [(i, i ^ (k * ACROSS)) for i in positions])
+
+    def over_places(x, j):
+        return lax.ppermute(x, "ctx", [(i, i ^ j) for i in positions])
+
+    def twin(x):
+        return near(lax.ppermute(raw(x), "fsdp", [(0, 1), (1, 0)]))
+
+    def with_lines(blocks):
+        return [blocks[0]] + [near(over_lines(raw(blocks[k]), k)) for k in range(1, LINES)]
+
+    def with_places(blocks):
+        return [blocks[0]] + [near(over_places(raw(blocks[j]), j)) for j in range(1, ACROSS)]
+
+    rows, width = tokens.shape[1], tokens.shape[2]
+    half = w_qkv.shape[0]
+    feed = w_in.shape[1]
+    head_cols = width // LINES
+    feed_cols = feed // LINES
+    qkv_cols = 3 * head_cols
+    length = rows * LINES * ACROSS
+    line_rows = rows * LINES
+    slot_rows = line_rows * 3 // 2
+    rotation = turn_tables(length)
+    packed_rows = half + head_cols + feed_cols + half + VEC
+    table = pltpu.SMEM((32, 128), jnp.int32)
+    one_copy = pltpu.SemaphoreType.DMA((1,))
+    block = 128 + 128 + VEC
+    qkv_block = 128 + 32 + VEC
+
+    last = []
+
+    def run(kernel, out_shapes, scratch, *operands, after=(), loose_in=0):
+        results = call(
+            kernel, out_shapes, scratch, *operands, after=(*after, *last), loose_in=loose_in
+        )
+        last[:] = results[:1]
+        return results
+
+    (packed,) = run(
+        prepare_kernel,
+        [near((packed_rows, width), BF16)],
+        [pltpu.SemaphoreType.DMA((6,))],
+        far(w_qkv), far(w_in), far(w_out), far(w_down),
+        *map(far, (ln_gain, ln_bias, b_out, b_down, qv_bias, b_in)),
+        loose_in=4,
+    )
+    (token_block,) = run(
+        pack_kernel,
+        [near((rows + VEC, width), BF16)],
+        [],
+        block_order.reshape(2), far(tokens[0]),
+    )
+    token_lines = with_lines([token_block] * LINES)
+    qkv, in_rows, out_rows, down_rows, vectors = run(
+        assemble_kernel,
+        [
+            near((width, qkv_cols), BF16),
+            near((width, feed_cols), BF16),
+            near((head_cols, width), BF16),
+            near((feed_cols, width), BF16),
+            near((2 * VEC, half), F32),
+        ],
+        [pltpu.VMEM((2 * VEC, half), BF16), pltpu.SemaphoreType.DMA((8,))],
+        packed, twin(packed),
+        loose_in=2,
+    )
+    first_cot = near(over_lines(cotangent[0], 1))
+    (held,) = run(
+        hold_kernel,
+        [((rows, width), BF16)],
+        [],
+        cotangent[0],
+        after=token_lines[1:] + [first_cot],
+    )
+    cot_lines = [cotangent[0], first_cot] + [near(over_lines(held, k)) for k in (2, 3)]
+    *slots, ln_low, ln_turned, normed = run(
+        project_kernel,
+        [near((slot_rows + VEC, 128), BF16)]
+        + [near((slot_rows + VEC, 128), BF16)] * 3
+        + [
+            near((line_rows, width), BF16),
+            near((width, line_rows), BF16),
+            near((line_rows, width), F32),
+        ],
+        [],
+        *token_lines, vectors, qkv,
+    )
+    slots_in = with_places(slots)
+    hidden, active_turned, feed_low = run(
+        feed_kernel,
+        [
+            near((line_rows, feed_cols), F32),
+            near((feed_cols, line_rows), BF16),
+            near((line_rows, width), F32),
+        ],
+        [pltpu.VMEM((line_rows, feed_cols), BF16)],
+        ln_low, in_rows, vectors, down_rows,
+    )
+    att_slots, qk_rows, kq_rows, value_rows, attended, lse, numbers = run(
+        attend_kernel,
+        [
+            near((line_rows * 2, 128), BF16),
+            near((length, 128), BF16),
+            near((length, 128), BF16),
+            near((length, 64), BF16),
+            near((length, 64), F32),
+            near((length, 1), F32),
+            near((32, 128), jnp.int32),
+        ],
+        [pltpu.VMEM((length, 128), BF16), table, one_copy],
+        *slots_in, *rotation,
+    )
+    *mixed, cot_rows = run(
+        back_rows_kernel,
+        [near((line_rows, 128), BF16)]
+        + [near((line_rows, 128), BF16)] * 3
+        + [near((line_rows, width), BF16)],
+        [],
+        *cot_lines, out_rows, att_slots,
+    )
+    mixed_in = with_places(mixed)
+    feed_send, feed_keep, feed_grad_low = run(
+        feed_back_kernel,
+        [
+            near((4 * block, width), BF16),
+            near((4 * block, width), F32),
+            near((line_rows, width), F32),
+        ],
+        [pltpu.VMEM((line_rows, feed_cols), BF16), pltpu.VMEM((256, 1024), F32)],
+        cot_rows, hidden, active_turned, ln_turned, in_rows, down_rows,
+    )
+    feed_twin = twin(feed_send)
+    low_keep, low_send, att_turned = run(
+        branch_kernel,
+        [
+            near((2 * rows, width), F32),
+            near((2 * rows, width), BF16),
+            near((head_cols, line_rows), BF16),
+        ],
+        [pltpu.VMEM((line_rows, width), F32)],
+        *mixed_in, feed_low, out_rows,
+    )
+    low_received = near(over_lines(raw(low_send), 1))
+    *grad_slots, bias_sums = run(
+        attend_back_kernel,
+        [near((slot_rows, 128), BF16)] + [near((slot_rows, 128), BF16)] * 3 + [near((8, 128), F32)],
+        [
+            pltpu.VMEM((length, 64), BF16),
+            pltpu.VMEM((128, length), F32),
+            pltpu.VMEM((64, length), F32),
+            pltpu.VMEM((length, 128), F32),
+            pltpu.VMEM((length, 64), F32),
+            table,
+            one_copy,
+        ],
+        *mixed_in, numbers, qk_rows, kq_rows, value_rows, attended, lse, *rotation,
+    )
+    grad_slots_in = with_places(grad_slots)
+    low_own, low_half = run(
+        halve_kernel,
+        [near((rows, width), F32), near((rows, width), BF16)],
+        [],
+        low_keep, low_received,
+    )
+    low_rest = near(over_lines(raw(low_half), 2))
+    feed_blocks = run(
+        share_twin_kernel,
+        [near((block, width), F32)] + [near((block, width), BF16)] * 3,
+        [],
+        feed_keep, feed_twin,
+    )
+    feed_in = with_places(feed_blocks)
+    *ln_slots, qkv_send, qkv_keep = run(
+        grads_kernel,
+        [near((rows, width), F32)]
+        + [near((rows, width), BF16)] * 3
+        + [near((4 * qkv_block, qkv_cols), BF16), near((4 * qkv_block, qkv_cols), F32)],
+        [
+            pltpu.VMEM((line_rows, qkv_cols), BF16),
+            pltpu.VMEM((line_rows, width), F32),
+            pltpu.VMEM((256, qkv_cols), F32),
+            pltpu.VMEM((head_cols, width), F32),
+        ],
+        *grad_slots_in, feed_grad_low, normed, ln_turned, qkv, att_turned, cot_rows,
+        bias_sums,
+    )
+    ln_in = with_lines(ln_slots)
+    (layer_out,) = run(
+        layer_kernel,
+        [((rows, width), BF16)],
+        [],
+        low_own, low_rest, token_block, vectors,
+    )
+    qkv_blocks = run(
+        share_twin_kernel,
+        [near((qkv_block, qkv_cols), F32)] + [near((qkv_block, qkv_cols), BF16)] * 3,
+        [],
+        qkv_keep, twin(qkv_send),
+    )
+    qkv_sums = with_places(qkv_blocks)
+    grad_down, grad_b_in, grad_b, *in_slots = run(
+        feed_sum_kernel,
+        [((128, width), F32), ((1, 128), F32), ((1, 32), F32), near((32, width), F32)]
+        + [near((32, width), BF16)] * 3,
+        [],
+        *feed_in,
+    )
+    in_parts = with_lines(in_slots)
+    grad_out, grad_qv, *qkv_parts = run(
+        grad_sum_kernel,
+        [((32, width), F32), ((2, 32), F32), near((32 + VEC, qkv_cols), F32)]
+        + [near((32 + VEC, qkv_cols), BF16)] * 3,
+        [],
+        *qkv_sums,
+    )
+    qkv_parts = with_lines(qkv_parts)
+    (grad_tokens,) = run(
+        tokens_kernel,
+        [((rows, width), BF16)],
+        [],
+        *ln_in, token_block, cot_rows, vectors,
+    )
+    (grad_in,) = run(join_in_kernel, [((32, feed), F32)], [], *in_parts)
+    grad_qkv, grad_gain, grad_shift = run(
+        join_qkv_kernel,
+        [((32, 3 * width), F32), ((1, 32), F32), ((1, 32), F32)],
+        [pltpu.VMEM((VEC, 32), F32)],
+        *qkv_parts,
+    )
+    return (
+        layer_out[None],
+        grad_tokens[None],
+        grad_gain[0],
+        grad_shift[0],
+        grad_qkv,
+        grad_qv,
+        grad_out,
+        grad_b[0],
+        grad_in,
+        grad_b_in[0],
+        grad_down,
+        grad_b[0],
+    )
+
+
 def solution(mesh):
+    one_head_each = mesh.shape["ctx"] == HEADS and mesh.shape["fsdp"] == 2
     return jax.shard_map(
-        body,
+        head_body if one_head_each else body,
         mesh=mesh,
         in_specs=(
             P("fsdp", "ctx", None),

time: 1490 us -> 166 us (0.11)
  waiting for transfers between devices: 1030 us -> 64.5 us
  matrix products: 132 us -> 0 us
  blocking collectives: 88.8 us -> 0 us
  other arithmetic: 78.8 us -> 0 us
  local copies, waits for them, and re-layouts: 83.1 us -> 5.41 us
  Pallas kernels: 0 us -> 42 us
    reduce_scatter x4 -> x0, waiting for transfers between devices: 670 us -> none  [the longest x1 187 us: body(): lax.psum_scatter(term_down_w, ('ctx', 'fsdp'), scatter_dimension=0, tiled...]
    ppermute x77 -> x35, waiting for transfers between devices: 220 us -> 64.5 us  [the longest x17 38 us: over_lines(): return lax.ppermute(x, 'ctx', [(i, i ^ k * ACROSS) for i in positions])]
    dot_general x96 -> x0, matrix products: 132 us -> none  [the longest x4 28.3 us: outer_sum(): lax.dot_general(left_side, right_side, (((0,), (0,)), ((), ())), preferre...]
    all_gather x6 -> x0, waiting for transfers between devices: 132 us -> none  [the longest x1 63.5 us: body(): piece_values = lax.all_gather(value_rows, 'ctx', axis=0, tiled=True)]
    convert_element_type x69 -> x0, other arithmetic: 68.4 us -> none  [the longest x16 27.5 us: send_home(): grad_keys.astype(jnp.bfloat16)]
    all_gather x7 -> x0, blocking collectives: 51.6 us -> none  [the longest x1 40.8 us: body(): piece_orders = lax.all_gather(block_order, 'ctx', axis=0, tiled=True)]
    pallas_call x0 -> x21, Pallas kernels: none -> 42 us  [call(): pl.pallas_call(body, name=name, out_shape=outs, in_specs=specs + [loose]...]
    unnamed x1 -> x0, blocking collectives: 37.2 us -> none
  transfers between devices with their start and end apart: 88 -> 35, of which waited for: 40 -> 16; matrix products, arithmetic and copies ran while one was open for 19% -> 0% of each run, Pallas kernels for 0% -> 23%
where the time goes in v2:
time: 166 us; the launch traced here: 165 us
  waiting for transfers between devices  64.5 us (39%)
  starting transfers between devices  52.6 us (32%)
  Pallas kernels  42 us (25%)
  local copies, waits for them, and re-layouts  5.41 us (3%)
    pallas_call x21, Pallas kernels, call(): pl.pallas_call(body, name=name, out_shape=outs, in_specs=specs + [loose]...  42 us
    ppermute x17, waiting for transfers between devices, over_lines(): return lax.ppermute(x, 'ctx', [(i, i ^ k * ACROSS) for i in positions])  38 us
    ppermute x17, starting transfers between devices, over_lines(): return lax.ppermute(x, 'ctx', [(i, i ^ k * ACROSS) for i in positions])  32.5 us
    ppermute x15, waiting for transfers between devices, over_places(): return lax.ppermute(x, 'ctx', [(i, i ^ j) for i in positions])  24.6 us
    ppermute x15, starting transfers between devices, over_places(): return lax.ppermute(x, 'ctx', [(i, i ^ j) for i in positions])  19.5 us
    unnamed x21, local copies, waits for them, and re-layouts  5.41 us
  transfers between devices with their start and end apart: 35, of which 16 were waited for; matrix products, arithmetic and copies ran while one was open for 0% of the time, Pallas kernels for 23%

profile of v2, /device:TPU:0, one launch (start us, length us, event | category | flops | bytes accessed | tf_op | source)
XLA Modules:
  0.0 165.4 jit_solution(15532654080621752499)
XLA Ops:
  0.7 3.1 %prepare.1.refs_2_.refs_0_ = bf16[2320,1024]{1,0:T(8,128)(2,1)S(1)} custom-call(bf16[512,3072]{1,0:T(8,128)(2,1)} %refs_0_.1, bf16[512,4096]{1,0:T(8,128)(2,1)} %refs_1_.1, bf16[512,1024]{1,0:T(8,128)(2,1)} %refs_2_.1, bf16[2048,1024]{1,0:T(8,128)(2,1)} %refs_3_.1, bf16[512]{0:T(512)(128)(2,1)} %refs_4_.2, bf16[512]{0:T(512)(128)(2,1)} %refs_5_.2, ...), custom_call_target="tpu_custom_call" | custom-call | tf_op jit(solution)/shard_map/prepare/pallas_call | solution.py:413
  3.8 0.5 collective-permute-start.4
  4.3 1.0 pack.1.refs_2_.refs_0_.refs_4_
  5.3 4.7 %collective-permute-start.3 = (bf16[144,1024]{1,0:T(8,128)(2,1)S(1)}, bf16[144,1024]{1,0:T(8,128)(2,1)S(1)}, u32[]{:S(2)}, u32[]{:S(2)}) collective-permute-start(bf16[144,1024]{1,0:T(8,128)(2,1)S(1)} %pack.1.refs_2_.refs_0_.refs_4_), channel_id=1, source_target_pairs={{0,24},{2,26},{4,28},{6,30},{8,16},{10,18},{12,20},{14,22},{16,8},... | collective-permute-start | bytes 884744 | tf_op jit(solution)/shard_map/ppermute | solution.py:988
  10.0 0.6 collective-permute-start.1
  10.6 1.4 collective-permute-start
  12.0 0.6 assemble.1
  12.7 23.3 %collective-permute-done.refs_4_.refs_1_ = bf16[128,1024]{1,0:T(8,128)(2,1)S(1)} collective-permute-done((bf16[128,1024]{1,0:T(8,128)(2,1)S(1)}, bf16[128,1024]{1,0:T(8,128)(2,1)S(1)}, u32[]{:S(2)}, u32[]{:S(2)}) %collective-permute-start) | collective-permute-done | bytes 262176 | tf_op jit(solution)/shard_map/ppermute | solution.py:988
  36.0 3.6 %collective-permute-start.6 = (bf16[128,1024]{1,0:T(8,128)(2,1)S(1)}, bf16[128,1024]{1,0:T(8,128)(2,1)S(1)}, u32[]{:S(2)}, u32[]{:S(2)}) collective-permute-start(bf16[128,1024]{1,0:T(8,128)(2,1)S(1)} %hold.1.refs_6_), channel_id=1, source_target_pairs={{0,24},{2,26},{4,28},{6,30},{8,16},{10,18},{12,20},{14,22},{16,8},... | collective-permute-start | bytes 786440 | tf_op jit(solution)/shard_map/ppermute | solution.py:988
  39.7 2.2 %project.1 = (bf16[784,128]{1,0:T(8,128)(2,1)S(1)}, bf16[784,128]{1,0:T(8,128)(2,1)S(1)}, bf16[784,128]{1,0:T(8,128)(2,1)S(1)}, bf16[784,128]{1,0:T(8,128)(2,1)S...) custom-call(bf16[144,1024]{1,0:T(8,128)(2,1)S(1)} %pack.1.refs_2_.refs_0_.refs_4_, ...), custom_call_target="tpu_custom_call" | custom-call | tf_op jit(solution)/shard_map/project/pallas_call | solution.py:413
  41.8 1.6 collective-permute-start.7
  43.4 1.5 collective-permute-start.8
  45.4 2.6 %feed.1 = (f32[512,1024]{1,0:T(8,128)S(1)}, bf16[1024,512]{1,0:T(8,128)(2,1)S(1)}, f32[512,1024]{1,0:T(8,128)S(1)}) custom-call(bf16[512,1024]{1,0:T(8,128)(2,1)S(1)} %get-tuple-element.89.refs_0_, bf16[1024,1024]{1,0:T(8,128)(2,1)S(1)} %get-tuple-element.90.refs_1_.refs_4_, f32[32,512]{1,0:T(8,128)S(1)} %get-tuple-element.84.refs_4_.refs_2_.refs_3_.refs_6_, ...), custom_call_target="tpu_custom_call" | custom-call | tf_op jit(solution)/shard_map/feed/pallas_call | solution.py:413
  48.0 1.8 %collective-permute-done.7.refs_1_ = bf16[784,128]{1,0:T(8,128)(2,1)S(1)} collective-permute-done((bf16[784,128]{1,0:T(8,128)(2,1)S(1)}, bf16[784,128]{1,0:T(8,128)(2,1)S(1)}, u32[]{:S(2)}, u32[]{:S(2)}) %collective-permute-start.7) | collective-permute-done | bytes 200736 | tf_op jit(solution)/shard_map/ppermute | solution.py:991
  49.8 4.3 %collective-permute-done.8.refs_2_ = bf16[784,128]{1,0:T(8,128)(2,1)S(1)} collective-permute-done((bf16[784,128]{1,0:T(8,128)(2,1)S(1)}, bf16[784,128]{1,0:T(8,128)(2,1)S(1)}, u32[]{:S(2)}, u32[]{:S(2)}) %collective-permute-start.8) | collective-permute-done | bytes 200736 | tf_op jit(solution)/shard_map/ppermute | solution.py:991
  54.1 6.3 %attend.1 = (bf16[1024,128]{1,0:T(8,128)(2,1)S(1)}, bf16[2048,128]{1,0:T(8,128)(2,1)S(1)}, bf16[2048,128]{1,0:T(8,128)(2,1)S(1)}, bf16[2048,64]{1,0:T(8,128)(2,1...) custom-call(bf16[784,128]{1,0:T(8,128)(2,1)S(1)} %get-tuple-element.85.refs_4_.refs_0_, ...), custom_call_target="tpu_custom_call" | custom-call | tf_op jit(solution)/shard_map/attend/pallas_call | solution.py:413
  60.4 1.6 collective-permute-done.5.refs_2_
  62.0 0.6 back_rows.1
  62.7 1.6 collective-permute-start.10
  64.2 1.5 collective-permute-start.11
  66.2 6.3 %feed_back.1 = (bf16[1088,1024]{1,0:T(8,128)(2,1)S(1)}, f32[1088,1024]{1,0:T(8,128)S(1)}, f32[512,1024]{1,0:T(8,128)S(1)}) custom-call(bf16[512,1024]{1,0:T(8,128)(2,1)S(1)} %get-tuple-element.99.refs_0_.refs_9_.refs_5_, f32[512,1024]{1,0:T(8,128)S(1)} %get-tuple-element.92.refs_6_.refs_1_, bf16[1024,512]{1,0:T(8,128)(2,1)S(1)} %get-tuple-element.100.refs_2_, ...), custom_call_target="tpu_custom_call" | custom-call | tf_op jit(solution)/shard_map/feed_back/pallas_call | solution.py:413
  72.7 0.8 branch.1
  73.6 8.4 %attend_back.1 = (bf16[768,128]{1,0:T(8,128)(2,1)S(1)}, bf16[768,128]{1,0:T(8,128)(2,1)S(1)}, bf16[768,128]{1,0:T(8,128)(2,1)S(1)}, bf16[768,128]{1,0:T(8,128)(2,1)S(1)}, f32[8,128]{1,0:T(8,128)S(1)}) custom-call(bf16[512,128]{1,0:T(8,128)(2,1)S(1)} %get-tuple-element.94.refs_6_.refs_0_, bf16[512,128]{1,0:T(8,128)(2,1)S(1)} %collective-permute-done.10.refs_1_, ...), custom_call_target="tpu_custom_call" | custom-call | tf_op jit(solution)/shard_map/attend_back/pallas_call | solution.py:413
  82.0 5.9 %collective-permute-done.13.refs_1_ = bf16[256,1024]{1,0:T(8,128)(2,1)S(1)} collective-permute-done((bf16[256,1024]{1,0:T(8,128)(2,1)S(1)}, bf16[256,1024]{1,0:T(8,128)(2,1)S(1)}, u32[]{:S(2)}, u32[]{:S(2)}) %collective-permute-start.13) | collective-permute-done | bytes 524320 | tf_op jit(solution)/shard_map/ppermute | solution.py:988
  88.0 1.1 collective-permute-start.14
  89.1 1.2 collective-permute-start.15
  90.3 1.3 collective-permute-start.16
  91.6 1.0 collective-permute-start.17
  92.9 1.3 collective-permute-start.26
  94.2 2.7 %collective-permute-done.15.refs_1_ = bf16[768,128]{1,0:T(8,128)(2,1)S(1)} collective-permute-done((bf16[768,128]{1,0:T(8,128)(2,1)S(1)}, bf16[768,128]{1,0:T(8,128)(2,1)S(1)}, u32[]{:S(2)}, u32[]{:S(2)}) %collective-permute-start.15) | collective-permute-done | bytes 196640 | tf_op jit(solution)/shard_map/ppermute | solution.py:991
  96.9 1.5 collective-permute-start.27
  98.4 2.0 %collective-permute-done.16.refs_2_ = bf16[768,128]{1,0:T(8,128)(2,1)S(1)} collective-permute-done((bf16[768,128]{1,0:T(8,128)(2,1)S(1)}, bf16[768,128]{1,0:T(8,128)(2,1)S(1)}, u32[]{:S(2)}, u32[]{:S(2)}) %collective-permute-start.16) | collective-permute-done | bytes 196640 | tf_op jit(solution)/shard_map/ppermute | solution.py:991
  100.4 2.0 %collective-permute-start.28 = (bf16[272,1024]{1,0:T(8,128)(2,1)S(1)}, bf16[272,1024]{1,0:T(8,128)(2,1)S(1)}, u32[]{:S(2)}, u32[]{:S(2)}) collective-permute-start(bf16[272,1024]{1,0:T(8,128)(2,1)S(1)} %get-tuple-element.135), channel_id=1, source_target_pairs={{0,6},{2,4},{4,2},{6,0},{8,14},{10,12},{12,10},{14,8},{16,22},{18,... | collective-permute-start | bytes 1671176 | tf_op jit(solution)/shard_map/ppermute | solution.py:991
  102.5 4.0 %grads.1 = (f32[128,1024]{1,0:T(8,128)S(1)}, bf16[128,1024]{1,0:T(8,128)(2,1)S(1)}, bf16[128,1024]{1,0:T(8,128)(2,1)S(1)}, bf16[128,1024]{1,0:T(8,128)(2,1)S(1)}...) custom-call(bf16[768,128]{1,0:T(8,128)(2,1)S(1)} %get-tuple-element.111.refs_2_.refs_0_, ...), custom_call_target="tpu_custom_call" | custom-call | tf_op jit(solution)/shard_map/grads/pallas_call | solution.py:413
  106.5 0.8 layer.1.refs_2_
  107.4 1.9 %collective-permute-done.22.refs_1_ = bf16[704,768]{1,0:T(8,128)(2,1)S(1)} collective-permute-done((bf16[704,768]{1,0:T(8,128)(2,1)S(1)}, bf16[704,768]{1,0:T(8,128)(2,1)S(1)}, u32[]{:S(2)}, u32[]{:S(2)}) %collective-permute-start.22) | collective-permute-done | bytes 1081376 | tf_op jit(solution)/shard_map/ppermute | solution.py:994
  109.2 0.9 copy-done.6
  110.4 2.1 %collective-permute-start.23 = (bf16[176,768]{1,0:T(8,128)(2,1)S(1)}, bf16[176,768]{1,0:T(8,128)(2,1)S(1)}, u32[]{:S(2)}, u32[]{:S(2)}) collective-permute-start(bf16[176,768]{1,0:T(8,128)(2,1)S(1)} %get-tuple-element.130), channel_id=1, source_target_pairs={{0,2},{2,0},{4,6},{6,4},{8,10},{10,8},{12,14},{14,12},{16,18},{18,... | collective-permute-start | bytes 811016 | tf_op jit(solution)/shard_map/ppermute | solution.py:991
  112.5 0.6 collective-permute-done.26.refs_1_
  113.1 1.9 %collective-permute-start.25 = (bf16[176,768]{1,0:T(8,128)(2,1)S(1)}, bf16[176,768]{1,0:T(8,128)(2,1)S(1)}, u32[]{:S(2)}, u32[]{:S(2)}) collective-permute-start(bf16[176,768]{1,0:T(8,128)(2,1)S(1)} %get-tuple-element.132), channel_id=1, source_target_pairs={{0,6},{2,4},{4,2},{6,0},{8,14},{10,12},{12,10},{14,8},{16,22},{18,... | collective-permute-start | bytes 811016 | tf_op jit(solution)/shard_map/ppermute | solution.py:991
  115.0 8.5 %collective-permute-done.27.refs_2_ = bf16[272,1024]{1,0:T(8,128)(2,1)S(1)} collective-permute-done((bf16[272,1024]{1,0:T(8,128)(2,1)S(1)}, bf16[272,1024]{1,0:T(8,128)(2,1)S(1)}, u32[]{:S(2)}, u32[]{:S(2)}) %collective-permute-start.27) | collective-permute-done | bytes 557088 | tf_op jit(solution)/shard_map/ppermute | solution.py:991
  123.6 2.2 %collective-permute-start.19 = (bf16[128,1024]{1,0:T(8,128)(2,1)S(1)}, bf16[128,1024]{1,0:T(8,128)(2,1)S(1)}, u32[]{:S(2)}, u32[]{:S(2)}) collective-permute-start(bf16[128,1024]{1,0:T(8,128)(2,1)S(1)} %get-tuple-element.124), channel_id=1, source_target_pairs={{0,8},{2,10},{4,12},{6,14},{8,0},{10,2},{12,4},{14,6},{16,24},{18,... | collective-permute-start | bytes 786440 | tf_op jit(solution)/shard_map/ppermute | solution.py:988
  126.1 1.9 %collective-permute-start.20 = (bf16[128,1024]{1,0:T(8,128)(2,1)S(1)}, bf16[128,1024]{1,0:T(8,128)(2,1)S(1)}, u32[]{:S(2)}, u32[]{:S(2)}) collective-permute-start(bf16[128,1024]{1,0:T(8,128)(2,1)S(1)} %get-tuple-element.125), channel_id=1, source_target_pairs={{0,16},{2,18},{4,20},{6,22},{8,24},{10,26},{12,28},{14,30},{16,0},... | collective-permute-start | bytes 786440 | tf_op jit(solution)/shard_map/ppermute | solution.py:988
  127.9 2.9 %collective-permute-done.23.refs_1_ = bf16[176,768]{1,0:T(8,128)(2,1)S(1)} collective-permute-done((bf16[176,768]{1,0:T(8,128)(2,1)S(1)}, bf16[176,768]{1,0:T(8,128)(2,1)S(1)}, u32[]{:S(2)}, u32[]{:S(2)}) %collective-permute-start.23) | collective-permute-done | bytes 270368 | tf_op jit(solution)/shard_map/ppermute | solution.py:991
  130.9 1.6 collective-permute-start.21
  132.5 1.0 feed_sum.1
  133.5 1.4 collective-permute-done.24.refs_2_
  134.9 2.5 %collective-permute-start.32 = (bf16[32,1024]{1,0:T(8,128)(2,1)S(1)}, bf16[32,1024]{1,0:T(8,128)(2,1)S(1)}, u32[]{:S(2)}, u32[]{:S(2)}) collective-permute-start(bf16[32,1024]{1,0:T(8,128)(2,1)S(1)} %get-tuple-element.143), channel_id=1, source_target_pairs={{0,8},{2,10},{4,12},{6,14},{8,0},{10,2},{12,4},{14,6},{16,24},{18,... | collective-permute-start | bytes 196616 | tf_op jit(solution)/shard_map/ppermute | solution.py:988
  137.4 1.0 copy-done.5
  138.5 0.7 grad_sum.1
  139.2 2.7 %collective-permute-start.30 = (bf16[48,768]{1,0:T(8,128)(2,1)S(1)}, bf16[48,768]{1,0:T(8,128)(2,1)S(1)}, u32[]{:S(2)}, u32[]{:S(2)}) collective-permute-start(bf16[48,768]{1,0:T(8,128)(2,1)S(1)} %get-tuple-element.140), channel_id=1, source_target_pairs={{0,16},{2,18},{4,20},{6,22},{8,24},{10,26},{12,28},{14,30},{16,0},... | collective-permute-start | bytes 221192 | tf_op jit(solution)/shard_map/ppermute | solution.py:988
  141.9 4.4 %collective-permute-done.20.refs_2_ = bf16[128,1024]{1,0:T(8,128)(2,1)S(1)} collective-permute-done((bf16[128,1024]{1,0:T(8,128)(2,1)S(1)}, bf16[128,1024]{1,0:T(8,128)(2,1)S(1)}, u32[]{:S(2)}, u32[]{:S(2)}) %collective-permute-start.20) | collective-permute-done | bytes 262176 | tf_op jit(solution)/shard_map/ppermute | solution.py:988
  146.3 2.9 %collective-permute-start.31 = (bf16[48,768]{1,0:T(8,128)(2,1)S(1)}, bf16[48,768]{1,0:T(8,128)(2,1)S(1)}, u32[]{:S(2)}, u32[]{:S(2)}) collective-permute-start(bf16[48,768]{1,0:T(8,128)(2,1)S(1)} %get-tuple-element.141), channel_id=1, source_target_pairs={{0,24},{2,26},{4,28},{6,30},{8,16},{10,18},{12,20},{14,22},{16,8},... | collective-permute-start | bytes 221192 | tf_op jit(solution)/shard_map/ppermute | solution.py:988
  149.2 5.9 %collective-permute-start.33 = (bf16[32,1024]{1,0:T(8,128)(2,1)S(1)}, bf16[32,1024]{1,0:T(8,128)(2,1)S(1)}, u32[]{:S(2)}, u32[]{:S(2)}) collective-permute-start(bf16[32,1024]{1,0:T(8,128)(2,1)S(1)} %get-tuple-element.144), channel_id=1, source_target_pairs={{0,16},{2,18},{4,20},{6,22},{8,24},{10,26},{12,28},{14,30},{16,0},... | collective-permute-start | bytes 196616 | tf_op jit(solution)/shard_map/ppermute | solution.py:988
  155.2 1.3 collective-permute-start.34
  156.4 0.9 copy-done.7
  157.3 1.2 tokens.1.refs_4_
  158.5 1.0 collective-permute-done.33.refs_2_
  159.5 1.7 %collective-permute-done.34.refs_3_ = bf16[32,1024]{1,0:T(8,128)(2,1)S(1)} collective-permute-done((bf16[32,1024]{1,0:T(8,128)(2,1)S(1)}, bf16[32,1024]{1,0:T(8,128)(2,1)S(1)}, u32[]{:S(2)}, u32[]{:S(2)}) %collective-permute-start.34) | collective-permute-done | bytes 65568 | tf_op jit(solution)/shard_map/ppermute | solution.py:988
  161.2 0.9 copy-done.3
  162.2 0.8 join_in.1.refs_4_
  163.1 1.0 copy-done.2
  164.1 0.8 join_qkv.1
  164.9 0.5 copy.28
  (48 shorter events, 2.2 us)
Async XLA Ops:
  0.6 3.6 %copy-start.8 = (s32[1,2]{1,0:T(1,128)S(1)}, s32[1,2]{1,0:T(1,128)}, u32[]{:S(2)}) copy-start(s32[1,2]{1,0:T(1,128)} %param.16) | copy-start | bytes 28
  3.8 8.3 %collective-permute-start.4 = (bf16[2320,1024]{1,0:T(8,128)(2,1)S(1)}, bf16[2320,1024]{1,0:T(8,128)(2,1)S(1)}, u32[]{:S(2)}, u32[]{:S(2)}) collective-permute-start(bf16[2320,1024]{1,0:T(8,128)(2,1)S(1)} %prepare.1.refs_2_.refs_0_), channel_id=1, source_target_pairs={{0,1},{1,0},{2,3},{3,2},{4,5},{5,4},{6,7},{7,6},{8,9},{9,8},{10,11... | collective-permute-start | bytes 14254088 | tf_op jit(solution)/shard_map/ppermute | solution.py:994
  4.3 6.4 %copy-start.4 = (bf16[1,128,1024]{2,1,0:T(8,128)(2,1)S(1)}, bf16[1,128,1024]{2,1,0:T(8,128)(2,1)}, u32[]{:S(2)}) copy-start(bf16[1,128,1024]{2,1,0:T(8,128)(2,1)} %param.27) | copy-start | bytes 786436
  5.3 30.7 %collective-permute-start.3 = (bf16[144,1024]{1,0:T(8,128)(2,1)S(1)}, bf16[144,1024]{1,0:T(8,128)(2,1)S(1)}, u32[]{:S(2)}, u32[]{:S(2)}) collective-permute-start(bf16[144,1024]{1,0:T(8,128)(2,1)S(1)} %pack.1.refs_2_.refs_0_.refs_4_), channel_id=1, source_target_pairs={{0,24},{2,26},{4,28},{6,30},{8,16},{10,18},{12,20},{14,22},{16,8},... | collective-permute-start | bytes 884744 | tf_op jit(solution)/shard_map/ppermute | solution.py:988
  10.0 26.0 %collective-permute-start.2 = (bf16[144,1024]{1,0:T(8,128)(2,1)S(1)}, bf16[144,1024]{1,0:T(8,128)(2,1)S(1)}, u32[]{:S(2)}, u32[]{:S(2)}) collective-permute-start(bf16[144,1024]{1,0:T(8,128)(2,1)S(1)} %pack.1.refs_2_.refs_0_.refs_4_), channel_id=1, source_target_pairs={{0,16},{2,18},{4,20},{6,22},{8,24},{10,26},{12,28},{14,30},{16,0},... | collective-permute-start | bytes 884744 | tf_op jit(solution)/shard_map/ppermute | solution.py:988
  10.0 26.0 %collective-permute-start.1 = (bf16[144,1024]{1,0:T(8,128)(2,1)S(1)}, bf16[144,1024]{1,0:T(8,128)(2,1)S(1)}, u32[]{:S(2)}, u32[]{:S(2)}) collective-permute-start(bf16[144,1024]{1,0:T(8,128)(2,1)S(1)} %pack.1.refs_2_.refs_0_.refs_4_), channel_id=1, source_target_pairs={{0,8},{2,10},{4,12},{6,14},{8,0},{10,2},{12,4},{14,6},{16,24},{18,... | collective-permute-start | bytes 884744 | tf_op jit(solution)/shard_map/ppermute | solution.py:988
  10.6 25.4 %collective-permute-start = (bf16[128,1024]{1,0:T(8,128)(2,1)S(1)}, bf16[128,1024]{1,0:T(8,128)(2,1)S(1)}, u32[]{:S(2)}, u32[]{:S(2)}) collective-permute-start(bf16[128,1024]{1,0:T(8,128)(2,1)S(1)} %bitcast.10), channel_id=1, source_target_pairs={{0,8},{2,10},{4,12},{6,14},{8,0},{10,2},{12,4},{14,6},{16,24},{18,... | collective-permute-start | bytes 786440 | tf_op jit(solution)/shard_map/ppermute | solution.py:988
  36.0 24.4 %collective-permute-start.6 = (bf16[128,1024]{1,0:T(8,128)(2,1)S(1)}, bf16[128,1024]{1,0:T(8,128)(2,1)S(1)}, u32[]{:S(2)}, u32[]{:S(2)}) collective-permute-start(bf16[128,1024]{1,0:T(8,128)(2,1)S(1)} %hold.1.refs_6_), channel_id=1, source_target_pairs={{0,24},{2,26},{4,28},{6,30},{8,16},{10,18},{12,20},{14,22},{16,8},... | collective-permute-start | bytes 786440 | tf_op jit(solution)/shard_map/ppermute | solution.py:988
  39.6 22.4 %collective-permute-start.5 = (bf16[128,1024]{1,0:T(8,128)(2,1)S(1)}, bf16[128,1024]{1,0:T(8,128)(2,1)S(1)}, u32[]{:S(2)}, u32[]{:S(2)}) collective-permute-start(bf16[128,1024]{1,0:T(8,128)(2,1)S(1)} %hold.1.refs_6_), channel_id=1, source_target_pairs={{0,16},{2,18},{4,20},{6,22},{8,24},{10,26},{12,28},{14,30},{16,0},... | collective-permute-start | bytes 786440 | tf_op jit(solution)/shard_map/ppermute | solution.py:988
  41.8 8.0 %collective-permute-start.7 = (bf16[784,128]{1,0:T(8,128)(2,1)S(1)}, bf16[784,128]{1,0:T(8,128)(2,1)S(1)}, u32[]{:S(2)}, u32[]{:S(2)}) collective-permute-start(bf16[784,128]{1,0:T(8,128)(2,1)S(1)} %get-tuple-element.86), channel_id=1, source_target_pairs={{0,2},{2,0},{4,6},{6,4},{8,10},{10,8},{12,14},{14,12},{16,18},{18,... | collective-permute-start | bytes 602120 | tf_op jit(solution)/shard_map/ppermute | solution.py:991
  43.4 10.7 %collective-permute-start.8 = (bf16[784,128]{1,0:T(8,128)(2,1)S(1)}, bf16[784,128]{1,0:T(8,128)(2,1)S(1)}, u32[]{:S(2)}, u32[]{:S(2)}) collective-permute-start(bf16[784,128]{1,0:T(8,128)(2,1)S(1)} %get-tuple-element.87), channel_id=1, source_target_pairs={{0,4},{2,6},{4,0},{6,2},{8,12},{10,14},{12,8},{14,10},{16,20},{18,... | collective-permute-start | bytes 602120 | tf_op jit(solution)/shard_map/ppermute | solution.py:991
  44.9 9.2 %collective-permute-start.9 = (bf16[784,128]{1,0:T(8,128)(2,1)S(1)}, bf16[784,128]{1,0:T(8,128)(2,1)S(1)}, u32[]{:S(2)}, u32[]{:S(2)}) collective-permute-start(bf16[784,128]{1,0:T(8,128)(2,1)S(1)} %get-tuple-element.88), channel_id=1, source_target_pairs={{0,6},{2,4},{4,2},{6,0},{8,14},{10,12},{12,10},{14,8},{16,22},{18,... | collective-permute-start | bytes 602120 | tf_op jit(solution)/shard_map/ppermute | solution.py:991
  45.4 8.7 %copy-start = (f32[2048,128]{1,0:T(8,128)S(1)}, f32[2048,128]{1,0:T(8,128)}, u32[]{:S(2)}) copy-start(f32[2048,128]{1,0:T(8,128)} %constant.5.clone.refs_5_.refs_11_) | copy-start | bytes 3145732
  45.4 8.7 %copy-start.1 = (f32[2048,128]{1,0:T(8,128)S(1)}, f32[2048,128]{1,0:T(8,128)}, u32[]{:S(2)}) copy-start(f32[2048,128]{1,0:T(8,128)} %constant.4.clone.refs_4_.refs_10_) | copy-start | bytes 3145732
  62.7 10.0 %collective-permute-start.10 = (bf16[512,128]{1,0:T(8,128)(2,1)S(1)}, bf16[512,128]{1,0:T(8,128)(2,1)S(1)}, u32[]{:S(2)}, u32[]{:S(2)}) collective-permute-start(bf16[512,128]{1,0:T(8,128)(2,1)S(1)} %get-tuple-element.95), channel_id=1, source_target_pairs={{0,2},{2,0},{4,6},{6,4},{8,10},{10,8},{12,14},{14,12},{16,18},{18,... | collective-permute-start | bytes 393224 | tf_op jit(solution)/shard_map/ppermute | solution.py:991
  64.2 8.4 %collective-permute-start.11 = (bf16[512,128]{1,0:T(8,128)(2,1)S(1)}, bf16[512,128]{1,0:T(8,128)(2,1)S(1)}, u32[]{:S(2)}, u32[]{:S(2)}) collective-permute-start(bf16[512,128]{1,0:T(8,128)(2,1)S(1)} %get-tuple-element.96), channel_id=1, source_target_pairs={{0,4},{2,6},{4,0},{6,2},{8,12},{10,14},{12,8},{14,10},{16,20},{18,... | collective-permute-start | bytes 393224 | tf_op jit(solution)/shard_map/ppermute | solution.py:991
  65.8 6.9 %collective-permute-start.12 = (bf16[512,128]{1,0:T(8,128)(2,1)S(1)}, bf16[512,128]{1,0:T(8,128)(2,1)S(1)}, u32[]{:S(2)}, u32[]{:S(2)}) collective-permute-start(bf16[512,128]{1,0:T(8,128)(2,1)S(1)} %get-tuple-element.97), channel_id=1, source_target_pairs={{0,6},{2,4},{4,2},{6,0},{8,14},{10,12},{12,10},{14,8},{16,22},{18,... | collective-permute-start | bytes 393224 | tf_op jit(solution)/shard_map/ppermute | solution.py:991
  72.6 20.0 %collective-permute-start.18 = (bf16[1088,1024]{1,0:T(8,128)(2,1)S(1)}, bf16[1088,1024]{1,0:T(8,128)(2,1)S(1)}, u32[]{:S(2)}, u32[]{:S(2)}) collective-permute-start(bf16[1088,1024]{1,0:T(8,128)(2,1)S(1)} %get-tuple-element.102.refs_6_), channel_id=1, source_target_pairs={{0,1},{1,0},{2,3},{3,2},{4,5},{5,4},{6,7},{7,6},{8,9},{9,8},{10,11... | collective-permute-start | bytes 6684680 | tf_op jit(solution)/shard_map/ppermute | solution.py:994
  73.5 14.4 %collective-permute-start.13 = (bf16[256,1024]{1,0:T(8,128)(2,1)S(1)}, bf16[256,1024]{1,0:T(8,128)(2,1)S(1)}, u32[]{:S(2)}, u32[]{:S(2)}) collective-permute-start(bf16[256,1024]{1,0:T(8,128)(2,1)S(1)} %get-tuple-element.104), channel_id=1, source_target_pairs={{0,8},{2,10},{4,12},{6,14},{8,0},{10,2},{12,4},{14,6},{16,24},{18,... | collective-permute-start | bytes 1572872 | tf_op jit(solution)/shard_map/ppermute | solution.py:988
  88.0 18.5 %collective-permute-start.14 = (bf16[128,1024]{1,0:T(8,128)(2,1)S(1)}, bf16[128,1024]{1,0:T(8,128)(2,1)S(1)}, u32[]{:S(2)}, u32[]{:S(2)}) collective-permute-start(bf16[128,1024]{1,0:T(8,128)(2,1)S(1)} %get-tuple-element.113), channel_id=1, source_target_pairs={{0,16},{2,18},{4,20},{6,22},{8,24},{10,26},{12,28},{14,30},{16,0},... | collective-permute-start | bytes 786440 | tf_op jit(solution)/shard_map/ppermute | solution.py:988
  89.1 7.8 %collective-permute-start.15 = (bf16[768,128]{1,0:T(8,128)(2,1)S(1)}, bf16[768,128]{1,0:T(8,128)(2,1)S(1)}, u32[]{:S(2)}, u32[]{:S(2)}) collective-permute-start(bf16[768,128]{1,0:T(8,128)(2,1)S(1)} %get-tuple-element.114), channel_id=1, source_target_pairs={{0,2},{2,0},{4,6},{6,4},{8,10},{10,8},{12,14},{14,12},{16,18},{18,... | collective-permute-start | bytes 589832 | tf_op jit(solution)/shard_map/ppermute | solution.py:991
  90.3 10.1 %collective-permute-start.16 = (bf16[768,128]{1,0:T(8,128)(2,1)S(1)}, bf16[768,128]{1,0:T(8,128)(2,1)S(1)}, u32[]{:S(2)}, u32[]{:S(2)}) collective-permute-start(bf16[768,128]{1,0:T(8,128)(2,1)S(1)} %get-tuple-element.115), channel_id=1, source_target_pairs={{0,4},{2,6},{4,0},{6,2},{8,12},{10,14},{12,8},{14,10},{16,20},{18,... | collective-permute-start | bytes 589832 | tf_op jit(solution)/shard_map/ppermute | solution.py:991
  91.6 10.9 %collective-permute-start.17 = (bf16[768,128]{1,0:T(8,128)(2,1)S(1)}, bf16[768,128]{1,0:T(8,128)(2,1)S(1)}, u32[]{:S(2)}, u32[]{:S(2)}) collective-permute-start(bf16[768,128]{1,0:T(8,128)(2,1)S(1)} %get-tuple-element.116), channel_id=1, source_target_pairs={{0,6},{2,4},{4,2},{6,0},{8,14},{10,12},{12,10},{14,8},{16,22},{18,... | collective-permute-start | bytes 589832 | tf_op jit(solution)/shard_map/ppermute | solution.py:991
  92.9 20.2 %collective-permute-start.26 = (bf16[272,1024]{1,0:T(8,128)(2,1)S(1)}, bf16[272,1024]{1,0:T(8,128)(2,1)S(1)}, u32[]{:S(2)}, u32[]{:S(2)}) collective-permute-start(bf16[272,1024]{1,0:T(8,128)(2,1)S(1)} %get-tuple-element.133), channel_id=1, source_target_pairs={{0,2},{2,0},{4,6},{6,4},{8,10},{10,8},{12,14},{14,12},{16,18},{18,... | collective-permute-start | bytes 1671176 | tf_op jit(solution)/shard_map/ppermute | solution.py:991
  96.9 26.6 %collective-permute-start.27 = (bf16[272,1024]{1,0:T(8,128)(2,1)S(1)}, bf16[272,1024]{1,0:T(8,128)(2,1)S(1)}, u32[]{:S(2)}, u32[]{:S(2)}) collective-permute-start(bf16[272,1024]{1,0:T(8,128)(2,1)S(1)} %get-tuple-element.134), channel_id=1, source_target_pairs={{0,4},{2,6},{4,0},{6,2},{8,12},{10,14},{12,8},{14,10},{16,20},{18,... | collective-permute-start | bytes 1671176 | tf_op jit(solution)/shard_map/ppermute | solution.py:991
  100.4 25.6 %collective-permute-start.28 = (bf16[272,1024]{1,0:T(8,128)(2,1)S(1)}, bf16[272,1024]{1,0:T(8,128)(2,1)S(1)}, u32[]{:S(2)}, u32[]{:S(2)}) collective-permute-start(bf16[272,1024]{1,0:T(8,128)(2,1)S(1)} %get-tuple-element.135), channel_id=1, source_target_pairs={{0,6},{2,4},{4,2},{6,0},{8,14},{10,12},{12,10},{14,8},{16,22},{18,... | collective-permute-start | bytes 1671176 | tf_op jit(solution)/shard_map/ppermute | solution.py:991
  106.4 2.8 %collective-permute-start.22 = (bf16[704,768]{1,0:T(8,128)(2,1)S(1)}, bf16[704,768]{1,0:T(8,128)(2,1)S(1)}, u32[]{:S(2)}, u32[]{:S(2)}) collective-permute-start(bf16[704,768]{1,0:T(8,128)(2,1)S(1)} %get-tuple-element.128), channel_id=1, source_target_pairs={{0,1},{1,0},{2,3},{3,2},{4,5},{5,4},{6,7},{7,6},{8,9},{9,8},{10,11... | collective-permute-start | bytes 3244040 | tf_op jit(solution)/shard_map/ppermute | solution.py:994
  109.2 1.0 copy-start.6
  110.4 20.5 %collective-permute-start.23 = (bf16[176,768]{1,0:T(8,128)(2,1)S(1)}, bf16[176,768]{1,0:T(8,128)(2,1)S(1)}, u32[]{:S(2)}, u32[]{:S(2)}) collective-permute-start(bf16[176,768]{1,0:T(8,128)(2,1)S(1)} %get-tuple-element.130), channel_id=1, source_target_pairs={{0,2},{2,0},{4,6},{6,4},{8,10},{10,8},{12,14},{14,12},{16,18},{18,... | collective-permute-start | bytes 811016 | tf_op jit(solution)/shard_map/ppermute | solution.py:991
  112.5 22.4 %collective-permute-start.24 = (bf16[176,768]{1,0:T(8,128)(2,1)S(1)}, bf16[176,768]{1,0:T(8,128)(2,1)S(1)}, u32[]{:S(2)}, u32[]{:S(2)}) collective-permute-start(bf16[176,768]{1,0:T(8,128)(2,1)S(1)} %get-tuple-element.131), channel_id=1, source_target_pairs={{0,4},{2,6},{4,0},{6,2},{8,12},{10,14},{12,8},{14,10},{16,20},{18,... | collective-permute-start | bytes 811016 | tf_op jit(solution)/shard_map/ppermute | solution.py:991
  113.1 24.3 %collective-permute-start.25 = (bf16[176,768]{1,0:T(8,128)(2,1)S(1)}, bf16[176,768]{1,0:T(8,128)(2,1)S(1)}, u32[]{:S(2)}, u32[]{:S(2)}) collective-permute-start(bf16[176,768]{1,0:T(8,128)(2,1)S(1)} %get-tuple-element.132), channel_id=1, source_target_pairs={{0,6},{2,4},{4,2},{6,0},{8,14},{10,12},{12,10},{14,8},{16,22},{18,... | collective-permute-start | bytes 811016 | tf_op jit(solution)/shard_map/ppermute | solution.py:991
  123.6 15.6 %collective-permute-start.19 = (bf16[128,1024]{1,0:T(8,128)(2,1)S(1)}, bf16[128,1024]{1,0:T(8,128)(2,1)S(1)}, u32[]{:S(2)}, u32[]{:S(2)}) collective-permute-start(bf16[128,1024]{1,0:T(8,128)(2,1)S(1)} %get-tuple-element.124), channel_id=1, source_target_pairs={{0,8},{2,10},{4,12},{6,14},{8,0},{10,2},{12,4},{14,6},{16,24},{18,... | collective-permute-start | bytes 786440 | tf_op jit(solution)/shard_map/ppermute | solution.py:988
  126.1 20.2 %collective-permute-start.20 = (bf16[128,1024]{1,0:T(8,128)(2,1)S(1)}, bf16[128,1024]{1,0:T(8,128)(2,1)S(1)}, u32[]{:S(2)}, u32[]{:S(2)}) collective-permute-start(bf16[128,1024]{1,0:T(8,128)(2,1)S(1)} %get-tuple-element.125), channel_id=1, source_target_pairs={{0,16},{2,18},{4,20},{6,22},{8,24},{10,26},{12,28},{14,30},{16,0},... | collective-permute-start | bytes 786440 | tf_op jit(solution)/shard_map/ppermute | solution.py:988
  130.9 18.3 %collective-permute-start.21 = (bf16[128,1024]{1,0:T(8,128)(2,1)S(1)}, bf16[128,1024]{1,0:T(8,128)(2,1)S(1)}, u32[]{:S(2)}, u32[]{:S(2)}) collective-permute-start(bf16[128,1024]{1,0:T(8,128)(2,1)S(1)} %get-tuple-element.126), channel_id=1, source_target_pairs={{0,24},{2,26},{4,28},{6,30},{8,16},{10,18},{12,20},{14,22},{16,8},... | collective-permute-start | bytes 786440 | tf_op jit(solution)/shard_map/ppermute | solution.py:988
  134.9 20.3 %collective-permute-start.32 = (bf16[32,1024]{1,0:T(8,128)(2,1)S(1)}, bf16[32,1024]{1,0:T(8,128)(2,1)S(1)}, u32[]{:S(2)}, u32[]{:S(2)}) collective-permute-start(bf16[32,1024]{1,0:T(8,128)(2,1)S(1)} %get-tuple-element.143), channel_id=1, source_target_pairs={{0,8},{2,10},{4,12},{6,14},{8,0},{10,2},{12,4},{14,6},{16,24},{18,... | collective-permute-start | bytes 196616 | tf_op jit(solution)/shard_map/ppermute | solution.py:988
  137.4 1.0 copy-start.5
  139.2 23.9 %collective-permute-start.29 = (bf16[48,768]{1,0:T(8,128)(2,1)S(1)}, bf16[48,768]{1,0:T(8,128)(2,1)S(1)}, u32[]{:S(2)}, u32[]{:S(2)}) collective-permute-start(bf16[48,768]{1,0:T(8,128)(2,1)S(1)} %get-tuple-element.139), channel_id=1, source_target_pairs={{0,8},{2,10},{4,12},{6,14},{8,0},{10,2},{12,4},{14,6},{16,24},{18,... | collective-permute-start | bytes 221192 | tf_op jit(solution)/shard_map/ppermute | solution.py:988
  139.2 23.9 %collective-permute-start.30 = (bf16[48,768]{1,0:T(8,128)(2,1)S(1)}, bf16[48,768]{1,0:T(8,128)(2,1)S(1)}, u32[]{:S(2)}, u32[]{:S(2)}) collective-permute-start(bf16[48,768]{1,0:T(8,128)(2,1)S(1)} %get-tuple-element.140), channel_id=1, source_target_pairs={{0,16},{2,18},{4,20},{6,22},{8,24},{10,26},{12,28},{14,30},{16,0},... | collective-permute-start | bytes 221192 | tf_op jit(solution)/shard_map/ppermute | solution.py:988
  146.3 16.7 %collective-permute-start.31 = (bf16[48,768]{1,0:T(8,128)(2,1)S(1)}, bf16[48,768]{1,0:T(8,128)(2,1)S(1)}, u32[]{:S(2)}, u32[]{:S(2)}) collective-permute-start(bf16[48,768]{1,0:T(8,128)(2,1)S(1)} %get-tuple-element.141), channel_id=1, source_target_pairs={{0,24},{2,26},{4,28},{6,30},{8,16},{10,18},{12,20},{14,22},{16,8},... | collective-permute-start | bytes 221192 | tf_op jit(solution)/shard_map/ppermute | solution.py:988
  149.2 10.3 %collective-permute-start.33 = (bf16[32,1024]{1,0:T(8,128)(2,1)S(1)}, bf16[32,1024]{1,0:T(8,128)(2,1)S(1)}, u32[]{:S(2)}, u32[]{:S(2)}) collective-permute-start(bf16[32,1024]{1,0:T(8,128)(2,1)S(1)} %get-tuple-element.144), channel_id=1, source_target_pairs={{0,16},{2,18},{4,20},{6,22},{8,24},{10,26},{12,28},{14,30},{16,0},... | collective-permute-start | bytes 196616 | tf_op jit(solution)/shard_map/ppermute | solution.py:988
  155.2 6.1 %collective-permute-start.34 = (bf16[32,1024]{1,0:T(8,128)(2,1)S(1)}, bf16[32,1024]{1,0:T(8,128)(2,1)S(1)}, u32[]{:S(2)}, u32[]{:S(2)}) collective-permute-start(bf16[32,1024]{1,0:T(8,128)(2,1)S(1)} %get-tuple-element.145), channel_id=1, source_target_pairs={{0,24},{2,26},{4,28},{6,30},{8,16},{10,18},{12,20},{14,22},{16,8},... | collective-permute-start | bytes 196616 | tf_op jit(solution)/shard_map/ppermute | solution.py:988
  156.4 0.9 copy-start.7
  157.3 7.5 %copy-start.9 = (f32[1,32]{1,0:T(1,128)S(1)}, f32[1,32]{1,0:T(1,128)}, u32[]{:S(2)}) copy-start(f32[1,32]{1,0:T(1,128)} %get-tuple-element.150) | copy-start | bytes 388
  161.2 1.0 copy-start.3
  163.0 1.0 copy-start.2

commit v3 on v2

--- a/solution.py
+++ b/solution.py
@@ -343,7 +343,7 @@
 F32 = jnp.float32
 BF16 = jnp.bfloat16
 VMEM_LIMIT = 16 * 1024 * 1024
-TIMES = {'branch': 500, 'layer': 500}
+TIMES = {'wait': 5, 'project': 80, 'feed_grad': 40, 'halve': 400, 'unpack': 20, 'feed_sum': 150, 'prepare': 150, 'back_rows': 80, 'feed_terms': 5, 'share_twin': 400, 'join_in': 5}
 
 VEC = 16
 
@@ -437,24 +437,19 @@
 
 def prepare_kernel(qkv, w_in, w_out, w_down, gain, shift, b_out, b_down, qv, b_in, packed, sems):
     line, _, _ = spot()
-    heads, feed = qkv.shape[1] // 12, w_in.shape[1] // LINES
+    feed = w_in.shape[1] // LINES
+    half, width = w_out.shape
     part = line % (LINES // 2)
     row = 0
     pairs = []
-    for source in (
+    sources = [
         w_in.at[:, pl.ds(pl.multiple_of(feed * line, 128), feed)],
-        w_out.at[pl.ds(pl.multiple_of(heads * part, 16), heads), :],
+        w_out,
         w_down.at[pl.ds(pl.multiple_of(feed * part, 16), feed), :],
-    ):
+    ]
+    for source in sources + [qkv.at[:, width * i : width * (i + 1)] for i in range(3)]:
         pairs.append((source, packed.at[row : row + source.shape[0], :]))
         row += source.shape[0]
-    half = qkv.shape[0]
-    for i in range(3):
-        columns = pl.ds(pl.multiple_of(heads * (LINES * i + line), 128), heads)
-        pairs.append(
-            (qkv.at[:, columns], packed.at[row : row + half, heads * i : heads * (i + 1)])
-        )
-    row += half
     rows = [x[...].astype(F32).reshape(1, half) for x in (gain, shift, b_out, b_down)]
     rows += [qv[...].astype(F32), b_in[...].astype(F32).reshape(4, half)]
     rows.append(jnp.zeros((VEC - 10, half), F32))
@@ -464,36 +459,48 @@
 
 def assemble_kernel(own, twin, qkv, w_in, w_out, w_down, vectors, low, sems):
     line, _, core = spot()
-    half = qkv.shape[0] // 2
-    heads, feed = w_out.shape[0], w_down.shape[0]
-    qkv_row = half + heads + feed
-    vec_row = qkv_row + half
+    width = w_out.shape[1]
+    half = width // 2
+    feed = w_down.shape[0]
+    down_row = 2 * half
+    qkv_row = down_row + feed
+    vec_row = qkv_row + 3 * half
     pairs = []
     for source, side in ((own, core), (twin, 1 - core)):
         rows = pl.ds(pl.multiple_of(half * side, half), half)
         pairs.append((source.at[:half, :], w_in.at[rows, :]))
-        pairs.append((source.at[qkv_row:vec_row, : 3 * heads], qkv.at[rows, :]))
+        pairs.append((source.at[half:down_row, :], w_out.at[rows, :]))
+        for i in range(3):
+            base = qkv_row + half * i
+            pairs.append(
+                (source.at[base : base + half, :], qkv.at[rows, width * i : width * (i + 1)])
+            )
         spare = pl.ds(pl.multiple_of(VEC * side, VEC), VEC)
         pairs.append((source.at[vec_row:, :half], low.at[spare, :]))
     holds = core == line // (LINES // 2)
 
     @pl.when(holds)
     def _():
-        rest = [
-            (own.at[half : half + heads, :], w_out),
-            (own.at[half + heads : qkv_row, :], w_down),
-        ]
-        run_copies(pairs + rest, sems)
+        run_copies(pairs + [(own.at[down_row:qkv_row, :], w_down)], sems)
 
     @pl.when(jnp.logical_not(holds))
     def _():
-        rest = [
-            (twin.at[half : half + heads, :], w_out),
-            (twin.at[half + heads : qkv_row, :], w_down),
-        ]
-        run_copies(pairs + rest, sems)
+        run_copies(pairs + [(twin.at[down_row:qkv_row, :], w_down)], sems)
 
     vectors[...] = low[...].astype(F32)
+
+
+def line_columns(qkv, part):
+    line, _, _ = spot()
+    width = qkv.shape[1] // 3
+    base = width * part + width // LINES * line
+    return qkv[:, pl.ds(pl.multiple_of(base, 128), width // LINES)]
+
+
+def line_rows_of(w_out):
+    line, _, _ = spot()
+    count = w_out.shape[0] // LINES
+    return w_out[pl.ds(pl.multiple_of(count * line, 16), count), :]
 
 
 def full_row(vectors, index):
@@ -509,10 +516,6 @@
     numbers = jnp.where(lane == 0, order[0], jnp.where(lane == 1, order[1], 0))
     packed[rows:, :128] = numbers.astype(F32).astype(BF16)
     packed[rows:, 128:] = jnp.zeros((VEC, tokens.shape[1] - 128), BF16)
-
-
-def hold_kernel(x, y):
-    y[...] = x[...]
 
 
 def reorder(chunks, place):
@@ -580,9 +583,9 @@
     lanes = pl.ds(pl.multiple_of(256 * (line % (LINES // 2)), 256), 256)
     bias_q = vectors[pl.ds(side + 4, 1), lanes]
     bias_v = vectors[pl.ds(side + 5, 1), lanes]
-    q_chunks = reorder(two_chunks(dot(ln_ref[...], qkv[:, :256]) + bias_q), place)
-    k_chunks = reorder(two_chunks(dot(ln_ref[...], qkv[:, 256:512])), place)
-    v_chunks = reorder(two_chunks(dot(ln_ref[...], qkv[:, 512:]) + bias_v), place)
+    q_chunks = reorder(two_chunks(dot(ln_ref[...], line_columns(qkv, 0)) + bias_q), place)
+    k_chunks = reorder(two_chunks(dot(ln_ref[...], line_columns(qkv, 1))), place)
+    v_chunks = reorder(two_chunks(dot(ln_ref[...], line_columns(qkv, 2)) + bias_v), place)
     total = ln_ref.shape[0]
     end = total * 3 // 2
     for slot, ref in enumerate((s0, s1, s2, s3)):
@@ -593,16 +596,14 @@
     lnt_ref[...] = ln_ref[...].T
 
 
-def back_rows_kernel(c0, c1, c2, c3, w_out, att, s0, s1, s2, s3, cot):
+def back_rows_kernel(c0, c1, c2, c3, w_out, s0, s1, s2, s3, cot):
     line, place, _ = spot()
     rows = c0.shape[0]
     for k, ref in enumerate((c0, c1, c2, c3)):
         cot[pl.ds(pl.multiple_of(rows * (line ^ k), rows), rows), :] = ref[...]
-    chunks = reorder(two_chunks(dot_nt(cot[...], w_out[...])), place)
-    fold = att.shape[0] // 4
+    chunks = reorder(two_chunks(dot_nt(cot[...], line_rows_of(w_out))), place)
     for slot, ref in enumerate((s0, s1, s2, s3)):
-        ref[:fold, :] = att[fold * slot : fold * (slot + 1), :]
-        ref[fold:, :] = fold_rows(chunks[slot // 2], slot).astype(BF16)
+        ref[...] = fold_rows(chunks[slot // 2], slot).astype(BF16)
 
 
 def block_rows(table):
@@ -644,7 +645,7 @@
 
 
 def attend_kernel(r0, r1, r2, r3, cosine, sine, *rest):
-    att_slots, qk_ref, kq_ref, v_ref, att_ref, lse_ref, table_ref, raw, table, sem = rest
+    qk_ref, kq_ref, v_ref, att_ref, lse_ref, table_ref, raw, table, sem = rest
     refs = (r0, r1, r2, r3)
     count = qk_ref.shape[0]
     lines = count // 4
@@ -672,10 +673,6 @@
         weighted = dot(weights.astype(BF16), v_ref[:keys, :])
         att_ref[rows, :] = weighted / total
         lse_ref[rows, :] = top + jnp.log(total)
-    for j, i, source in block_rows(table):
-        start = lines // 2 * j + 64 * (i % 4)
-        lanes = slice(0, 64) if i < 4 else slice(64, 128)
-        att_slots[start : start + 64, lanes] = att_ref[source, :].astype(BF16)
 
 
 def attend_back_kernel(r0, r1, r2, r3, table_ref, qk_ref, kq_ref, v_ref, att_ref, *rest):
@@ -685,7 +682,7 @@
     count = qk_ref.shape[0]
     lines = count // 4
     run_copies([(table_ref, table)], sem)
-    sort_rows(table, refs, ga_ref, lines // 2, True)
+    sort_rows(table, refs, ga_ref, 0, True)
     mask = allowed_tile()
     kt_ref[...] = jnp.zeros_like(kt_ref)
     vt_ref[...] = jnp.zeros_like(vt_ref)
@@ -726,9 +723,19 @@
         outs[j][64 * i : 64 * (i + 1), :] = gqk[source, :].astype(BF16)
         start = lines + 64 * (i % 4)
         outs[j][start : start + 64, lanes] = gv[source, :].astype(BF16)
-
-
-def feed_kernel(ln, w_in, vectors, w_down, hidden_ref, actt_ref, low_ref, act_ref):
+        start += lines // 2
+        outs[j][start : start + 64, lanes] = att_ref[source, :].astype(BF16)
+
+
+def split_lines(low, keep, send):
+    line, _, _ = spot()
+    rows = low.shape[0] // LINES
+    for k, (ref, base) in enumerate(((keep, 0), (send, 0), (keep, rows), (send, rows))):
+        part = pl.ds(pl.multiple_of(rows * (line ^ k), rows), rows)
+        ref[base : base + rows, :] = low[part, :].astype(ref.dtype)
+
+
+def feed_kernel(ln, w_in, vectors, w_down, hidden_ref, actt_ref, keep, send, act_ref, low_ref):
     line, _, _ = spot()
     row = VEC * (line // (LINES // 2)) + 6 + 2 * (line % (LINES // 2))
     bias = jnp.concatenate([vectors[pl.ds(row, 1), :], vectors[pl.ds(row + 1, 1), :]], 1)
@@ -742,26 +749,30 @@
     for f in range(4):
         cols = slice(256 * f, 256 * (f + 1))
         low_ref[:, cols] = dot(act_ref[...], w_down[:, cols])
-
-
-def feed_back_kernel(cot_ref, hidden, actt, lnt, w_in, w_down, *rest):
-    send, keep, low_ref, gh_ref, chunk_ref = rest
-    line, _, core = spot()
-    cot = cot_ref[...]
-    block = send.shape[0] // 4
-    sums = jnp.zeros((1, 1024), F32)
-    cot_sum = jnp.sum(cot.astype(F32), 0, keepdims=True)
-    bias_sums = []
+    split_lines(low_ref, keep, send)
+
+
+def feed_grad_kernel(cot, hidden, w_in, w_down, gh_ref, sums, low_ref, keep, send):
     for f in range(4):
         cols = slice(256 * f, 256 * (f + 1))
-        grad_active = dot_nt(cot, w_down[cols, :])
+        grad_active = dot_nt(cot[...], w_down[cols, :])
         h = hidden[:, cols]
         slope = 0.5 * (1.0 + lax.erf(h * 0.7071067811865476)) + h * jnp.exp(
             -0.5 * h * h
         ) * 0.3989422804014327
         grad_hidden = (slope * grad_active).astype(BF16)
         gh_ref[:, cols] = grad_hidden
-        bias_sums.append(jnp.sum(grad_hidden.astype(F32), 0, keepdims=True))
+        total = jnp.sum(grad_hidden.astype(F32), 0, keepdims=True)
+        sums[:, cols] = jnp.broadcast_to(total, (8, 256))
+    for i in range(4):
+        low_ref[:, 256 * i : 256 * (i + 1)] = dot_nt(gh_ref[...], w_in[256 * i : 256 * (i + 1), :])
+    split_lines(low_ref, keep, send)
+
+
+def feed_terms_kernel(cot_ref, actt, lnt, gh, sums, send, keep, chunk_ref):
+    line, _, core = spot()
+    cot = cot_ref[...]
+    block = send.shape[0] // 4
     for f in range(4):
         chunk_ref[...] = dot(actt[256 * f : 256 * (f + 1), :], cot)
         base = block * f
@@ -770,7 +781,7 @@
         ].astype(BF16)
         keep[base : base + 128, :] = chunk_ref[pl.ds(pl.multiple_of(core * 128, 128), 128), :]
     for z in range(4):
-        chunk_ref[...] = dot(lnt[256 * z : 256 * (z + 1), :], gh_ref[...])
+        chunk_ref[...] = dot(lnt[256 * z : 256 * (z + 1), :], gh[...])
         for f in range(4):
             base = block * f + 128 + 32 * z
             send[base : base + 32, :] = chunk_ref[
@@ -779,6 +790,7 @@
             keep[base : base + 32, :] = chunk_ref[
                 pl.ds(pl.multiple_of(64 * f + 32 * core, 32), 32), :
             ]
+    cot_sum = jnp.sum(cot.astype(F32), 0, keepdims=True)
     picked = jnp.where(
         line < 2,
         jnp.where(line == 0, cot_sum[:, 0:256], cot_sum[:, 256:512]),
@@ -786,15 +798,13 @@
     )
     zero = jnp.zeros((1, 640), F32)
     for f in range(4):
-        even, odd = bias_sums[f][:, :128], bias_sums[f][:, 128:]
+        even, odd = sums[:1, 256 * f : 256 * f + 128], sums[:1, 256 * f + 128 : 256 * f + 256]
         first = core == 0
         base = block * f + 256
         given = jnp.concatenate([jnp.where(first, odd, even), picked, zero], 1)
         kept = jnp.concatenate([jnp.where(first, even, odd), picked, zero], 1)
         send[base : base + VEC, :] = jnp.broadcast_to(given, (VEC, 1024)).astype(BF16)
         keep[base : base + VEC, :] = jnp.broadcast_to(kept, (VEC, 1024))
-    for i in range(4):
-        low_ref[:, 256 * i : 256 * (i + 1)] = dot_nt(gh_ref[...], w_in[256 * i : 256 * (i + 1), :])
 
 
 def share_twin_kernel(keep, received, o0, o1, o2, o3):
@@ -830,57 +840,50 @@
         ref[...] = total(rows).astype(ref.dtype)
 
 
-def branch_kernel(r0, r1, r2, r3, low, w_out, keep, send, att_t, low_ref):
-    line, place, _ = spot()
-    fold = r0.shape[0] // 2
-    parts = [ref[:fold, :].astype(F32) for ref in (r0, r1, r2, r3)]
-    chunks = reorder((unfold_pair(parts[0], parts[1]), unfold_pair(parts[2], parts[3])), place)
-    attended = jnp.concatenate(chunks, 1).astype(BF16)
-    att_t[...] = attended.T
-    low_ref[...] = low[...] + dot(attended, w_out[...])
-    rows = low_ref.shape[0] // 4
-    for k, (ref, base) in enumerate(((keep, 0), (send, 0), (keep, rows), (send, rows))):
-        part = pl.ds(pl.multiple_of(rows * (line ^ k), rows), rows)
-        ref[base : base + rows, :] = low_ref[part, :].astype(ref.dtype)
-
-
 def halve_kernel(keep, received, own, send):
     rows = own.shape[0]
     own[...] = keep[:rows, :] + received[:rows, :].astype(F32)
     send[...] = (keep[rows:, :] + received[rows:, :].astype(F32)).astype(BF16)
 
 
-def grads_kernel(r0, r1, r2, r3, low, normed, lnt, qkv, att_t, cot, head_sums, *rest):
-    s0, s1, s2, s3, send, keep, g_ref, low_ref, chunk_ref, out_ref = rest
-    line, place, core = spot()
-    rows = s0.shape[0]
-    total = 4 * rows
+def unpack_kernel(r0, r1, r2, r3, mixed, att_t, s1, s2, s3):
+    line, place, _ = spot()
+    rows = s1.shape[0]
+    total = LINES * rows
+    fold = total // 2
     parts = [ref[...].astype(F32) for ref in (r0, r1, r2, r3)]
     keep_left = left_lanes(total)
-    queries, keys, values = [], [], []
+    chunks = [[], [], [], []]
     for pair in range(2):
-        even, odd = parts[2 * pair][:total], parts[2 * pair + 1][:total]
-        queries.append(jnp.where(keep_left, even, pltpu.roll(odd, 64, 1)))
-        keys.append(jnp.where(keep_left, pltpu.roll(even, 64, 1), odd))
-        values.append(unfold_pair(parts[2 * pair][total:], parts[2 * pair + 1][total:]))
-    for index, chunks in enumerate((queries, keys, values)):
-        for pair, chunk in enumerate(reorder(chunks, place)):
+        one, two = parts[2 * pair], parts[2 * pair + 1]
+        even, odd = one[:total], two[:total]
+        values, attended = slice(total, total + fold), slice(total + fold, total + 2 * fold)
+        chunks[0].append(unfold_pair(one[attended], two[attended]))
+        chunks[1].append(jnp.where(keep_left, even, pltpu.roll(odd, 64, 1)))
+        chunks[2].append(jnp.where(keep_left, pltpu.roll(even, 64, 1), odd))
+        chunks[3].append(unfold_pair(one[values], two[values]))
+    for index, both in enumerate(chunks):
+        for pair, chunk in enumerate(reorder(both, place)):
             base = 256 * index + 128 * pair
-            g_ref[:, base : base + 128] = chunk.astype(BF16)
-    for i in range(4):
-        cols = slice(256 * i, 256 * (i + 1))
-        low_ref[:, cols] = low[:, cols] + dot_nt(g_ref[...], qkv[cols, :])
-    sum_gain = jnp.zeros((1, 1024), F32)
-    sum_bias = jnp.zeros((1, 1024), F32)
-    for k, out in enumerate((s0, s1, s2, s3)):
-        part = pl.ds(pl.multiple_of(rows * (line ^ k), rows), rows)
-        grad = low_ref[part, :]
-        out[...] = grad.astype(out.dtype)
-        sum_gain = sum_gain + jnp.sum(grad * normed[part, :], 0, keepdims=True)
-        sum_bias = sum_bias + jnp.sum(grad, 0, keepdims=True)
+            mixed[:, base : base + 128] = chunk.astype(BF16)
+    for k, ref in ((1, s1), (2, s2), (3, s3)):
+        ref[...] = mixed[pl.ds(pl.multiple_of(rows * (line ^ k), rows), rows), :]
+    att_t[...] = mixed[:, :256].T
+
+
+def grads_kernel(mixed, low, normed, lnt, qkv, att_t, cot, head_sums, *rest):
+    send, keep, low_ref, chunk_ref, out_ref = rest
+    _, place, core = spot()
+    low_ref[...] = low[...]
+    for i in range(3):
+        cols = slice(256 * (i + 1), 256 * (i + 2))
+        low_ref[...] += dot_nt(mixed[:, cols], line_columns(qkv, i))
+    grad = low_ref[...]
+    sum_gain = jnp.sum(grad * normed[...], 0, keepdims=True)
+    sum_bias = jnp.sum(grad, 0, keepdims=True)
     block = send.shape[0] // 4
     for z in range(4):
-        chunk_ref[...] = dot(lnt[256 * z : 256 * (z + 1), :], g_ref[...])
+        chunk_ref[...] = dot(lnt[256 * z : 256 * (z + 1), :], mixed[:, 256:])
         for f in range(4):
             base = block * f + 32 * z
             send[base : base + 32, :] = chunk_ref[
@@ -937,22 +940,33 @@
     bias[...] = vec_ref[pl.ds(4 + line, 1), :]
 
 
-def layer_kernel(own, received, tokens, vectors, out):
-    total = own[...] + received[...].astype(F32) + tokens[: own.shape[0], :].astype(F32)
-    out[...] = (total + full_row(vectors, 2) + full_row(vectors, 3)).astype(BF16)
-
-
-def tokens_kernel(own, r1, r2, r3, tokens, cot, vectors, out):
-    grad_ln = own[...] + r1[...].astype(F32) + r2[...].astype(F32) + r3[...].astype(F32)
+def wait_kernel(out):
+    out[...] = jnp.zeros_like(out)
+
+
+def tokens_kernel(mixed, r1, r2, r3, qkv, w_out, *rest):
+    low, low_rest, grad, grad_rest, tokens, cot, vectors, layer_out, grad_tokens = rest
     line, _, _ = spot()
-    rows = own.shape[0]
-    normed, inverse = normalise(tokens[:rows, :])
+    rows = low.shape[0]
+    mine = pl.ds(pl.multiple_of(rows * line, rows), rows)
+    branch = low[...] + low_rest[...].astype(F32)
+    grad_ln = grad[...] + grad_rest[...].astype(F32)
+    for k, ref in enumerate((mixed.at[mine, :], r1, r2, r3)):
+        base = 256 * (line ^ k)
+        part = pl.ds(pl.multiple_of(base, 256), 256)
+        branch = branch + dot(ref[:, :256], w_out[part, :])
+        for i in range(3):
+            part = pl.ds(pl.multiple_of(base + 1024 * i, 256), 256)
+            grad_ln = grad_ln + dot_nt(ref[:, 256 * (i + 1) : 256 * (i + 2)], qkv[:, part])
+    own = tokens[:rows, :]
+    branch = branch + own.astype(F32)
+    layer_out[...] = (branch + full_row(vectors, 2) + full_row(vectors, 3)).astype(BF16)
+    normed, inverse = normalise(own)
     g = grad_ln * full_row(vectors, 0)
-    grad = inverse * (
+    back = inverse * (
         g - jnp.mean(g, -1, keepdims=True) - normed * jnp.mean(g * normed, -1, keepdims=True)
     )
-    mine = cot[pl.ds(pl.multiple_of(rows * line, rows), rows), :]
-    out[...] = (mine.astype(F32) + grad).astype(BF16)
+    grad_tokens[...] = (cot[mine, :].astype(F32) + back).astype(BF16)
 
 
 def turn_tables(count):
@@ -996,6 +1010,10 @@
     def with_lines(blocks):
         return [blocks[0]] + [near(over_lines(raw(blocks[k]), k)) for k in range(1, LINES)]
 
+    def from_lines(x):
+        far_one = over_lines(raw(x), 2)
+        return [near(over_lines(raw(x), 1)), near(far_one), near(over_lines(far_one, 1))]
+
     def with_places(blocks):
         return [blocks[0]] + [near(over_places(raw(blocks[j]), j)) for j in range(1, ACROSS)]
 
@@ -1009,7 +1027,7 @@
     line_rows = rows * LINES
     slot_rows = line_rows * 3 // 2
     rotation = turn_tables(length)
-    packed_rows = half + head_cols + feed_cols + half + VEC
+    packed_rows = 5 * half + feed_cols + VEC
     table = pltpu.SMEM((32, 128), jnp.int32)
     one_copy = pltpu.SemaphoreType.DMA((1,))
     block = 128 + 128 + VEC
@@ -1023,7 +1041,6 @@
         )
         last[:] = results[:1]
         return results
-
     (packed,) = run(
         prepare_kernel,
         [near((packed_rows, width), BF16)],
@@ -1038,33 +1055,31 @@
         [],
         block_order.reshape(2), far(tokens[0]),
     )
-    token_lines = with_lines([token_block] * LINES)
-    qkv, in_rows, out_rows, down_rows, vectors = run(
+    from_two = over_lines(raw(token_block), 2)
+    token_lines = [
+        token_block,
+        near(over_lines(raw(token_block), 1)),
+        near(from_two),
+        near(over_lines(from_two, 1)),
+    ]
+    cot_lines = [near(cotangent[0]), *from_lines(cotangent[0])]
+    run(wait_kernel, [near((8, 128), F32)], [], after=[near(from_two)])
+    qkv, in_rows, w_out_full, down_rows, vectors = run(
         assemble_kernel,
         [
-            near((width, qkv_cols), BF16),
+            near((width, 3 * width), BF16),
             near((width, feed_cols), BF16),
-            near((head_cols, width), BF16),
+            near((width, width), BF16),
             near((feed_cols, width), BF16),
             near((2 * VEC, half), F32),
         ],
-        [pltpu.VMEM((2 * VEC, half), BF16), pltpu.SemaphoreType.DMA((8,))],
+        [pltpu.VMEM((2 * VEC, half), BF16), pltpu.SemaphoreType.DMA((13,))],
         packed, twin(packed),
         loose_in=2,
     )
-    first_cot = near(over_lines(cotangent[0], 1))
-    (held,) = run(
-        hold_kernel,
-        [((rows, width), BF16)],
-        [],
-        cotangent[0],
-        after=token_lines[1:] + [first_cot],
-    )
-    cot_lines = [cotangent[0], first_cot] + [near(over_lines(held, k)) for k in (2, 3)]
     *slots, ln_low, ln_turned, normed = run(
         project_kernel,
-        [near((slot_rows + VEC, 128), BF16)]
-        + [near((slot_rows + VEC, 128), BF16)] * 3
+        [near((slot_rows + VEC, 128), BF16)] * 4
         + [
             near((line_rows, width), BF16),
             near((width, line_rows), BF16),
@@ -1074,20 +1089,41 @@
         *token_lines, vectors, qkv,
     )
     slots_in = with_places(slots)
-    hidden, active_turned, feed_low = run(
+    hidden, active_turned, low_keep, low_send = run(
         feed_kernel,
         [
             near((line_rows, feed_cols), F32),
             near((feed_cols, line_rows), BF16),
+            near((2 * rows, width), F32),
+            near((2 * rows, width), BF16),
+        ],
+        [pltpu.VMEM((line_rows, feed_cols), BF16), pltpu.VMEM((line_rows, width), F32)],
+        ln_low, in_rows, vectors, down_rows,
+    )
+    low_received = near(over_lines(raw(low_send), 1))
+    *back_slots, cot_rows = run(
+        back_rows_kernel,
+        [near((line_rows // 2, 128), BF16)] * 4 + [near((line_rows, width), BF16)],
+        [],
+        *cot_lines, w_out_full,
+    )
+    back_in = with_places(back_slots)
+    grad_hidden, hidden_sums, feed_grad_low, grad_keep, grad_send = run(
+        feed_grad_kernel,
+        [
+            near((line_rows, feed_cols), BF16),
+            near((8, feed_cols), F32),
             near((line_rows, width), F32),
+            near((2 * rows, width), F32),
+            near((2 * rows, width), BF16),
         ],
-        [pltpu.VMEM((line_rows, feed_cols), BF16)],
-        ln_low, in_rows, vectors, down_rows,
-    )
-    att_slots, qk_rows, kq_rows, value_rows, attended, lse, numbers = run(
+        [],
+        cot_rows, hidden, in_rows, down_rows,
+    )
+    grad_received = near(over_lines(raw(grad_send), 1))
+    qk_rows, kq_rows, value_rows, attended, lse, numbers = run(
         attend_kernel,
         [
-            near((line_rows * 2, 128), BF16),
             near((length, 128), BF16),
             near((length, 128), BF16),
             near((length, 64), BF16),
@@ -1098,40 +1134,16 @@
         [pltpu.VMEM((length, 128), BF16), table, one_copy],
         *slots_in, *rotation,
     )
-    *mixed, cot_rows = run(
-        back_rows_kernel,
-        [near((line_rows, 128), BF16)]
-        + [near((line_rows, 128), BF16)] * 3
-        + [near((line_rows, width), BF16)],
-        [],
-        *cot_lines, out_rows, att_slots,
-    )
-    mixed_in = with_places(mixed)
-    feed_send, feed_keep, feed_grad_low = run(
-        feed_back_kernel,
-        [
-            near((4 * block, width), BF16),
-            near((4 * block, width), F32),
-            near((line_rows, width), F32),
-        ],
-        [pltpu.VMEM((line_rows, feed_cols), BF16), pltpu.VMEM((256, 1024), F32)],
-        cot_rows, hidden, active_turned, ln_turned, in_rows, down_rows,
+    feed_send, feed_keep = run(
+        feed_terms_kernel,
+        [near((4 * block, width), BF16), near((4 * block, width), F32)],
+        [pltpu.VMEM((256, 1024), F32)],
+        cot_rows, active_turned, ln_turned, grad_hidden, hidden_sums,
     )
     feed_twin = twin(feed_send)
-    low_keep, low_send, att_turned = run(
-        branch_kernel,
-        [
-            near((2 * rows, width), F32),
-            near((2 * rows, width), BF16),
-            near((head_cols, line_rows), BF16),
-        ],
-        [pltpu.VMEM((line_rows, width), F32)],
-        *mixed_in, feed_low, out_rows,
-    )
-    low_received = near(over_lines(raw(low_send), 1))
     *grad_slots, bias_sums = run(
         attend_back_kernel,
-        [near((slot_rows, 128), BF16)] + [near((slot_rows, 128), BF16)] * 3 + [near((8, 128), F32)],
+        [near((line_rows * 2, 128), BF16)] * 4 + [near((8, 128), F32)],
         [
             pltpu.VMEM((length, 64), BF16),
             pltpu.VMEM((128, length), F32),
@@ -1141,7 +1153,7 @@
             table,
             one_copy,
         ],
-        *mixed_in, numbers, qk_rows, kq_rows, value_rows, attended, lse, *rotation,
+        *back_in, numbers, qk_rows, kq_rows, value_rows, attended, lse, *rotation,
     )
     grad_slots_in = with_places(grad_slots)
     low_own, low_half = run(
@@ -1158,32 +1170,37 @@
         feed_keep, feed_twin,
     )
     feed_in = with_places(feed_blocks)
-    *ln_slots, qkv_send, qkv_keep = run(
+    mixed, att_turned, *mixed_slots = run(
+        unpack_kernel,
+        [near((line_rows, width), BF16), near((head_cols, line_rows), BF16)]
+        + [near((rows, width), BF16)] * 3,
+        [],
+        *grad_slots_in,
+    )
+    _, *mixed_in = with_lines([mixed, *mixed_slots])
+    qkv_send, qkv_keep = run(
         grads_kernel,
-        [near((rows, width), F32)]
-        + [near((rows, width), BF16)] * 3
-        + [near((4 * qkv_block, qkv_cols), BF16), near((4 * qkv_block, qkv_cols), F32)],
+        [near((4 * qkv_block, qkv_cols), BF16), near((4 * qkv_block, qkv_cols), F32)],
         [
-            pltpu.VMEM((line_rows, qkv_cols), BF16),
             pltpu.VMEM((line_rows, width), F32),
             pltpu.VMEM((256, qkv_cols), F32),
             pltpu.VMEM((head_cols, width), F32),
         ],
-        *grad_slots_in, feed_grad_low, normed, ln_turned, qkv, att_turned, cot_rows,
-        bias_sums,
-    )
-    ln_in = with_lines(ln_slots)
-    (layer_out,) = run(
-        layer_kernel,
-        [((rows, width), BF16)],
+        mixed, feed_grad_low, normed, ln_turned, qkv, att_turned, cot_rows, bias_sums,
+    )
+    qkv_terms = twin(qkv_send)
+    grad_own, grad_half = run(
+        halve_kernel,
+        [near((rows, width), F32), near((rows, width), BF16)],
         [],
-        low_own, low_rest, token_block, vectors,
-    )
+        grad_keep, grad_received,
+    )
+    grad_rest = near(over_lines(raw(grad_half), 2))
     qkv_blocks = run(
         share_twin_kernel,
         [near((qkv_block, qkv_cols), F32)] + [near((qkv_block, qkv_cols), BF16)] * 3,
         [],
-        qkv_keep, twin(qkv_send),
+        qkv_keep, qkv_terms,
     )
     qkv_sums = with_places(qkv_blocks)
     grad_down, grad_b_in, grad_b, *in_slots = run(
@@ -1202,11 +1219,12 @@
         *qkv_sums,
     )
     qkv_parts = with_lines(qkv_parts)
-    (grad_tokens,) = run(
+    layer_out, grad_tokens = run(
         tokens_kernel,
-        [((rows, width), BF16)],
+        [((rows, width), BF16), ((rows, width), BF16)],
         [],
-        *ln_in, token_block, cot_rows, vectors,
+        mixed, *mixed_in, qkv, w_out_full, low_own, low_rest, grad_own, grad_rest,
+        token_block, cot_rows, vectors,
     )
     (grad_in,) = run(join_in_kernel, [((32, feed), F32)], [], *in_parts)
     grad_qkv, grad_gain, grad_shift = run(

time: 166 us -> 160 us (0.964)
  waiting for transfers between devices: 64.5 us -> 58.5 us
  Pallas kernels: 42 us -> 45.4 us
  starting transfers between devices: 52.6 us -> 50.7 us
    ppermute x15, waiting for transfers between devices: 24.6 us -> 13.4 us  [over_places(): return lax.ppermute(x, 'ctx', [(i, i ^ j) for i in positions])]
    ppermute x17 -> x19, waiting for transfers between devices: 38 us -> 44.6 us  [over_lines(): return lax.ppermute(x, 'ctx', [(i, i ^ k * ACROSS) for i in positions])]
    pallas_call x21 -> x22, Pallas kernels: 42 us -> 45.4 us  [call(): pl.pallas_call(body, name=name, out_shape=outs, in_specs=specs + [loose]...]
    unnamed x21 -> x23, local copies, waits for them, and re-layouts: 5.41 us -> 4.47 us
    ppermute x17 -> x19, starting transfers between devices: 32.5 us -> 32.1 us  [over_lines(): return lax.ppermute(x, 'ctx', [(i, i ^ k * ACROSS) for i in positions])]
  transfers between devices with their start and end apart: 35 -> 37, of which waited for: 16 -> 11; matrix products, arithmetic and copies ran while one was open for 0% -> 0% of each run, Pallas kernels for 23% -> 25%
where the time goes in v3:
time: 160 us
  waiting for transfers between devices  58.5 us (37%)
  starting transfers between devices  50.7 us (32%)
  Pallas kernels  45.4 us (28%)
  local copies, waits for them, and re-layouts  4.47 us (3%)
    pallas_call x22, Pallas kernels, call(): pl.pallas_call(body, name=name, out_shape=outs, in_specs=specs + [loose]...  45.4 us
    ppermute x19, waiting for transfers between devices, over_lines(): return lax.ppermute(x, 'ctx', [(i, i ^ k * ACROSS) for i in positions])  44.6 us
    ppermute x19, starting transfers between devices, over_lines(): return lax.ppermute(x, 'ctx', [(i, i ^ k * ACROSS) for i in positions])  32.1 us
    ppermute x15, starting transfers between devices, over_places(): return lax.ppermute(x, 'ctx', [(i, i ^ j) for i in positions])  18 us
    ppermute x15, waiting for transfers between devices, over_places(): return lax.ppermute(x, 'ctx', [(i, i ^ j) for i in positions])  13.4 us
    unnamed x23, local copies, waits for them, and re-layouts  4.47 us
  transfers between devices with their start and end apart: 37, of which 11 were waited for; matrix products, arithmetic and copies ran while one was open for 0% of the time, Pallas kernels for 25%

profile of v3, /device:TPU:0, one launch (start us, length us, event | category | flops | bytes accessed | tf_op | source)
XLA Modules:
  0.0 160.0 jit_solution(16525279243134917160)
XLA Ops:
  0.7 4.0 %prepare.1.refs_2_.refs_0_ = bf16[3600,1024]{1,0:T(8,128)(2,1)S(1)} custom-call(bf16[512,3072]{1,0:T(8,128)(2,1)} %refs_0_.1, bf16[512,4096]{1,0:T(8,128)(2,1)} %refs_1_.1, bf16[512,1024]{1,0:T(8,128)(2,1)} %refs_2_.1, bf16[2048,1024]{1,0:T(8,128)(2,1)} %refs_3_.1, bf16[512]{0:T(512)(128)(2,1)} %refs_4_.2, bf16[512]{0:T(512)(128)(2,1)} %refs_5_.2, ...), custom_call_target="tpu_custom_call" | custom-call | flops 17250000896 | tf_op jit(solution)/shard_map/prepare/pallas_call | solution.py:413
  4.6 0.5 collective-permute-start.3
  5.2 1.0 pack.1.refs_1_.refs_0_.refs_10_
  6.2 3.7 %collective-permute-start.4 = (bf16[144,1024]{1,0:T(8,128)(2,1)S(1)}, bf16[144,1024]{1,0:T(8,128)(2,1)S(1)}, u32[]{:S(2)}, u32[]{:S(2)}) collective-permute-start(bf16[144,1024]{1,0:T(8,128)(2,1)S(1)} %pack.1.refs_1_.refs_0_.refs_10_), channel_id=1, source_target_pairs={{0,16},{2,18},{4,20},{6,22},{8,24},{10,26},{12,28},{14,30},{16,0},... | collective-permute-start | bytes 884744 | tf_op jit(solution)/shard_map/ppermute | solution.py:1002
  10.0 1.8 %collective-permute-start.5 = (bf16[144,1024]{1,0:T(8,128)(2,1)S(1)}, bf16[144,1024]{1,0:T(8,128)(2,1)S(1)}, u32[]{:S(2)}, u32[]{:S(2)}) collective-permute-start(bf16[144,1024]{1,0:T(8,128)(2,1)S(1)} %pack.1.refs_1_.refs_0_.refs_10_), channel_id=1, source_target_pairs={{0,8},{2,10},{4,12},{6,14},{8,0},{10,2},{12,4},{14,6},{16,24},{18,... | collective-permute-start | bytes 884744 | tf_op jit(solution)/shard_map/ppermute | solution.py:1002
  11.8 17.9 %collective-permute-done.4.refs_0_.refs_2_ = bf16[144,1024]{1,0:T(8,128)(2,1)S(1)} collective-permute-done((bf16[144,1024]{1,0:T(8,128)(2,1)S(1)}, bf16[144,1024]{1,0:T(8,128)(2,1)S(1)}, u32[]{:S(2)}, u32[]{:S(2)}) %collective-permute-start.4) | collective-permute-done | bytes 294944 | tf_op jit(solution)/shard_map/ppermute | solution.py:1002
  29.7 0.6 collective-permute-start.6
  30.2 1.5 collective-permute-start
  31.7 3.5 %collective-permute-done.1.refs_2_ = bf16[128,1024]{1,0:T(8,128)(2,1)S(1)} collective-permute-done((bf16[128,1024]{1,0:T(8,128)(2,1)S(1)}, bf16[128,1024]{1,0:T(8,128)(2,1)S(1)}, u32[]{:S(2)}, u32[]{:S(2)}) %collective-permute-start.1) | collective-permute-done | bytes 262176 | tf_op jit(solution)/shard_map/ppermute | solution.py:1002
  35.2 0.7 collective-permute-start.2
  35.9 1.4 assemble.1
  37.3 4.2 %collective-permute-done.6.refs_3_ = bf16[144,1024]{1,0:T(8,128)(2,1)S(1)} collective-permute-done((bf16[144,1024]{1,0:T(8,128)(2,1)S(1)}, bf16[144,1024]{1,0:T(8,128)(2,1)S(1)}, u32[]{:S(2)}, u32[]{:S(2)}) %collective-permute-start.6) | collective-permute-done | bytes 294944 | tf_op jit(solution)/shard_map/ppermute | solution.py:1002
  41.5 2.2 %project.1 = (bf16[784,128]{1,0:T(8,128)(2,1)S(1)}, bf16[784,128]{1,0:T(8,128)(2,1)S(1)}, bf16[784,128]{1,0:T(8,128)(2,1)S(1)}, bf16[784,128]{1,0:T(8,128)(2,1)S...) custom-call(bf16[144,1024]{1,0:T(8,128)(2,1)S(1)} %pack.1.refs_1_.refs_0_.refs_10_, ...), custom_call_target="tpu_custom_call" | custom-call | flops 9200000000 | tf_op jit(solution)/shard_map/project/pallas_call | solution.py:413
  43.7 1.6 collective-permute-start.10
  45.3 1.5 collective-permute-start.11
  46.8 0.4 collective-permute-start.12
  47.3 2.7 %feed.1 = (f32[512,1024]{1,0:T(8,128)S(1)}, bf16[1024,512]{1,0:T(8,128)(2,1)S(1)}, f32[256,1024]{1,0:T(8,128)S(1)}, bf16[256,1024]{1,0:T(8,128)(2,1)S(1)}) custom-call(bf16[512,1024]{1,0:T(8,128)(2,1)S(1)} %get-tuple-element.91.refs_0_, bf16[1024,1024]{1,0:T(8,128)(2,1)S(1)} %get-tuple-element.92.refs_1_.refs_2_, ...), custom_call_target="tpu_custom_call" | custom-call | tf_op jit(solution)/shard_map/feed/pallas_call | solution.py:413
  50.1 2.6 %collective-permute-done.2.refs_3_ = bf16[128,1024]{1,0:T(8,128)(2,1)S(1)} collective-permute-done((bf16[128,1024]{1,0:T(8,128)(2,1)S(1)}, bf16[128,1024]{1,0:T(8,128)(2,1)S(1)}, u32[]{:S(2)}, u32[]{:S(2)}) %collective-permute-start.2) | collective-permute-done | bytes 262176 | tf_op jit(solution)/shard_map/ppermute | solution.py:1002
  52.7 0.6 back_rows.1
  53.4 1.6 %collective-permute-start.7 = (bf16[256,128]{1,0:T(8,128)(2,1)S(1)}, bf16[256,128]{1,0:T(8,128)(2,1)S(1)}, u32[]{:S(2)}, u32[]{:S(2)}) collective-permute-start(bf16[256,128]{1,0:T(8,128)(2,1)S(1)} %get-tuple-element.97), channel_id=1, source_target_pairs={{0,2},{2,0},{4,6},{6,4},{8,10},{10,8},{12,14},{14,12},{16,18},{18,... | collective-permute-start | bytes 196616 | tf_op jit(solution)/shard_map/ppermute | solution.py:1005
  55.0 1.5 collective-permute-start.8
  56.5 1.1 collective-permute-start.9
  57.6 3.2 %feed_grad.1 = (bf16[512,1024]{1,0:T(8,128)(2,1)S(1)}, f32[8,1024]{1,0:T(8,128)S(1)}, f32[512,1024]{1,0:T(8,128)S(1)}, f32[256,1024]{1,0:T(8,128)S(1)}, bf16[256,1024]{1,0:T(8,128)(2,1)S(1)}) custom-call(bf16[512,1024]{1,0:T(8,128)(2,1)S(1)} %get-tuple-element.103.refs_0_.refs_6_.refs_11_, f32[512,1024]{1,0:T(8,128)S(1)} %get-tuple-element.95.refs_5_.refs_1_, ...), custom_call_target="tpu_custom_call" | custom-call | flops 4600000000 | tf_op jit(solution)/shard_map/feed_grad/pallas_call | solution.py:413
  60.9 6.3 %attend.1 = (bf16[2048,128]{1,0:T(8,128)(2,1)S(1)}, bf16[2048,128]{1,0:T(8,128)(2,1)S(1)}, bf16[2048,64]{1,0:T(8,128)(2,1)S(1)}, f32[2048,64]{1,0:T(8,128)S(1)},...) custom-call(bf16[784,128]{1,0:T(8,128)(2,1)S(1)} %get-tuple-element.94.refs_4_.refs_0_, ...), custom_call_target="tpu_custom_call" | custom-call | tf_op jit(solution)/shard_map/attend/pallas_call | solution.py:413
  67.2 3.5 %feed_terms.1 = (bf16[1088,1024]{1,0:T(8,128)(2,1)S(1)}, f32[1088,1024]{1,0:T(8,128)S(1)}) custom-call(bf16[512,1024]{1,0:T(8,128)(2,1)S(1)} %get-tuple-element.103.refs_0_.refs_6_.refs_11_, bf16[1024,512]{1,0:T(8,128)(2,1)S(1)} %get-tuple-element.111.refs_1_, bf16[1024,512]{1,0:T(8,128)(2,1)S(1)} %get-tuple-element.112.refs_2_.refs_3_, ...), custom_call_target="tpu_custom_call" | custom-call | flops 575000000 | tf_op jit(solution)/shard_map/feed_terms/pallas_call | solution.py:413
  70.9 8.5 %attend_back.1 = (bf16[1024,128]{1,0:T(8,128)(2,1)S(1)}, bf16[1024,128]{1,0:T(8,128)(2,1)S(1)}, bf16[1024,128]{1,0:T(8,128)(2,1)S(1)}, bf16[1024,128]{1,0:T(8,128)(2,1)S(1)}, f32[8,128]{1,0:T(8,128)S(1)}) custom-call(bf16[256,128]{1,0:T(8,128)(2,1)S(1)} %get-tuple-element.96.refs_4_.refs_0_, bf16[256,128]{1,0:T(8,128)(2,1)S(1)} %collective-permute-done.7.refs_1_, ...), custom_call_target="tpu_custom_call" | custom-call | tf_op jit(solution)/shard_map/attend_back/pallas_call | solution.py:413
  79.4 1.6 collective-permute-start.13
  80.9 0.9 collective-permute-start.14
  81.8 1.1 collective-permute-start.15
  83.0 4.1 %collective-permute-start.21 = (bf16[128,1024]{1,0:T(8,128)(2,1)S(1)}, bf16[128,1024]{1,0:T(8,128)(2,1)S(1)}, u32[]{:S(2)}, u32[]{:S(2)}) collective-permute-start(bf16[128,1024]{1,0:T(8,128)(2,1)S(1)} %get-tuple-element.128), channel_id=1, source_target_pairs={{0,16},{2,18},{4,20},{6,22},{8,24},{10,26},{12,28},{14,30},{16,0},... | collective-permute-start | bytes 786440 | tf_op jit(solution)/shard_map/ppermute | solution.py:1002
  87.1 0.4 share_twin.2
  87.5 1.1 collective-permute-done.13.refs_1_
  88.5 1.5 collective-permute-start.28
  90.0 4.9 %collective-permute-done.14.refs_2_ = bf16[1024,128]{1,0:T(8,128)(2,1)S(1)} collective-permute-done((bf16[1024,128]{1,0:T(8,128)(2,1)S(1)}, bf16[1024,128]{1,0:T(8,128)(2,1)S(1)}, u32[]{:S(2)}, u32[]{:S(2)}) %collective-permute-start.14) | collective-permute-done | bytes 262176 | tf_op jit(solution)/shard_map/ppermute | solution.py:1005
  94.9 0.9 collective-permute-start.29
  95.8 0.8 collective-permute-start.30
  96.6 1.1 unpack.1
  97.7 3.0 %grads.1 = (bf16[704,768]{1,0:T(8,128)(2,1)S(1)}, f32[704,768]{1,0:T(8,128)S(1)}) custom-call(bf16[512,1024]{1,0:T(8,128)(2,1)S(1)} %get-tuple-element.124.refs_0_.refs_8_, f32[512,1024]{1,0:T(8,128)S(1)} %get-tuple-element.131.refs_1_, f32[512,1024]{1,0:T(8,128)S(1)} %get-tuple-element.132.refs_2_, ...), custom_call_target="tpu_custom_call" | custom-call | tf_op jit(solution)/shard_map/grads/pallas_call | solution.py:413
  101.0 2.1 %collective-permute-start.18 = (bf16[128,1024]{1,0:T(8,128)(2,1)S(1)}, bf16[128,1024]{1,0:T(8,128)(2,1)S(1)}, u32[]{:S(2)}, u32[]{:S(2)}) collective-permute-start(bf16[128,1024]{1,0:T(8,128)(2,1)S(1)} %get-tuple-element.125), channel_id=1, source_target_pairs={{0,8},{2,10},{4,12},{6,14},{8,0},{10,2},{12,4},{14,6},{16,24},{18,... | collective-permute-start | bytes 786440 | tf_op jit(solution)/shard_map/ppermute | solution.py:1002
  103.0 0.5 collective-permute-done.24.refs_1_
  103.5 4.0 %collective-permute-start.19 = (bf16[128,1024]{1,0:T(8,128)(2,1)S(1)}, bf16[128,1024]{1,0:T(8,128)(2,1)S(1)}, u32[]{:S(2)}, u32[]{:S(2)}) collective-permute-start(bf16[128,1024]{1,0:T(8,128)(2,1)S(1)} %get-tuple-element.126), channel_id=1, source_target_pairs={{0,16},{2,18},{4,20},{6,22},{8,24},{10,26},{12,28},{14,30},{16,0},... | collective-permute-start | bytes 786440 | tf_op jit(solution)/shard_map/ppermute | solution.py:1002
  107.8 6.9 %collective-permute-done.18.refs_1_ = bf16[128,1024]{1,0:T(8,128)(2,1)S(1)} collective-permute-done((bf16[128,1024]{1,0:T(8,128)(2,1)S(1)}, bf16[128,1024]{1,0:T(8,128)(2,1)S(1)}, u32[]{:S(2)}, u32[]{:S(2)}) %collective-permute-start.18) | collective-permute-done | bytes 262176 | tf_op jit(solution)/shard_map/ppermute | solution.py:1002
  114.7 1.7 %collective-permute-start.20 = (bf16[128,1024]{1,0:T(8,128)(2,1)S(1)}, bf16[128,1024]{1,0:T(8,128)(2,1)S(1)}, u32[]{:S(2)}, u32[]{:S(2)}) collective-permute-start(bf16[128,1024]{1,0:T(8,128)(2,1)S(1)} %get-tuple-element.127), channel_id=1, source_target_pairs={{0,24},{2,26},{4,28},{6,30},{8,16},{10,18},{12,20},{14,22},{16,8},... | collective-permute-start | bytes 786440 | tf_op jit(solution)/shard_map/ppermute | solution.py:1002
  116.4 9.5 %collective-permute-done.19.refs_2_ = bf16[128,1024]{1,0:T(8,128)(2,1)S(1)} collective-permute-done((bf16[128,1024]{1,0:T(8,128)(2,1)S(1)}, bf16[128,1024]{1,0:T(8,128)(2,1)S(1)}, u32[]{:S(2)}, u32[]{:S(2)}) %collective-permute-start.19) | collective-permute-done | bytes 262176 | tf_op jit(solution)/shard_map/ppermute | solution.py:1002
  125.9 1.9 %collective-permute-start.25 = (bf16[176,768]{1,0:T(8,128)(2,1)S(1)}, bf16[176,768]{1,0:T(8,128)(2,1)S(1)}, u32[]{:S(2)}, u32[]{:S(2)}) collective-permute-start(bf16[176,768]{1,0:T(8,128)(2,1)S(1)} %get-tuple-element.140), channel_id=1, source_target_pairs={{0,2},{2,0},{4,6},{6,4},{8,10},{10,8},{12,14},{14,12},{16,18},{18,... | collective-permute-start | bytes 811016 | tf_op jit(solution)/shard_map/ppermute | solution.py:1005
  127.8 0.9 collective-permute-start.26
  128.6 0.8 collective-permute-start.27
  129.4 1.1 feed_sum.1
  130.5 4.9 %collective-permute-done.25.refs_1_ = bf16[176,768]{1,0:T(8,128)(2,1)S(1)} collective-permute-done((bf16[176,768]{1,0:T(8,128)(2,1)S(1)}, bf16[176,768]{1,0:T(8,128)(2,1)S(1)}, u32[]{:S(2)}, u32[]{:S(2)}) %collective-permute-start.25) | collective-permute-done | bytes 270368 | tf_op jit(solution)/shard_map/ppermute | solution.py:1005
  135.3 3.0 %collective-permute-start.34 = (bf16[32,1024]{1,0:T(8,128)(2,1)S(1)}, bf16[32,1024]{1,0:T(8,128)(2,1)S(1)}, u32[]{:S(2)}, u32[]{:S(2)}) collective-permute-start(bf16[32,1024]{1,0:T(8,128)(2,1)S(1)} %get-tuple-element.155), channel_id=1, source_target_pairs={{0,8},{2,10},{4,12},{6,14},{8,0},{10,2},{12,4},{14,6},{16,24},{18,... | collective-permute-start | bytes 196616 | tf_op jit(solution)/shard_map/ppermute | solution.py:1002
  138.3 2.5 %collective-permute-done.26.refs_2_ = bf16[176,768]{1,0:T(8,128)(2,1)S(1)} collective-permute-done((bf16[176,768]{1,0:T(8,128)(2,1)S(1)}, bf16[176,768]{1,0:T(8,128)(2,1)S(1)}, u32[]{:S(2)}, u32[]{:S(2)}) %collective-permute-start.26) | collective-permute-done | bytes 270368 | tf_op jit(solution)/shard_map/ppermute | solution.py:1005
  140.8 2.6 %collective-permute-start.35 = (bf16[32,1024]{1,0:T(8,128)(2,1)S(1)}, bf16[32,1024]{1,0:T(8,128)(2,1)S(1)}, u32[]{:S(2)}, u32[]{:S(2)}) collective-permute-start(bf16[32,1024]{1,0:T(8,128)(2,1)S(1)} %get-tuple-element.156), channel_id=1, source_target_pairs={{0,16},{2,18},{4,20},{6,22},{8,24},{10,26},{12,28},{14,30},{16,0},... | collective-permute-start | bytes 196616 | tf_op jit(solution)/shard_map/ppermute | solution.py:1002
  143.5 1.8 %collective-permute-start.36 = (bf16[32,1024]{1,0:T(8,128)(2,1)S(1)}, bf16[32,1024]{1,0:T(8,128)(2,1)S(1)}, u32[]{:S(2)}, u32[]{:S(2)}) collective-permute-start(bf16[32,1024]{1,0:T(8,128)(2,1)S(1)} %get-tuple-element.157), channel_id=1, source_target_pairs={{0,24},{2,26},{4,28},{6,30},{8,16},{10,18},{12,20},{14,22},{16,8},... | collective-permute-start | bytes 196616 | tf_op jit(solution)/shard_map/ppermute | solution.py:1002
  145.2 1.0 copy-done.2
  146.3 0.7 grad_sum.1
  147.0 2.6 %collective-permute-start.32 = (bf16[48,768]{1,0:T(8,128)(2,1)S(1)}, bf16[48,768]{1,0:T(8,128)(2,1)S(1)}, u32[]{:S(2)}, u32[]{:S(2)}) collective-permute-start(bf16[48,768]{1,0:T(8,128)(2,1)S(1)} %get-tuple-element.152), channel_id=1, source_target_pairs={{0,16},{2,18},{4,20},{6,22},{8,24},{10,26},{12,28},{14,30},{16,0},... | collective-permute-start | bytes 221192 | tf_op jit(solution)/shard_map/ppermute | solution.py:1002
  149.6 1.8 %collective-permute-start.33 = (bf16[48,768]{1,0:T(8,128)(2,1)S(1)}, bf16[48,768]{1,0:T(8,128)(2,1)S(1)}, u32[]{:S(2)}, u32[]{:S(2)}) collective-permute-start(bf16[48,768]{1,0:T(8,128)(2,1)S(1)} %get-tuple-element.153), channel_id=1, source_target_pairs={{0,24},{2,26},{4,28},{6,30},{8,16},{10,18},{12,20},{14,22},{16,8},... | collective-permute-start | bytes 221192 | tf_op jit(solution)/shard_map/ppermute | solution.py:1002
  151.4 0.9 copy-done.6
  152.3 3.5 %tokens.1 = (bf16[128,1024]{1,0:T(8,128)(2,1)}, bf16[128,1024]{1,0:T(8,128)(2,1)}) custom-call(bf16[512,1024]{1,0:T(8,128)(2,1)S(1)} %get-tuple-element.124.refs_0_.refs_8_, bf16[128,1024]{1,0:T(8,128)(2,1)S(1)} %collective-permute-done.18.refs_1_, bf16[128,1024]{1,0:T(8,128)(2,1)S(1)} %collective-permute-done.19.refs_2_, ...), custom_call_target="tpu_custom_call" | custom-call | tf_op jit(solution)/shard_map/tokens/pallas_call | solution.py:413
  155.8 0.9 copy-done.9
  156.8 0.8 join_in.1.refs_4_
  157.6 1.0 copy-done.3
  158.7 0.8 join_qkv.1
  159.5 0.5 copy.28
  (55 shorter events, 1.0 us)
Async XLA Ops:
  0.6 4.5 %copy-start.7 = (s32[1,2]{1,0:T(1,128)S(1)}, s32[1,2]{1,0:T(1,128)}, u32[]{:S(2)}) copy-start(s32[1,2]{1,0:T(1,128)} %param.16) | copy-start | bytes 28
  4.6 31.2 %collective-permute-start.3 = (bf16[3600,1024]{1,0:T(8,128)(2,1)S(1)}, bf16[3600,1024]{1,0:T(8,128)(2,1)S(1)}, u32[]{:S(2)}, u32[]{:S(2)}) collective-permute-start(bf16[3600,1024]{1,0:T(8,128)(2,1)S(1)} %prepare.1.refs_2_.refs_0_), channel_id=1, source_target_pairs={{0,1},{1,0},{2,3},{3,2},{4,5},{5,4},{6,7},{7,6},{8,9},{9,8},{10,11... | collective-permute-start | bytes 22118408 | tf_op jit(solution)/shard_map/ppermute | solution.py:1008
  5.2 4.7 %copy-start.8 = (bf16[1,128,1024]{2,1,0:T(8,128)(2,1)S(1)}, bf16[1,128,1024]{2,1,0:T(8,128)(2,1)}, u32[]{:S(2)}) copy-start(bf16[1,128,1024]{2,1,0:T(8,128)(2,1)} %param.27) | copy-start | bytes 786436
  6.2 23.5 %collective-permute-start.4 = (bf16[144,1024]{1,0:T(8,128)(2,1)S(1)}, bf16[144,1024]{1,0:T(8,128)(2,1)S(1)}, u32[]{:S(2)}, u32[]{:S(2)}) collective-permute-start(bf16[144,1024]{1,0:T(8,128)(2,1)S(1)} %pack.1.refs_1_.refs_0_.refs_10_), channel_id=1, source_target_pairs={{0,16},{2,18},{4,20},{6,22},{8,24},{10,26},{12,28},{14,30},{16,0},... | collective-permute-start | bytes 884744 | tf_op jit(solution)/shard_map/ppermute | solution.py:1002
  9.9 25.3 %collective-permute-start.1 = (bf16[128,1024]{1,0:T(8,128)(2,1)S(1)}, bf16[128,1024]{1,0:T(8,128)(2,1)S(1)}, u32[]{:S(2)}, u32[]{:S(2)}) collective-permute-start(bf16[128,1024]{1,0:T(8,128)(2,1)S(1)} %bitcast.10), channel_id=1, source_target_pairs={{0,16},{2,18},{4,20},{6,22},{8,24},{10,26},{12,28},{14,30},{16,0},... | collective-permute-start | bytes 786440 | tf_op jit(solution)/shard_map/ppermute | solution.py:1002
  10.0 27.3 %collective-permute-start.5 = (bf16[144,1024]{1,0:T(8,128)(2,1)S(1)}, bf16[144,1024]{1,0:T(8,128)(2,1)S(1)}, u32[]{:S(2)}, u32[]{:S(2)}) collective-permute-start(bf16[144,1024]{1,0:T(8,128)(2,1)S(1)} %pack.1.refs_1_.refs_0_.refs_10_), channel_id=1, source_target_pairs={{0,8},{2,10},{4,12},{6,14},{8,0},{10,2},{12,4},{14,6},{16,24},{18,... | collective-permute-start | bytes 884744 | tf_op jit(solution)/shard_map/ppermute | solution.py:1002
  29.7 11.8 %collective-permute-start.6 = (bf16[144,1024]{1,0:T(8,128)(2,1)S(1)}, bf16[144,1024]{1,0:T(8,128)(2,1)S(1)}, u32[]{:S(2)}, u32[]{:S(2)}) collective-permute-start(bf16[144,1024]{1,0:T(8,128)(2,1)S(1)} %collective-permute-done.4.refs_0_.refs_2_), channel_id=1, source_target_pairs={{0,8},{2,10},{4,12},{6,14},{8,0},{10,2},{12,4},{14,6},{16,24},{18,... | collective-permute-start | bytes 884744 | tf_op jit(solution)/shard_map/ppermute | solution.py:1002
  30.2 19.8 %collective-permute-start = (bf16[128,1024]{1,0:T(8,128)(2,1)S(1)}, bf16[128,1024]{1,0:T(8,128)(2,1)S(1)}, u32[]{:S(2)}, u32[]{:S(2)}) collective-permute-start(bf16[128,1024]{1,0:T(8,128)(2,1)S(1)} %bitcast.11), channel_id=1, source_target_pairs={{0,8},{2,10},{4,12},{6,14},{8,0},{10,2},{12,4},{14,6},{16,24},{18,... | collective-permute-start | bytes 786440 | tf_op jit(solution)/shard_map/ppermute | solution.py:1002
  35.2 17.5 %collective-permute-start.2 = (bf16[128,1024]{1,0:T(8,128)(2,1)S(1)}, bf16[128,1024]{1,0:T(8,128)(2,1)S(1)}, u32[]{:S(2)}, u32[]{:S(2)}) collective-permute-start(bf16[128,1024]{1,0:T(8,128)(2,1)S(1)} %collective-permute-done.1.refs_2_), channel_id=1, source_target_pairs={{0,8},{2,10},{4,12},{6,14},{8,0},{10,2},{12,4},{14,6},{16,24},{18,... | collective-permute-start | bytes 786440 | tf_op jit(solution)/shard_map/ppermute | solution.py:1002
  37.3 10.0 %copy-start.4 = (f32[32,512]{1,0:T(8,128)}, f32[32,512]{1,0:T(8,128)S(1)}, u32[]{:S(2)}) copy-start(f32[32,512]{1,0:T(8,128)S(1)} %get-tuple-element.89.refs_4_.refs_2_.refs_12_) | copy-start | bytes 196612
  43.7 11.3 %collective-permute-start.10 = (bf16[784,128]{1,0:T(8,128)(2,1)S(1)}, bf16[784,128]{1,0:T(8,128)(2,1)S(1)}, u32[]{:S(2)}, u32[]{:S(2)}) collective-permute-start(bf16[784,128]{1,0:T(8,128)(2,1)S(1)} %get-tuple-element.100), channel_id=1, source_target_pairs={{0,2},{2,0},{4,6},{6,4},{8,10},{10,8},{12,14},{14,12},{16,18},{18,... | collective-permute-start | bytes 602120 | tf_op jit(solution)/shard_map/ppermute | solution.py:1005
  45.3 11.2 %collective-permute-start.11 = (bf16[784,128]{1,0:T(8,128)(2,1)S(1)}, bf16[784,128]{1,0:T(8,128)(2,1)S(1)}, u32[]{:S(2)}, u32[]{:S(2)}) collective-permute-start(bf16[784,128]{1,0:T(8,128)(2,1)S(1)} %get-tuple-element.101), channel_id=1, source_target_pairs={{0,4},{2,6},{4,0},{6,2},{8,12},{10,14},{12,8},{14,10},{16,20},{18,... | collective-permute-start | bytes 602120 | tf_op jit(solution)/shard_map/ppermute | solution.py:1005
  46.8 14.0 %collective-permute-start.12 = (bf16[784,128]{1,0:T(8,128)(2,1)S(1)}, bf16[784,128]{1,0:T(8,128)(2,1)S(1)}, u32[]{:S(2)}, u32[]{:S(2)}) collective-permute-start(bf16[784,128]{1,0:T(8,128)(2,1)S(1)} %get-tuple-element.102), channel_id=1, source_target_pairs={{0,6},{2,4},{4,2},{6,0},{8,14},{10,12},{12,10},{14,8},{16,22},{18,... | collective-permute-start | bytes 602120 | tf_op jit(solution)/shard_map/ppermute | solution.py:1005
  50.0 31.8 %collective-permute-start.17 = (bf16[256,1024]{1,0:T(8,128)(2,1)S(1)}, bf16[256,1024]{1,0:T(8,128)(2,1)S(1)}, u32[]{:S(2)}, u32[]{:S(2)}) collective-permute-start(bf16[256,1024]{1,0:T(8,128)(2,1)S(1)} %get-tuple-element.121), channel_id=1, source_target_pairs={{0,8},{2,10},{4,12},{6,14},{8,0},{10,2},{12,4},{14,6},{16,24},{18,... | collective-permute-start | bytes 1572872 | tf_op jit(solution)/shard_map/ppermute | solution.py:1002
  53.4 17.4 %collective-permute-start.7 = (bf16[256,128]{1,0:T(8,128)(2,1)S(1)}, bf16[256,128]{1,0:T(8,128)(2,1)S(1)}, u32[]{:S(2)}, u32[]{:S(2)}) collective-permute-start(bf16[256,128]{1,0:T(8,128)(2,1)S(1)} %get-tuple-element.97), channel_id=1, source_target_pairs={{0,2},{2,0},{4,6},{6,4},{8,10},{10,8},{12,14},{14,12},{16,18},{18,... | collective-permute-start | bytes 196616 | tf_op jit(solution)/shard_map/ppermute | solution.py:1005
  55.0 15.9 %collective-permute-start.8 = (bf16[256,128]{1,0:T(8,128)(2,1)S(1)}, bf16[256,128]{1,0:T(8,128)(2,1)S(1)}, u32[]{:S(2)}, u32[]{:S(2)}) collective-permute-start(bf16[256,128]{1,0:T(8,128)(2,1)S(1)} %get-tuple-element.98), channel_id=1, source_target_pairs={{0,4},{2,6},{4,0},{6,2},{8,12},{10,14},{12,8},{14,10},{16,20},{18,... | collective-permute-start | bytes 196616 | tf_op jit(solution)/shard_map/ppermute | solution.py:1005
  56.5 14.4 %collective-permute-start.9 = (bf16[256,128]{1,0:T(8,128)(2,1)S(1)}, bf16[256,128]{1,0:T(8,128)(2,1)S(1)}, u32[]{:S(2)}, u32[]{:S(2)}) collective-permute-start(bf16[256,128]{1,0:T(8,128)(2,1)S(1)} %get-tuple-element.99), channel_id=1, source_target_pairs={{0,6},{2,4},{4,2},{6,0},{8,14},{10,12},{12,10},{14,8},{16,22},{18,... | collective-permute-start | bytes 196616 | tf_op jit(solution)/shard_map/ppermute | solution.py:1005
  57.6 3.3 %copy-start = (f32[2048,128]{1,0:T(8,128)S(1)}, f32[2048,128]{1,0:T(8,128)}, u32[]{:S(2)}) copy-start(f32[2048,128]{1,0:T(8,128)} %constant.5.clone.refs_5_.refs_11_) | copy-start | bytes 3145732
  57.6 3.3 %copy-start.1 = (f32[2048,128]{1,0:T(8,128)S(1)}, f32[2048,128]{1,0:T(8,128)}, u32[]{:S(2)}) copy-start(f32[2048,128]{1,0:T(8,128)} %constant.4.clone.refs_4_.refs_10_) | copy-start | bytes 3145732
  60.8 39.9 %collective-permute-start.22 = (bf16[256,1024]{1,0:T(8,128)(2,1)S(1)}, bf16[256,1024]{1,0:T(8,128)(2,1)S(1)}, u32[]{:S(2)}, u32[]{:S(2)}) collective-permute-start(bf16[256,1024]{1,0:T(8,128)(2,1)S(1)} %get-tuple-element.130), channel_id=1, source_target_pairs={{0,8},{2,10},{4,12},{6,14},{8,0},{10,2},{12,4},{14,6},{16,24},{18,... | collective-permute-start | bytes 1572872 | tf_op jit(solution)/shard_map/ppermute | solution.py:1002
  70.8 12.2 %collective-permute-start.16 = (bf16[1088,1024]{1,0:T(8,128)(2,1)S(1)}, bf16[1088,1024]{1,0:T(8,128)(2,1)S(1)}, u32[]{:S(2)}, u32[]{:S(2)}) collective-permute-start(bf16[1088,1024]{1,0:T(8,128)(2,1)S(1)} %get-tuple-element.114.refs_12_), channel_id=1, source_target_pairs={{0,1},{1,0},{2,3},{3,2},{4,5},{5,4},{6,7},{7,6},{8,9},{9,8},{10,11... | collective-permute-start | bytes 6684680 | tf_op jit(solution)/shard_map/ppermute | solution.py:1008
  79.4 9.2 %collective-permute-start.13 = (bf16[1024,128]{1,0:T(8,128)(2,1)S(1)}, bf16[1024,128]{1,0:T(8,128)(2,1)S(1)}, u32[]{:S(2)}, u32[]{:S(2)}) collective-permute-start(bf16[1024,128]{1,0:T(8,128)(2,1)S(1)} %get-tuple-element.116), channel_id=1, source_target_pairs={{0,2},{2,0},{4,6},{6,4},{8,10},{10,8},{12,14},{14,12},{16,18},{18,... | collective-permute-start | bytes 786440 | tf_op jit(solution)/shard_map/ppermute | solution.py:1005
  80.9 14.0 %collective-permute-start.14 = (bf16[1024,128]{1,0:T(8,128)(2,1)S(1)}, bf16[1024,128]{1,0:T(8,128)(2,1)S(1)}, u32[]{:S(2)}, u32[]{:S(2)}) collective-permute-start(bf16[1024,128]{1,0:T(8,128)(2,1)S(1)} %get-tuple-element.117), channel_id=1, source_target_pairs={{0,4},{2,6},{4,0},{6,2},{8,12},{10,14},{12,8},{14,10},{16,20},{18,... | collective-permute-start | bytes 786440 | tf_op jit(solution)/shard_map/ppermute | solution.py:1005
  81.8 14.0 %collective-permute-start.15 = (bf16[1024,128]{1,0:T(8,128)(2,1)S(1)}, bf16[1024,128]{1,0:T(8,128)(2,1)S(1)}, u32[]{:S(2)}, u32[]{:S(2)}) collective-permute-start(bf16[1024,128]{1,0:T(8,128)(2,1)S(1)} %get-tuple-element.118), channel_id=1, source_target_pairs={{0,6},{2,4},{4,2},{6,0},{8,14},{10,12},{12,10},{14,8},{16,22},{18,... | collective-permute-start | bytes 786440 | tf_op jit(solution)/shard_map/ppermute | solution.py:1005
  83.0 18.0 %collective-permute-start.21 = (bf16[128,1024]{1,0:T(8,128)(2,1)S(1)}, bf16[128,1024]{1,0:T(8,128)(2,1)S(1)}, u32[]{:S(2)}, u32[]{:S(2)}) collective-permute-start(bf16[128,1024]{1,0:T(8,128)(2,1)S(1)} %get-tuple-element.128), channel_id=1, source_target_pairs={{0,16},{2,18},{4,20},{6,22},{8,24},{10,26},{12,28},{14,30},{16,0},... | collective-permute-start | bytes 786440 | tf_op jit(solution)/shard_map/ppermute | solution.py:1002
  88.5 37.4 %collective-permute-start.28 = (bf16[272,1024]{1,0:T(8,128)(2,1)S(1)}, bf16[272,1024]{1,0:T(8,128)(2,1)S(1)}, u32[]{:S(2)}, u32[]{:S(2)}) collective-permute-start(bf16[272,1024]{1,0:T(8,128)(2,1)S(1)} %get-tuple-element.143), channel_id=1, source_target_pairs={{0,2},{2,0},{4,6},{6,4},{8,10},{10,8},{12,14},{14,12},{16,18},{18,... | collective-permute-start | bytes 1671176 | tf_op jit(solution)/shard_map/ppermute | solution.py:1005
  94.9 32.8 %collective-permute-start.29 = (bf16[272,1024]{1,0:T(8,128)(2,1)S(1)}, bf16[272,1024]{1,0:T(8,128)(2,1)S(1)}, u32[]{:S(2)}, u32[]{:S(2)}) collective-permute-start(bf16[272,1024]{1,0:T(8,128)(2,1)S(1)} %get-tuple-element.144), channel_id=1, source_target_pairs={{0,4},{2,6},{4,0},{6,2},{8,12},{10,14},{12,8},{14,10},{16,20},{18,... | collective-permute-start | bytes 1671176 | tf_op jit(solution)/shard_map/ppermute | solution.py:1005
  95.8 32.9 %collective-permute-start.30 = (bf16[272,1024]{1,0:T(8,128)(2,1)S(1)}, bf16[272,1024]{1,0:T(8,128)(2,1)S(1)}, u32[]{:S(2)}, u32[]{:S(2)}) collective-permute-start(bf16[272,1024]{1,0:T(8,128)(2,1)S(1)} %get-tuple-element.145), channel_id=1, source_target_pairs={{0,6},{2,4},{4,2},{6,0},{8,14},{10,12},{12,10},{14,8},{16,22},{18,... | collective-permute-start | bytes 1671176 | tf_op jit(solution)/shard_map/ppermute | solution.py:1005
  100.8 2.8 %collective-permute-start.24 = (bf16[704,768]{1,0:T(8,128)(2,1)S(1)}, bf16[704,768]{1,0:T(8,128)(2,1)S(1)}, u32[]{:S(2)}, u32[]{:S(2)}) collective-permute-start(bf16[704,768]{1,0:T(8,128)(2,1)S(1)} %get-tuple-element.135.refs_2_), channel_id=1, source_target_pairs={{0,1},{1,0},{2,3},{3,2},{4,5},{5,4},{6,7},{7,6},{8,9},{9,8},{10,11... | collective-permute-start | bytes 3244040 | tf_op jit(solution)/shard_map/ppermute | solution.py:1008
  101.0 13.7 %collective-permute-start.18 = (bf16[128,1024]{1,0:T(8,128)(2,1)S(1)}, bf16[128,1024]{1,0:T(8,128)(2,1)S(1)}, u32[]{:S(2)}, u32[]{:S(2)}) collective-permute-start(bf16[128,1024]{1,0:T(8,128)(2,1)S(1)} %get-tuple-element.125), channel_id=1, source_target_pairs={{0,8},{2,10},{4,12},{6,14},{8,0},{10,2},{12,4},{14,6},{16,24},{18,... | collective-permute-start | bytes 786440 | tf_op jit(solution)/shard_map/ppermute | solution.py:1002
  103.5 22.4 %collective-permute-start.19 = (bf16[128,1024]{1,0:T(8,128)(2,1)S(1)}, bf16[128,1024]{1,0:T(8,128)(2,1)S(1)}, u32[]{:S(2)}, u32[]{:S(2)}) collective-permute-start(bf16[128,1024]{1,0:T(8,128)(2,1)S(1)} %get-tuple-element.126), channel_id=1, source_target_pairs={{0,16},{2,18},{4,20},{6,22},{8,24},{10,26},{12,28},{14,30},{16,0},... | collective-permute-start | bytes 786440 | tf_op jit(solution)/shard_map/ppermute | solution.py:1002
  114.7 32.3 %collective-permute-start.20 = (bf16[128,1024]{1,0:T(8,128)(2,1)S(1)}, bf16[128,1024]{1,0:T(8,128)(2,1)S(1)}, u32[]{:S(2)}, u32[]{:S(2)}) collective-permute-start(bf16[128,1024]{1,0:T(8,128)(2,1)S(1)} %get-tuple-element.127), channel_id=1, source_target_pairs={{0,24},{2,26},{4,28},{6,30},{8,16},{10,18},{12,20},{14,22},{16,8},... | collective-permute-start | bytes 786440 | tf_op jit(solution)/shard_map/ppermute | solution.py:1002
  125.9 21.1 %collective-permute-start.23 = (bf16[128,1024]{1,0:T(8,128)(2,1)S(1)}, bf16[128,1024]{1,0:T(8,128)(2,1)S(1)}, u32[]{:S(2)}, u32[]{:S(2)}) collective-permute-start(bf16[128,1024]{1,0:T(8,128)(2,1)S(1)} %get-tuple-element.137), channel_id=1, source_target_pairs={{0,16},{2,18},{4,20},{6,22},{8,24},{10,26},{12,28},{14,30},{16,0},... | collective-permute-start | bytes 786440 | tf_op jit(solution)/shard_map/ppermute | solution.py:1002
  125.9 9.4 %collective-permute-start.25 = (bf16[176,768]{1,0:T(8,128)(2,1)S(1)}, bf16[176,768]{1,0:T(8,128)(2,1)S(1)}, u32[]{:S(2)}, u32[]{:S(2)}) collective-permute-start(bf16[176,768]{1,0:T(8,128)(2,1)S(1)} %get-tuple-element.140), channel_id=1, source_target_pairs={{0,2},{2,0},{4,6},{6,4},{8,10},{10,8},{12,14},{14,12},{16,18},{18,... | collective-permute-start | bytes 811016 | tf_op jit(solution)/shard_map/ppermute | solution.py:1005
  127.8 13.0 %collective-permute-start.26 = (bf16[176,768]{1,0:T(8,128)(2,1)S(1)}, bf16[176,768]{1,0:T(8,128)(2,1)S(1)}, u32[]{:S(2)}, u32[]{:S(2)}) collective-permute-start(bf16[176,768]{1,0:T(8,128)(2,1)S(1)} %get-tuple-element.141), channel_id=1, source_target_pairs={{0,4},{2,6},{4,0},{6,2},{8,12},{10,14},{12,8},{14,10},{16,20},{18,... | collective-permute-start | bytes 811016 | tf_op jit(solution)/shard_map/ppermute | solution.py:1005
  128.6 14.8 %collective-permute-start.27 = (bf16[176,768]{1,0:T(8,128)(2,1)S(1)}, bf16[176,768]{1,0:T(8,128)(2,1)S(1)}, u32[]{:S(2)}, u32[]{:S(2)}) collective-permute-start(bf16[176,768]{1,0:T(8,128)(2,1)S(1)} %get-tuple-element.142), channel_id=1, source_target_pairs={{0,6},{2,4},{4,2},{6,0},{8,14},{10,12},{12,10},{14,8},{16,22},{18,... | collective-permute-start | bytes 811016 | tf_op jit(solution)/shard_map/ppermute | solution.py:1005
  129.4 22.0 %copy-start.5 = (f32[32,512]{1,0:T(8,128)S(1)}, f32[32,512]{1,0:T(8,128)}, u32[]{:S(2)}) copy-start(f32[32,512]{1,0:T(8,128)} %copy-done.4) | copy-start | bytes 196612
  135.3 14.3 %collective-permute-start.34 = (bf16[32,1024]{1,0:T(8,128)(2,1)S(1)}, bf16[32,1024]{1,0:T(8,128)(2,1)S(1)}, u32[]{:S(2)}, u32[]{:S(2)}) collective-permute-start(bf16[32,1024]{1,0:T(8,128)(2,1)S(1)} %get-tuple-element.155), channel_id=1, source_target_pairs={{0,8},{2,10},{4,12},{6,14},{8,0},{10,2},{12,4},{14,6},{16,24},{18,... | collective-permute-start | bytes 196616 | tf_op jit(solution)/shard_map/ppermute | solution.py:1002
  140.8 15.0 %collective-permute-start.35 = (bf16[32,1024]{1,0:T(8,128)(2,1)S(1)}, bf16[32,1024]{1,0:T(8,128)(2,1)S(1)}, u32[]{:S(2)}, u32[]{:S(2)}) collective-permute-start(bf16[32,1024]{1,0:T(8,128)(2,1)S(1)} %get-tuple-element.156), channel_id=1, source_target_pairs={{0,16},{2,18},{4,20},{6,22},{8,24},{10,26},{12,28},{14,30},{16,0},... | collective-permute-start | bytes 196616 | tf_op jit(solution)/shard_map/ppermute | solution.py:1002
  143.5 12.4 %collective-permute-start.36 = (bf16[32,1024]{1,0:T(8,128)(2,1)S(1)}, bf16[32,1024]{1,0:T(8,128)(2,1)S(1)}, u32[]{:S(2)}, u32[]{:S(2)}) collective-permute-start(bf16[32,1024]{1,0:T(8,128)(2,1)S(1)} %get-tuple-element.157), channel_id=1, source_target_pairs={{0,24},{2,26},{4,28},{6,30},{8,16},{10,18},{12,20},{14,22},{16,8},... | collective-permute-start | bytes 196616 | tf_op jit(solution)/shard_map/ppermute | solution.py:1002
  145.2 1.0 copy-start.2
  147.0 10.6 %collective-permute-start.31 = (bf16[48,768]{1,0:T(8,128)(2,1)S(1)}, bf16[48,768]{1,0:T(8,128)(2,1)S(1)}, u32[]{:S(2)}, u32[]{:S(2)}) collective-permute-start(bf16[48,768]{1,0:T(8,128)(2,1)S(1)} %get-tuple-element.151), channel_id=1, source_target_pairs={{0,8},{2,10},{4,12},{6,14},{8,0},{10,2},{12,4},{14,6},{16,24},{18,... | collective-permute-start | bytes 221192 | tf_op jit(solution)/shard_map/ppermute | solution.py:1002
  147.0 10.6 %collective-permute-start.32 = (bf16[48,768]{1,0:T(8,128)(2,1)S(1)}, bf16[48,768]{1,0:T(8,128)(2,1)S(1)}, u32[]{:S(2)}, u32[]{:S(2)}) collective-permute-start(bf16[48,768]{1,0:T(8,128)(2,1)S(1)} %get-tuple-element.152), channel_id=1, source_target_pairs={{0,16},{2,18},{4,20},{6,22},{8,24},{10,26},{12,28},{14,30},{16,0},... | collective-permute-start | bytes 221192 | tf_op jit(solution)/shard_map/ppermute | solution.py:1002
  149.6 8.0 %collective-permute-start.33 = (bf16[48,768]{1,0:T(8,128)(2,1)S(1)}, bf16[48,768]{1,0:T(8,128)(2,1)S(1)}, u32[]{:S(2)}, u32[]{:S(2)}) collective-permute-start(bf16[48,768]{1,0:T(8,128)(2,1)S(1)} %get-tuple-element.153), channel_id=1, source_target_pairs={{0,24},{2,26},{4,28},{6,30},{8,16},{10,18},{12,20},{14,22},{16,8},... | collective-permute-start | bytes 221192 | tf_op jit(solution)/shard_map/ppermute | solution.py:1002
  151.4 0.9 copy-start.6
  155.8 3.7 %copy-start.10 = (f32[1,32]{1,0:T(1,128)S(1)}, f32[1,32]{1,0:T(1,128)}, u32[]{:S(2)}) copy-start(f32[1,32]{1,0:T(1,128)} %get-tuple-element.162) | copy-start | bytes 388
  155.8 1.0 copy-start.9
  157.6 1.0 copy-start.3

commit v4 on v3

--- a/solution.py
+++ b/solution.py
@@ -343,7 +343,7 @@
 F32 = jnp.float32
 BF16 = jnp.bfloat16
 VMEM_LIMIT = 16 * 1024 * 1024
-TIMES = {'wait': 5, 'project': 80, 'feed_grad': 40, 'halve': 400, 'unpack': 20, 'feed_sum': 150, 'prepare': 150, 'back_rows': 80, 'feed_terms': 5, 'share_twin': 400, 'join_in': 5}
+TIMES = {'hold': 5000, 'project': 80, 'feed_grad': 40, 'halve': 400, 'unpack': 150, 'feed_sum': 150, 'back_rows': 80, 'feed_terms': 5, 'share_twin': 400, 'join_in': 5}
 
 VEC = 16
 
@@ -940,8 +940,8 @@
     bias[...] = vec_ref[pl.ds(4 + line, 1), :]
 
 
-def wait_kernel(out):
-    out[...] = jnp.zeros_like(out)
+def hold_kernel(x, out):
+    out[...] = x[...]
 
 
 def tokens_kernel(mixed, r1, r2, r3, qkv, w_out, *rest):
@@ -1010,10 +1010,6 @@
     def with_lines(blocks):
         return [blocks[0]] + [near(over_lines(raw(blocks[k]), k)) for k in range(1, LINES)]
 
-    def from_lines(x):
-        far_one = over_lines(raw(x), 2)
-        return [near(over_lines(raw(x), 1)), near(far_one), near(over_lines(far_one, 1))]
-
     def with_places(blocks):
         return [blocks[0]] + [near(over_places(raw(blocks[j]), j)) for j in range(1, ACROSS)]
 
@@ -1041,6 +1037,19 @@
         )
         last[:] = results[:1]
         return results
+    (token_block,) = run(
+        pack_kernel,
+        [near((rows + VEC, width), BF16)],
+        [],
+        block_order.reshape(2), far(tokens[0]),
+    )
+    from_two = over_lines(raw(token_block), 2)
+    token_lines = [
+        token_block,
+        near(over_lines(raw(token_block), 1)),
+        near(from_two),
+        near(over_lines(from_two, 1)),
+    ]
     (packed,) = run(
         prepare_kernel,
         [near((packed_rows, width), BF16)],
@@ -1049,21 +1058,14 @@
         *map(far, (ln_gain, ln_bias, b_out, b_down, qv_bias, b_in)),
         loose_in=4,
     )
-    (token_block,) = run(
-        pack_kernel,
-        [near((rows + VEC, width), BF16)],
+    (cot_own,) = run(
+        hold_kernel,
+        [near((rows, width), BF16)],
         [],
-        block_order.reshape(2), far(tokens[0]),
-    )
-    from_two = over_lines(raw(token_block), 2)
-    token_lines = [
-        token_block,
-        near(over_lines(raw(token_block), 1)),
-        near(from_two),
-        near(over_lines(from_two, 1)),
-    ]
-    cot_lines = [near(cotangent[0]), *from_lines(cotangent[0])]
-    run(wait_kernel, [near((8, 128), F32)], [], after=[near(from_two)])
+        far(cotangent[0]),
+        after=token_lines[1:3],
+    )
+    cot_lines = with_lines([cot_own] * LINES)
     qkv, in_rows, w_out_full, down_rows, vectors = run(
         assemble_kernel,
         [
@@ -1163,13 +1165,13 @@
         low_keep, low_received,
     )
     low_rest = near(over_lines(raw(low_half), 2))
-    feed_blocks = run(
-        share_twin_kernel,
-        [near((block, width), F32)] + [near((block, width), BF16)] * 3,
+    grad_own, grad_half = run(
+        halve_kernel,
+        [near((rows, width), F32), near((rows, width), BF16)],
         [],
-        feed_keep, feed_twin,
-    )
-    feed_in = with_places(feed_blocks)
+        grad_keep, grad_received,
+    )
+    grad_rest = near(over_lines(raw(grad_half), 2))
     mixed, att_turned, *mixed_slots = run(
         unpack_kernel,
         [near((line_rows, width), BF16), near((head_cols, line_rows), BF16)]
@@ -1189,13 +1191,13 @@
         mixed, feed_grad_low, normed, ln_turned, qkv, att_turned, cot_rows, bias_sums,
     )
     qkv_terms = twin(qkv_send)
-    grad_own, grad_half = run(
-        halve_kernel,
-        [near((rows, width), F32), near((rows, width), BF16)],
+    feed_blocks = run(
+        share_twin_kernel,
+        [near((block, width), F32)] + [near((block, width), BF16)] * 3,
         [],
-        grad_keep, grad_received,
-    )
-    grad_rest = near(over_lines(raw(grad_half), 2))
+        feed_keep, feed_twin,
+    )
+    feed_in = with_places(feed_blocks)
     qkv_blocks = run(
         share_twin_kernel,
         [near((qkv_block, qkv_cols), F32)] + [near((qkv_block, qkv_cols), BF16)] * 3,
@@ -1211,6 +1213,13 @@
         *feed_in,
     )
     in_parts = with_lines(in_slots)
+    layer_out, grad_tokens = run(
+        tokens_kernel,
+        [((rows, width), BF16), ((rows, width), BF16)],
+        [],
+        mixed, *mixed_in, qkv, w_out_full, low_own, low_rest, grad_own, grad_rest,
+        token_block, cot_rows, vectors,
+    )
     grad_out, grad_qv, *qkv_parts = run(
         grad_sum_kernel,
         [((32, width), F32), ((2, 32), F32), near((32 + VEC, qkv_cols), F32)]
@@ -1219,13 +1228,6 @@
         *qkv_sums,
     )
     qkv_parts = with_lines(qkv_parts)
-    layer_out, grad_tokens = run(
-        tokens_kernel,
-        [((rows, width), BF16), ((rows, width), BF16)],
-        [],
-        mixed, *mixed_in, qkv, w_out_full, low_own, low_rest, grad_own, grad_rest,
-        token_block, cot_rows, vectors,
-    )
     (grad_in,) = run(join_in_kernel, [((32, feed), F32)], [], *in_parts)
     grad_qkv, grad_gain, grad_shift = run(
         join_qkv_kernel,

time: 160 us -> 153 us (0.956)
  waiting for transfers between devices: 58.5 us -> 46.4 us
  Pallas kernels: 45.4 us -> 54.1 us
  starting transfers between devices: 50.7 us -> 45.9 us
    ppermute x19, waiting for transfers between devices: 44.6 us -> 24.3 us  [over_lines(): return lax.ppermute(x, 'ctx', [(i, i ^ k * ACROSS) for i in positions])]
    pallas_call x22, Pallas kernels: 45.4 us -> 54.1 us  [call(): pl.pallas_call(body, name=name, out_shape=outs, in_specs=specs + [loose]...]
    ppermute x15, waiting for transfers between devices: 13.4 us -> 21 us  [over_places(): return lax.ppermute(x, 'ctx', [(i, i ^ j) for i in positions])]
    ppermute x19, starting transfers between devices: 32.1 us -> 26.2 us  [over_lines(): return lax.ppermute(x, 'ctx', [(i, i ^ k * ACROSS) for i in positions])]
    unnamed x23 -> x27, local copies, waits for them, and re-layouts: 4.47 us -> 5.13 us
  transfers between devices with their start and end apart: 37 -> 37, of which waited for: 11 -> 12; matrix products, arithmetic and copies ran while one was open for 0% -> 0% of each run, Pallas kernels for 25% -> 34%
where the time goes in v4:
time: 153 us; the launch traced here: 152 us
  Pallas kernels  54.1 us (35%)
  waiting for transfers between devices  46.4 us (30%)
  starting transfers between devices  45.9 us (30%)
  local copies, waits for them, and re-layouts  5.13 us (3%)
    pallas_call x22, Pallas kernels, call(): pl.pallas_call(body, name=name, out_shape=outs, in_specs=specs + [loose]...  54.1 us
    ppermute x19, starting transfers between devices, over_lines(): return lax.ppermute(x, 'ctx', [(i, i ^ k * ACROSS) for i in positions])  26.2 us
    ppermute x19, waiting for transfers between devices, over_lines(): return lax.ppermute(x, 'ctx', [(i, i ^ k * ACROSS) for i in positions])  24.3 us
    ppermute x15, waiting for transfers between devices, over_places(): return lax.ppermute(x, 'ctx', [(i, i ^ j) for i in positions])  21 us
    ppermute x15, starting transfers between devices, over_places(): return lax.ppermute(x, 'ctx', [(i, i ^ j) for i in positions])  19.4 us
    unnamed x27, local copies, waits for them, and re-layouts  5.13 us
  transfers between devices with their start and end apart: 37, of which 12 were waited for; matrix products, arithmetic and copies ran while one was open for 0% of the time, Pallas kernels for 34%

profile of v4, /device:TPU:0, one launch (start us, length us, event | category | flops | bytes accessed | tf_op | source)
XLA Modules:
  0.0 152.5 jit_solution(2570371217154263890)
XLA Ops:
  0.7 0.6 copy-done.10
  1.3 1.0 pack.1.refs_10_.refs_0_
  2.3 4.1 %collective-permute-start.1 = (bf16[144,1024]{1,0:T(8,128)(2,1)S(1)}, bf16[144,1024]{1,0:T(8,128)(2,1)}, u32[]{:S(2)}, u32[]{:S(2)}) collective-permute-start(bf16[144,1024]{1,0:T(8,128)(2,1)S(1)} %pack.1.refs_10_.refs_0_), channel_id=1, source_target_pairs={{0,16},{2,18},{4,20},{6,22},{8,24},{10,26},{12,28},{14,30},{16,0},... | collective-permute-start | bytes 884744 | tf_op jit(solution)/shard_map/ppermute | solution.py:1002
  6.4 1.6 %collective-permute-start = (bf16[144,1024]{1,0:T(8,128)(2,1)S(1)}, bf16[144,1024]{1,0:T(8,128)(2,1)S(1)}, u32[]{:S(2)}, u32[]{:S(2)}) collective-permute-start(bf16[144,1024]{1,0:T(8,128)(2,1)S(1)} %pack.1.refs_10_.refs_0_), channel_id=1, source_target_pairs={{0,8},{2,10},{4,12},{6,14},{8,0},{10,2},{12,4},{14,6},{16,24},{18,... | collective-permute-start | bytes 884744 | tf_op jit(solution)/shard_map/ppermute | solution.py:1002
  8.0 6.9 %prepare.1.refs_3_.refs_0_ = bf16[3600,1024]{1,0:T(8,128)(2,1)} custom-call(bf16[512,3072]{1,0:T(8,128)(2,1)} %refs_0_.1, bf16[512,4096]{1,0:T(8,128)(2,1)} %refs_1_.1, bf16[512,1024]{1,0:T(8,128)(2,1)} %refs_2_.1, bf16[2048,1024]{1,0:T(8,128)(2,1)} %refs_3_.1, bf16[512]{0:T(512)(128)(2,1)} %refs_4_.2, bf16[512]{0:T(512)(128)(2,1)} %refs_5_.2, ...), custom_call_target="tpu_custom_call" | custom-call | tf_op jit(solution)/shard_map/prepare/pallas_call | solution.py:413
  15.0 5.0 %collective-permute-done.1.refs_2_ = bf16[144,1024]{1,0:T(8,128)(2,1)} collective-permute-done((bf16[144,1024]{1,0:T(8,128)(2,1)S(1)}, bf16[144,1024]{1,0:T(8,128)(2,1)}, u32[]{:S(2)}, u32[]{:S(2)}) %collective-permute-start.1) | collective-permute-done | bytes 294944 | tf_op jit(solution)/shard_map/ppermute | solution.py:1002
  19.9 0.5 collective-permute-start.6
  20.5 1.0 hold.1.refs_2_.refs_0_
  21.4 3.0 %collective-permute-start.4 = (bf16[128,1024]{1,0:T(8,128)(2,1)S(1)}, bf16[128,1024]{1,0:T(8,128)(2,1)S(1)}, u32[]{:S(2)}, u32[]{:S(2)}) collective-permute-start(bf16[128,1024]{1,0:T(8,128)(2,1)S(1)} %hold.1.refs_2_.refs_0_), channel_id=1, source_target_pairs={{0,24},{2,26},{4,28},{6,30},{8,16},{10,18},{12,20},{14,22},{16,8},... | collective-permute-start | bytes 786440 | tf_op jit(solution)/shard_map/ppermute | solution.py:1002
  24.4 0.6 collective-permute-start.3
  25.1 0.8 collective-permute-start.2
  25.9 1.1 collective-permute-done.5.refs_1_
  27.0 4.8 %assemble.1 = (bf16[1024,3072]{1,0:T(8,128)(2,1)S(1)}, bf16[1024,1024]{1,0:T(8,128)(2,1)S(1)}, bf16[1024,1024]{1,0:T(8,128)(2,1)S(1)}, bf16[1024,1024]{1,0:T(8,128)(2,1)S(1)}, f32[32,512]{1,0:T(8,128)S(1)}) custom-call(bf16[3600,1024]{1,0:T(8,128)(2,1)} %prepare.1.refs_3_.refs_0_, bf16[3600,1024]{1,0:T(8,128)(2,1)} %collective-permute-done.5.refs_1_, ...), custom_call_target="tpu_custom_call" | custom-call | tf_op jit(solution)/shard_map/assemble/pallas_call | solution.py:413
  31.9 3.7 %project.1 = (bf16[784,128]{1,0:T(8,128)(2,1)S(1)}, bf16[784,128]{1,0:T(8,128)(2,1)S(1)}, bf16[784,128]{1,0:T(8,128)(2,1)S(1)}, bf16[784,128]{1,0:T(8,128)(2,1)S...) custom-call(bf16[144,1024]{1,0:T(8,128)(2,1)S(1)} %copy-done.3, ...), custom_call_target="tpu_custom_call" | custom-call | flops 9200000000 | tf_op jit(solution)/shard_map/project/pallas_call | solution.py:413
  35.5 1.5 %collective-permute-start.10 = (bf16[784,128]{1,0:T(8,128)(2,1)S(1)}, bf16[784,128]{1,0:T(8,128)(2,1)S(1)}, u32[]{:S(2)}, u32[]{:S(2)}) collective-permute-start(bf16[784,128]{1,0:T(8,128)(2,1)S(1)} %get-tuple-element.100), channel_id=1, source_target_pairs={{0,2},{2,0},{4,6},{6,4},{8,10},{10,8},{12,14},{14,12},{16,18},{18,... | collective-permute-start | bytes 602120 | tf_op jit(solution)/shard_map/ppermute | solution.py:1005
  37.1 1.5 collective-permute-start.11
  38.6 2.7 %feed.1 = (f32[512,1024]{1,0:T(8,128)S(1)}, bf16[1024,512]{1,0:T(8,128)(2,1)S(1)}, f32[256,1024]{1,0:T(8,128)S(1)}, bf16[256,1024]{1,0:T(8,128)(2,1)S(1)}) custom-call(bf16[512,1024]{1,0:T(8,128)(2,1)S(1)} %get-tuple-element.91.refs_0_, bf16[1024,1024]{1,0:T(8,128)(2,1)S(1)} %get-tuple-element.92.refs_1_.refs_2_, ...), custom_call_target="tpu_custom_call" | custom-call | tf_op jit(solution)/shard_map/feed/pallas_call | solution.py:413
  41.4 0.5 collective-permute-start.12
  41.9 6.1 %collective-permute-done.3.refs_2_ = bf16[128,1024]{1,0:T(8,128)(2,1)S(1)} collective-permute-done((bf16[128,1024]{1,0:T(8,128)(2,1)S(1)}, bf16[128,1024]{1,0:T(8,128)(2,1)S(1)}, u32[]{:S(2)}, u32[]{:S(2)}) %collective-permute-start.3) | collective-permute-done | bytes 262176 | tf_op jit(solution)/shard_map/ppermute | solution.py:1002
  48.1 0.7 back_rows.1
  48.7 1.6 %collective-permute-start.7 = (bf16[256,128]{1,0:T(8,128)(2,1)S(1)}, bf16[256,128]{1,0:T(8,128)(2,1)S(1)}, u32[]{:S(2)}, u32[]{:S(2)}) collective-permute-start(bf16[256,128]{1,0:T(8,128)(2,1)S(1)} %get-tuple-element.97), channel_id=1, source_target_pairs={{0,2},{2,0},{4,6},{6,4},{8,10},{10,8},{12,14},{14,12},{16,18},{18,... | collective-permute-start | bytes 196616 | tf_op jit(solution)/shard_map/ppermute | solution.py:1005
  50.3 1.5 collective-permute-start.8
  51.8 0.5 collective-permute-start.9
  52.3 3.2 %feed_grad.1 = (bf16[512,1024]{1,0:T(8,128)(2,1)S(1)}, f32[8,1024]{1,0:T(8,128)S(1)}, f32[512,1024]{1,0:T(8,128)S(1)}, f32[256,1024]{1,0:T(8,128)S(1)}, bf16[256,1024]{1,0:T(8,128)(2,1)S(1)}) custom-call(bf16[512,1024]{1,0:T(8,128)(2,1)S(1)} %get-tuple-element.103.refs_0_.refs_6_.refs_11_, f32[512,1024]{1,0:T(8,128)S(1)} %get-tuple-element.95.refs_5_.refs_1_, ...), custom_call_target="tpu_custom_call" | custom-call | flops 4600000000 | tf_op jit(solution)/shard_map/feed_grad/pallas_call | solution.py:413
  55.5 2.1 %collective-permute-start.16 = (bf16[256,1024]{1,0:T(8,128)(2,1)S(1)}, bf16[256,1024]{1,0:T(8,128)(2,1)S(1)}, u32[]{:S(2)}, u32[]{:S(2)}) collective-permute-start(bf16[256,1024]{1,0:T(8,128)(2,1)S(1)} %get-tuple-element.120), channel_id=1, source_target_pairs={{0,8},{2,10},{4,12},{6,14},{8,0},{10,2},{12,4},{14,6},{16,24},{18,... | collective-permute-start | bytes 1572872 | tf_op jit(solution)/shard_map/ppermute | solution.py:1002
  57.6 6.4 %attend.1 = (bf16[2048,128]{1,0:T(8,128)(2,1)S(1)}, bf16[2048,128]{1,0:T(8,128)(2,1)S(1)}, bf16[2048,64]{1,0:T(8,128)(2,1)S(1)}, f32[2048,64]{1,0:T(8,128)S(1)},...) custom-call(bf16[784,128]{1,0:T(8,128)(2,1)S(1)} %get-tuple-element.94.refs_4_.refs_0_, ...), custom_call_target="tpu_custom_call" | custom-call | tf_op jit(solution)/shard_map/attend/pallas_call | solution.py:413
  63.9 3.5 %feed_terms.1 = (bf16[1088,1024]{1,0:T(8,128)(2,1)S(1)}, f32[1088,1024]{1,0:T(8,128)S(1)}) custom-call(bf16[512,1024]{1,0:T(8,128)(2,1)S(1)} %get-tuple-element.103.refs_0_.refs_6_.refs_11_, bf16[1024,512]{1,0:T(8,128)(2,1)S(1)} %get-tuple-element.111.refs_1_, bf16[1024,512]{1,0:T(8,128)(2,1)S(1)} %get-tuple-element.112.refs_2_.refs_3_, ...), custom_call_target="tpu_custom_call" | custom-call | flops 575000000 | tf_op jit(solution)/shard_map/feed_terms/pallas_call | solution.py:413
  67.6 8.5 %attend_back.1 = (bf16[1024,128]{1,0:T(8,128)(2,1)S(1)}, bf16[1024,128]{1,0:T(8,128)(2,1)S(1)}, bf16[1024,128]{1,0:T(8,128)(2,1)S(1)}, bf16[1024,128]{1,0:T(8,128)(2,1)S(1)}, f32[8,128]{1,0:T(8,128)S(1)}) custom-call(bf16[256,128]{1,0:T(8,128)(2,1)S(1)} %get-tuple-element.96.refs_4_.refs_0_, bf16[256,128]{1,0:T(8,128)(2,1)S(1)} %collective-permute-done.7.refs_1_, ...), custom_call_target="tpu_custom_call" | custom-call | tf_op jit(solution)/shard_map/attend_back/pallas_call | solution.py:413
  76.1 1.6 %collective-permute-start.13 = (bf16[1024,128]{1,0:T(8,128)(2,1)S(1)}, bf16[1024,128]{1,0:T(8,128)(2,1)S(1)}, u32[]{:S(2)}, u32[]{:S(2)}) collective-permute-start(bf16[1024,128]{1,0:T(8,128)(2,1)S(1)} %get-tuple-element.116), channel_id=1, source_target_pairs={{0,2},{2,0},{4,6},{6,4},{8,10},{10,8},{12,14},{14,12},{16,18},{18,... | collective-permute-start | bytes 786440 | tf_op jit(solution)/shard_map/ppermute | solution.py:1005
  77.6 1.5 %collective-permute-start.14 = (bf16[1024,128]{1,0:T(8,128)(2,1)S(1)}, bf16[1024,128]{1,0:T(8,128)(2,1)S(1)}, u32[]{:S(2)}, u32[]{:S(2)}) collective-permute-start(bf16[1024,128]{1,0:T(8,128)(2,1)S(1)} %get-tuple-element.117), channel_id=1, source_target_pairs={{0,4},{2,6},{4,0},{6,2},{8,12},{10,14},{12,8},{14,10},{16,20},{18,... | collective-permute-start | bytes 786440 | tf_op jit(solution)/shard_map/ppermute | solution.py:1005
  79.9 1.3 collective-permute-start.22
  81.2 4.1 %collective-permute-done.13.refs_1_ = bf16[1024,128]{1,0:T(8,128)(2,1)S(1)} collective-permute-done((bf16[1024,128]{1,0:T(8,128)(2,1)S(1)}, bf16[1024,128]{1,0:T(8,128)(2,1)S(1)}, u32[]{:S(2)}, u32[]{:S(2)}) %collective-permute-start.13) | collective-permute-done | bytes 262176 | tf_op jit(solution)/shard_map/ppermute | solution.py:1005
  85.2 1.2 collective-permute-start.21
  86.5 5.2 %collective-permute-done.14.refs_2_ = bf16[1024,128]{1,0:T(8,128)(2,1)S(1)} collective-permute-done((bf16[1024,128]{1,0:T(8,128)(2,1)S(1)}, bf16[1024,128]{1,0:T(8,128)(2,1)S(1)}, u32[]{:S(2)}, u32[]{:S(2)}) %collective-permute-start.14) | collective-permute-done | bytes 262176 | tf_op jit(solution)/shard_map/ppermute | solution.py:1005
  91.6 0.9 unpack.1
  92.7 3.0 %grads.1 = (bf16[704,768]{1,0:T(8,128)(2,1)S(1)}, f32[704,768]{1,0:T(8,128)S(1)}) custom-call(bf16[512,1024]{1,0:T(8,128)(2,1)S(1)} %get-tuple-element.125.refs_0_.refs_8_, f32[512,1024]{1,0:T(8,128)S(1)} %get-tuple-element.132.refs_1_, f32[512,1024]{1,0:T(8,128)S(1)} %get-tuple-element.133.refs_2_, ...), custom_call_target="tpu_custom_call" | custom-call | tf_op jit(solution)/shard_map/grads/pallas_call | solution.py:413
  95.8 0.6 share_twin.2
  96.4 1.3 collective-permute-start.24
  97.7 2.4 %collective-permute-done.22.refs_9_ = bf16[128,1024]{1,0:T(8,128)(2,1)S(1)} collective-permute-done((bf16[128,1024]{1,0:T(8,128)(2,1)S(1)}, bf16[128,1024]{1,0:T(8,128)(2,1)S(1)}, u32[]{:S(2)}, u32[]{:S(2)}) %collective-permute-start.22) | collective-permute-done | bytes 262176 | tf_op jit(solution)/shard_map/ppermute | solution.py:1002
  100.1 1.5 collective-permute-start.25
  101.7 1.4 collective-permute-start.26
  103.3 2.3 %collective-permute-done.21.refs_7_ = bf16[128,1024]{1,0:T(8,128)(2,1)S(1)} collective-permute-done((bf16[128,1024]{1,0:T(8,128)(2,1)S(1)}, bf16[128,1024]{1,0:T(8,128)(2,1)S(1)}, u32[]{:S(2)}, u32[]{:S(2)}) %collective-permute-start.21) | collective-permute-done | bytes 262176 | tf_op jit(solution)/shard_map/ppermute | solution.py:1002
  105.7 5.6 %collective-permute-done.18.refs_1_ = bf16[128,1024]{1,0:T(8,128)(2,1)S(1)} collective-permute-done((bf16[128,1024]{1,0:T(8,128)(2,1)S(1)}, bf16[128,1024]{1,0:T(8,128)(2,1)S(1)}, u32[]{:S(2)}, u32[]{:S(2)}) %collective-permute-start.18) | collective-permute-done | bytes 262176 | tf_op jit(solution)/shard_map/ppermute | solution.py:1002
  111.3 2.1 %collective-permute-start.20 = (bf16[128,1024]{1,0:T(8,128)(2,1)S(1)}, bf16[128,1024]{1,0:T(8,128)(2,1)S(1)}, u32[]{:S(2)}, u32[]{:S(2)}) collective-permute-start(bf16[128,1024]{1,0:T(8,128)(2,1)S(1)} %get-tuple-element.128), channel_id=1, source_target_pairs={{0,24},{2,26},{4,28},{6,30},{8,16},{10,18},{12,20},{14,22},{16,8},... | collective-permute-start | bytes 786440 | tf_op jit(solution)/shard_map/ppermute | solution.py:1002
  113.4 1.5 collective-permute-start.28
  114.9 11.6 %collective-permute-done.25.refs_2_ = bf16[272,1024]{1,0:T(8,128)(2,1)S(1)} collective-permute-done((bf16[272,1024]{1,0:T(8,128)(2,1)S(1)}, bf16[272,1024]{1,0:T(8,128)(2,1)S(1)}, u32[]{:S(2)}, u32[]{:S(2)}) %collective-permute-start.25) | collective-permute-done | bytes 557088 | tf_op jit(solution)/shard_map/ppermute | solution.py:1005
  126.5 1.5 collective-permute-start.29
  128.0 1.4 collective-permute-start.30
  129.4 1.1 feed_sum.1
  130.5 2.7 %collective-permute-start.35 = (bf16[32,1024]{1,0:T(8,128)(2,1)S(1)}, bf16[32,1024]{1,0:T(8,128)(2,1)S(1)}, u32[]{:S(2)}, u32[]{:S(2)}) collective-permute-start(bf16[32,1024]{1,0:T(8,128)(2,1)S(1)} %get-tuple-element.155), channel_id=1, source_target_pairs={{0,16},{2,18},{4,20},{6,22},{8,24},{10,26},{12,28},{14,30},{16,0},... | collective-permute-start | bytes 196616 | tf_op jit(solution)/shard_map/ppermute | solution.py:1002
  133.2 1.7 %collective-permute-start.36 = (bf16[32,1024]{1,0:T(8,128)(2,1)S(1)}, bf16[32,1024]{1,0:T(8,128)(2,1)S(1)}, u32[]{:S(2)}, u32[]{:S(2)}) collective-permute-start(bf16[32,1024]{1,0:T(8,128)(2,1)S(1)} %get-tuple-element.156), channel_id=1, source_target_pairs={{0,24},{2,26},{4,28},{6,30},{8,16},{10,18},{12,20},{14,22},{16,8},... | collective-permute-start | bytes 196616 | tf_op jit(solution)/shard_map/ppermute | solution.py:1002
  134.9 1.0 copy-done.8
  135.9 3.5 %tokens.1 = (bf16[128,1024]{1,0:T(8,128)(2,1)}, bf16[128,1024]{1,0:T(8,128)(2,1)}) custom-call(bf16[512,1024]{1,0:T(8,128)(2,1)S(1)} %get-tuple-element.125.refs_0_.refs_8_, bf16[128,1024]{1,0:T(8,128)(2,1)S(1)} %collective-permute-done.18.refs_1_, bf16[128,1024]{1,0:T(8,128)(2,1)S(1)} %collective-permute-done.19.refs_2_, ...), custom_call_target="tpu_custom_call" | custom-call | tf_op jit(solution)/shard_map/tokens/pallas_call | solution.py:413
  139.6 0.9 copy-done.9
  140.6 0.7 grad_sum.1
  141.3 2.7 %collective-permute-start.32 = (bf16[48,768]{1,0:T(8,128)(2,1)S(1)}, bf16[48,768]{1,0:T(8,128)(2,1)S(1)}, u32[]{:S(2)}, u32[]{:S(2)}) collective-permute-start(bf16[48,768]{1,0:T(8,128)(2,1)S(1)} %get-tuple-element.151), channel_id=1, source_target_pairs={{0,16},{2,18},{4,20},{6,22},{8,24},{10,26},{12,28},{14,30},{16,0},... | collective-permute-start | bytes 221192 | tf_op jit(solution)/shard_map/ppermute | solution.py:1002
  144.0 1.7 %collective-permute-start.33 = (bf16[48,768]{1,0:T(8,128)(2,1)S(1)}, bf16[48,768]{1,0:T(8,128)(2,1)S(1)}, u32[]{:S(2)}, u32[]{:S(2)}) collective-permute-start(bf16[48,768]{1,0:T(8,128)(2,1)S(1)} %get-tuple-element.152), channel_id=1, source_target_pairs={{0,24},{2,26},{4,28},{6,30},{8,16},{10,18},{12,20},{14,22},{16,8},... | collective-permute-start | bytes 221192 | tf_op jit(solution)/shard_map/ppermute | solution.py:1002
  145.7 0.9 copy-done.11
  146.6 0.8 join_in.1.refs_4_
  147.4 0.7 collective-permute-done.32.refs_2_
  148.1 2.0 %collective-permute-done.33.refs_3_ = bf16[48,768]{1,0:T(8,128)(2,1)S(1)} collective-permute-done((bf16[48,768]{1,0:T(8,128)(2,1)S(1)}, bf16[48,768]{1,0:T(8,128)(2,1)S(1)}, u32[]{:S(2)}, u32[]{:S(2)}) %collective-permute-start.33) | collective-permute-done | bytes 73760 | tf_op jit(solution)/shard_map/ppermute | solution.py:1002
  150.2 1.0 copy-done.7
  151.2 0.8 join_qkv.1
  152.0 0.5 copy.28
  (59 shorter events, 1.5 us)
Async XLA Ops:
  0.6 0.7 copy-start.10
  2.3 12.6 %copy-start.2 = (bf16[144,1024]{1,0:T(8,128)(2,1)}, bf16[144,1024]{1,0:T(8,128)(2,1)S(1)}, u32[]{:S(2)}) copy-start(bf16[144,1024]{1,0:T(8,128)(2,1)S(1)} %pack.1.refs_10_.refs_0_) | copy-start | bytes 884740
  2.3 17.6 %collective-permute-start.1 = (bf16[144,1024]{1,0:T(8,128)(2,1)S(1)}, bf16[144,1024]{1,0:T(8,128)(2,1)}, u32[]{:S(2)}, u32[]{:S(2)}) collective-permute-start(bf16[144,1024]{1,0:T(8,128)(2,1)S(1)} %pack.1.refs_10_.refs_0_), channel_id=1, source_target_pairs={{0,16},{2,18},{4,20},{6,22},{8,24},{10,26},{12,28},{14,30},{16,0},... | collective-permute-start | bytes 884744 | tf_op jit(solution)/shard_map/ppermute | solution.py:1002
  6.4 14.1 %collective-permute-start = (bf16[144,1024]{1,0:T(8,128)(2,1)S(1)}, bf16[144,1024]{1,0:T(8,128)(2,1)S(1)}, u32[]{:S(2)}, u32[]{:S(2)}) collective-permute-start(bf16[144,1024]{1,0:T(8,128)(2,1)S(1)} %pack.1.refs_10_.refs_0_), channel_id=1, source_target_pairs={{0,8},{2,10},{4,12},{6,14},{8,0},{10,2},{12,4},{14,6},{16,24},{18,... | collective-permute-start | bytes 884744 | tf_op jit(solution)/shard_map/ppermute | solution.py:1002
  14.9 12.1 %collective-permute-start.5 = (bf16[3600,1024]{1,0:T(8,128)(2,1)}, bf16[3600,1024]{1,0:T(8,128)(2,1)}, u32[]{:S(2)}, u32[]{:S(2)}) collective-permute-start(bf16[3600,1024]{1,0:T(8,128)(2,1)} %prepare.1.refs_3_.refs_0_), channel_id=1, source_target_pairs={{0,1},{1,0},{2,3},{3,2},{4,5},{5,4},{6,7},{7,6},{8,9},{9,8},{10,11... | collective-permute-start | bytes 22118408 | tf_op jit(solution)/shard_map/ppermute | solution.py:1008
  19.9 11.9 %collective-permute-start.6 = (bf16[144,1024]{1,0:T(8,128)(2,1)}, bf16[144,1024]{1,0:T(8,128)(2,1)}, u32[]{:S(2)}, u32[]{:S(2)}) collective-permute-start(bf16[144,1024]{1,0:T(8,128)(2,1)} %collective-permute-done.1.refs_2_), channel_id=1, source_target_pairs={{0,8},{2,10},{4,12},{6,14},{8,0},{10,2},{12,4},{14,6},{16,24},{18,... | collective-permute-start | bytes 884744 | tf_op jit(solution)/shard_map/ppermute | solution.py:1002
  21.4 10.4 %copy-start.3 = (bf16[144,1024]{1,0:T(8,128)(2,1)S(1)}, bf16[144,1024]{1,0:T(8,128)(2,1)}, u32[]{:S(2)}) copy-start(bf16[144,1024]{1,0:T(8,128)(2,1)} %copy-done.2) | copy-start | bytes 884740
  21.4 19.9 %collective-permute-start.4 = (bf16[128,1024]{1,0:T(8,128)(2,1)S(1)}, bf16[128,1024]{1,0:T(8,128)(2,1)S(1)}, u32[]{:S(2)}, u32[]{:S(2)}) collective-permute-start(bf16[128,1024]{1,0:T(8,128)(2,1)S(1)} %hold.1.refs_2_.refs_0_), channel_id=1, source_target_pairs={{0,24},{2,26},{4,28},{6,30},{8,16},{10,18},{12,20},{14,22},{16,8},... | collective-permute-start | bytes 786440 | tf_op jit(solution)/shard_map/ppermute | solution.py:1002
  24.4 23.6 %collective-permute-start.3 = (bf16[128,1024]{1,0:T(8,128)(2,1)S(1)}, bf16[128,1024]{1,0:T(8,128)(2,1)S(1)}, u32[]{:S(2)}, u32[]{:S(2)}) collective-permute-start(bf16[128,1024]{1,0:T(8,128)(2,1)S(1)} %hold.1.refs_2_.refs_0_), channel_id=1, source_target_pairs={{0,16},{2,18},{4,20},{6,22},{8,24},{10,26},{12,28},{14,30},{16,0},... | collective-permute-start | bytes 786440 | tf_op jit(solution)/shard_map/ppermute | solution.py:1002
  25.1 23.0 %collective-permute-start.2 = (bf16[128,1024]{1,0:T(8,128)(2,1)S(1)}, bf16[128,1024]{1,0:T(8,128)(2,1)S(1)}, u32[]{:S(2)}, u32[]{:S(2)}) collective-permute-start(bf16[128,1024]{1,0:T(8,128)(2,1)S(1)} %hold.1.refs_2_.refs_0_), channel_id=1, source_target_pairs={{0,8},{2,10},{4,12},{6,14},{8,0},{10,2},{12,4},{14,6},{16,24},{18,... | collective-permute-start | bytes 786440 | tf_op jit(solution)/shard_map/ppermute | solution.py:1002
  31.8 16.2 %copy-start.5 = (bf16[1024,1024]{1,0:T(8,128)(2,1)}, bf16[1024,1024]{1,0:T(8,128)(2,1)S(1)}, u32[]{:S(2)}) copy-start(bf16[1024,1024]{1,0:T(8,128)(2,1)S(1)} %get-tuple-element.88.refs_4_.refs_5_) | copy-start | bytes 6291460
  35.5 14.8 %collective-permute-start.10 = (bf16[784,128]{1,0:T(8,128)(2,1)S(1)}, bf16[784,128]{1,0:T(8,128)(2,1)S(1)}, u32[]{:S(2)}, u32[]{:S(2)}) collective-permute-start(bf16[784,128]{1,0:T(8,128)(2,1)S(1)} %get-tuple-element.100), channel_id=1, source_target_pairs={{0,2},{2,0},{4,6},{6,4},{8,10},{10,8},{12,14},{14,12},{16,18},{18,... | collective-permute-start | bytes 602120 | tf_op jit(solution)/shard_map/ppermute | solution.py:1005
  37.1 14.7 %collective-permute-start.11 = (bf16[784,128]{1,0:T(8,128)(2,1)S(1)}, bf16[784,128]{1,0:T(8,128)(2,1)S(1)}, u32[]{:S(2)}, u32[]{:S(2)}) collective-permute-start(bf16[784,128]{1,0:T(8,128)(2,1)S(1)} %get-tuple-element.101), channel_id=1, source_target_pairs={{0,4},{2,6},{4,0},{6,2},{8,12},{10,14},{12,8},{14,10},{16,20},{18,... | collective-permute-start | bytes 602120 | tf_op jit(solution)/shard_map/ppermute | solution.py:1005
  41.4 14.1 %collective-permute-start.12 = (bf16[784,128]{1,0:T(8,128)(2,1)S(1)}, bf16[784,128]{1,0:T(8,128)(2,1)S(1)}, u32[]{:S(2)}, u32[]{:S(2)}) collective-permute-start(bf16[784,128]{1,0:T(8,128)(2,1)S(1)} %get-tuple-element.102), channel_id=1, source_target_pairs={{0,6},{2,4},{4,2},{6,0},{8,14},{10,12},{12,10},{14,8},{16,22},{18,... | collective-permute-start | bytes 602120 | tf_op jit(solution)/shard_map/ppermute | solution.py:1005
  48.0 31.1 %collective-permute-start.17 = (bf16[256,1024]{1,0:T(8,128)(2,1)S(1)}, bf16[256,1024]{1,0:T(8,128)(2,1)S(1)}, u32[]{:S(2)}, u32[]{:S(2)}) collective-permute-start(bf16[256,1024]{1,0:T(8,128)(2,1)S(1)} %get-tuple-element.122), channel_id=1, source_target_pairs={{0,8},{2,10},{4,12},{6,14},{8,0},{10,2},{12,4},{14,6},{16,24},{18,... | collective-permute-start | bytes 1572872 | tf_op jit(solution)/shard_map/ppermute | solution.py:1002
  48.7 18.7 %collective-permute-start.7 = (bf16[256,128]{1,0:T(8,128)(2,1)S(1)}, bf16[256,128]{1,0:T(8,128)(2,1)S(1)}, u32[]{:S(2)}, u32[]{:S(2)}) collective-permute-start(bf16[256,128]{1,0:T(8,128)(2,1)S(1)} %get-tuple-element.97), channel_id=1, source_target_pairs={{0,2},{2,0},{4,6},{6,4},{8,10},{10,8},{12,14},{14,12},{16,18},{18,... | collective-permute-start | bytes 196616 | tf_op jit(solution)/shard_map/ppermute | solution.py:1005
  50.3 17.2 %collective-permute-start.8 = (bf16[256,128]{1,0:T(8,128)(2,1)S(1)}, bf16[256,128]{1,0:T(8,128)(2,1)S(1)}, u32[]{:S(2)}, u32[]{:S(2)}) collective-permute-start(bf16[256,128]{1,0:T(8,128)(2,1)S(1)} %get-tuple-element.98), channel_id=1, source_target_pairs={{0,4},{2,6},{4,0},{6,2},{8,12},{10,14},{12,8},{14,10},{16,20},{18,... | collective-permute-start | bytes 196616 | tf_op jit(solution)/shard_map/ppermute | solution.py:1005
  51.8 15.7 %collective-permute-start.9 = (bf16[256,128]{1,0:T(8,128)(2,1)S(1)}, bf16[256,128]{1,0:T(8,128)(2,1)S(1)}, u32[]{:S(2)}, u32[]{:S(2)}) collective-permute-start(bf16[256,128]{1,0:T(8,128)(2,1)S(1)} %get-tuple-element.99), channel_id=1, source_target_pairs={{0,6},{2,4},{4,2},{6,0},{8,14},{10,12},{12,10},{14,8},{16,22},{18,... | collective-permute-start | bytes 196616 | tf_op jit(solution)/shard_map/ppermute | solution.py:1005
  52.3 5.3 %copy-start = (f32[2048,128]{1,0:T(8,128)S(1)}, f32[2048,128]{1,0:T(8,128)}, u32[]{:S(2)}) copy-start(f32[2048,128]{1,0:T(8,128)} %constant.5.clone.refs_5_.refs_11_) | copy-start | bytes 3145732
  52.3 5.3 %copy-start.1 = (f32[2048,128]{1,0:T(8,128)S(1)}, f32[2048,128]{1,0:T(8,128)}, u32[]{:S(2)}) copy-start(f32[2048,128]{1,0:T(8,128)} %constant.4.clone.refs_4_.refs_10_) | copy-start | bytes 3145732
  55.5 24.3 %collective-permute-start.16 = (bf16[256,1024]{1,0:T(8,128)(2,1)S(1)}, bf16[256,1024]{1,0:T(8,128)(2,1)S(1)}, u32[]{:S(2)}, u32[]{:S(2)}) collective-permute-start(bf16[256,1024]{1,0:T(8,128)(2,1)S(1)} %get-tuple-element.120), channel_id=1, source_target_pairs={{0,8},{2,10},{4,12},{6,14},{8,0},{10,2},{12,4},{14,6},{16,24},{18,... | collective-permute-start | bytes 1572872 | tf_op jit(solution)/shard_map/ppermute | solution.py:1002
  67.5 28.3 %collective-permute-start.23 = (bf16[1088,1024]{1,0:T(8,128)(2,1)S(1)}, bf16[1088,1024]{1,0:T(8,128)(2,1)S(1)}, u32[]{:S(2)}, u32[]{:S(2)}) collective-permute-start(bf16[1088,1024]{1,0:T(8,128)(2,1)S(1)} %get-tuple-element.114.refs_12_), channel_id=1, source_target_pairs={{0,1},{1,0},{2,3},{3,2},{4,5},{5,4},{6,7},{7,6},{8,9},{9,8},{10,11... | collective-permute-start | bytes 6684680 | tf_op jit(solution)/shard_map/ppermute | solution.py:1008
  76.1 9.2 %collective-permute-start.13 = (bf16[1024,128]{1,0:T(8,128)(2,1)S(1)}, bf16[1024,128]{1,0:T(8,128)(2,1)S(1)}, u32[]{:S(2)}, u32[]{:S(2)}) collective-permute-start(bf16[1024,128]{1,0:T(8,128)(2,1)S(1)} %get-tuple-element.116), channel_id=1, source_target_pairs={{0,2},{2,0},{4,6},{6,4},{8,10},{10,8},{12,14},{14,12},{16,18},{18,... | collective-permute-start | bytes 786440 | tf_op jit(solution)/shard_map/ppermute | solution.py:1005
  77.6 14.0 %collective-permute-start.14 = (bf16[1024,128]{1,0:T(8,128)(2,1)S(1)}, bf16[1024,128]{1,0:T(8,128)(2,1)S(1)}, u32[]{:S(2)}, u32[]{:S(2)}) collective-permute-start(bf16[1024,128]{1,0:T(8,128)(2,1)S(1)} %get-tuple-element.117), channel_id=1, source_target_pairs={{0,4},{2,6},{4,0},{6,2},{8,12},{10,14},{12,8},{14,10},{16,20},{18,... | collective-permute-start | bytes 786440 | tf_op jit(solution)/shard_map/ppermute | solution.py:1005
  79.2 12.5 %collective-permute-start.15 = (bf16[1024,128]{1,0:T(8,128)(2,1)S(1)}, bf16[1024,128]{1,0:T(8,128)(2,1)S(1)}, u32[]{:S(2)}, u32[]{:S(2)}) collective-permute-start(bf16[1024,128]{1,0:T(8,128)(2,1)S(1)} %get-tuple-element.118), channel_id=1, source_target_pairs={{0,6},{2,4},{4,2},{6,0},{8,14},{10,12},{12,10},{14,8},{16,22},{18,... | collective-permute-start | bytes 786440 | tf_op jit(solution)/shard_map/ppermute | solution.py:1005
  79.9 20.2 %collective-permute-start.22 = (bf16[128,1024]{1,0:T(8,128)(2,1)S(1)}, bf16[128,1024]{1,0:T(8,128)(2,1)S(1)}, u32[]{:S(2)}, u32[]{:S(2)}) collective-permute-start(bf16[128,1024]{1,0:T(8,128)(2,1)S(1)} %get-tuple-element.130), channel_id=1, source_target_pairs={{0,16},{2,18},{4,20},{6,22},{8,24},{10,26},{12,28},{14,30},{16,0},... | collective-permute-start | bytes 786440 | tf_op jit(solution)/shard_map/ppermute | solution.py:1002
  85.2 20.4 %collective-permute-start.21 = (bf16[128,1024]{1,0:T(8,128)(2,1)S(1)}, bf16[128,1024]{1,0:T(8,128)(2,1)S(1)}, u32[]{:S(2)}, u32[]{:S(2)}) collective-permute-start(bf16[128,1024]{1,0:T(8,128)(2,1)S(1)} %get-tuple-element.129), channel_id=1, source_target_pairs={{0,16},{2,18},{4,20},{6,22},{8,24},{10,26},{12,28},{14,30},{16,0},... | collective-permute-start | bytes 786440 | tf_op jit(solution)/shard_map/ppermute | solution.py:1002
  92.6 18.7 %collective-permute-start.18 = (bf16[128,1024]{1,0:T(8,128)(2,1)S(1)}, bf16[128,1024]{1,0:T(8,128)(2,1)S(1)}, u32[]{:S(2)}, u32[]{:S(2)}) collective-permute-start(bf16[128,1024]{1,0:T(8,128)(2,1)S(1)} %get-tuple-element.126), channel_id=1, source_target_pairs={{0,8},{2,10},{4,12},{6,14},{8,0},{10,2},{12,4},{14,6},{16,24},{18,... | collective-permute-start | bytes 786440 | tf_op jit(solution)/shard_map/ppermute | solution.py:1002
  95.7 6.0 %collective-permute-start.27 = (bf16[704,768]{1,0:T(8,128)(2,1)S(1)}, bf16[704,768]{1,0:T(8,128)(2,1)S(1)}, u32[]{:S(2)}, u32[]{:S(2)}) collective-permute-start(bf16[704,768]{1,0:T(8,128)(2,1)S(1)} %get-tuple-element.136.refs_2_), channel_id=1, source_target_pairs={{0,1},{1,0},{2,3},{3,2},{4,5},{5,4},{6,7},{7,6},{8,9},{9,8},{10,11... | collective-permute-start | bytes 3244040 | tf_op jit(solution)/shard_map/ppermute | solution.py:1008
  96.4 17.0 %collective-permute-start.24 = (bf16[272,1024]{1,0:T(8,128)(2,1)S(1)}, bf16[272,1024]{1,0:T(8,128)(2,1)S(1)}, u32[]{:S(2)}, u32[]{:S(2)}) collective-permute-start(bf16[272,1024]{1,0:T(8,128)(2,1)S(1)} %get-tuple-element.138), channel_id=1, source_target_pairs={{0,2},{2,0},{4,6},{6,4},{8,10},{10,8},{12,14},{14,12},{16,18},{18,... | collective-permute-start | bytes 1671176 | tf_op jit(solution)/shard_map/ppermute | solution.py:1005
  100.1 26.3 %collective-permute-start.25 = (bf16[272,1024]{1,0:T(8,128)(2,1)S(1)}, bf16[272,1024]{1,0:T(8,128)(2,1)S(1)}, u32[]{:S(2)}, u32[]{:S(2)}) collective-permute-start(bf16[272,1024]{1,0:T(8,128)(2,1)S(1)} %get-tuple-element.139), channel_id=1, source_target_pairs={{0,4},{2,6},{4,0},{6,2},{8,12},{10,14},{12,8},{14,10},{16,20},{18,... | collective-permute-start | bytes 1671176 | tf_op jit(solution)/shard_map/ppermute | solution.py:1005
  101.7 26.3 %collective-permute-start.26 = (bf16[272,1024]{1,0:T(8,128)(2,1)S(1)}, bf16[272,1024]{1,0:T(8,128)(2,1)S(1)}, u32[]{:S(2)}, u32[]{:S(2)}) collective-permute-start(bf16[272,1024]{1,0:T(8,128)(2,1)S(1)} %get-tuple-element.140), channel_id=1, source_target_pairs={{0,6},{2,4},{4,2},{6,0},{8,14},{10,12},{12,10},{14,8},{16,22},{18,... | collective-permute-start | bytes 1671176 | tf_op jit(solution)/shard_map/ppermute | solution.py:1005
  105.7 24.8 %collective-permute-start.19 = (bf16[128,1024]{1,0:T(8,128)(2,1)S(1)}, bf16[128,1024]{1,0:T(8,128)(2,1)S(1)}, u32[]{:S(2)}, u32[]{:S(2)}) collective-permute-start(bf16[128,1024]{1,0:T(8,128)(2,1)S(1)} %get-tuple-element.127), channel_id=1, source_target_pairs={{0,16},{2,18},{4,20},{6,22},{8,24},{10,26},{12,28},{14,30},{16,0},... | collective-permute-start | bytes 786440 | tf_op jit(solution)/shard_map/ppermute | solution.py:1002
  111.3 19.2 %collective-permute-start.20 = (bf16[128,1024]{1,0:T(8,128)(2,1)S(1)}, bf16[128,1024]{1,0:T(8,128)(2,1)S(1)}, u32[]{:S(2)}, u32[]{:S(2)}) collective-permute-start(bf16[128,1024]{1,0:T(8,128)(2,1)S(1)} %get-tuple-element.128), channel_id=1, source_target_pairs={{0,24},{2,26},{4,28},{6,30},{8,16},{10,18},{12,20},{14,22},{16,8},... | collective-permute-start | bytes 786440 | tf_op jit(solution)/shard_map/ppermute | solution.py:1002
  113.4 19.8 %collective-permute-start.28 = (bf16[176,768]{1,0:T(8,128)(2,1)S(1)}, bf16[176,768]{1,0:T(8,128)(2,1)S(1)}, u32[]{:S(2)}, u32[]{:S(2)}) collective-permute-start(bf16[176,768]{1,0:T(8,128)(2,1)S(1)} %get-tuple-element.146), channel_id=1, source_target_pairs={{0,2},{2,0},{4,6},{6,4},{8,10},{10,8},{12,14},{14,12},{16,18},{18,... | collective-permute-start | bytes 811016 | tf_op jit(solution)/shard_map/ppermute | solution.py:1005
  126.5 13.2 %collective-permute-start.29 = (bf16[176,768]{1,0:T(8,128)(2,1)S(1)}, bf16[176,768]{1,0:T(8,128)(2,1)S(1)}, u32[]{:S(2)}, u32[]{:S(2)}) collective-permute-start(bf16[176,768]{1,0:T(8,128)(2,1)S(1)} %get-tuple-element.147), channel_id=1, source_target_pairs={{0,4},{2,6},{4,0},{6,2},{8,12},{10,14},{12,8},{14,10},{16,20},{18,... | collective-permute-start | bytes 811016 | tf_op jit(solution)/shard_map/ppermute | solution.py:1005
  128.0 11.6 %collective-permute-start.30 = (bf16[176,768]{1,0:T(8,128)(2,1)S(1)}, bf16[176,768]{1,0:T(8,128)(2,1)S(1)}, u32[]{:S(2)}, u32[]{:S(2)}) collective-permute-start(bf16[176,768]{1,0:T(8,128)(2,1)S(1)} %get-tuple-element.148), channel_id=1, source_target_pairs={{0,6},{2,4},{4,2},{6,0},{8,14},{10,12},{12,10},{14,8},{16,22},{18,... | collective-permute-start | bytes 811016 | tf_op jit(solution)/shard_map/ppermute | solution.py:1005
  129.4 5.5 %copy-start.4 = (bf16[144,1024]{1,0:T(8,128)(2,1)S(1)}, bf16[144,1024]{1,0:T(8,128)(2,1)}, u32[]{:S(2)}) copy-start(bf16[144,1024]{1,0:T(8,128)(2,1)} %copy-done.2) | copy-start | bytes 884740
  129.4 5.5 %copy-start.6 = (bf16[1024,1024]{1,0:T(8,128)(2,1)S(1)}, bf16[1024,1024]{1,0:T(8,128)(2,1)}, u32[]{:S(2)}) copy-start(bf16[1024,1024]{1,0:T(8,128)(2,1)} %copy-done.5) | copy-start | bytes 6291460
  130.5 13.5 %collective-permute-start.34 = (bf16[32,1024]{1,0:T(8,128)(2,1)S(1)}, bf16[32,1024]{1,0:T(8,128)(2,1)S(1)}, u32[]{:S(2)}, u32[]{:S(2)}) collective-permute-start(bf16[32,1024]{1,0:T(8,128)(2,1)S(1)} %get-tuple-element.154), channel_id=1, source_target_pairs={{0,8},{2,10},{4,12},{6,14},{8,0},{10,2},{12,4},{14,6},{16,24},{18,... | collective-permute-start | bytes 196616 | tf_op jit(solution)/shard_map/ppermute | solution.py:1002
  130.5 15.2 %collective-permute-start.35 = (bf16[32,1024]{1,0:T(8,128)(2,1)S(1)}, bf16[32,1024]{1,0:T(8,128)(2,1)S(1)}, u32[]{:S(2)}, u32[]{:S(2)}) collective-permute-start(bf16[32,1024]{1,0:T(8,128)(2,1)S(1)} %get-tuple-element.155), channel_id=1, source_target_pairs={{0,16},{2,18},{4,20},{6,22},{8,24},{10,26},{12,28},{14,30},{16,0},... | collective-permute-start | bytes 196616 | tf_op jit(solution)/shard_map/ppermute | solution.py:1002
  133.2 12.5 %collective-permute-start.36 = (bf16[32,1024]{1,0:T(8,128)(2,1)S(1)}, bf16[32,1024]{1,0:T(8,128)(2,1)S(1)}, u32[]{:S(2)}, u32[]{:S(2)}) collective-permute-start(bf16[32,1024]{1,0:T(8,128)(2,1)S(1)} %get-tuple-element.156), channel_id=1, source_target_pairs={{0,24},{2,26},{4,28},{6,30},{8,16},{10,18},{12,20},{14,22},{16,8},... | collective-permute-start | bytes 196616 | tf_op jit(solution)/shard_map/ppermute | solution.py:1002
  134.9 1.0 copy-start.8
  139.6 1.0 copy-start.9
  140.6 11.4 %copy-start.12 = (f32[1,32]{1,0:T(1,128)S(1)}, f32[1,32]{1,0:T(1,128)}, u32[]{:S(2)}) copy-start(f32[1,32]{1,0:T(1,128)} %get-tuple-element.162) | copy-start | bytes 388
  141.3 6.2 %collective-permute-start.31 = (bf16[48,768]{1,0:T(8,128)(2,1)S(1)}, bf16[48,768]{1,0:T(8,128)(2,1)S(1)}, u32[]{:S(2)}, u32[]{:S(2)}) collective-permute-start(bf16[48,768]{1,0:T(8,128)(2,1)S(1)} %get-tuple-element.150), channel_id=1, source_target_pairs={{0,8},{2,10},{4,12},{6,14},{8,0},{10,2},{12,4},{14,6},{16,24},{18,... | collective-permute-start | bytes 221192 | tf_op jit(solution)/shard_map/ppermute | solution.py:1002
  141.3 6.8 %collective-permute-start.32 = (bf16[48,768]{1,0:T(8,128)(2,1)S(1)}, bf16[48,768]{1,0:T(8,128)(2,1)S(1)}, u32[]{:S(2)}, u32[]{:S(2)}) collective-permute-start(bf16[48,768]{1,0:T(8,128)(2,1)S(1)} %get-tuple-element.151), channel_id=1, source_target_pairs={{0,16},{2,18},{4,20},{6,22},{8,24},{10,26},{12,28},{14,30},{16,0},... | collective-permute-start | bytes 221192 | tf_op jit(solution)/shard_map/ppermute | solution.py:1002
  144.0 6.2 %collective-permute-start.33 = (bf16[48,768]{1,0:T(8,128)(2,1)S(1)}, bf16[48,768]{1,0:T(8,128)(2,1)S(1)}, u32[]{:S(2)}, u32[]{:S(2)}) collective-permute-start(bf16[48,768]{1,0:T(8,128)(2,1)S(1)} %get-tuple-element.152), channel_id=1, source_target_pairs={{0,24},{2,26},{4,28},{6,30},{8,16},{10,18},{12,20},{14,22},{16,8},... | collective-permute-start | bytes 221192 | tf_op jit(solution)/shard_map/ppermute | solution.py:1002
  145.7 0.9 copy-start.11
  150.1 1.0 copy-start.7

commit v5 on v4

--- a/solution.py
+++ b/solution.py
@@ -343,7 +343,7 @@
 F32 = jnp.float32
 BF16 = jnp.bfloat16
 VMEM_LIMIT = 16 * 1024 * 1024
-TIMES = {'hold': 5000, 'project': 80, 'feed_grad': 40, 'halve': 400, 'unpack': 150, 'feed_sum': 150, 'back_rows': 80, 'feed_terms': 5, 'share_twin': 400, 'join_in': 5}
+TIMES = {'hold': 5000, 'feed_grad': 40, 'halve': 400, 'unpack': 150, 'feed_sum': 150, 'feed_terms': 5, 'share_twin': 400, 'join_in': 5, 'attend': 20, 'grads': 40}
 
 VEC = 16
 
@@ -374,6 +374,14 @@
 
 def raw(x):
     return x[0] if isinstance(x, (Far, Near)) else x
+
+
+def placed(x):
+    if isinstance(x, Far):
+        return pltpu.with_memory_space_constraint(x[0], pltpu.HBM)
+    if isinstance(x, Near):
+        return pltpu.with_memory_space_constraint(x[0], pltpu.VMEM)
+    return x
 
 
 def spot():
@@ -386,12 +394,7 @@
     loose = pl.BlockSpec(memory_space=pl.ANY)
     arrays, specs = [], []
     for x in operands:
-        if isinstance(x, Far):
-            arrays.append(pltpu.with_memory_space_constraint(x[0], pltpu.HBM))
-        elif isinstance(x, Near):
-            arrays.append(pltpu.with_memory_space_constraint(x[0], pltpu.VMEM))
-        else:
-            arrays.append(x)
+        arrays.append(placed(x))
         if arrays[-1].dtype == jnp.int32 and arrays[-1].ndim == 1:
             specs.append(pl.BlockSpec(memory_space=pltpu.SMEM))
         else:
@@ -421,7 +424,7 @@
         cost_estimate=pl.CostEstimate(
             flops=TIMES.get(name, 0) * 115_000_000, bytes_accessed=0, transcendentals=0
         ),
-    )(*arrays, *map(raw, after))
+    )(*arrays, *map(placed, after))
     return [
         near(x) if isinstance(shape, Near) else x for x, shape in zip(results, out_shapes)
     ]
@@ -1035,7 +1038,7 @@
         results = call(
             kernel, out_shapes, scratch, *operands, after=(*after, *last), loose_in=loose_in
         )
-        last[:] = results[:1]
+        last[:] = [far(results[0])] if isinstance(out_shapes[0], Far) else results[:1]
         return results
     (token_block,) = run(
         pack_kernel,
@@ -1065,7 +1068,13 @@
         far(cotangent[0]),
         after=token_lines[1:3],
     )
-    cot_lines = with_lines([cot_own] * LINES)
+    cot_two = over_lines(raw(cot_own), 2)
+    cot_lines = [
+        cot_own,
+        near(over_lines(raw(cot_own), 1)),
+        near(cot_two),
+        near(over_lines(cot_two, 1)),
+    ]
     qkv, in_rows, w_out_full, down_rows, vectors = run(
         assemble_kernel,
         [
@@ -1103,6 +1112,19 @@
         ln_low, in_rows, vectors, down_rows,
     )
     low_received = near(over_lines(raw(low_send), 1))
+    qk_rows, kq_rows, value_rows, attended, lse, numbers = run(
+        attend_kernel,
+        [
+            near((length, 128), BF16),
+            near((length, 128), BF16),
+            near((length, 64), BF16),
+            near((length, 64), F32),
+            near((length, 1), F32),
+            near((32, 128), jnp.int32),
+        ],
+        [pltpu.VMEM((length, 128), BF16), table, one_copy],
+        *slots_in, *rotation,
+    )
     *back_slots, cot_rows = run(
         back_rows_kernel,
         [near((line_rows // 2, 128), BF16)] * 4 + [near((line_rows, width), BF16)],
@@ -1123,19 +1145,6 @@
         cot_rows, hidden, in_rows, down_rows,
     )
     grad_received = near(over_lines(raw(grad_send), 1))
-    qk_rows, kq_rows, value_rows, attended, lse, numbers = run(
-        attend_kernel,
-        [
-            near((length, 128), BF16),
-            near((length, 128), BF16),
-            near((length, 64), BF16),
-            near((length, 64), F32),
-            near((length, 1), F32),
-            near((32, 128), jnp.int32),
-        ],
-        [pltpu.VMEM((length, 128), BF16), table, one_copy],
-        *slots_in, *rotation,
-    )
     feed_send, feed_keep = run(
         feed_terms_kernel,
         [near((4 * block, width), BF16), near((4 * block, width), F32)],
@@ -1207,7 +1216,7 @@
     qkv_sums = with_places(qkv_blocks)
     grad_down, grad_b_in, grad_b, *in_slots = run(
         feed_sum_kernel,
-        [((128, width), F32), ((1, 128), F32), ((1, 32), F32), near((32, width), F32)]
+        [far((128, width), F32), ((1, 128), F32), ((1, 32), F32), near((32, width), F32)]
         + [near((32, width), BF16)] * 3,
         [],
         *feed_in,
@@ -1215,23 +1224,23 @@
     in_parts = with_lines(in_slots)
     layer_out, grad_tokens = run(
         tokens_kernel,
-        [((rows, width), BF16), ((rows, width), BF16)],
+        [far((rows, width), BF16), far((rows, width), BF16)],
         [],
         mixed, *mixed_in, qkv, w_out_full, low_own, low_rest, grad_own, grad_rest,
-        token_block, cot_rows, vectors,
+        far(tokens[0]), cot_rows, vectors,
     )
     grad_out, grad_qv, *qkv_parts = run(
         grad_sum_kernel,
-        [((32, width), F32), ((2, 32), F32), near((32 + VEC, qkv_cols), F32)]
+        [far((32, width), F32), far((2, 32), F32), near((32 + VEC, qkv_cols), F32)]
         + [near((32 + VEC, qkv_cols), BF16)] * 3,
         [],
         *qkv_sums,
     )
     qkv_parts = with_lines(qkv_parts)
-    (grad_in,) = run(join_in_kernel, [((32, feed), F32)], [], *in_parts)
+    (grad_in,) = run(join_in_kernel, [far((32, feed), F32)], [], *in_parts)
     grad_qkv, grad_gain, grad_shift = run(
         join_qkv_kernel,
-        [((32, 3 * width), F32), ((1, 32), F32), ((1, 32), F32)],
+        [far((32, 3 * width), F32), ((1, 32), F32), ((1, 32), F32)],
         [pltpu.VMEM((VEC, 32), F32)],
         *qkv_parts,
     )

time: 153 us -> 149 us (0.974)
  waiting for transfers between devices: 46.4 us -> 40.9 us
  starting transfers between devices: 45.9 us -> 51.3 us
  local copies, waits for them, and re-layouts: 5.13 us -> 1.18 us
    ppermute x19, waiting for transfers between devices: 24.3 us -> 18.9 us  [over_lines(): return lax.ppermute(x, 'ctx', [(i, i ^ k * ACROSS) for i in positions])]
    ppermute x19, starting transfers between devices: 26.2 us -> 31.3 us  [over_lines(): return lax.ppermute(x, 'ctx', [(i, i ^ k * ACROSS) for i in positions])]
    unnamed x27 -> x13, local copies, waits for them, and re-layouts: 5.13 us -> 1.18 us
  transfers between devices with their start and end apart: 37 -> 37, of which waited for: 12 -> 14; matrix products, arithmetic and copies ran while one was open for 0% -> 0% of each run, Pallas kernels for 34% -> 35%
where the time goes in v5:
time: 149 us; the launch traced here: 148 us
  Pallas kernels  54 us (36%)
  starting transfers between devices  51.3 us (34%)
  waiting for transfers between devices  40.9 us (27%)
    pallas_call x22, Pallas kernels, call(): pl.pallas_call(body, name=name, out_shape=outs, in_specs=specs + [loose]...  54 us
    ppermute x19, starting transfers between devices, over_lines(): return lax.ppermute(x, 'ctx', [(i, i ^ k * ACROSS) for i in positions])  31.3 us
    ppermute x15, waiting for transfers between devices, over_places(): return lax.ppermute(x, 'ctx', [(i, i ^ j) for i in positions])  19.9 us
    ppermute x15, starting transfers between devices, over_places(): return lax.ppermute(x, 'ctx', [(i, i ^ j) for i in positions])  19.7 us
    ppermute x19, waiting for transfers between devices, over_lines(): return lax.ppermute(x, 'ctx', [(i, i ^ k * ACROSS) for i in positions])  18.9 us
  transfers between devices with their start and end apart: 37, of which 14 were waited for; matrix products, arithmetic and copies ran while one was open for 0% of the time, Pallas kernels for 35%

profile of v5, /device:TPU:0, one launch (start us, length us, event | category | flops | bytes accessed | tf_op | source)
XLA Modules:
  0.0 148.2 jit_solution(9696761907097612889)
XLA Ops:
  0.7 0.6 copy-done.4
  1.3 1.0 pack.1.refs_10_.refs_0_
  2.3 4.1 %collective-permute-start.1 = (bf16[144,1024]{1,0:T(8,128)(2,1)S(1)}, bf16[144,1024]{1,0:T(8,128)(2,1)}, u32[]{:S(2)}, u32[]{:S(2)}) collective-permute-start(bf16[144,1024]{1,0:T(8,128)(2,1)S(1)} %pack.1.refs_10_.refs_0_), channel_id=1, source_target_pairs={{0,16},{2,18},{4,20},{6,22},{8,24},{10,26},{12,28},{14,30},{16,0},... | collective-permute-start | bytes 884744 | tf_op jit(solution)/shard_map/ppermute | solution.py:1005
  6.4 1.6 %collective-permute-start = (bf16[144,1024]{1,0:T(8,128)(2,1)S(1)}, bf16[144,1024]{1,0:T(8,128)(2,1)S(1)}, u32[]{:S(2)}, u32[]{:S(2)}) collective-permute-start(bf16[144,1024]{1,0:T(8,128)(2,1)S(1)} %pack.1.refs_10_.refs_0_), channel_id=1, source_target_pairs={{0,8},{2,10},{4,12},{6,14},{8,0},{10,2},{12,4},{14,6},{16,24},{18,... | collective-permute-start | bytes 884744 | tf_op jit(solution)/shard_map/ppermute | solution.py:1005
  8.0 6.9 %prepare.1.refs_3_.refs_0_ = bf16[3600,1024]{1,0:T(8,128)(2,1)} custom-call(bf16[512,3072]{1,0:T(8,128)(2,1)} %refs_0_.1, bf16[512,4096]{1,0:T(8,128)(2,1)} %refs_1_.1, bf16[512,1024]{1,0:T(8,128)(2,1)} %refs_2_.1, bf16[2048,1024]{1,0:T(8,128)(2,1)} %refs_3_.1, bf16[512]{0:T(512)(128)(2,1)} %refs_4_.2, bf16[512]{0:T(512)(128)(2,1)} %refs_5_.2, ...), custom_call_target="tpu_custom_call" | custom-call | tf_op jit(solution)/shard_map/prepare/pallas_call | solution.py:416
  15.0 5.0 %collective-permute-done.1.refs_2_ = bf16[144,1024]{1,0:T(8,128)(2,1)} collective-permute-done((bf16[144,1024]{1,0:T(8,128)(2,1)S(1)}, bf16[144,1024]{1,0:T(8,128)(2,1)}, u32[]{:S(2)}, u32[]{:S(2)}) %collective-permute-start.1) | collective-permute-done | bytes 294944 | tf_op jit(solution)/shard_map/ppermute | solution.py:1005
  19.9 0.5 collective-permute-start.6
  20.5 1.0 hold.1.refs_2_.refs_0_
  21.4 3.6 %collective-permute-start.3 = (bf16[128,1024]{1,0:T(8,128)(2,1)S(1)}, bf16[128,1024]{1,0:T(8,128)(2,1)S(1)}, u32[]{:S(2)}, u32[]{:S(2)}) collective-permute-start(bf16[128,1024]{1,0:T(8,128)(2,1)S(1)} %hold.1.refs_2_.refs_0_), channel_id=1, source_target_pairs={{0,16},{2,18},{4,20},{6,22},{8,24},{10,26},{12,28},{14,30},{16,0},... | collective-permute-start | bytes 786440 | tf_op jit(solution)/shard_map/ppermute | solution.py:1005
  25.0 2.0 %collective-permute-done.5.refs_1_ = bf16[3600,1024]{1,0:T(8,128)(2,1)} collective-permute-done((bf16[3600,1024]{1,0:T(8,128)(2,1)}, bf16[3600,1024]{1,0:T(8,128)(2,1)}, u32[]{:S(2)}, u32[]{:S(2)}) %collective-permute-start.5) | collective-permute-done | bytes 7372832 | tf_op jit(solution)/shard_map/ppermute | solution.py:1011
  27.0 4.8 %assemble.1 = (bf16[1024,3072]{1,0:T(8,128)(2,1)S(1)}, bf16[1024,1024]{1,0:T(8,128)(2,1)S(1)}, bf16[1024,1024]{1,0:T(8,128)(2,1)S(1)}, bf16[1024,1024]{1,0:T(8,128)(2,1)S(1)}, f32[32,512]{1,0:T(8,128)S(1)}) custom-call(bf16[3600,1024]{1,0:T(8,128)(2,1)} %prepare.1.refs_3_.refs_0_, bf16[3600,1024]{1,0:T(8,128)(2,1)} %collective-permute-done.5.refs_1_, ...), custom_call_target="tpu_custom_call" | custom-call | tf_op jit(solution)/shard_map/assemble/pallas_call | solution.py:416
  31.8 1.8 %collective-permute-done.6.refs_3_ = bf16[144,1024]{1,0:T(8,128)(2,1)} collective-permute-done((bf16[144,1024]{1,0:T(8,128)(2,1)}, bf16[144,1024]{1,0:T(8,128)(2,1)}, u32[]{:S(2)}, u32[]{:S(2)}) %collective-permute-start.6) | collective-permute-done | bytes 294944 | tf_op jit(solution)/shard_map/ppermute | solution.py:1005
  33.6 3.2 %project.1 = (bf16[784,128]{1,0:T(8,128)(2,1)S(1)}, bf16[784,128]{1,0:T(8,128)(2,1)S(1)}, bf16[784,128]{1,0:T(8,128)(2,1)S(1)}, bf16[784,128]{1,0:T(8,128)(2,1)S...) custom-call(bf16[144,1024]{1,0:T(8,128)(2,1)S(1)} %copy-done.1, ...), custom_call_target="tpu_custom_call" | custom-call | tf_op jit(solution)/shard_map/project/pallas_call | solution.py:416
  36.9 1.3 collective-permute-start.7
  38.2 1.5 %collective-permute-start.8 = (bf16[784,128]{1,0:T(8,128)(2,1)S(1)}, bf16[784,128]{1,0:T(8,128)(2,1)S(1)}, u32[]{:S(2)}, u32[]{:S(2)}) collective-permute-start(bf16[784,128]{1,0:T(8,128)(2,1)S(1)} %get-tuple-element.93), channel_id=1, source_target_pairs={{0,4},{2,6},{4,0},{6,2},{8,12},{10,14},{12,8},{14,10},{16,20},{18,... | collective-permute-start | bytes 602120 | tf_op jit(solution)/shard_map/ppermute | solution.py:1008
  39.7 0.7 collective-permute-start.9
  40.4 2.0 %collective-permute-start.4 = (bf16[128,1024]{1,0:T(8,128)(2,1)S(1)}, bf16[128,1024]{1,0:T(8,128)(2,1)S(1)}, u32[]{:S(2)}, u32[]{:S(2)}) collective-permute-start(bf16[128,1024]{1,0:T(8,128)(2,1)S(1)} %collective-permute-done.3.refs_2_), channel_id=1, source_target_pairs={{0,8},{2,10},{4,12},{6,14},{8,0},{10,2},{12,4},{14,6},{16,24},{18,... | collective-permute-start | bytes 786440 | tf_op jit(solution)/shard_map/ppermute | solution.py:1005
  42.5 2.7 %feed.1 = (f32[512,1024]{1,0:T(8,128)S(1)}, bf16[1024,512]{1,0:T(8,128)(2,1)S(1)}, f32[256,1024]{1,0:T(8,128)S(1)}, bf16[256,1024]{1,0:T(8,128)(2,1)S(1)}) custom-call(bf16[512,1024]{1,0:T(8,128)(2,1)S(1)} %get-tuple-element.95.refs_0_, bf16[1024,1024]{1,0:T(8,128)(2,1)S(1)} %get-tuple-element.96.refs_1_.refs_2_, ...), custom_call_target="tpu_custom_call" | custom-call | tf_op jit(solution)/shard_map/feed/pallas_call | solution.py:416
  45.3 2.7 %collective-permute-done.8.refs_2_ = bf16[784,128]{1,0:T(8,128)(2,1)S(1)} collective-permute-done((bf16[784,128]{1,0:T(8,128)(2,1)S(1)}, bf16[784,128]{1,0:T(8,128)(2,1)S(1)}, u32[]{:S(2)}, u32[]{:S(2)}) %collective-permute-start.8) | collective-permute-done | bytes 200736 | tf_op jit(solution)/shard_map/ppermute | solution.py:1008
  48.0 6.1 %attend.1 = (bf16[2048,128]{1,0:T(8,128)(2,1)S(1)}, bf16[2048,128]{1,0:T(8,128)(2,1)S(1)}, bf16[2048,64]{1,0:T(8,128)(2,1)S(1)}, f32[2048,64]{1,0:T(8,128)S(1)},...) custom-call(bf16[784,128]{1,0:T(8,128)(2,1)S(1)} %get-tuple-element.91.refs_4_.refs_0_, ...), custom_call_target="tpu_custom_call" | custom-call | flops 2300000000 | tf_op jit(solution)/shard_map/attend/pallas_call | solution.py:416
  54.1 1.2 collective-permute-done.4.refs_3_
  55.3 0.6 back_rows.1
  56.0 1.3 collective-permute-start.10
  57.3 1.5 %collective-permute-start.11 = (bf16[256,128]{1,0:T(8,128)(2,1)S(1)}, bf16[256,128]{1,0:T(8,128)(2,1)S(1)}, u32[]{:S(2)}, u32[]{:S(2)}) collective-permute-start(bf16[256,128]{1,0:T(8,128)(2,1)S(1)} %get-tuple-element.102), channel_id=1, source_target_pairs={{0,4},{2,6},{4,0},{6,2},{8,12},{10,14},{12,8},{14,10},{16,20},{18,... | collective-permute-start | bytes 196616 | tf_op jit(solution)/shard_map/ppermute | solution.py:1008
  58.8 0.7 collective-permute-start.12
  59.5 3.3 %feed_grad.1 = (bf16[512,1024]{1,0:T(8,128)(2,1)S(1)}, f32[8,1024]{1,0:T(8,128)S(1)}, f32[512,1024]{1,0:T(8,128)S(1)}, f32[256,1024]{1,0:T(8,128)S(1)}, bf16[256,1024]{1,0:T(8,128)(2,1)S(1)}) custom-call(bf16[512,1024]{1,0:T(8,128)(2,1)S(1)} %get-tuple-element.109.refs_0_.refs_6_.refs_11_, f32[512,1024]{1,0:T(8,128)S(1)} %get-tuple-element.98.refs_6_.refs_1_, ...), custom_call_target="tpu_custom_call" | custom-call | flops 4600000000 | tf_op jit(solution)/shard_map/feed_grad/pallas_call | solution.py:416
  62.9 3.5 %feed_terms.1 = (bf16[1088,1024]{1,0:T(8,128)(2,1)S(1)}, f32[1088,1024]{1,0:T(8,128)S(1)}) custom-call(bf16[512,1024]{1,0:T(8,128)(2,1)S(1)} %get-tuple-element.109.refs_0_.refs_6_.refs_11_, bf16[1024,512]{1,0:T(8,128)(2,1)S(1)} %get-tuple-element.110.refs_1_, bf16[1024,512]{1,0:T(8,128)(2,1)S(1)} %get-tuple-element.111.refs_2_.refs_3_, ...), custom_call_target="tpu_custom_call" | custom-call | flops 575000000 | tf_op jit(solution)/shard_map/feed_terms/pallas_call | solution.py:416
  66.6 8.3 %attend_back.1 = (bf16[1024,128]{1,0:T(8,128)(2,1)S(1)}, bf16[1024,128]{1,0:T(8,128)(2,1)S(1)}, bf16[1024,128]{1,0:T(8,128)(2,1)S(1)}, bf16[1024,128]{1,0:T(8,128)(2,1)S(1)}, f32[8,128]{1,0:T(8,128)S(1)}) custom-call(bf16[256,128]{1,0:T(8,128)(2,1)S(1)} %get-tuple-element.100.refs_4_.refs_0_, bf16[256,128]{1,0:T(8,128)(2,1)S(1)} %collective-permute-done.10.refs_1_, ...), custom_call_target="tpu_custom_call" | custom-call | tf_op jit(solution)/shard_map/attend_back/pallas_call | solution.py:416
  74.9 1.3 collective-permute-start.13
  76.2 1.5 %collective-permute-start.14 = (bf16[1024,128]{1,0:T(8,128)(2,1)S(1)}, bf16[1024,128]{1,0:T(8,128)(2,1)S(1)}, u32[]{:S(2)}, u32[]{:S(2)}) collective-permute-start(bf16[1024,128]{1,0:T(8,128)(2,1)S(1)} %get-tuple-element.117), channel_id=1, source_target_pairs={{0,4},{2,6},{4,0},{6,2},{8,12},{10,14},{12,8},{14,10},{16,20},{18,... | collective-permute-start | bytes 786440 | tf_op jit(solution)/shard_map/ppermute | solution.py:1008
  77.7 0.7 collective-permute-start.15
  78.5 3.1 %collective-permute-start.21 = (bf16[128,1024]{1,0:T(8,128)(2,1)S(1)}, bf16[128,1024]{1,0:T(8,128)(2,1)S(1)}, u32[]{:S(2)}, u32[]{:S(2)}) collective-permute-start(bf16[128,1024]{1,0:T(8,128)(2,1)S(1)} %get-tuple-element.129), channel_id=1, source_target_pairs={{0,16},{2,18},{4,20},{6,22},{8,24},{10,26},{12,28},{14,30},{16,0},... | collective-permute-start | bytes 786440 | tf_op jit(solution)/shard_map/ppermute | solution.py:1005
  81.8 2.3 %collective-permute-done.13.refs_1_ = bf16[1024,128]{1,0:T(8,128)(2,1)S(1)} collective-permute-done((bf16[1024,128]{1,0:T(8,128)(2,1)S(1)}, bf16[1024,128]{1,0:T(8,128)(2,1)S(1)}, u32[]{:S(2)}, u32[]{:S(2)}) %collective-permute-start.13) | collective-permute-done | bytes 262176 | tf_op jit(solution)/shard_map/ppermute | solution.py:1008
  84.0 3.1 %collective-permute-start.22 = (bf16[128,1024]{1,0:T(8,128)(2,1)S(1)}, bf16[128,1024]{1,0:T(8,128)(2,1)S(1)}, u32[]{:S(2)}, u32[]{:S(2)}) collective-permute-start(bf16[128,1024]{1,0:T(8,128)(2,1)S(1)} %get-tuple-element.130), channel_id=1, source_target_pairs={{0,16},{2,18},{4,20},{6,22},{8,24},{10,26},{12,28},{14,30},{16,0},... | collective-permute-start | bytes 786440 | tf_op jit(solution)/shard_map/ppermute | solution.py:1005
  87.1 3.1 %collective-permute-done.14.refs_2_ = bf16[1024,128]{1,0:T(8,128)(2,1)S(1)} collective-permute-done((bf16[1024,128]{1,0:T(8,128)(2,1)S(1)}, bf16[1024,128]{1,0:T(8,128)(2,1)S(1)}, u32[]{:S(2)}, u32[]{:S(2)}) %collective-permute-start.14) | collective-permute-done | bytes 262176 | tf_op jit(solution)/shard_map/ppermute | solution.py:1008
  90.2 0.9 unpack.1
  91.2 2.1 %collective-permute-start.18 = (bf16[128,1024]{1,0:T(8,128)(2,1)S(1)}, bf16[128,1024]{1,0:T(8,128)(2,1)S(1)}, u32[]{:S(2)}, u32[]{:S(2)}) collective-permute-start(bf16[128,1024]{1,0:T(8,128)(2,1)S(1)} %get-tuple-element.126), channel_id=1, source_target_pairs={{0,8},{2,10},{4,12},{6,14},{8,0},{10,2},{12,4},{14,6},{16,24},{18,... | collective-permute-start | bytes 786440 | tf_op jit(solution)/shard_map/ppermute | solution.py:1005
  93.2 3.0 %grads.1 = (bf16[704,768]{1,0:T(8,128)(2,1)S(1)}, f32[704,768]{1,0:T(8,128)S(1)}) custom-call(bf16[512,1024]{1,0:T(8,128)(2,1)S(1)} %get-tuple-element.125.refs_0_.refs_8_, f32[512,1024]{1,0:T(8,128)S(1)} %get-tuple-element.132.refs_1_, f32[512,1024]{1,0:T(8,128)S(1)} %get-tuple-element.133.refs_2_, ...), custom_call_target="tpu_custom_call" | custom-call | flops 4600000000 | tf_op jit(solution)/shard_map/grads/pallas_call | solution.py:416
  96.3 0.4 share_twin.2
  96.7 1.3 collective-permute-start.24
  97.9 2.2 %collective-permute-done.21.refs_7_ = bf16[128,1024]{1,0:T(8,128)(2,1)S(1)} collective-permute-done((bf16[128,1024]{1,0:T(8,128)(2,1)S(1)}, bf16[128,1024]{1,0:T(8,128)(2,1)S(1)}, u32[]{:S(2)}, u32[]{:S(2)}) %collective-permute-start.21) | collective-permute-done | bytes 262176 | tf_op jit(solution)/shard_map/ppermute | solution.py:1005
  100.1 1.3 collective-permute-start.25
  101.5 1.4 collective-permute-start.26
  102.9 0.2 share_twin.3
  103.1 1.6 %collective-permute-done.22.refs_9_ = bf16[128,1024]{1,0:T(8,128)(2,1)S(1)} collective-permute-done((bf16[128,1024]{1,0:T(8,128)(2,1)S(1)}, bf16[128,1024]{1,0:T(8,128)(2,1)S(1)}, u32[]{:S(2)}, u32[]{:S(2)}) %collective-permute-start.22) | collective-permute-done | bytes 262176 | tf_op jit(solution)/shard_map/ppermute | solution.py:1005
  104.7 4.6 %collective-permute-done.18.refs_1_ = bf16[128,1024]{1,0:T(8,128)(2,1)S(1)} collective-permute-done((bf16[128,1024]{1,0:T(8,128)(2,1)S(1)}, bf16[128,1024]{1,0:T(8,128)(2,1)S(1)}, u32[]{:S(2)}, u32[]{:S(2)}) %collective-permute-start.18) | collective-permute-done | bytes 262176 | tf_op jit(solution)/shard_map/ppermute | solution.py:1005
  109.4 2.4 %collective-permute-start.20 = (bf16[128,1024]{1,0:T(8,128)(2,1)S(1)}, bf16[128,1024]{1,0:T(8,128)(2,1)S(1)}, u32[]{:S(2)}, u32[]{:S(2)}) collective-permute-start(bf16[128,1024]{1,0:T(8,128)(2,1)S(1)} %get-tuple-element.128), channel_id=1, source_target_pairs={{0,24},{2,26},{4,28},{6,30},{8,16},{10,18},{12,20},{14,22},{16,8},... | collective-permute-start | bytes 786440 | tf_op jit(solution)/shard_map/ppermute | solution.py:1005
  111.7 0.4 collective-permute-done.24.refs_1_
  112.2 1.2 collective-permute-start.28
  113.4 11.4 %collective-permute-done.25.refs_2_ = bf16[272,1024]{1,0:T(8,128)(2,1)S(1)} collective-permute-done((bf16[272,1024]{1,0:T(8,128)(2,1)S(1)}, bf16[272,1024]{1,0:T(8,128)(2,1)S(1)}, u32[]{:S(2)}, u32[]{:S(2)}) %collective-permute-start.25) | collective-permute-done | bytes 557088 | tf_op jit(solution)/shard_map/ppermute | solution.py:1008
  124.8 2.5 %collective-permute-start.29 = (bf16[176,768]{1,0:T(8,128)(2,1)S(1)}, bf16[176,768]{1,0:T(8,128)(2,1)S(1)}, u32[]{:S(2)}, u32[]{:S(2)}) collective-permute-start(bf16[176,768]{1,0:T(8,128)(2,1)S(1)} %get-tuple-element.147), channel_id=1, source_target_pairs={{0,4},{2,6},{4,0},{6,2},{8,12},{10,14},{12,8},{14,10},{16,20},{18,... | collective-permute-start | bytes 811016 | tf_op jit(solution)/shard_map/ppermute | solution.py:1008
  127.3 1.3 collective-permute-start.30
  128.6 1.0 feed_sum.1
  129.6 1.5 %collective-permute-start.35 = (bf16[32,1024]{1,0:T(8,128)(2,1)S(1)}, bf16[32,1024]{1,0:T(8,128)(2,1)S(1)}, u32[]{:S(2)}, u32[]{:S(2)}) collective-permute-start(bf16[32,1024]{1,0:T(8,128)(2,1)S(1)} %get-tuple-element.155), channel_id=1, source_target_pairs={{0,16},{2,18},{4,20},{6,22},{8,24},{10,26},{12,28},{14,30},{16,0},... | collective-permute-start | bytes 196616 | tf_op jit(solution)/shard_map/ppermute | solution.py:1005
  131.1 2.9 %collective-permute-start.36 = (bf16[32,1024]{1,0:T(8,128)(2,1)S(1)}, bf16[32,1024]{1,0:T(8,128)(2,1)S(1)}, u32[]{:S(2)}, u32[]{:S(2)}) collective-permute-start(bf16[32,1024]{1,0:T(8,128)(2,1)S(1)} %get-tuple-element.156), channel_id=1, source_target_pairs={{0,24},{2,26},{4,28},{6,30},{8,16},{10,18},{12,20},{14,22},{16,8},... | collective-permute-start | bytes 196616 | tf_op jit(solution)/shard_map/ppermute | solution.py:1005
  134.0 4.5 %tokens.1 = (bf16[128,1024]{1,0:T(8,128)(2,1)}, bf16[128,1024]{1,0:T(8,128)(2,1)}) custom-call(bf16[512,1024]{1,0:T(8,128)(2,1)S(1)} %get-tuple-element.125.refs_0_.refs_8_, bf16[128,1024]{1,0:T(8,128)(2,1)S(1)} %collective-permute-done.18.refs_1_, bf16[128,1024]{1,0:T(8,128)(2,1)S(1)} %collective-permute-done.19.refs_2_, ...), custom_call_target="tpu_custom_call" | custom-call | tf_op jit(solution)/shard_map/tokens/pallas_call | solution.py:416
  138.5 0.7 grad_sum.1
  139.2 1.5 %collective-permute-start.32 = (bf16[48,768]{1,0:T(8,128)(2,1)S(1)}, bf16[48,768]{1,0:T(8,128)(2,1)S(1)}, u32[]{:S(2)}, u32[]{:S(2)}) collective-permute-start(bf16[48,768]{1,0:T(8,128)(2,1)S(1)} %get-tuple-element.151), channel_id=1, source_target_pairs={{0,16},{2,18},{4,20},{6,22},{8,24},{10,26},{12,28},{14,30},{16,0},... | collective-permute-start | bytes 221192 | tf_op jit(solution)/shard_map/ppermute | solution.py:1005
  140.7 2.9 %collective-permute-start.33 = (bf16[48,768]{1,0:T(8,128)(2,1)S(1)}, bf16[48,768]{1,0:T(8,128)(2,1)S(1)}, u32[]{:S(2)}, u32[]{:S(2)}) collective-permute-start(bf16[48,768]{1,0:T(8,128)(2,1)S(1)} %get-tuple-element.152), channel_id=1, source_target_pairs={{0,24},{2,26},{4,28},{6,30},{8,16},{10,18},{12,20},{14,22},{16,8},... | collective-permute-start | bytes 221192 | tf_op jit(solution)/shard_map/ppermute | solution.py:1005
  143.6 0.8 join_in.1.refs_4_
  144.5 1.6 %collective-permute-done.32.refs_2_ = bf16[48,768]{1,0:T(8,128)(2,1)S(1)} collective-permute-done((bf16[48,768]{1,0:T(8,128)(2,1)S(1)}, bf16[48,768]{1,0:T(8,128)(2,1)S(1)}, u32[]{:S(2)}, u32[]{:S(2)}) %collective-permute-start.32) | collective-permute-done | bytes 73760 | tf_op jit(solution)/shard_map/ppermute | solution.py:1005
  146.0 0.9 collective-permute-done.33.refs_3_
  146.9 0.8 join_qkv.1
  147.7 0.5 copy.28
  (45 shorter events, 0.7 us)
Async XLA Ops:
  0.6 0.7 copy-start.4
  2.3 12.6 %copy-start = (bf16[144,1024]{1,0:T(8,128)(2,1)}, bf16[144,1024]{1,0:T(8,128)(2,1)S(1)}, u32[]{:S(2)}) copy-start(bf16[144,1024]{1,0:T(8,128)(2,1)S(1)} %pack.1.refs_10_.refs_0_) | copy-start | bytes 884740
  2.3 17.6 %collective-permute-start.1 = (bf16[144,1024]{1,0:T(8,128)(2,1)S(1)}, bf16[144,1024]{1,0:T(8,128)(2,1)}, u32[]{:S(2)}, u32[]{:S(2)}) collective-permute-start(bf16[144,1024]{1,0:T(8,128)(2,1)S(1)} %pack.1.refs_10_.refs_0_), channel_id=1, source_target_pairs={{0,16},{2,18},{4,20},{6,22},{8,24},{10,26},{12,28},{14,30},{16,0},... | collective-permute-start | bytes 884744 | tf_op jit(solution)/shard_map/ppermute | solution.py:1005
  6.4 14.1 %collective-permute-start = (bf16[144,1024]{1,0:T(8,128)(2,1)S(1)}, bf16[144,1024]{1,0:T(8,128)(2,1)S(1)}, u32[]{:S(2)}, u32[]{:S(2)}) collective-permute-start(bf16[144,1024]{1,0:T(8,128)(2,1)S(1)} %pack.1.refs_10_.refs_0_), channel_id=1, source_target_pairs={{0,8},{2,10},{4,12},{6,14},{8,0},{10,2},{12,4},{14,6},{16,24},{18,... | collective-permute-start | bytes 884744 | tf_op jit(solution)/shard_map/ppermute | solution.py:1005
  14.9 12.1 %collective-permute-start.5 = (bf16[3600,1024]{1,0:T(8,128)(2,1)}, bf16[3600,1024]{1,0:T(8,128)(2,1)}, u32[]{:S(2)}, u32[]{:S(2)}) collective-permute-start(bf16[3600,1024]{1,0:T(8,128)(2,1)} %prepare.1.refs_3_.refs_0_), channel_id=1, source_target_pairs={{0,1},{1,0},{2,3},{3,2},{4,5},{5,4},{6,7},{7,6},{8,9},{9,8},{10,11... | collective-permute-start | bytes 22118408 | tf_op jit(solution)/shard_map/ppermute | solution.py:1011
  19.9 13.7 %collective-permute-start.6 = (bf16[144,1024]{1,0:T(8,128)(2,1)}, bf16[144,1024]{1,0:T(8,128)(2,1)}, u32[]{:S(2)}, u32[]{:S(2)}) collective-permute-start(bf16[144,1024]{1,0:T(8,128)(2,1)} %collective-permute-done.1.refs_2_), channel_id=1, source_target_pairs={{0,8},{2,10},{4,12},{6,14},{8,0},{10,2},{12,4},{14,6},{16,24},{18,... | collective-permute-start | bytes 884744 | tf_op jit(solution)/shard_map/ppermute | solution.py:1005
  21.4 12.2 %copy-start.1 = (bf16[144,1024]{1,0:T(8,128)(2,1)S(1)}, bf16[144,1024]{1,0:T(8,128)(2,1)}, u32[]{:S(2)}) copy-start(bf16[144,1024]{1,0:T(8,128)(2,1)} %copy-done) | copy-start | bytes 884740
  21.4 19.0 %collective-permute-start.3 = (bf16[128,1024]{1,0:T(8,128)(2,1)S(1)}, bf16[128,1024]{1,0:T(8,128)(2,1)S(1)}, u32[]{:S(2)}, u32[]{:S(2)}) collective-permute-start(bf16[128,1024]{1,0:T(8,128)(2,1)S(1)} %hold.1.refs_2_.refs_0_), channel_id=1, source_target_pairs={{0,16},{2,18},{4,20},{6,22},{8,24},{10,26},{12,28},{14,30},{16,0},... | collective-permute-start | bytes 786440 | tf_op jit(solution)/shard_map/ppermute | solution.py:1005
  36.9 8.3 %collective-permute-start.7 = (bf16[784,128]{1,0:T(8,128)(2,1)S(1)}, bf16[784,128]{1,0:T(8,128)(2,1)S(1)}, u32[]{:S(2)}, u32[]{:S(2)}) collective-permute-start(bf16[784,128]{1,0:T(8,128)(2,1)S(1)} %get-tuple-element.92), channel_id=1, source_target_pairs={{0,2},{2,0},{4,6},{6,4},{8,10},{10,8},{12,14},{14,12},{16,18},{18,... | collective-permute-start | bytes 602120 | tf_op jit(solution)/shard_map/ppermute | solution.py:1008
  38.2 9.7 %collective-permute-start.8 = (bf16[784,128]{1,0:T(8,128)(2,1)S(1)}, bf16[784,128]{1,0:T(8,128)(2,1)S(1)}, u32[]{:S(2)}, u32[]{:S(2)}) collective-permute-start(bf16[784,128]{1,0:T(8,128)(2,1)S(1)} %get-tuple-element.93), channel_id=1, source_target_pairs={{0,4},{2,6},{4,0},{6,2},{8,12},{10,14},{12,8},{14,10},{16,20},{18,... | collective-permute-start | bytes 602120 | tf_op jit(solution)/shard_map/ppermute | solution.py:1008
  39.7 8.2 %collective-permute-start.9 = (bf16[784,128]{1,0:T(8,128)(2,1)S(1)}, bf16[784,128]{1,0:T(8,128)(2,1)S(1)}, u32[]{:S(2)}, u32[]{:S(2)}) collective-permute-start(bf16[784,128]{1,0:T(8,128)(2,1)S(1)} %get-tuple-element.94), channel_id=1, source_target_pairs={{0,6},{2,4},{4,2},{6,0},{8,14},{10,12},{12,10},{14,8},{16,22},{18,... | collective-permute-start | bytes 602120 | tf_op jit(solution)/shard_map/ppermute | solution.py:1008
  40.4 13.6 %collective-permute-start.2 = (bf16[128,1024]{1,0:T(8,128)(2,1)S(1)}, bf16[128,1024]{1,0:T(8,128)(2,1)S(1)}, u32[]{:S(2)}, u32[]{:S(2)}) collective-permute-start(bf16[128,1024]{1,0:T(8,128)(2,1)S(1)} %hold.1.refs_2_.refs_0_), channel_id=1, source_target_pairs={{0,8},{2,10},{4,12},{6,14},{8,0},{10,2},{12,4},{14,6},{16,24},{18,... | collective-permute-start | bytes 786440 | tf_op jit(solution)/shard_map/ppermute | solution.py:1005
  40.4 14.9 %collective-permute-start.4 = (bf16[128,1024]{1,0:T(8,128)(2,1)S(1)}, bf16[128,1024]{1,0:T(8,128)(2,1)S(1)}, u32[]{:S(2)}, u32[]{:S(2)}) collective-permute-start(bf16[128,1024]{1,0:T(8,128)(2,1)S(1)} %collective-permute-done.3.refs_2_), channel_id=1, source_target_pairs={{0,8},{2,10},{4,12},{6,14},{8,0},{10,2},{12,4},{14,6},{16,24},{18,... | collective-permute-start | bytes 786440 | tf_op jit(solution)/shard_map/ppermute | solution.py:1005
  42.5 5.5 %copy-start.2 = (f32[2048,128]{1,0:T(8,128)S(1)}, f32[2048,128]{1,0:T(8,128)}, u32[]{:S(2)}) copy-start(f32[2048,128]{1,0:T(8,128)} %constant.5.clone.refs_5_.refs_11_) | copy-start | bytes 3145732
  42.5 5.5 %copy-start.3 = (f32[2048,128]{1,0:T(8,128)S(1)}, f32[2048,128]{1,0:T(8,128)}, u32[]{:S(2)}) copy-start(f32[2048,128]{1,0:T(8,128)} %constant.4.clone.refs_4_.refs_10_) | copy-start | bytes 3145732
  45.2 32.5 %collective-permute-start.17 = (bf16[256,1024]{1,0:T(8,128)(2,1)S(1)}, bf16[256,1024]{1,0:T(8,128)(2,1)S(1)}, u32[]{:S(2)}, u32[]{:S(2)}) collective-permute-start(bf16[256,1024]{1,0:T(8,128)(2,1)S(1)} %get-tuple-element.122), channel_id=1, source_target_pairs={{0,8},{2,10},{4,12},{6,14},{8,0},{10,2},{12,4},{14,6},{16,24},{18,... | collective-permute-start | bytes 1572872 | tf_op jit(solution)/shard_map/ppermute | solution.py:1005
  56.0 10.5 %collective-permute-start.10 = (bf16[256,128]{1,0:T(8,128)(2,1)S(1)}, bf16[256,128]{1,0:T(8,128)(2,1)S(1)}, u32[]{:S(2)}, u32[]{:S(2)}) collective-permute-start(bf16[256,128]{1,0:T(8,128)(2,1)S(1)} %get-tuple-element.101), channel_id=1, source_target_pairs={{0,2},{2,0},{4,6},{6,4},{8,10},{10,8},{12,14},{14,12},{16,18},{18,... | collective-permute-start | bytes 196616 | tf_op jit(solution)/shard_map/ppermute | solution.py:1008
  57.3 9.3 %collective-permute-start.11 = (bf16[256,128]{1,0:T(8,128)(2,1)S(1)}, bf16[256,128]{1,0:T(8,128)(2,1)S(1)}, u32[]{:S(2)}, u32[]{:S(2)}) collective-permute-start(bf16[256,128]{1,0:T(8,128)(2,1)S(1)} %get-tuple-element.102), channel_id=1, source_target_pairs={{0,4},{2,6},{4,0},{6,2},{8,12},{10,14},{12,8},{14,10},{16,20},{18,... | collective-permute-start | bytes 196616 | tf_op jit(solution)/shard_map/ppermute | solution.py:1008
  58.8 7.8 %collective-permute-start.12 = (bf16[256,128]{1,0:T(8,128)(2,1)S(1)}, bf16[256,128]{1,0:T(8,128)(2,1)S(1)}, u32[]{:S(2)}, u32[]{:S(2)}) collective-permute-start(bf16[256,128]{1,0:T(8,128)(2,1)S(1)} %get-tuple-element.103), channel_id=1, source_target_pairs={{0,6},{2,4},{4,2},{6,0},{8,14},{10,12},{12,10},{14,8},{16,22},{18,... | collective-permute-start | bytes 196616 | tf_op jit(solution)/shard_map/ppermute | solution.py:1008
  62.9 15.7 %collective-permute-start.16 = (bf16[256,1024]{1,0:T(8,128)(2,1)S(1)}, bf16[256,1024]{1,0:T(8,128)(2,1)S(1)}, u32[]{:S(2)}, u32[]{:S(2)}) collective-permute-start(bf16[256,1024]{1,0:T(8,128)(2,1)S(1)} %get-tuple-element.120), channel_id=1, source_target_pairs={{0,8},{2,10},{4,12},{6,14},{8,0},{10,2},{12,4},{14,6},{16,24},{18,... | collective-permute-start | bytes 1572872 | tf_op jit(solution)/shard_map/ppermute | solution.py:1005
  66.5 29.8 %collective-permute-start.23 = (bf16[1088,1024]{1,0:T(8,128)(2,1)S(1)}, bf16[1088,1024]{1,0:T(8,128)(2,1)S(1)}, u32[]{:S(2)}, u32[]{:S(2)}) collective-permute-start(bf16[1088,1024]{1,0:T(8,128)(2,1)S(1)} %get-tuple-element.114.refs_12_), channel_id=1, source_target_pairs={{0,1},{1,0},{2,3},{3,2},{4,5},{5,4},{6,7},{7,6},{8,9},{9,8},{10,11... | collective-permute-start | bytes 6684680 | tf_op jit(solution)/shard_map/ppermute | solution.py:1011
  74.9 9.2 %collective-permute-start.13 = (bf16[1024,128]{1,0:T(8,128)(2,1)S(1)}, bf16[1024,128]{1,0:T(8,128)(2,1)S(1)}, u32[]{:S(2)}, u32[]{:S(2)}) collective-permute-start(bf16[1024,128]{1,0:T(8,128)(2,1)S(1)} %get-tuple-element.116), channel_id=1, source_target_pairs={{0,2},{2,0},{4,6},{6,4},{8,10},{10,8},{12,14},{14,12},{16,18},{18,... | collective-permute-start | bytes 786440 | tf_op jit(solution)/shard_map/ppermute | solution.py:1008
  76.2 14.0 %collective-permute-start.14 = (bf16[1024,128]{1,0:T(8,128)(2,1)S(1)}, bf16[1024,128]{1,0:T(8,128)(2,1)S(1)}, u32[]{:S(2)}, u32[]{:S(2)}) collective-permute-start(bf16[1024,128]{1,0:T(8,128)(2,1)S(1)} %get-tuple-element.117), channel_id=1, source_target_pairs={{0,4},{2,6},{4,0},{6,2},{8,12},{10,14},{12,8},{14,10},{16,20},{18,... | collective-permute-start | bytes 786440 | tf_op jit(solution)/shard_map/ppermute | solution.py:1008
  77.7 12.5 %collective-permute-start.15 = (bf16[1024,128]{1,0:T(8,128)(2,1)S(1)}, bf16[1024,128]{1,0:T(8,128)(2,1)S(1)}, u32[]{:S(2)}, u32[]{:S(2)}) collective-permute-start(bf16[1024,128]{1,0:T(8,128)(2,1)S(1)} %get-tuple-element.118), channel_id=1, source_target_pairs={{0,6},{2,4},{4,2},{6,0},{8,14},{10,12},{12,10},{14,8},{16,22},{18,... | collective-permute-start | bytes 786440 | tf_op jit(solution)/shard_map/ppermute | solution.py:1008
  78.5 21.6 %collective-permute-start.21 = (bf16[128,1024]{1,0:T(8,128)(2,1)S(1)}, bf16[128,1024]{1,0:T(8,128)(2,1)S(1)}, u32[]{:S(2)}, u32[]{:S(2)}) collective-permute-start(bf16[128,1024]{1,0:T(8,128)(2,1)S(1)} %get-tuple-element.129), channel_id=1, source_target_pairs={{0,16},{2,18},{4,20},{6,22},{8,24},{10,26},{12,28},{14,30},{16,0},... | collective-permute-start | bytes 786440 | tf_op jit(solution)/shard_map/ppermute | solution.py:1005
  84.0 20.7 %collective-permute-start.22 = (bf16[128,1024]{1,0:T(8,128)(2,1)S(1)}, bf16[128,1024]{1,0:T(8,128)(2,1)S(1)}, u32[]{:S(2)}, u32[]{:S(2)}) collective-permute-start(bf16[128,1024]{1,0:T(8,128)(2,1)S(1)} %get-tuple-element.130), channel_id=1, source_target_pairs={{0,16},{2,18},{4,20},{6,22},{8,24},{10,26},{12,28},{14,30},{16,0},... | collective-permute-start | bytes 786440 | tf_op jit(solution)/shard_map/ppermute | solution.py:1005
  91.2 18.2 %collective-permute-start.18 = (bf16[128,1024]{1,0:T(8,128)(2,1)S(1)}, bf16[128,1024]{1,0:T(8,128)(2,1)S(1)}, u32[]{:S(2)}, u32[]{:S(2)}) collective-permute-start(bf16[128,1024]{1,0:T(8,128)(2,1)S(1)} %get-tuple-element.126), channel_id=1, source_target_pairs={{0,8},{2,10},{4,12},{6,14},{8,0},{10,2},{12,4},{14,6},{16,24},{18,... | collective-permute-start | bytes 786440 | tf_op jit(solution)/shard_map/ppermute | solution.py:1005
  96.2 5.3 %collective-permute-start.27 = (bf16[704,768]{1,0:T(8,128)(2,1)S(1)}, bf16[704,768]{1,0:T(8,128)(2,1)S(1)}, u32[]{:S(2)}, u32[]{:S(2)}) collective-permute-start(bf16[704,768]{1,0:T(8,128)(2,1)S(1)} %get-tuple-element.136.refs_2_), channel_id=1, source_target_pairs={{0,1},{1,0},{2,3},{3,2},{4,5},{5,4},{6,7},{7,6},{8,9},{9,8},{10,11... | collective-permute-start | bytes 3244040 | tf_op jit(solution)/shard_map/ppermute | solution.py:1011
  96.7 15.5 %collective-permute-start.24 = (bf16[272,1024]{1,0:T(8,128)(2,1)S(1)}, bf16[272,1024]{1,0:T(8,128)(2,1)S(1)}, u32[]{:S(2)}, u32[]{:S(2)}) collective-permute-start(bf16[272,1024]{1,0:T(8,128)(2,1)S(1)} %get-tuple-element.138), channel_id=1, source_target_pairs={{0,2},{2,0},{4,6},{6,4},{8,10},{10,8},{12,14},{14,12},{16,18},{18,... | collective-permute-start | bytes 1671176 | tf_op jit(solution)/shard_map/ppermute | solution.py:1008
  100.1 24.6 %collective-permute-start.25 = (bf16[272,1024]{1,0:T(8,128)(2,1)S(1)}, bf16[272,1024]{1,0:T(8,128)(2,1)S(1)}, u32[]{:S(2)}, u32[]{:S(2)}) collective-permute-start(bf16[272,1024]{1,0:T(8,128)(2,1)S(1)} %get-tuple-element.139), channel_id=1, source_target_pairs={{0,4},{2,6},{4,0},{6,2},{8,12},{10,14},{12,8},{14,10},{16,20},{18,... | collective-permute-start | bytes 1671176 | tf_op jit(solution)/shard_map/ppermute | solution.py:1008
  101.5 25.8 %collective-permute-start.26 = (bf16[272,1024]{1,0:T(8,128)(2,1)S(1)}, bf16[272,1024]{1,0:T(8,128)(2,1)S(1)}, u32[]{:S(2)}, u32[]{:S(2)}) collective-permute-start(bf16[272,1024]{1,0:T(8,128)(2,1)S(1)} %get-tuple-element.140), channel_id=1, source_target_pairs={{0,6},{2,4},{4,2},{6,0},{8,14},{10,12},{12,10},{14,8},{16,22},{18,... | collective-permute-start | bytes 1671176 | tf_op jit(solution)/shard_map/ppermute | solution.py:1008
  104.7 24.9 %collective-permute-start.19 = (bf16[128,1024]{1,0:T(8,128)(2,1)S(1)}, bf16[128,1024]{1,0:T(8,128)(2,1)S(1)}, u32[]{:S(2)}, u32[]{:S(2)}) collective-permute-start(bf16[128,1024]{1,0:T(8,128)(2,1)S(1)} %get-tuple-element.127), channel_id=1, source_target_pairs={{0,16},{2,18},{4,20},{6,22},{8,24},{10,26},{12,28},{14,30},{16,0},... | collective-permute-start | bytes 786440 | tf_op jit(solution)/shard_map/ppermute | solution.py:1005
  109.4 20.3 %collective-permute-start.20 = (bf16[128,1024]{1,0:T(8,128)(2,1)S(1)}, bf16[128,1024]{1,0:T(8,128)(2,1)S(1)}, u32[]{:S(2)}, u32[]{:S(2)}) collective-permute-start(bf16[128,1024]{1,0:T(8,128)(2,1)S(1)} %get-tuple-element.128), channel_id=1, source_target_pairs={{0,24},{2,26},{4,28},{6,30},{8,16},{10,18},{12,20},{14,22},{16,8},... | collective-permute-start | bytes 786440 | tf_op jit(solution)/shard_map/ppermute | solution.py:1005
  112.2 19.0 %collective-permute-start.28 = (bf16[176,768]{1,0:T(8,128)(2,1)S(1)}, bf16[176,768]{1,0:T(8,128)(2,1)S(1)}, u32[]{:S(2)}, u32[]{:S(2)}) collective-permute-start(bf16[176,768]{1,0:T(8,128)(2,1)S(1)} %get-tuple-element.146), channel_id=1, source_target_pairs={{0,2},{2,0},{4,6},{6,4},{8,10},{10,8},{12,14},{14,12},{16,18},{18,... | collective-permute-start | bytes 811016 | tf_op jit(solution)/shard_map/ppermute | solution.py:1008
  124.8 13.7 %collective-permute-start.29 = (bf16[176,768]{1,0:T(8,128)(2,1)S(1)}, bf16[176,768]{1,0:T(8,128)(2,1)S(1)}, u32[]{:S(2)}, u32[]{:S(2)}) collective-permute-start(bf16[176,768]{1,0:T(8,128)(2,1)S(1)} %get-tuple-element.147), channel_id=1, source_target_pairs={{0,4},{2,6},{4,0},{6,2},{8,12},{10,14},{12,8},{14,10},{16,20},{18,... | collective-permute-start | bytes 811016 | tf_op jit(solution)/shard_map/ppermute | solution.py:1008
  127.3 11.2 %collective-permute-start.30 = (bf16[176,768]{1,0:T(8,128)(2,1)S(1)}, bf16[176,768]{1,0:T(8,128)(2,1)S(1)}, u32[]{:S(2)}, u32[]{:S(2)}) collective-permute-start(bf16[176,768]{1,0:T(8,128)(2,1)S(1)} %get-tuple-element.148), channel_id=1, source_target_pairs={{0,6},{2,4},{4,2},{6,0},{8,14},{10,12},{12,10},{14,8},{16,22},{18,... | collective-permute-start | bytes 811016 | tf_op jit(solution)/shard_map/ppermute | solution.py:1008
  129.6 11.1 %collective-permute-start.34 = (bf16[32,1024]{1,0:T(8,128)(2,1)S(1)}, bf16[32,1024]{1,0:T(8,128)(2,1)S(1)}, u32[]{:S(2)}, u32[]{:S(2)}) collective-permute-start(bf16[32,1024]{1,0:T(8,128)(2,1)S(1)} %get-tuple-element.154), channel_id=1, source_target_pairs={{0,8},{2,10},{4,12},{6,14},{8,0},{10,2},{12,4},{14,6},{16,24},{18,... | collective-permute-start | bytes 196616 | tf_op jit(solution)/shard_map/ppermute | solution.py:1005
  129.6 14.0 %collective-permute-start.35 = (bf16[32,1024]{1,0:T(8,128)(2,1)S(1)}, bf16[32,1024]{1,0:T(8,128)(2,1)S(1)}, u32[]{:S(2)}, u32[]{:S(2)}) collective-permute-start(bf16[32,1024]{1,0:T(8,128)(2,1)S(1)} %get-tuple-element.155), channel_id=1, source_target_pairs={{0,16},{2,18},{4,20},{6,22},{8,24},{10,26},{12,28},{14,30},{16,0},... | collective-permute-start | bytes 196616 | tf_op jit(solution)/shard_map/ppermute | solution.py:1005
  131.1 12.5 %collective-permute-start.36 = (bf16[32,1024]{1,0:T(8,128)(2,1)S(1)}, bf16[32,1024]{1,0:T(8,128)(2,1)S(1)}, u32[]{:S(2)}, u32[]{:S(2)}) collective-permute-start(bf16[32,1024]{1,0:T(8,128)(2,1)S(1)} %get-tuple-element.156), channel_id=1, source_target_pairs={{0,24},{2,26},{4,28},{6,30},{8,16},{10,18},{12,20},{14,22},{16,8},... | collective-permute-start | bytes 196616 | tf_op jit(solution)/shard_map/ppermute | solution.py:1005
  138.5 9.2 %copy-start.5 = (f32[1,32]{1,0:T(1,128)S(1)}, f32[1,32]{1,0:T(1,128)}, u32[]{:S(2)}) copy-start(f32[1,32]{1,0:T(1,128)} %get-tuple-element.162) | copy-start | bytes 388
  139.2 5.2 %collective-permute-start.31 = (bf16[48,768]{1,0:T(8,128)(2,1)S(1)}, bf16[48,768]{1,0:T(8,128)(2,1)S(1)}, u32[]{:S(2)}, u32[]{:S(2)}) collective-permute-start(bf16[48,768]{1,0:T(8,128)(2,1)S(1)} %get-tuple-element.150), channel_id=1, source_target_pairs={{0,8},{2,10},{4,12},{6,14},{8,0},{10,2},{12,4},{14,6},{16,24},{18,... | collective-permute-start | bytes 221192 | tf_op jit(solution)/shard_map/ppermute | solution.py:1005
  139.2 6.8 %collective-permute-start.32 = (bf16[48,768]{1,0:T(8,128)(2,1)S(1)}, bf16[48,768]{1,0:T(8,128)(2,1)S(1)}, u32[]{:S(2)}, u32[]{:S(2)}) collective-permute-start(bf16[48,768]{1,0:T(8,128)(2,1)S(1)} %get-tuple-element.151), channel_id=1, source_target_pairs={{0,16},{2,18},{4,20},{6,22},{8,24},{10,26},{12,28},{14,30},{16,0},... | collective-permute-start | bytes 221192 | tf_op jit(solution)/shard_map/ppermute | solution.py:1005
  140.7 6.2 %collective-permute-start.33 = (bf16[48,768]{1,0:T(8,128)(2,1)S(1)}, bf16[48,768]{1,0:T(8,128)(2,1)S(1)}, u32[]{:S(2)}, u32[]{:S(2)}) collective-permute-start(bf16[48,768]{1,0:T(8,128)(2,1)S(1)} %get-tuple-element.152), channel_id=1, source_target_pairs={{0,24},{2,26},{4,28},{6,30},{8,16},{10,18},{12,20},{14,22},{16,8},... | collective-permute-start | bytes 221192 | tf_op jit(solution)/shard_map/ppermute | solution.py:1005

commit v6 on v5

--- a/solution.py
+++ b/solution.py
@@ -939,8 +939,8 @@
             out[:, cols] = ref[:32, 256 * part : 256 * (part + 1)].astype(F32)
         vec = vec + ref[32:, 512:768].astype(F32)
     vec_ref[...] = owned_lanes(vec)
-    gain[...] = vec_ref[pl.ds(line, 1), :]
-    bias[...] = vec_ref[pl.ds(4 + line, 1), :]
+    gain[...] = vec_ref[pl.ds(line, 1), :].reshape(32)
+    bias[...] = vec_ref[pl.ds(4 + line, 1), :].reshape(32)
 
 
 def hold_kernel(x, out):
@@ -1044,7 +1044,7 @@
         pack_kernel,
         [near((rows + VEC, width), BF16)],
         [],
-        block_order.reshape(2), far(tokens[0]),
+        far(block_order.reshape(2)), far(tokens[0]),
     )
     from_two = over_lines(raw(token_block), 2)
     token_lines = [
@@ -1240,15 +1240,15 @@
     (grad_in,) = run(join_in_kernel, [far((32, feed), F32)], [], *in_parts)
     grad_qkv, grad_gain, grad_shift = run(
         join_qkv_kernel,
-        [far((32, 3 * width), F32), ((1, 32), F32), ((1, 32), F32)],
+        [far((32, 3 * width), F32), far((32,), F32), far((32,), F32)],
         [pltpu.VMEM((VEC, 32), F32)],
         *qkv_parts,
     )
     return (
         layer_out[None],
         grad_tokens[None],
-        grad_gain[0],
-        grad_shift[0],
+        grad_gain,
+        grad_shift,
         grad_qkv,
         grad_qv,
         grad_out,

time: 149 us -> 148 us (level)
  no operation moved by 1% of the time
where the time goes in v6:
time: 148 us
  Pallas kernels  54 us (36%)
  starting transfers between devices  51.3 us (35%)
  waiting for transfers between devices  40.8 us (28%)
    pallas_call x22, Pallas kernels, call(): pl.pallas_call(body, name=name, out_shape=outs, in_specs=specs + [loose]...  54 us
    ppermute x19, starting transfers between devices, over_lines(): return lax.ppermute(x, 'ctx', [(i, i ^ k * ACROSS) for i in positions])  31.3 us
    ppermute x15, waiting for transfers between devices, over_places(): return lax.ppermute(x, 'ctx', [(i, i ^ j) for i in positions])  19.9 us
    ppermute x15, starting transfers between devices, over_places(): return lax.ppermute(x, 'ctx', [(i, i ^ j) for i in positions])  19.9 us
    ppermute x19, waiting for transfers between devices, over_lines(): return lax.ppermute(x, 'ctx', [(i, i ^ k * ACROSS) for i in positions])  19 us
  transfers between devices with their start and end apart: 37, of which 14 were waited for; matrix products, arithmetic and copies ran while one was open for 0% of the time, Pallas kernels for 35%

profile of v6, /device:TPU:0, one launch (start us, length us, event | category | flops | bytes accessed | tf_op | source)
XLA Modules:
  0.0 147.6 jit_solution(3430140374276916146)
XLA Ops:
  0.6 1.0 pack.1.refs_10_.refs_0_
  1.6 4.1 %collective-permute-start.1 = (bf16[144,1024]{1,0:T(8,128)(2,1)S(1)}, bf16[144,1024]{1,0:T(8,128)(2,1)}, u32[]{:S(2)}, u32[]{:S(2)}) collective-permute-start(bf16[144,1024]{1,0:T(8,128)(2,1)S(1)} %pack.1.refs_10_.refs_0_), channel_id=1, source_target_pairs={{0,16},{2,18},{4,20},{6,22},{8,24},{10,26},{12,28},{14,30},{16,0},... | collective-permute-start | bytes 884744 | tf_op jit(solution)/shard_map/ppermute | solution.py:1005
  5.7 1.6 %collective-permute-start = (bf16[144,1024]{1,0:T(8,128)(2,1)S(1)}, bf16[144,1024]{1,0:T(8,128)(2,1)S(1)}, u32[]{:S(2)}, u32[]{:S(2)}) collective-permute-start(bf16[144,1024]{1,0:T(8,128)(2,1)S(1)} %pack.1.refs_10_.refs_0_), channel_id=1, source_target_pairs={{0,8},{2,10},{4,12},{6,14},{8,0},{10,2},{12,4},{14,6},{16,24},{18,... | collective-permute-start | bytes 884744 | tf_op jit(solution)/shard_map/ppermute | solution.py:1005
  7.3 6.9 %prepare.1.refs_3_.refs_0_ = bf16[3600,1024]{1,0:T(8,128)(2,1)} custom-call(bf16[512,3072]{1,0:T(8,128)(2,1)} %refs_0_.1, bf16[512,4096]{1,0:T(8,128)(2,1)} %refs_1_.1, bf16[512,1024]{1,0:T(8,128)(2,1)} %refs_2_.1, bf16[2048,1024]{1,0:T(8,128)(2,1)} %refs_3_.1, bf16[512]{0:T(512)(128)(2,1)} %refs_4_.2, bf16[512]{0:T(512)(128)(2,1)} %refs_5_.2, ...), custom_call_target="tpu_custom_call" | custom-call | tf_op jit(solution)/shard_map/prepare/pallas_call | solution.py:416
  14.3 5.0 %collective-permute-done.1.refs_2_ = bf16[144,1024]{1,0:T(8,128)(2,1)} collective-permute-done((bf16[144,1024]{1,0:T(8,128)(2,1)S(1)}, bf16[144,1024]{1,0:T(8,128)(2,1)}, u32[]{:S(2)}, u32[]{:S(2)}) %collective-permute-start.1) | collective-permute-done | bytes 294944 | tf_op jit(solution)/shard_map/ppermute | solution.py:1005
  19.3 0.5 collective-permute-start.6
  19.8 1.0 hold.1.refs_2_.refs_0_
  20.8 3.6 %collective-permute-start.3 = (bf16[128,1024]{1,0:T(8,128)(2,1)S(1)}, bf16[128,1024]{1,0:T(8,128)(2,1)S(1)}, u32[]{:S(2)}, u32[]{:S(2)}) collective-permute-start(bf16[128,1024]{1,0:T(8,128)(2,1)S(1)} %hold.1.refs_2_.refs_0_), channel_id=1, source_target_pairs={{0,16},{2,18},{4,20},{6,22},{8,24},{10,26},{12,28},{14,30},{16,0},... | collective-permute-start | bytes 786440 | tf_op jit(solution)/shard_map/ppermute | solution.py:1005
  24.3 2.0 %collective-permute-done.5.refs_1_ = bf16[3600,1024]{1,0:T(8,128)(2,1)} collective-permute-done((bf16[3600,1024]{1,0:T(8,128)(2,1)}, bf16[3600,1024]{1,0:T(8,128)(2,1)}, u32[]{:S(2)}, u32[]{:S(2)}) %collective-permute-start.5) | collective-permute-done | bytes 7372832 | tf_op jit(solution)/shard_map/ppermute | solution.py:1011
  26.3 4.8 %assemble.1 = (bf16[1024,3072]{1,0:T(8,128)(2,1)S(1)}, bf16[1024,1024]{1,0:T(8,128)(2,1)S(1)}, bf16[1024,1024]{1,0:T(8,128)(2,1)S(1)}, bf16[1024,1024]{1,0:T(8,128)(2,1)S(1)}, f32[32,512]{1,0:T(8,128)S(1)}) custom-call(bf16[3600,1024]{1,0:T(8,128)(2,1)} %prepare.1.refs_3_.refs_0_, bf16[3600,1024]{1,0:T(8,128)(2,1)} %collective-permute-done.5.refs_1_, ...), custom_call_target="tpu_custom_call" | custom-call | tf_op jit(solution)/shard_map/assemble/pallas_call | solution.py:416
  31.2 1.8 %collective-permute-done.6.refs_3_ = bf16[144,1024]{1,0:T(8,128)(2,1)} collective-permute-done((bf16[144,1024]{1,0:T(8,128)(2,1)}, bf16[144,1024]{1,0:T(8,128)(2,1)}, u32[]{:S(2)}, u32[]{:S(2)}) %collective-permute-start.6) | collective-permute-done | bytes 294944 | tf_op jit(solution)/shard_map/ppermute | solution.py:1005
  33.0 3.2 %project.1 = (bf16[784,128]{1,0:T(8,128)(2,1)S(1)}, bf16[784,128]{1,0:T(8,128)(2,1)S(1)}, bf16[784,128]{1,0:T(8,128)(2,1)S(1)}, bf16[784,128]{1,0:T(8,128)(2,1)S...) custom-call(bf16[144,1024]{1,0:T(8,128)(2,1)S(1)} %copy-done.1, ...), custom_call_target="tpu_custom_call" | custom-call | tf_op jit(solution)/shard_map/project/pallas_call | solution.py:416
  36.2 1.3 collective-permute-start.7
  37.5 1.5 %collective-permute-start.8 = (bf16[784,128]{1,0:T(8,128)(2,1)S(1)}, bf16[784,128]{1,0:T(8,128)(2,1)S(1)}, u32[]{:S(2)}, u32[]{:S(2)}) collective-permute-start(bf16[784,128]{1,0:T(8,128)(2,1)S(1)} %get-tuple-element.93), channel_id=1, source_target_pairs={{0,4},{2,6},{4,0},{6,2},{8,12},{10,14},{12,8},{14,10},{16,20},{18,... | collective-permute-start | bytes 602120 | tf_op jit(solution)/shard_map/ppermute | solution.py:1008
  39.1 0.7 collective-permute-start.9
  39.8 2.0 %collective-permute-start.4 = (bf16[128,1024]{1,0:T(8,128)(2,1)S(1)}, bf16[128,1024]{1,0:T(8,128)(2,1)S(1)}, u32[]{:S(2)}, u32[]{:S(2)}) collective-permute-start(bf16[128,1024]{1,0:T(8,128)(2,1)S(1)} %collective-permute-done.3.refs_2_), channel_id=1, source_target_pairs={{0,8},{2,10},{4,12},{6,14},{8,0},{10,2},{12,4},{14,6},{16,24},{18,... | collective-permute-start | bytes 786440 | tf_op jit(solution)/shard_map/ppermute | solution.py:1005
  41.8 2.7 %feed.1 = (f32[512,1024]{1,0:T(8,128)S(1)}, bf16[1024,512]{1,0:T(8,128)(2,1)S(1)}, f32[256,1024]{1,0:T(8,128)S(1)}, bf16[256,1024]{1,0:T(8,128)(2,1)S(1)}) custom-call(bf16[512,1024]{1,0:T(8,128)(2,1)S(1)} %get-tuple-element.95.refs_0_, bf16[1024,1024]{1,0:T(8,128)(2,1)S(1)} %get-tuple-element.96.refs_1_.refs_2_, ...), custom_call_target="tpu_custom_call" | custom-call | tf_op jit(solution)/shard_map/feed/pallas_call | solution.py:416
  44.6 2.7 %collective-permute-done.8.refs_2_ = bf16[784,128]{1,0:T(8,128)(2,1)S(1)} collective-permute-done((bf16[784,128]{1,0:T(8,128)(2,1)S(1)}, bf16[784,128]{1,0:T(8,128)(2,1)S(1)}, u32[]{:S(2)}, u32[]{:S(2)}) %collective-permute-start.8) | collective-permute-done | bytes 200736 | tf_op jit(solution)/shard_map/ppermute | solution.py:1008
  47.3 6.1 %attend.1 = (bf16[2048,128]{1,0:T(8,128)(2,1)S(1)}, bf16[2048,128]{1,0:T(8,128)(2,1)S(1)}, bf16[2048,64]{1,0:T(8,128)(2,1)S(1)}, f32[2048,64]{1,0:T(8,128)S(1)},...) custom-call(bf16[784,128]{1,0:T(8,128)(2,1)S(1)} %get-tuple-element.91.refs_4_.refs_0_, ...), custom_call_target="tpu_custom_call" | custom-call | flops 2300000000 | tf_op jit(solution)/shard_map/attend/pallas_call | solution.py:416
  53.4 1.2 collective-permute-done.4.refs_3_
  54.6 0.6 back_rows.1
  55.3 1.3 collective-permute-start.10
  56.6 1.5 %collective-permute-start.11 = (bf16[256,128]{1,0:T(8,128)(2,1)S(1)}, bf16[256,128]{1,0:T(8,128)(2,1)S(1)}, u32[]{:S(2)}, u32[]{:S(2)}) collective-permute-start(bf16[256,128]{1,0:T(8,128)(2,1)S(1)} %get-tuple-element.102), channel_id=1, source_target_pairs={{0,4},{2,6},{4,0},{6,2},{8,12},{10,14},{12,8},{14,10},{16,20},{18,... | collective-permute-start | bytes 196616 | tf_op jit(solution)/shard_map/ppermute | solution.py:1008
  58.1 0.7 collective-permute-start.12
  58.8 3.4 %feed_grad.1 = (bf16[512,1024]{1,0:T(8,128)(2,1)S(1)}, f32[8,1024]{1,0:T(8,128)S(1)}, f32[512,1024]{1,0:T(8,128)S(1)}, f32[256,1024]{1,0:T(8,128)S(1)}, bf16[256,1024]{1,0:T(8,128)(2,1)S(1)}) custom-call(bf16[512,1024]{1,0:T(8,128)(2,1)S(1)} %get-tuple-element.109.refs_0_.refs_6_.refs_11_, f32[512,1024]{1,0:T(8,128)S(1)} %get-tuple-element.98.refs_6_.refs_1_, ...), custom_call_target="tpu_custom_call" | custom-call | flops 4600000000 | tf_op jit(solution)/shard_map/feed_grad/pallas_call | solution.py:416
  62.3 3.5 %feed_terms.1 = (bf16[1088,1024]{1,0:T(8,128)(2,1)S(1)}, f32[1088,1024]{1,0:T(8,128)S(1)}) custom-call(bf16[512,1024]{1,0:T(8,128)(2,1)S(1)} %get-tuple-element.109.refs_0_.refs_6_.refs_11_, bf16[1024,512]{1,0:T(8,128)(2,1)S(1)} %get-tuple-element.110.refs_1_, bf16[1024,512]{1,0:T(8,128)(2,1)S(1)} %get-tuple-element.111.refs_2_.refs_3_, ...), custom_call_target="tpu_custom_call" | custom-call | flops 575000000 | tf_op jit(solution)/shard_map/feed_terms/pallas_call | solution.py:416
  65.9 8.3 %attend_back.1 = (bf16[1024,128]{1,0:T(8,128)(2,1)S(1)}, bf16[1024,128]{1,0:T(8,128)(2,1)S(1)}, bf16[1024,128]{1,0:T(8,128)(2,1)S(1)}, bf16[1024,128]{1,0:T(8,128)(2,1)S(1)}, f32[8,128]{1,0:T(8,128)S(1)}) custom-call(bf16[256,128]{1,0:T(8,128)(2,1)S(1)} %get-tuple-element.100.refs_4_.refs_0_, bf16[256,128]{1,0:T(8,128)(2,1)S(1)} %collective-permute-done.10.refs_1_, ...), custom_call_target="tpu_custom_call" | custom-call | tf_op jit(solution)/shard_map/attend_back/pallas_call | solution.py:416
  74.2 1.3 collective-permute-start.13
  75.5 1.5 %collective-permute-start.14 = (bf16[1024,128]{1,0:T(8,128)(2,1)S(1)}, bf16[1024,128]{1,0:T(8,128)(2,1)S(1)}, u32[]{:S(2)}, u32[]{:S(2)}) collective-permute-start(bf16[1024,128]{1,0:T(8,128)(2,1)S(1)} %get-tuple-element.117), channel_id=1, source_target_pairs={{0,4},{2,6},{4,0},{6,2},{8,12},{10,14},{12,8},{14,10},{16,20},{18,... | collective-permute-start | bytes 786440 | tf_op jit(solution)/shard_map/ppermute | solution.py:1008
  77.0 0.7 collective-permute-start.15
  77.9 3.1 %collective-permute-start.21 = (bf16[128,1024]{1,0:T(8,128)(2,1)S(1)}, bf16[128,1024]{1,0:T(8,128)(2,1)S(1)}, u32[]{:S(2)}, u32[]{:S(2)}) collective-permute-start(bf16[128,1024]{1,0:T(8,128)(2,1)S(1)} %get-tuple-element.129), channel_id=1, source_target_pairs={{0,16},{2,18},{4,20},{6,22},{8,24},{10,26},{12,28},{14,30},{16,0},... | collective-permute-start | bytes 786440 | tf_op jit(solution)/shard_map/ppermute | solution.py:1005
  81.0 0.1 halve.3
  81.1 2.3 %collective-permute-done.13.refs_1_ = bf16[1024,128]{1,0:T(8,128)(2,1)S(1)} collective-permute-done((bf16[1024,128]{1,0:T(8,128)(2,1)S(1)}, bf16[1024,128]{1,0:T(8,128)(2,1)S(1)}, u32[]{:S(2)}, u32[]{:S(2)}) %collective-permute-start.13) | collective-permute-done | bytes 262176 | tf_op jit(solution)/shard_map/ppermute | solution.py:1008
  83.4 3.1 %collective-permute-start.22 = (bf16[128,1024]{1,0:T(8,128)(2,1)S(1)}, bf16[128,1024]{1,0:T(8,128)(2,1)S(1)}, u32[]{:S(2)}, u32[]{:S(2)}) collective-permute-start(bf16[128,1024]{1,0:T(8,128)(2,1)S(1)} %get-tuple-element.130), channel_id=1, source_target_pairs={{0,16},{2,18},{4,20},{6,22},{8,24},{10,26},{12,28},{14,30},{16,0},... | collective-permute-start | bytes 786440 | tf_op jit(solution)/shard_map/ppermute | solution.py:1005
  86.4 3.1 %collective-permute-done.14.refs_2_ = bf16[1024,128]{1,0:T(8,128)(2,1)S(1)} collective-permute-done((bf16[1024,128]{1,0:T(8,128)(2,1)S(1)}, bf16[1024,128]{1,0:T(8,128)(2,1)S(1)}, u32[]{:S(2)}, u32[]{:S(2)}) %collective-permute-start.14) | collective-permute-done | bytes 262176 | tf_op jit(solution)/shard_map/ppermute | solution.py:1008
  89.5 0.9 unpack.1
  90.5 2.1 %collective-permute-start.18 = (bf16[128,1024]{1,0:T(8,128)(2,1)S(1)}, bf16[128,1024]{1,0:T(8,128)(2,1)S(1)}, u32[]{:S(2)}, u32[]{:S(2)}) collective-permute-start(bf16[128,1024]{1,0:T(8,128)(2,1)S(1)} %get-tuple-element.126), channel_id=1, source_target_pairs={{0,8},{2,10},{4,12},{6,14},{8,0},{10,2},{12,4},{14,6},{16,24},{18,... | collective-permute-start | bytes 786440 | tf_op jit(solution)/shard_map/ppermute | solution.py:1005
  92.6 3.0 %grads.1 = (bf16[704,768]{1,0:T(8,128)(2,1)S(1)}, f32[704,768]{1,0:T(8,128)S(1)}) custom-call(bf16[512,1024]{1,0:T(8,128)(2,1)S(1)} %get-tuple-element.125.refs_0_.refs_8_, f32[512,1024]{1,0:T(8,128)S(1)} %get-tuple-element.132.refs_1_, f32[512,1024]{1,0:T(8,128)S(1)} %get-tuple-element.133.refs_2_, ...), custom_call_target="tpu_custom_call" | custom-call | flops 4600000000 | tf_op jit(solution)/shard_map/grads/pallas_call | solution.py:416
  95.6 0.4 share_twin.2
  96.0 1.3 collective-permute-start.24
  97.3 2.2 %collective-permute-done.21.refs_7_ = bf16[128,1024]{1,0:T(8,128)(2,1)S(1)} collective-permute-done((bf16[128,1024]{1,0:T(8,128)(2,1)S(1)}, bf16[128,1024]{1,0:T(8,128)(2,1)S(1)}, u32[]{:S(2)}, u32[]{:S(2)}) %collective-permute-start.21) | collective-permute-done | bytes 262176 | tf_op jit(solution)/shard_map/ppermute | solution.py:1005
  99.5 1.4 collective-permute-start.25
  100.8 1.4 collective-permute-start.26
  102.3 0.2 share_twin.3
  102.5 1.6 %collective-permute-done.22.refs_9_ = bf16[128,1024]{1,0:T(8,128)(2,1)S(1)} collective-permute-done((bf16[128,1024]{1,0:T(8,128)(2,1)S(1)}, bf16[128,1024]{1,0:T(8,128)(2,1)S(1)}, u32[]{:S(2)}, u32[]{:S(2)}) %collective-permute-start.22) | collective-permute-done | bytes 262176 | tf_op jit(solution)/shard_map/ppermute | solution.py:1005
  104.1 4.7 %collective-permute-done.18.refs_1_ = bf16[128,1024]{1,0:T(8,128)(2,1)S(1)} collective-permute-done((bf16[128,1024]{1,0:T(8,128)(2,1)S(1)}, bf16[128,1024]{1,0:T(8,128)(2,1)S(1)}, u32[]{:S(2)}, u32[]{:S(2)}) %collective-permute-start.18) | collective-permute-done | bytes 262176 | tf_op jit(solution)/shard_map/ppermute | solution.py:1005
  108.7 2.3 %collective-permute-start.20 = (bf16[128,1024]{1,0:T(8,128)(2,1)S(1)}, bf16[128,1024]{1,0:T(8,128)(2,1)S(1)}, u32[]{:S(2)}, u32[]{:S(2)}) collective-permute-start(bf16[128,1024]{1,0:T(8,128)(2,1)S(1)} %get-tuple-element.128), channel_id=1, source_target_pairs={{0,24},{2,26},{4,28},{6,30},{8,16},{10,18},{12,20},{14,22},{16,8},... | collective-permute-start | bytes 786440 | tf_op jit(solution)/shard_map/ppermute | solution.py:1005
  111.0 0.5 collective-permute-done.24.refs_1_
  111.5 1.2 collective-permute-start.28
  112.7 11.4 %collective-permute-done.25.refs_2_ = bf16[272,1024]{1,0:T(8,128)(2,1)S(1)} collective-permute-done((bf16[272,1024]{1,0:T(8,128)(2,1)S(1)}, bf16[272,1024]{1,0:T(8,128)(2,1)S(1)}, u32[]{:S(2)}, u32[]{:S(2)}) %collective-permute-start.25) | collective-permute-done | bytes 557088 | tf_op jit(solution)/shard_map/ppermute | solution.py:1008
  124.1 2.5 %collective-permute-start.29 = (bf16[176,768]{1,0:T(8,128)(2,1)S(1)}, bf16[176,768]{1,0:T(8,128)(2,1)S(1)}, u32[]{:S(2)}, u32[]{:S(2)}) collective-permute-start(bf16[176,768]{1,0:T(8,128)(2,1)S(1)} %get-tuple-element.147), channel_id=1, source_target_pairs={{0,4},{2,6},{4,0},{6,2},{8,12},{10,14},{12,8},{14,10},{16,20},{18,... | collective-permute-start | bytes 811016 | tf_op jit(solution)/shard_map/ppermute | solution.py:1008
  126.6 1.4 collective-permute-start.30
  128.0 1.0 feed_sum.1
  129.0 1.5 %collective-permute-start.35 = (bf16[32,1024]{1,0:T(8,128)(2,1)S(1)}, bf16[32,1024]{1,0:T(8,128)(2,1)S(1)}, u32[]{:S(2)}, u32[]{:S(2)}) collective-permute-start(bf16[32,1024]{1,0:T(8,128)(2,1)S(1)} %get-tuple-element.155), channel_id=1, source_target_pairs={{0,16},{2,18},{4,20},{6,22},{8,24},{10,26},{12,28},{14,30},{16,0},... | collective-permute-start | bytes 196616 | tf_op jit(solution)/shard_map/ppermute | solution.py:1005
  130.6 2.8 %collective-permute-start.36 = (bf16[32,1024]{1,0:T(8,128)(2,1)S(1)}, bf16[32,1024]{1,0:T(8,128)(2,1)S(1)}, u32[]{:S(2)}, u32[]{:S(2)}) collective-permute-start(bf16[32,1024]{1,0:T(8,128)(2,1)S(1)} %get-tuple-element.156), channel_id=1, source_target_pairs={{0,24},{2,26},{4,28},{6,30},{8,16},{10,18},{12,20},{14,22},{16,8},... | collective-permute-start | bytes 196616 | tf_op jit(solution)/shard_map/ppermute | solution.py:1005
  133.4 4.5 %tokens.1 = (bf16[128,1024]{1,0:T(8,128)(2,1)}, bf16[128,1024]{1,0:T(8,128)(2,1)}) custom-call(bf16[512,1024]{1,0:T(8,128)(2,1)S(1)} %get-tuple-element.125.refs_0_.refs_8_, bf16[128,1024]{1,0:T(8,128)(2,1)S(1)} %collective-permute-done.18.refs_1_, bf16[128,1024]{1,0:T(8,128)(2,1)S(1)} %collective-permute-done.19.refs_2_, ...), custom_call_target="tpu_custom_call" | custom-call | tf_op jit(solution)/shard_map/tokens/pallas_call | solution.py:416
  137.9 0.7 grad_sum.1
  138.6 1.5 %collective-permute-start.32 = (bf16[48,768]{1,0:T(8,128)(2,1)S(1)}, bf16[48,768]{1,0:T(8,128)(2,1)S(1)}, u32[]{:S(2)}, u32[]{:S(2)}) collective-permute-start(bf16[48,768]{1,0:T(8,128)(2,1)S(1)} %get-tuple-element.151), channel_id=1, source_target_pairs={{0,16},{2,18},{4,20},{6,22},{8,24},{10,26},{12,28},{14,30},{16,0},... | collective-permute-start | bytes 221192 | tf_op jit(solution)/shard_map/ppermute | solution.py:1005
  140.1 2.9 %collective-permute-start.33 = (bf16[48,768]{1,0:T(8,128)(2,1)S(1)}, bf16[48,768]{1,0:T(8,128)(2,1)S(1)}, u32[]{:S(2)}, u32[]{:S(2)}) collective-permute-start(bf16[48,768]{1,0:T(8,128)(2,1)S(1)} %get-tuple-element.152), channel_id=1, source_target_pairs={{0,24},{2,26},{4,28},{6,30},{8,16},{10,18},{12,20},{14,22},{16,8},... | collective-permute-start | bytes 221192 | tf_op jit(solution)/shard_map/ppermute | solution.py:1005
  143.0 0.8 join_in.1.refs_4_
  143.8 1.6 %collective-permute-done.32.refs_2_ = bf16[48,768]{1,0:T(8,128)(2,1)S(1)} collective-permute-done((bf16[48,768]{1,0:T(8,128)(2,1)S(1)}, bf16[48,768]{1,0:T(8,128)(2,1)S(1)}, u32[]{:S(2)}, u32[]{:S(2)}) %collective-permute-start.32) | collective-permute-done | bytes 73760 | tf_op jit(solution)/shard_map/ppermute | solution.py:1005
  145.4 0.9 collective-permute-done.33.refs_3_
  146.3 0.8 join_qkv.1
  147.1 0.5 copy.28
  (43 shorter events, 0.6 us)
Async XLA Ops:
  1.6 12.6 %copy-start = (bf16[144,1024]{1,0:T(8,128)(2,1)}, bf16[144,1024]{1,0:T(8,128)(2,1)S(1)}, u32[]{:S(2)}) copy-start(bf16[144,1024]{1,0:T(8,128)(2,1)S(1)} %pack.1.refs_10_.refs_0_) | copy-start | bytes 884740
  1.6 17.6 %collective-permute-start.1 = (bf16[144,1024]{1,0:T(8,128)(2,1)S(1)}, bf16[144,1024]{1,0:T(8,128)(2,1)}, u32[]{:S(2)}, u32[]{:S(2)}) collective-permute-start(bf16[144,1024]{1,0:T(8,128)(2,1)S(1)} %pack.1.refs_10_.refs_0_), channel_id=1, source_target_pairs={{0,16},{2,18},{4,20},{6,22},{8,24},{10,26},{12,28},{14,30},{16,0},... | collective-permute-start | bytes 884744 | tf_op jit(solution)/shard_map/ppermute | solution.py:1005
  5.7 14.1 %collective-permute-start = (bf16[144,1024]{1,0:T(8,128)(2,1)S(1)}, bf16[144,1024]{1,0:T(8,128)(2,1)S(1)}, u32[]{:S(2)}, u32[]{:S(2)}) collective-permute-start(bf16[144,1024]{1,0:T(8,128)(2,1)S(1)} %pack.1.refs_10_.refs_0_), channel_id=1, source_target_pairs={{0,8},{2,10},{4,12},{6,14},{8,0},{10,2},{12,4},{14,6},{16,24},{18,... | collective-permute-start | bytes 884744 | tf_op jit(solution)/shard_map/ppermute | solution.py:1005
  14.2 12.1 %collective-permute-start.5 = (bf16[3600,1024]{1,0:T(8,128)(2,1)}, bf16[3600,1024]{1,0:T(8,128)(2,1)}, u32[]{:S(2)}, u32[]{:S(2)}) collective-permute-start(bf16[3600,1024]{1,0:T(8,128)(2,1)} %prepare.1.refs_3_.refs_0_), channel_id=1, source_target_pairs={{0,1},{1,0},{2,3},{3,2},{4,5},{5,4},{6,7},{7,6},{8,9},{9,8},{10,11... | collective-permute-start | bytes 22118408 | tf_op jit(solution)/shard_map/ppermute | solution.py:1011
  19.3 13.7 %collective-permute-start.6 = (bf16[144,1024]{1,0:T(8,128)(2,1)}, bf16[144,1024]{1,0:T(8,128)(2,1)}, u32[]{:S(2)}, u32[]{:S(2)}) collective-permute-start(bf16[144,1024]{1,0:T(8,128)(2,1)} %collective-permute-done.1.refs_2_), channel_id=1, source_target_pairs={{0,8},{2,10},{4,12},{6,14},{8,0},{10,2},{12,4},{14,6},{16,24},{18,... | collective-permute-start | bytes 884744 | tf_op jit(solution)/shard_map/ppermute | solution.py:1005
  20.8 12.2 %copy-start.1 = (bf16[144,1024]{1,0:T(8,128)(2,1)S(1)}, bf16[144,1024]{1,0:T(8,128)(2,1)}, u32[]{:S(2)}) copy-start(bf16[144,1024]{1,0:T(8,128)(2,1)} %copy-done) | copy-start | bytes 884740
  20.8 19.0 %collective-permute-start.3 = (bf16[128,1024]{1,0:T(8,128)(2,1)S(1)}, bf16[128,1024]{1,0:T(8,128)(2,1)S(1)}, u32[]{:S(2)}, u32[]{:S(2)}) collective-permute-start(bf16[128,1024]{1,0:T(8,128)(2,1)S(1)} %hold.1.refs_2_.refs_0_), channel_id=1, source_target_pairs={{0,16},{2,18},{4,20},{6,22},{8,24},{10,26},{12,28},{14,30},{16,0},... | collective-permute-start | bytes 786440 | tf_op jit(solution)/shard_map/ppermute | solution.py:1005
  36.2 8.3 %collective-permute-start.7 = (bf16[784,128]{1,0:T(8,128)(2,1)S(1)}, bf16[784,128]{1,0:T(8,128)(2,1)S(1)}, u32[]{:S(2)}, u32[]{:S(2)}) collective-permute-start(bf16[784,128]{1,0:T(8,128)(2,1)S(1)} %get-tuple-element.92), channel_id=1, source_target_pairs={{0,2},{2,0},{4,6},{6,4},{8,10},{10,8},{12,14},{14,12},{16,18},{18,... | collective-permute-start | bytes 602120 | tf_op jit(solution)/shard_map/ppermute | solution.py:1008
  37.5 9.8 %collective-permute-start.8 = (bf16[784,128]{1,0:T(8,128)(2,1)S(1)}, bf16[784,128]{1,0:T(8,128)(2,1)S(1)}, u32[]{:S(2)}, u32[]{:S(2)}) collective-permute-start(bf16[784,128]{1,0:T(8,128)(2,1)S(1)} %get-tuple-element.93), channel_id=1, source_target_pairs={{0,4},{2,6},{4,0},{6,2},{8,12},{10,14},{12,8},{14,10},{16,20},{18,... | collective-permute-start | bytes 602120 | tf_op jit(solution)/shard_map/ppermute | solution.py:1008
  39.1 8.2 %collective-permute-start.9 = (bf16[784,128]{1,0:T(8,128)(2,1)S(1)}, bf16[784,128]{1,0:T(8,128)(2,1)S(1)}, u32[]{:S(2)}, u32[]{:S(2)}) collective-permute-start(bf16[784,128]{1,0:T(8,128)(2,1)S(1)} %get-tuple-element.94), channel_id=1, source_target_pairs={{0,6},{2,4},{4,2},{6,0},{8,14},{10,12},{12,10},{14,8},{16,22},{18,... | collective-permute-start | bytes 602120 | tf_op jit(solution)/shard_map/ppermute | solution.py:1008
  39.8 13.6 %collective-permute-start.2 = (bf16[128,1024]{1,0:T(8,128)(2,1)S(1)}, bf16[128,1024]{1,0:T(8,128)(2,1)S(1)}, u32[]{:S(2)}, u32[]{:S(2)}) collective-permute-start(bf16[128,1024]{1,0:T(8,128)(2,1)S(1)} %hold.1.refs_2_.refs_0_), channel_id=1, source_target_pairs={{0,8},{2,10},{4,12},{6,14},{8,0},{10,2},{12,4},{14,6},{16,24},{18,... | collective-permute-start | bytes 786440 | tf_op jit(solution)/shard_map/ppermute | solution.py:1005
  39.8 14.9 %collective-permute-start.4 = (bf16[128,1024]{1,0:T(8,128)(2,1)S(1)}, bf16[128,1024]{1,0:T(8,128)(2,1)S(1)}, u32[]{:S(2)}, u32[]{:S(2)}) collective-permute-start(bf16[128,1024]{1,0:T(8,128)(2,1)S(1)} %collective-permute-done.3.refs_2_), channel_id=1, source_target_pairs={{0,8},{2,10},{4,12},{6,14},{8,0},{10,2},{12,4},{14,6},{16,24},{18,... | collective-permute-start | bytes 786440 | tf_op jit(solution)/shard_map/ppermute | solution.py:1005
  41.8 5.5 %copy-start.2 = (f32[2048,128]{1,0:T(8,128)S(1)}, f32[2048,128]{1,0:T(8,128)}, u32[]{:S(2)}) copy-start(f32[2048,128]{1,0:T(8,128)} %constant.5.clone.refs_5_.refs_11_) | copy-start | bytes 3145732
  41.8 5.5 %copy-start.3 = (f32[2048,128]{1,0:T(8,128)S(1)}, f32[2048,128]{1,0:T(8,128)}, u32[]{:S(2)}) copy-start(f32[2048,128]{1,0:T(8,128)} %constant.4.clone.refs_4_.refs_10_) | copy-start | bytes 3145732
  44.5 32.5 %collective-permute-start.17 = (bf16[256,1024]{1,0:T(8,128)(2,1)S(1)}, bf16[256,1024]{1,0:T(8,128)(2,1)S(1)}, u32[]{:S(2)}, u32[]{:S(2)}) collective-permute-start(bf16[256,1024]{1,0:T(8,128)(2,1)S(1)} %get-tuple-element.122), channel_id=1, source_target_pairs={{0,8},{2,10},{4,12},{6,14},{8,0},{10,2},{12,4},{14,6},{16,24},{18,... | collective-permute-start | bytes 1572872 | tf_op jit(solution)/shard_map/ppermute | solution.py:1005
  55.3 10.5 %collective-permute-start.10 = (bf16[256,128]{1,0:T(8,128)(2,1)S(1)}, bf16[256,128]{1,0:T(8,128)(2,1)S(1)}, u32[]{:S(2)}, u32[]{:S(2)}) collective-permute-start(bf16[256,128]{1,0:T(8,128)(2,1)S(1)} %get-tuple-element.101), channel_id=1, source_target_pairs={{0,2},{2,0},{4,6},{6,4},{8,10},{10,8},{12,14},{14,12},{16,18},{18,... | collective-permute-start | bytes 196616 | tf_op jit(solution)/shard_map/ppermute | solution.py:1008
  56.6 9.3 %collective-permute-start.11 = (bf16[256,128]{1,0:T(8,128)(2,1)S(1)}, bf16[256,128]{1,0:T(8,128)(2,1)S(1)}, u32[]{:S(2)}, u32[]{:S(2)}) collective-permute-start(bf16[256,128]{1,0:T(8,128)(2,1)S(1)} %get-tuple-element.102), channel_id=1, source_target_pairs={{0,4},{2,6},{4,0},{6,2},{8,12},{10,14},{12,8},{14,10},{16,20},{18,... | collective-permute-start | bytes 196616 | tf_op jit(solution)/shard_map/ppermute | solution.py:1008
  58.1 7.8 %collective-permute-start.12 = (bf16[256,128]{1,0:T(8,128)(2,1)S(1)}, bf16[256,128]{1,0:T(8,128)(2,1)S(1)}, u32[]{:S(2)}, u32[]{:S(2)}) collective-permute-start(bf16[256,128]{1,0:T(8,128)(2,1)S(1)} %get-tuple-element.103), channel_id=1, source_target_pairs={{0,6},{2,4},{4,2},{6,0},{8,14},{10,12},{12,10},{14,8},{16,22},{18,... | collective-permute-start | bytes 196616 | tf_op jit(solution)/shard_map/ppermute | solution.py:1008
  62.2 15.7 %collective-permute-start.16 = (bf16[256,1024]{1,0:T(8,128)(2,1)S(1)}, bf16[256,1024]{1,0:T(8,128)(2,1)S(1)}, u32[]{:S(2)}, u32[]{:S(2)}) collective-permute-start(bf16[256,1024]{1,0:T(8,128)(2,1)S(1)} %get-tuple-element.120), channel_id=1, source_target_pairs={{0,8},{2,10},{4,12},{6,14},{8,0},{10,2},{12,4},{14,6},{16,24},{18,... | collective-permute-start | bytes 1572872 | tf_op jit(solution)/shard_map/ppermute | solution.py:1005
  65.8 29.8 %collective-permute-start.23 = (bf16[1088,1024]{1,0:T(8,128)(2,1)S(1)}, bf16[1088,1024]{1,0:T(8,128)(2,1)S(1)}, u32[]{:S(2)}, u32[]{:S(2)}) collective-permute-start(bf16[1088,1024]{1,0:T(8,128)(2,1)S(1)} %get-tuple-element.114.refs_12_), channel_id=1, source_target_pairs={{0,1},{1,0},{2,3},{3,2},{4,5},{5,4},{6,7},{7,6},{8,9},{9,8},{10,11... | collective-permute-start | bytes 6684680 | tf_op jit(solution)/shard_map/ppermute | solution.py:1011
  74.2 9.2 %collective-permute-start.13 = (bf16[1024,128]{1,0:T(8,128)(2,1)S(1)}, bf16[1024,128]{1,0:T(8,128)(2,1)S(1)}, u32[]{:S(2)}, u32[]{:S(2)}) collective-permute-start(bf16[1024,128]{1,0:T(8,128)(2,1)S(1)} %get-tuple-element.116), channel_id=1, source_target_pairs={{0,2},{2,0},{4,6},{6,4},{8,10},{10,8},{12,14},{14,12},{16,18},{18,... | collective-permute-start | bytes 786440 | tf_op jit(solution)/shard_map/ppermute | solution.py:1008
  75.5 14.0 %collective-permute-start.14 = (bf16[1024,128]{1,0:T(8,128)(2,1)S(1)}, bf16[1024,128]{1,0:T(8,128)(2,1)S(1)}, u32[]{:S(2)}, u32[]{:S(2)}) collective-permute-start(bf16[1024,128]{1,0:T(8,128)(2,1)S(1)} %get-tuple-element.117), channel_id=1, source_target_pairs={{0,4},{2,6},{4,0},{6,2},{8,12},{10,14},{12,8},{14,10},{16,20},{18,... | collective-permute-start | bytes 786440 | tf_op jit(solution)/shard_map/ppermute | solution.py:1008
  77.0 12.5 %collective-permute-start.15 = (bf16[1024,128]{1,0:T(8,128)(2,1)S(1)}, bf16[1024,128]{1,0:T(8,128)(2,1)S(1)}, u32[]{:S(2)}, u32[]{:S(2)}) collective-permute-start(bf16[1024,128]{1,0:T(8,128)(2,1)S(1)} %get-tuple-element.118), channel_id=1, source_target_pairs={{0,6},{2,4},{4,2},{6,0},{8,14},{10,12},{12,10},{14,8},{16,22},{18,... | collective-permute-start | bytes 786440 | tf_op jit(solution)/shard_map/ppermute | solution.py:1008
  77.9 21.6 %collective-permute-start.21 = (bf16[128,1024]{1,0:T(8,128)(2,1)S(1)}, bf16[128,1024]{1,0:T(8,128)(2,1)S(1)}, u32[]{:S(2)}, u32[]{:S(2)}) collective-permute-start(bf16[128,1024]{1,0:T(8,128)(2,1)S(1)} %get-tuple-element.129), channel_id=1, source_target_pairs={{0,16},{2,18},{4,20},{6,22},{8,24},{10,26},{12,28},{14,30},{16,0},... | collective-permute-start | bytes 786440 | tf_op jit(solution)/shard_map/ppermute | solution.py:1005
  83.4 20.7 %collective-permute-start.22 = (bf16[128,1024]{1,0:T(8,128)(2,1)S(1)}, bf16[128,1024]{1,0:T(8,128)(2,1)S(1)}, u32[]{:S(2)}, u32[]{:S(2)}) collective-permute-start(bf16[128,1024]{1,0:T(8,128)(2,1)S(1)} %get-tuple-element.130), channel_id=1, source_target_pairs={{0,16},{2,18},{4,20},{6,22},{8,24},{10,26},{12,28},{14,30},{16,0},... | collective-permute-start | bytes 786440 | tf_op jit(solution)/shard_map/ppermute | solution.py:1005
  90.5 18.2 %collective-permute-start.18 = (bf16[128,1024]{1,0:T(8,128)(2,1)S(1)}, bf16[128,1024]{1,0:T(8,128)(2,1)S(1)}, u32[]{:S(2)}, u32[]{:S(2)}) collective-permute-start(bf16[128,1024]{1,0:T(8,128)(2,1)S(1)} %get-tuple-element.126), channel_id=1, source_target_pairs={{0,8},{2,10},{4,12},{6,14},{8,0},{10,2},{12,4},{14,6},{16,24},{18,... | collective-permute-start | bytes 786440 | tf_op jit(solution)/shard_map/ppermute | solution.py:1005
  95.5 5.3 %collective-permute-start.27 = (bf16[704,768]{1,0:T(8,128)(2,1)S(1)}, bf16[704,768]{1,0:T(8,128)(2,1)S(1)}, u32[]{:S(2)}, u32[]{:S(2)}) collective-permute-start(bf16[704,768]{1,0:T(8,128)(2,1)S(1)} %get-tuple-element.136.refs_2_), channel_id=1, source_target_pairs={{0,1},{1,0},{2,3},{3,2},{4,5},{5,4},{6,7},{7,6},{8,9},{9,8},{10,11... | collective-permute-start | bytes 3244040 | tf_op jit(solution)/shard_map/ppermute | solution.py:1011
  96.0 15.5 %collective-permute-start.24 = (bf16[272,1024]{1,0:T(8,128)(2,1)S(1)}, bf16[272,1024]{1,0:T(8,128)(2,1)S(1)}, u32[]{:S(2)}, u32[]{:S(2)}) collective-permute-start(bf16[272,1024]{1,0:T(8,128)(2,1)S(1)} %get-tuple-element.138), channel_id=1, source_target_pairs={{0,2},{2,0},{4,6},{6,4},{8,10},{10,8},{12,14},{14,12},{16,18},{18,... | collective-permute-start | bytes 1671176 | tf_op jit(solution)/shard_map/ppermute | solution.py:1008
  99.5 24.6 %collective-permute-start.25 = (bf16[272,1024]{1,0:T(8,128)(2,1)S(1)}, bf16[272,1024]{1,0:T(8,128)(2,1)S(1)}, u32[]{:S(2)}, u32[]{:S(2)}) collective-permute-start(bf16[272,1024]{1,0:T(8,128)(2,1)S(1)} %get-tuple-element.139), channel_id=1, source_target_pairs={{0,4},{2,6},{4,0},{6,2},{8,12},{10,14},{12,8},{14,10},{16,20},{18,... | collective-permute-start | bytes 1671176 | tf_op jit(solution)/shard_map/ppermute | solution.py:1008
  100.8 25.7 %collective-permute-start.26 = (bf16[272,1024]{1,0:T(8,128)(2,1)S(1)}, bf16[272,1024]{1,0:T(8,128)(2,1)S(1)}, u32[]{:S(2)}, u32[]{:S(2)}) collective-permute-start(bf16[272,1024]{1,0:T(8,128)(2,1)S(1)} %get-tuple-element.140), channel_id=1, source_target_pairs={{0,6},{2,4},{4,2},{6,0},{8,14},{10,12},{12,10},{14,8},{16,22},{18,... | collective-permute-start | bytes 1671176 | tf_op jit(solution)/shard_map/ppermute | solution.py:1008
  104.1 24.9 %collective-permute-start.19 = (bf16[128,1024]{1,0:T(8,128)(2,1)S(1)}, bf16[128,1024]{1,0:T(8,128)(2,1)S(1)}, u32[]{:S(2)}, u32[]{:S(2)}) collective-permute-start(bf16[128,1024]{1,0:T(8,128)(2,1)S(1)} %get-tuple-element.127), channel_id=1, source_target_pairs={{0,16},{2,18},{4,20},{6,22},{8,24},{10,26},{12,28},{14,30},{16,0},... | collective-permute-start | bytes 786440 | tf_op jit(solution)/shard_map/ppermute | solution.py:1005
  108.7 20.3 %collective-permute-start.20 = (bf16[128,1024]{1,0:T(8,128)(2,1)S(1)}, bf16[128,1024]{1,0:T(8,128)(2,1)S(1)}, u32[]{:S(2)}, u32[]{:S(2)}) collective-permute-start(bf16[128,1024]{1,0:T(8,128)(2,1)S(1)} %get-tuple-element.128), channel_id=1, source_target_pairs={{0,24},{2,26},{4,28},{6,30},{8,16},{10,18},{12,20},{14,22},{16,8},... | collective-permute-start | bytes 786440 | tf_op jit(solution)/shard_map/ppermute | solution.py:1005
  111.5 19.1 %collective-permute-start.28 = (bf16[176,768]{1,0:T(8,128)(2,1)S(1)}, bf16[176,768]{1,0:T(8,128)(2,1)S(1)}, u32[]{:S(2)}, u32[]{:S(2)}) collective-permute-start(bf16[176,768]{1,0:T(8,128)(2,1)S(1)} %get-tuple-element.146), channel_id=1, source_target_pairs={{0,2},{2,0},{4,6},{6,4},{8,10},{10,8},{12,14},{14,12},{16,18},{18,... | collective-permute-start | bytes 811016 | tf_op jit(solution)/shard_map/ppermute | solution.py:1008
  124.1 13.8 %collective-permute-start.29 = (bf16[176,768]{1,0:T(8,128)(2,1)S(1)}, bf16[176,768]{1,0:T(8,128)(2,1)S(1)}, u32[]{:S(2)}, u32[]{:S(2)}) collective-permute-start(bf16[176,768]{1,0:T(8,128)(2,1)S(1)} %get-tuple-element.147), channel_id=1, source_target_pairs={{0,4},{2,6},{4,0},{6,2},{8,12},{10,14},{12,8},{14,10},{16,20},{18,... | collective-permute-start | bytes 811016 | tf_op jit(solution)/shard_map/ppermute | solution.py:1008
  126.6 11.3 %collective-permute-start.30 = (bf16[176,768]{1,0:T(8,128)(2,1)S(1)}, bf16[176,768]{1,0:T(8,128)(2,1)S(1)}, u32[]{:S(2)}, u32[]{:S(2)}) collective-permute-start(bf16[176,768]{1,0:T(8,128)(2,1)S(1)} %get-tuple-element.148), channel_id=1, source_target_pairs={{0,6},{2,4},{4,2},{6,0},{8,14},{10,12},{12,10},{14,8},{16,22},{18,... | collective-permute-start | bytes 811016 | tf_op jit(solution)/shard_map/ppermute | solution.py:1008
  129.0 11.1 %collective-permute-start.34 = (bf16[32,1024]{1,0:T(8,128)(2,1)S(1)}, bf16[32,1024]{1,0:T(8,128)(2,1)S(1)}, u32[]{:S(2)}, u32[]{:S(2)}) collective-permute-start(bf16[32,1024]{1,0:T(8,128)(2,1)S(1)} %get-tuple-element.154), channel_id=1, source_target_pairs={{0,8},{2,10},{4,12},{6,14},{8,0},{10,2},{12,4},{14,6},{16,24},{18,... | collective-permute-start | bytes 196616 | tf_op jit(solution)/shard_map/ppermute | solution.py:1005
  129.0 14.0 %collective-permute-start.35 = (bf16[32,1024]{1,0:T(8,128)(2,1)S(1)}, bf16[32,1024]{1,0:T(8,128)(2,1)S(1)}, u32[]{:S(2)}, u32[]{:S(2)}) collective-permute-start(bf16[32,1024]{1,0:T(8,128)(2,1)S(1)} %get-tuple-element.155), channel_id=1, source_target_pairs={{0,16},{2,18},{4,20},{6,22},{8,24},{10,26},{12,28},{14,30},{16,0},... | collective-permute-start | bytes 196616 | tf_op jit(solution)/shard_map/ppermute | solution.py:1005
  130.6 12.4 %collective-permute-start.36 = (bf16[32,1024]{1,0:T(8,128)(2,1)S(1)}, bf16[32,1024]{1,0:T(8,128)(2,1)S(1)}, u32[]{:S(2)}, u32[]{:S(2)}) collective-permute-start(bf16[32,1024]{1,0:T(8,128)(2,1)S(1)} %get-tuple-element.156), channel_id=1, source_target_pairs={{0,24},{2,26},{4,28},{6,30},{8,16},{10,18},{12,20},{14,22},{16,8},... | collective-permute-start | bytes 196616 | tf_op jit(solution)/shard_map/ppermute | solution.py:1005
  137.9 9.2 %copy-start.4 = (f32[1,32]{1,0:T(1,128)S(1)}, f32[1,32]{1,0:T(1,128)}, u32[]{:S(2)}) copy-start(f32[1,32]{1,0:T(1,128)} %get-tuple-element.162) | copy-start | bytes 388
  138.6 5.2 %collective-permute-start.31 = (bf16[48,768]{1,0:T(8,128)(2,1)S(1)}, bf16[48,768]{1,0:T(8,128)(2,1)S(1)}, u32[]{:S(2)}, u32[]{:S(2)}) collective-permute-start(bf16[48,768]{1,0:T(8,128)(2,1)S(1)} %get-tuple-element.150), channel_id=1, source_target_pairs={{0,8},{2,10},{4,12},{6,14},{8,0},{10,2},{12,4},{14,6},{16,24},{18,... | collective-permute-start | bytes 221192 | tf_op jit(solution)/shard_map/ppermute | solution.py:1005
  138.6 6.8 %collective-permute-start.32 = (bf16[48,768]{1,0:T(8,128)(2,1)S(1)}, bf16[48,768]{1,0:T(8,128)(2,1)S(1)}, u32[]{:S(2)}, u32[]{:S(2)}) collective-permute-start(bf16[48,768]{1,0:T(8,128)(2,1)S(1)} %get-tuple-element.151), channel_id=1, source_target_pairs={{0,16},{2,18},{4,20},{6,22},{8,24},{10,26},{12,28},{14,30},{16,0},... | collective-permute-start | bytes 221192 | tf_op jit(solution)/shard_map/ppermute | solution.py:1005
  140.1 6.2 %collective-permute-start.33 = (bf16[48,768]{1,0:T(8,128)(2,1)S(1)}, bf16[48,768]{1,0:T(8,128)(2,1)S(1)}, u32[]{:S(2)}, u32[]{:S(2)}) collective-permute-start(bf16[48,768]{1,0:T(8,128)(2,1)S(1)} %get-tuple-element.152), channel_id=1, source_target_pairs={{0,24},{2,26},{4,28},{6,30},{8,16},{10,18},{12,20},{14,22},{16,8},... | collective-permute-start | bytes 221192 | tf_op jit(solution)/shard_map/ppermute | solution.py:1005

commit v7 on v6

--- a/solution.py
+++ b/solution.py
@@ -836,8 +836,8 @@
     line, _, _ = spot()
     total = adder(own, r1, r2, r3)
     down_ref[...] = total(slice(0, 128))
-    bias_in[...] = total(slice(256, 264), slice(0, 128))[:1]
-    bias_out[...] = owned_lanes(total(slice(256, 264), slice(128, 384)))[:1]
+    bias_in[...] = total(slice(256, 264), slice(0, 128))[:1].reshape(128)
+    bias_out[...] = owned_lanes(total(slice(256, 264), slice(128, 384)))[:1].reshape(32)
     for slot, ref in enumerate((i0, i1, i2, i3)):
         rows = pl.ds(pl.multiple_of(128 + 32 * (line ^ slot), 32), 32)
         ref[...] = total(rows).astype(ref.dtype)
@@ -1216,7 +1216,7 @@
     qkv_sums = with_places(qkv_blocks)
     grad_down, grad_b_in, grad_b, *in_slots = run(
         feed_sum_kernel,
-        [far((128, width), F32), ((1, 128), F32), ((1, 32), F32), near((32, width), F32)]
+        [far((128, width), F32), far((128,), F32), far((32,), F32), near((32, width), F32)]
         + [near((32, width), BF16)] * 3,
         [],
         *feed_in,
@@ -1252,11 +1252,11 @@
         grad_qkv,
         grad_qv,
         grad_out,
-        grad_b[0],
+        grad_b,
         grad_in,
-        grad_b_in[0],
+        grad_b_in,
         grad_down,
-        grad_b[0],
+        grad_b,
     )
 
 

time: 148 us -> 148 us (level)
  no operation moved by 1% of the time
where the time goes in v7:
time: 148 us
  Pallas kernels  54 us (36%)
  starting transfers between devices  51.3 us (35%)
  waiting for transfers between devices  40.8 us (28%)
    pallas_call x22, Pallas kernels, call(): pl.pallas_call(body, name=name, out_shape=outs, in_specs=specs + [loose]...  54 us
    ppermute x19, starting transfers between devices, over_lines(): return lax.ppermute(x, 'ctx', [(i, i ^ k * ACROSS) for i in positions])  31.3 us
    ppermute x15, waiting for transfers between devices, over_places(): return lax.ppermute(x, 'ctx', [(i, i ^ j) for i in positions])  19.9 us
    ppermute x15, starting transfers between devices, over_places(): return lax.ppermute(x, 'ctx', [(i, i ^ j) for i in positions])  19.9 us
    ppermute x19, waiting for transfers between devices, over_lines(): return lax.ppermute(x, 'ctx', [(i, i ^ k * ACROSS) for i in positions])  19 us
  transfers between devices with their start and end apart: 37, of which 14 were waited for; matrix products, arithmetic and copies ran while one was open for 0% of the time, Pallas kernels for 35%

profile of v7, /device:TPU:0, one launch (start us, length us, event | category | flops | bytes accessed | tf_op | source)
XLA Modules:
  0.0 147.6 jit_solution(3890632673741308497)
XLA Ops:
  0.6 1.0 pack.1.refs_10_.refs_0_
  1.6 4.1 %collective-permute-start.1 = (bf16[144,1024]{1,0:T(8,128)(2,1)S(1)}, bf16[144,1024]{1,0:T(8,128)(2,1)}, u32[]{:S(2)}, u32[]{:S(2)}) collective-permute-start(bf16[144,1024]{1,0:T(8,128)(2,1)S(1)} %pack.1.refs_10_.refs_0_), channel_id=1, source_target_pairs={{0,16},{2,18},{4,20},{6,22},{8,24},{10,26},{12,28},{14,30},{16,0},... | collective-permute-start | bytes 884744 | tf_op jit(solution)/shard_map/ppermute | solution.py:1005
  5.7 1.6 %collective-permute-start = (bf16[144,1024]{1,0:T(8,128)(2,1)S(1)}, bf16[144,1024]{1,0:T(8,128)(2,1)S(1)}, u32[]{:S(2)}, u32[]{:S(2)}) collective-permute-start(bf16[144,1024]{1,0:T(8,128)(2,1)S(1)} %pack.1.refs_10_.refs_0_), channel_id=1, source_target_pairs={{0,8},{2,10},{4,12},{6,14},{8,0},{10,2},{12,4},{14,6},{16,24},{18,... | collective-permute-start | bytes 884744 | tf_op jit(solution)/shard_map/ppermute | solution.py:1005
  7.3 6.9 %prepare.1.refs_3_.refs_0_ = bf16[3600,1024]{1,0:T(8,128)(2,1)} custom-call(bf16[512,3072]{1,0:T(8,128)(2,1)} %refs_0_.1, bf16[512,4096]{1,0:T(8,128)(2,1)} %refs_1_.1, bf16[512,1024]{1,0:T(8,128)(2,1)} %refs_2_.1, bf16[2048,1024]{1,0:T(8,128)(2,1)} %refs_3_.1, bf16[512]{0:T(512)(128)(2,1)} %refs_4_.2, bf16[512]{0:T(512)(128)(2,1)} %refs_5_.2, ...), custom_call_target="tpu_custom_call" | custom-call | tf_op jit(solution)/shard_map/prepare/pallas_call | solution.py:416
  14.3 5.0 %collective-permute-done.1.refs_2_ = bf16[144,1024]{1,0:T(8,128)(2,1)} collective-permute-done((bf16[144,1024]{1,0:T(8,128)(2,1)S(1)}, bf16[144,1024]{1,0:T(8,128)(2,1)}, u32[]{:S(2)}, u32[]{:S(2)}) %collective-permute-start.1) | collective-permute-done | bytes 294944 | tf_op jit(solution)/shard_map/ppermute | solution.py:1005
  19.3 0.5 collective-permute-start.6
  19.8 1.0 hold.1.refs_2_.refs_0_
  20.8 3.6 %collective-permute-start.3 = (bf16[128,1024]{1,0:T(8,128)(2,1)S(1)}, bf16[128,1024]{1,0:T(8,128)(2,1)S(1)}, u32[]{:S(2)}, u32[]{:S(2)}) collective-permute-start(bf16[128,1024]{1,0:T(8,128)(2,1)S(1)} %hold.1.refs_2_.refs_0_), channel_id=1, source_target_pairs={{0,16},{2,18},{4,20},{6,22},{8,24},{10,26},{12,28},{14,30},{16,0},... | collective-permute-start | bytes 786440 | tf_op jit(solution)/shard_map/ppermute | solution.py:1005
  24.3 2.0 %collective-permute-done.5.refs_1_ = bf16[3600,1024]{1,0:T(8,128)(2,1)} collective-permute-done((bf16[3600,1024]{1,0:T(8,128)(2,1)}, bf16[3600,1024]{1,0:T(8,128)(2,1)}, u32[]{:S(2)}, u32[]{:S(2)}) %collective-permute-start.5) | collective-permute-done | bytes 7372832 | tf_op jit(solution)/shard_map/ppermute | solution.py:1011
  26.3 4.8 %assemble.1 = (bf16[1024,3072]{1,0:T(8,128)(2,1)S(1)}, bf16[1024,1024]{1,0:T(8,128)(2,1)S(1)}, bf16[1024,1024]{1,0:T(8,128)(2,1)S(1)}, bf16[1024,1024]{1,0:T(8,128)(2,1)S(1)}, f32[32,512]{1,0:T(8,128)S(1)}) custom-call(bf16[3600,1024]{1,0:T(8,128)(2,1)} %prepare.1.refs_3_.refs_0_, bf16[3600,1024]{1,0:T(8,128)(2,1)} %collective-permute-done.5.refs_1_, ...), custom_call_target="tpu_custom_call" | custom-call | tf_op jit(solution)/shard_map/assemble/pallas_call | solution.py:416
  31.2 1.8 %collective-permute-done.6.refs_3_ = bf16[144,1024]{1,0:T(8,128)(2,1)} collective-permute-done((bf16[144,1024]{1,0:T(8,128)(2,1)}, bf16[144,1024]{1,0:T(8,128)(2,1)}, u32[]{:S(2)}, u32[]{:S(2)}) %collective-permute-start.6) | collective-permute-done | bytes 294944 | tf_op jit(solution)/shard_map/ppermute | solution.py:1005
  33.0 3.2 %project.1 = (bf16[784,128]{1,0:T(8,128)(2,1)S(1)}, bf16[784,128]{1,0:T(8,128)(2,1)S(1)}, bf16[784,128]{1,0:T(8,128)(2,1)S(1)}, bf16[784,128]{1,0:T(8,128)(2,1)S...) custom-call(bf16[144,1024]{1,0:T(8,128)(2,1)S(1)} %copy-done.1, ...), custom_call_target="tpu_custom_call" | custom-call | tf_op jit(solution)/shard_map/project/pallas_call | solution.py:416
  36.2 1.3 collective-permute-start.7
  37.5 1.5 %collective-permute-start.8 = (bf16[784,128]{1,0:T(8,128)(2,1)S(1)}, bf16[784,128]{1,0:T(8,128)(2,1)S(1)}, u32[]{:S(2)}, u32[]{:S(2)}) collective-permute-start(bf16[784,128]{1,0:T(8,128)(2,1)S(1)} %get-tuple-element.93), channel_id=1, source_target_pairs={{0,4},{2,6},{4,0},{6,2},{8,12},{10,14},{12,8},{14,10},{16,20},{18,... | collective-permute-start | bytes 602120 | tf_op jit(solution)/shard_map/ppermute | solution.py:1008
  39.1 0.7 collective-permute-start.9
  39.8 2.0 %collective-permute-start.4 = (bf16[128,1024]{1,0:T(8,128)(2,1)S(1)}, bf16[128,1024]{1,0:T(8,128)(2,1)S(1)}, u32[]{:S(2)}, u32[]{:S(2)}) collective-permute-start(bf16[128,1024]{1,0:T(8,128)(2,1)S(1)} %collective-permute-done.3.refs_2_), channel_id=1, source_target_pairs={{0,8},{2,10},{4,12},{6,14},{8,0},{10,2},{12,4},{14,6},{16,24},{18,... | collective-permute-start | bytes 786440 | tf_op jit(solution)/shard_map/ppermute | solution.py:1005
  41.8 2.7 %feed.1 = (f32[512,1024]{1,0:T(8,128)S(1)}, bf16[1024,512]{1,0:T(8,128)(2,1)S(1)}, f32[256,1024]{1,0:T(8,128)S(1)}, bf16[256,1024]{1,0:T(8,128)(2,1)S(1)}) custom-call(bf16[512,1024]{1,0:T(8,128)(2,1)S(1)} %get-tuple-element.95.refs_0_, bf16[1024,1024]{1,0:T(8,128)(2,1)S(1)} %get-tuple-element.96.refs_1_.refs_2_, ...), custom_call_target="tpu_custom_call" | custom-call | tf_op jit(solution)/shard_map/feed/pallas_call | solution.py:416
  44.6 2.7 %collective-permute-done.8.refs_2_ = bf16[784,128]{1,0:T(8,128)(2,1)S(1)} collective-permute-done((bf16[784,128]{1,0:T(8,128)(2,1)S(1)}, bf16[784,128]{1,0:T(8,128)(2,1)S(1)}, u32[]{:S(2)}, u32[]{:S(2)}) %collective-permute-start.8) | collective-permute-done | bytes 200736 | tf_op jit(solution)/shard_map/ppermute | solution.py:1008
  47.3 6.1 %attend.1 = (bf16[2048,128]{1,0:T(8,128)(2,1)S(1)}, bf16[2048,128]{1,0:T(8,128)(2,1)S(1)}, bf16[2048,64]{1,0:T(8,128)(2,1)S(1)}, f32[2048,64]{1,0:T(8,128)S(1)},...) custom-call(bf16[784,128]{1,0:T(8,128)(2,1)S(1)} %get-tuple-element.91.refs_4_.refs_0_, ...), custom_call_target="tpu_custom_call" | custom-call | flops 2300000000 | tf_op jit(solution)/shard_map/attend/pallas_call | solution.py:416
  53.4 1.2 collective-permute-done.4.refs_3_
  54.6 0.6 back_rows.1
  55.3 1.3 collective-permute-start.10
  56.6 1.5 %collective-permute-start.11 = (bf16[256,128]{1,0:T(8,128)(2,1)S(1)}, bf16[256,128]{1,0:T(8,128)(2,1)S(1)}, u32[]{:S(2)}, u32[]{:S(2)}) collective-permute-start(bf16[256,128]{1,0:T(8,128)(2,1)S(1)} %get-tuple-element.102), channel_id=1, source_target_pairs={{0,4},{2,6},{4,0},{6,2},{8,12},{10,14},{12,8},{14,10},{16,20},{18,... | collective-permute-start | bytes 196616 | tf_op jit(solution)/shard_map/ppermute | solution.py:1008
  58.1 0.7 collective-permute-start.12
  58.8 3.4 %feed_grad.1 = (bf16[512,1024]{1,0:T(8,128)(2,1)S(1)}, f32[8,1024]{1,0:T(8,128)S(1)}, f32[512,1024]{1,0:T(8,128)S(1)}, f32[256,1024]{1,0:T(8,128)S(1)}, bf16[256,1024]{1,0:T(8,128)(2,1)S(1)}) custom-call(bf16[512,1024]{1,0:T(8,128)(2,1)S(1)} %get-tuple-element.109.refs_0_.refs_6_.refs_11_, f32[512,1024]{1,0:T(8,128)S(1)} %get-tuple-element.98.refs_6_.refs_1_, ...), custom_call_target="tpu_custom_call" | custom-call | flops 4600000000 | tf_op jit(solution)/shard_map/feed_grad/pallas_call | solution.py:416
  62.3 3.5 %feed_terms.1 = (bf16[1088,1024]{1,0:T(8,128)(2,1)S(1)}, f32[1088,1024]{1,0:T(8,128)S(1)}) custom-call(bf16[512,1024]{1,0:T(8,128)(2,1)S(1)} %get-tuple-element.109.refs_0_.refs_6_.refs_11_, bf16[1024,512]{1,0:T(8,128)(2,1)S(1)} %get-tuple-element.110.refs_1_, bf16[1024,512]{1,0:T(8,128)(2,1)S(1)} %get-tuple-element.111.refs_2_.refs_3_, ...), custom_call_target="tpu_custom_call" | custom-call | flops 575000000 | tf_op jit(solution)/shard_map/feed_terms/pallas_call | solution.py:416
  65.9 8.3 %attend_back.1 = (bf16[1024,128]{1,0:T(8,128)(2,1)S(1)}, bf16[1024,128]{1,0:T(8,128)(2,1)S(1)}, bf16[1024,128]{1,0:T(8,128)(2,1)S(1)}, bf16[1024,128]{1,0:T(8,128)(2,1)S(1)}, f32[8,128]{1,0:T(8,128)S(1)}) custom-call(bf16[256,128]{1,0:T(8,128)(2,1)S(1)} %get-tuple-element.100.refs_4_.refs_0_, bf16[256,128]{1,0:T(8,128)(2,1)S(1)} %collective-permute-done.10.refs_1_, ...), custom_call_target="tpu_custom_call" | custom-call | tf_op jit(solution)/shard_map/attend_back/pallas_call | solution.py:416
  74.2 1.3 collective-permute-start.13
  75.5 1.5 %collective-permute-start.14 = (bf16[1024,128]{1,0:T(8,128)(2,1)S(1)}, bf16[1024,128]{1,0:T(8,128)(2,1)S(1)}, u32[]{:S(2)}, u32[]{:S(2)}) collective-permute-start(bf16[1024,128]{1,0:T(8,128)(2,1)S(1)} %get-tuple-element.117), channel_id=1, source_target_pairs={{0,4},{2,6},{4,0},{6,2},{8,12},{10,14},{12,8},{14,10},{16,20},{18,... | collective-permute-start | bytes 786440 | tf_op jit(solution)/shard_map/ppermute | solution.py:1008
  77.0 0.7 collective-permute-start.15
  77.9 3.1 %collective-permute-start.21 = (bf16[128,1024]{1,0:T(8,128)(2,1)S(1)}, bf16[128,1024]{1,0:T(8,128)(2,1)S(1)}, u32[]{:S(2)}, u32[]{:S(2)}) collective-permute-start(bf16[128,1024]{1,0:T(8,128)(2,1)S(1)} %get-tuple-element.129), channel_id=1, source_target_pairs={{0,16},{2,18},{4,20},{6,22},{8,24},{10,26},{12,28},{14,30},{16,0},... | collective-permute-start | bytes 786440 | tf_op jit(solution)/shard_map/ppermute | solution.py:1005
  81.0 0.1 halve.3
  81.1 2.3 %collective-permute-done.13.refs_1_ = bf16[1024,128]{1,0:T(8,128)(2,1)S(1)} collective-permute-done((bf16[1024,128]{1,0:T(8,128)(2,1)S(1)}, bf16[1024,128]{1,0:T(8,128)(2,1)S(1)}, u32[]{:S(2)}, u32[]{:S(2)}) %collective-permute-start.13) | collective-permute-done | bytes 262176 | tf_op jit(solution)/shard_map/ppermute | solution.py:1008
  83.4 3.1 %collective-permute-start.22 = (bf16[128,1024]{1,0:T(8,128)(2,1)S(1)}, bf16[128,1024]{1,0:T(8,128)(2,1)S(1)}, u32[]{:S(2)}, u32[]{:S(2)}) collective-permute-start(bf16[128,1024]{1,0:T(8,128)(2,1)S(1)} %get-tuple-element.130), channel_id=1, source_target_pairs={{0,16},{2,18},{4,20},{6,22},{8,24},{10,26},{12,28},{14,30},{16,0},... | collective-permute-start | bytes 786440 | tf_op jit(solution)/shard_map/ppermute | solution.py:1005
  86.4 3.1 %collective-permute-done.14.refs_2_ = bf16[1024,128]{1,0:T(8,128)(2,1)S(1)} collective-permute-done((bf16[1024,128]{1,0:T(8,128)(2,1)S(1)}, bf16[1024,128]{1,0:T(8,128)(2,1)S(1)}, u32[]{:S(2)}, u32[]{:S(2)}) %collective-permute-start.14) | collective-permute-done | bytes 262176 | tf_op jit(solution)/shard_map/ppermute | solution.py:1008
  89.5 0.9 unpack.1
  90.5 2.1 %collective-permute-start.18 = (bf16[128,1024]{1,0:T(8,128)(2,1)S(1)}, bf16[128,1024]{1,0:T(8,128)(2,1)S(1)}, u32[]{:S(2)}, u32[]{:S(2)}) collective-permute-start(bf16[128,1024]{1,0:T(8,128)(2,1)S(1)} %get-tuple-element.126), channel_id=1, source_target_pairs={{0,8},{2,10},{4,12},{6,14},{8,0},{10,2},{12,4},{14,6},{16,24},{18,... | collective-permute-start | bytes 786440 | tf_op jit(solution)/shard_map/ppermute | solution.py:1005
  92.6 3.0 %grads.1 = (bf16[704,768]{1,0:T(8,128)(2,1)S(1)}, f32[704,768]{1,0:T(8,128)S(1)}) custom-call(bf16[512,1024]{1,0:T(8,128)(2,1)S(1)} %get-tuple-element.125.refs_0_.refs_8_, f32[512,1024]{1,0:T(8,128)S(1)} %get-tuple-element.132.refs_1_, f32[512,1024]{1,0:T(8,128)S(1)} %get-tuple-element.133.refs_2_, ...), custom_call_target="tpu_custom_call" | custom-call | flops 4600000000 | tf_op jit(solution)/shard_map/grads/pallas_call | solution.py:416
  95.6 0.4 share_twin.2
  96.0 1.3 collective-permute-start.24
  97.3 2.2 %collective-permute-done.21.refs_7_ = bf16[128,1024]{1,0:T(8,128)(2,1)S(1)} collective-permute-done((bf16[128,1024]{1,0:T(8,128)(2,1)S(1)}, bf16[128,1024]{1,0:T(8,128)(2,1)S(1)}, u32[]{:S(2)}, u32[]{:S(2)}) %collective-permute-start.21) | collective-permute-done | bytes 262176 | tf_op jit(solution)/shard_map/ppermute | solution.py:1005
  99.5 1.4 collective-permute-start.25
  100.8 1.4 collective-permute-start.26
  102.3 0.2 share_twin.3
  102.5 1.6 %collective-permute-done.22.refs_9_ = bf16[128,1024]{1,0:T(8,128)(2,1)S(1)} collective-permute-done((bf16[128,1024]{1,0:T(8,128)(2,1)S(1)}, bf16[128,1024]{1,0:T(8,128)(2,1)S(1)}, u32[]{:S(2)}, u32[]{:S(2)}) %collective-permute-start.22) | collective-permute-done | bytes 262176 | tf_op jit(solution)/shard_map/ppermute | solution.py:1005
  104.1 4.7 %collective-permute-done.18.refs_1_ = bf16[128,1024]{1,0:T(8,128)(2,1)S(1)} collective-permute-done((bf16[128,1024]{1,0:T(8,128)(2,1)S(1)}, bf16[128,1024]{1,0:T(8,128)(2,1)S(1)}, u32[]{:S(2)}, u32[]{:S(2)}) %collective-permute-start.18) | collective-permute-done | bytes 262176 | tf_op jit(solution)/shard_map/ppermute | solution.py:1005
  108.7 2.3 %collective-permute-start.20 = (bf16[128,1024]{1,0:T(8,128)(2,1)S(1)}, bf16[128,1024]{1,0:T(8,128)(2,1)S(1)}, u32[]{:S(2)}, u32[]{:S(2)}) collective-permute-start(bf16[128,1024]{1,0:T(8,128)(2,1)S(1)} %get-tuple-element.128), channel_id=1, source_target_pairs={{0,24},{2,26},{4,28},{6,30},{8,16},{10,18},{12,20},{14,22},{16,8},... | collective-permute-start | bytes 786440 | tf_op jit(solution)/shard_map/ppermute | solution.py:1005
  111.0 0.5 collective-permute-done.24.refs_1_
  111.5 1.2 collective-permute-start.28
  112.7 11.4 %collective-permute-done.25.refs_2_ = bf16[272,1024]{1,0:T(8,128)(2,1)S(1)} collective-permute-done((bf16[272,1024]{1,0:T(8,128)(2,1)S(1)}, bf16[272,1024]{1,0:T(8,128)(2,1)S(1)}, u32[]{:S(2)}, u32[]{:S(2)}) %collective-permute-start.25) | collective-permute-done | bytes 557088 | tf_op jit(solution)/shard_map/ppermute | solution.py:1008
  124.1 2.5 %collective-permute-start.29 = (bf16[176,768]{1,0:T(8,128)(2,1)S(1)}, bf16[176,768]{1,0:T(8,128)(2,1)S(1)}, u32[]{:S(2)}, u32[]{:S(2)}) collective-permute-start(bf16[176,768]{1,0:T(8,128)(2,1)S(1)} %get-tuple-element.147), channel_id=1, source_target_pairs={{0,4},{2,6},{4,0},{6,2},{8,12},{10,14},{12,8},{14,10},{16,20},{18,... | collective-permute-start | bytes 811016 | tf_op jit(solution)/shard_map/ppermute | solution.py:1008
  126.6 1.4 collective-permute-start.30
  128.0 1.0 feed_sum.1
  129.0 1.5 %collective-permute-start.35 = (bf16[32,1024]{1,0:T(8,128)(2,1)S(1)}, bf16[32,1024]{1,0:T(8,128)(2,1)S(1)}, u32[]{:S(2)}, u32[]{:S(2)}) collective-permute-start(bf16[32,1024]{1,0:T(8,128)(2,1)S(1)} %get-tuple-element.155), channel_id=1, source_target_pairs={{0,16},{2,18},{4,20},{6,22},{8,24},{10,26},{12,28},{14,30},{16,0},... | collective-permute-start | bytes 196616 | tf_op jit(solution)/shard_map/ppermute | solution.py:1005
  130.5 2.8 %collective-permute-start.36 = (bf16[32,1024]{1,0:T(8,128)(2,1)S(1)}, bf16[32,1024]{1,0:T(8,128)(2,1)S(1)}, u32[]{:S(2)}, u32[]{:S(2)}) collective-permute-start(bf16[32,1024]{1,0:T(8,128)(2,1)S(1)} %get-tuple-element.156), channel_id=1, source_target_pairs={{0,24},{2,26},{4,28},{6,30},{8,16},{10,18},{12,20},{14,22},{16,8},... | collective-permute-start | bytes 196616 | tf_op jit(solution)/shard_map/ppermute | solution.py:1005
  133.4 4.5 %tokens.1 = (bf16[128,1024]{1,0:T(8,128)(2,1)}, bf16[128,1024]{1,0:T(8,128)(2,1)}) custom-call(bf16[512,1024]{1,0:T(8,128)(2,1)S(1)} %get-tuple-element.125.refs_0_.refs_8_, bf16[128,1024]{1,0:T(8,128)(2,1)S(1)} %collective-permute-done.18.refs_1_, bf16[128,1024]{1,0:T(8,128)(2,1)S(1)} %collective-permute-done.19.refs_2_, ...), custom_call_target="tpu_custom_call" | custom-call | tf_op jit(solution)/shard_map/tokens/pallas_call | solution.py:416
  137.9 0.7 grad_sum.1
  138.6 1.5 %collective-permute-start.32 = (bf16[48,768]{1,0:T(8,128)(2,1)S(1)}, bf16[48,768]{1,0:T(8,128)(2,1)S(1)}, u32[]{:S(2)}, u32[]{:S(2)}) collective-permute-start(bf16[48,768]{1,0:T(8,128)(2,1)S(1)} %get-tuple-element.151), channel_id=1, source_target_pairs={{0,16},{2,18},{4,20},{6,22},{8,24},{10,26},{12,28},{14,30},{16,0},... | collective-permute-start | bytes 221192 | tf_op jit(solution)/shard_map/ppermute | solution.py:1005
  140.1 2.9 %collective-permute-start.33 = (bf16[48,768]{1,0:T(8,128)(2,1)S(1)}, bf16[48,768]{1,0:T(8,128)(2,1)S(1)}, u32[]{:S(2)}, u32[]{:S(2)}) collective-permute-start(bf16[48,768]{1,0:T(8,128)(2,1)S(1)} %get-tuple-element.152), channel_id=1, source_target_pairs={{0,24},{2,26},{4,28},{6,30},{8,16},{10,18},{12,20},{14,22},{16,8},... | collective-permute-start | bytes 221192 | tf_op jit(solution)/shard_map/ppermute | solution.py:1005
  143.0 0.8 join_in.1.refs_4_
  143.8 1.6 %collective-permute-done.32.refs_2_ = bf16[48,768]{1,0:T(8,128)(2,1)S(1)} collective-permute-done((bf16[48,768]{1,0:T(8,128)(2,1)S(1)}, bf16[48,768]{1,0:T(8,128)(2,1)S(1)}, u32[]{:S(2)}, u32[]{:S(2)}) %collective-permute-start.32) | collective-permute-done | bytes 73760 | tf_op jit(solution)/shard_map/ppermute | solution.py:1005
  145.4 0.9 collective-permute-done.33.refs_3_
  146.3 0.8 join_qkv.1
  147.1 0.5 copy.28
  (43 shorter events, 0.6 us)
Async XLA Ops:
  1.6 12.6 %copy-start = (bf16[144,1024]{1,0:T(8,128)(2,1)}, bf16[144,1024]{1,0:T(8,128)(2,1)S(1)}, u32[]{:S(2)}) copy-start(bf16[144,1024]{1,0:T(8,128)(2,1)S(1)} %pack.1.refs_10_.refs_0_) | copy-start | bytes 884740
  1.6 17.6 %collective-permute-start.1 = (bf16[144,1024]{1,0:T(8,128)(2,1)S(1)}, bf16[144,1024]{1,0:T(8,128)(2,1)}, u32[]{:S(2)}, u32[]{:S(2)}) collective-permute-start(bf16[144,1024]{1,0:T(8,128)(2,1)S(1)} %pack.1.refs_10_.refs_0_), channel_id=1, source_target_pairs={{0,16},{2,18},{4,20},{6,22},{8,24},{10,26},{12,28},{14,30},{16,0},... | collective-permute-start | bytes 884744 | tf_op jit(solution)/shard_map/ppermute | solution.py:1005
  5.7 14.1 %collective-permute-start = (bf16[144,1024]{1,0:T(8,128)(2,1)S(1)}, bf16[144,1024]{1,0:T(8,128)(2,1)S(1)}, u32[]{:S(2)}, u32[]{:S(2)}) collective-permute-start(bf16[144,1024]{1,0:T(8,128)(2,1)S(1)} %pack.1.refs_10_.refs_0_), channel_id=1, source_target_pairs={{0,8},{2,10},{4,12},{6,14},{8,0},{10,2},{12,4},{14,6},{16,24},{18,... | collective-permute-start | bytes 884744 | tf_op jit(solution)/shard_map/ppermute | solution.py:1005
  14.2 12.1 %collective-permute-start.5 = (bf16[3600,1024]{1,0:T(8,128)(2,1)}, bf16[3600,1024]{1,0:T(8,128)(2,1)}, u32[]{:S(2)}, u32[]{:S(2)}) collective-permute-start(bf16[3600,1024]{1,0:T(8,128)(2,1)} %prepare.1.refs_3_.refs_0_), channel_id=1, source_target_pairs={{0,1},{1,0},{2,3},{3,2},{4,5},{5,4},{6,7},{7,6},{8,9},{9,8},{10,11... | collective-permute-start | bytes 22118408 | tf_op jit(solution)/shard_map/ppermute | solution.py:1011
  19.3 13.7 %collective-permute-start.6 = (bf16[144,1024]{1,0:T(8,128)(2,1)}, bf16[144,1024]{1,0:T(8,128)(2,1)}, u32[]{:S(2)}, u32[]{:S(2)}) collective-permute-start(bf16[144,1024]{1,0:T(8,128)(2,1)} %collective-permute-done.1.refs_2_), channel_id=1, source_target_pairs={{0,8},{2,10},{4,12},{6,14},{8,0},{10,2},{12,4},{14,6},{16,24},{18,... | collective-permute-start | bytes 884744 | tf_op jit(solution)/shard_map/ppermute | solution.py:1005
  20.8 12.2 %copy-start.1 = (bf16[144,1024]{1,0:T(8,128)(2,1)S(1)}, bf16[144,1024]{1,0:T(8,128)(2,1)}, u32[]{:S(2)}) copy-start(bf16[144,1024]{1,0:T(8,128)(2,1)} %copy-done) | copy-start | bytes 884740
  20.8 19.0 %collective-permute-start.3 = (bf16[128,1024]{1,0:T(8,128)(2,1)S(1)}, bf16[128,1024]{1,0:T(8,128)(2,1)S(1)}, u32[]{:S(2)}, u32[]{:S(2)}) collective-permute-start(bf16[128,1024]{1,0:T(8,128)(2,1)S(1)} %hold.1.refs_2_.refs_0_), channel_id=1, source_target_pairs={{0,16},{2,18},{4,20},{6,22},{8,24},{10,26},{12,28},{14,30},{16,0},... | collective-permute-start | bytes 786440 | tf_op jit(solution)/shard_map/ppermute | solution.py:1005
  36.2 8.3 %collective-permute-start.7 = (bf16[784,128]{1,0:T(8,128)(2,1)S(1)}, bf16[784,128]{1,0:T(8,128)(2,1)S(1)}, u32[]{:S(2)}, u32[]{:S(2)}) collective-permute-start(bf16[784,128]{1,0:T(8,128)(2,1)S(1)} %get-tuple-element.92), channel_id=1, source_target_pairs={{0,2},{2,0},{4,6},{6,4},{8,10},{10,8},{12,14},{14,12},{16,18},{18,... | collective-permute-start | bytes 602120 | tf_op jit(solution)/shard_map/ppermute | solution.py:1008
  37.5 9.8 %collective-permute-start.8 = (bf16[784,128]{1,0:T(8,128)(2,1)S(1)}, bf16[784,128]{1,0:T(8,128)(2,1)S(1)}, u32[]{:S(2)}, u32[]{:S(2)}) collective-permute-start(bf16[784,128]{1,0:T(8,128)(2,1)S(1)} %get-tuple-element.93), channel_id=1, source_target_pairs={{0,4},{2,6},{4,0},{6,2},{8,12},{10,14},{12,8},{14,10},{16,20},{18,... | collective-permute-start | bytes 602120 | tf_op jit(solution)/shard_map/ppermute | solution.py:1008
  39.1 8.2 %collective-permute-start.9 = (bf16[784,128]{1,0:T(8,128)(2,1)S(1)}, bf16[784,128]{1,0:T(8,128)(2,1)S(1)}, u32[]{:S(2)}, u32[]{:S(2)}) collective-permute-start(bf16[784,128]{1,0:T(8,128)(2,1)S(1)} %get-tuple-element.94), channel_id=1, source_target_pairs={{0,6},{2,4},{4,2},{6,0},{8,14},{10,12},{12,10},{14,8},{16,22},{18,... | collective-permute-start | bytes 602120 | tf_op jit(solution)/shard_map/ppermute | solution.py:1008
  39.8 13.6 %collective-permute-start.2 = (bf16[128,1024]{1,0:T(8,128)(2,1)S(1)}, bf16[128,1024]{1,0:T(8,128)(2,1)S(1)}, u32[]{:S(2)}, u32[]{:S(2)}) collective-permute-start(bf16[128,1024]{1,0:T(8,128)(2,1)S(1)} %hold.1.refs_2_.refs_0_), channel_id=1, source_target_pairs={{0,8},{2,10},{4,12},{6,14},{8,0},{10,2},{12,4},{14,6},{16,24},{18,... | collective-permute-start | bytes 786440 | tf_op jit(solution)/shard_map/ppermute | solution.py:1005
  39.8 14.9 %collective-permute-start.4 = (bf16[128,1024]{1,0:T(8,128)(2,1)S(1)}, bf16[128,1024]{1,0:T(8,128)(2,1)S(1)}, u32[]{:S(2)}, u32[]{:S(2)}) collective-permute-start(bf16[128,1024]{1,0:T(8,128)(2,1)S(1)} %collective-permute-done.3.refs_2_), channel_id=1, source_target_pairs={{0,8},{2,10},{4,12},{6,14},{8,0},{10,2},{12,4},{14,6},{16,24},{18,... | collective-permute-start | bytes 786440 | tf_op jit(solution)/shard_map/ppermute | solution.py:1005
  41.8 5.5 %copy-start.2 = (f32[2048,128]{1,0:T(8,128)S(1)}, f32[2048,128]{1,0:T(8,128)}, u32[]{:S(2)}) copy-start(f32[2048,128]{1,0:T(8,128)} %constant.5.clone.refs_5_.refs_11_) | copy-start | bytes 3145732
  41.8 5.5 %copy-start.3 = (f32[2048,128]{1,0:T(8,128)S(1)}, f32[2048,128]{1,0:T(8,128)}, u32[]{:S(2)}) copy-start(f32[2048,128]{1,0:T(8,128)} %constant.4.clone.refs_4_.refs_10_) | copy-start | bytes 3145732
  44.5 32.5 %collective-permute-start.17 = (bf16[256,1024]{1,0:T(8,128)(2,1)S(1)}, bf16[256,1024]{1,0:T(8,128)(2,1)S(1)}, u32[]{:S(2)}, u32[]{:S(2)}) collective-permute-start(bf16[256,1024]{1,0:T(8,128)(2,1)S(1)} %get-tuple-element.122), channel_id=1, source_target_pairs={{0,8},{2,10},{4,12},{6,14},{8,0},{10,2},{12,4},{14,6},{16,24},{18,... | collective-permute-start | bytes 1572872 | tf_op jit(solution)/shard_map/ppermute | solution.py:1005
  55.3 10.5 %collective-permute-start.10 = (bf16[256,128]{1,0:T(8,128)(2,1)S(1)}, bf16[256,128]{1,0:T(8,128)(2,1)S(1)}, u32[]{:S(2)}, u32[]{:S(2)}) collective-permute-start(bf16[256,128]{1,0:T(8,128)(2,1)S(1)} %get-tuple-element.101), channel_id=1, source_target_pairs={{0,2},{2,0},{4,6},{6,4},{8,10},{10,8},{12,14},{14,12},{16,18},{18,... | collective-permute-start | bytes 196616 | tf_op jit(solution)/shard_map/ppermute | solution.py:1008
  56.6 9.3 %collective-permute-start.11 = (bf16[256,128]{1,0:T(8,128)(2,1)S(1)}, bf16[256,128]{1,0:T(8,128)(2,1)S(1)}, u32[]{:S(2)}, u32[]{:S(2)}) collective-permute-start(bf16[256,128]{1,0:T(8,128)(2,1)S(1)} %get-tuple-element.102), channel_id=1, source_target_pairs={{0,4},{2,6},{4,0},{6,2},{8,12},{10,14},{12,8},{14,10},{16,20},{18,... | collective-permute-start | bytes 196616 | tf_op jit(solution)/shard_map/ppermute | solution.py:1008
  58.1 7.8 %collective-permute-start.12 = (bf16[256,128]{1,0:T(8,128)(2,1)S(1)}, bf16[256,128]{1,0:T(8,128)(2,1)S(1)}, u32[]{:S(2)}, u32[]{:S(2)}) collective-permute-start(bf16[256,128]{1,0:T(8,128)(2,1)S(1)} %get-tuple-element.103), channel_id=1, source_target_pairs={{0,6},{2,4},{4,2},{6,0},{8,14},{10,12},{12,10},{14,8},{16,22},{18,... | collective-permute-start | bytes 196616 | tf_op jit(solution)/shard_map/ppermute | solution.py:1008
  62.2 15.7 %collective-permute-start.16 = (bf16[256,1024]{1,0:T(8,128)(2,1)S(1)}, bf16[256,1024]{1,0:T(8,128)(2,1)S(1)}, u32[]{:S(2)}, u32[]{:S(2)}) collective-permute-start(bf16[256,1024]{1,0:T(8,128)(2,1)S(1)} %get-tuple-element.120), channel_id=1, source_target_pairs={{0,8},{2,10},{4,12},{6,14},{8,0},{10,2},{12,4},{14,6},{16,24},{18,... | collective-permute-start | bytes 1572872 | tf_op jit(solution)/shard_map/ppermute | solution.py:1005
  65.8 29.8 %collective-permute-start.23 = (bf16[1088,1024]{1,0:T(8,128)(2,1)S(1)}, bf16[1088,1024]{1,0:T(8,128)(2,1)S(1)}, u32[]{:S(2)}, u32[]{:S(2)}) collective-permute-start(bf16[1088,1024]{1,0:T(8,128)(2,1)S(1)} %get-tuple-element.114.refs_12_), channel_id=1, source_target_pairs={{0,1},{1,0},{2,3},{3,2},{4,5},{5,4},{6,7},{7,6},{8,9},{9,8},{10,11... | collective-permute-start | bytes 6684680 | tf_op jit(solution)/shard_map/ppermute | solution.py:1011
  74.2 9.2 %collective-permute-start.13 = (bf16[1024,128]{1,0:T(8,128)(2,1)S(1)}, bf16[1024,128]{1,0:T(8,128)(2,1)S(1)}, u32[]{:S(2)}, u32[]{:S(2)}) collective-permute-start(bf16[1024,128]{1,0:T(8,128)(2,1)S(1)} %get-tuple-element.116), channel_id=1, source_target_pairs={{0,2},{2,0},{4,6},{6,4},{8,10},{10,8},{12,14},{14,12},{16,18},{18,... | collective-permute-start | bytes 786440 | tf_op jit(solution)/shard_map/ppermute | solution.py:1008
  75.5 14.0 %collective-permute-start.14 = (bf16[1024,128]{1,0:T(8,128)(2,1)S(1)}, bf16[1024,128]{1,0:T(8,128)(2,1)S(1)}, u32[]{:S(2)}, u32[]{:S(2)}) collective-permute-start(bf16[1024,128]{1,0:T(8,128)(2,1)S(1)} %get-tuple-element.117), channel_id=1, source_target_pairs={{0,4},{2,6},{4,0},{6,2},{8,12},{10,14},{12,8},{14,10},{16,20},{18,... | collective-permute-start | bytes 786440 | tf_op jit(solution)/shard_map/ppermute | solution.py:1008
  77.0 12.5 %collective-permute-start.15 = (bf16[1024,128]{1,0:T(8,128)(2,1)S(1)}, bf16[1024,128]{1,0:T(8,128)(2,1)S(1)}, u32[]{:S(2)}, u32[]{:S(2)}) collective-permute-start(bf16[1024,128]{1,0:T(8,128)(2,1)S(1)} %get-tuple-element.118), channel_id=1, source_target_pairs={{0,6},{2,4},{4,2},{6,0},{8,14},{10,12},{12,10},{14,8},{16,22},{18,... | collective-permute-start | bytes 786440 | tf_op jit(solution)/shard_map/ppermute | solution.py:1008
  77.9 21.6 %collective-permute-start.21 = (bf16[128,1024]{1,0:T(8,128)(2,1)S(1)}, bf16[128,1024]{1,0:T(8,128)(2,1)S(1)}, u32[]{:S(2)}, u32[]{:S(2)}) collective-permute-start(bf16[128,1024]{1,0:T(8,128)(2,1)S(1)} %get-tuple-element.129), channel_id=1, source_target_pairs={{0,16},{2,18},{4,20},{6,22},{8,24},{10,26},{12,28},{14,30},{16,0},... | collective-permute-start | bytes 786440 | tf_op jit(solution)/shard_map/ppermute | solution.py:1005
  83.4 20.7 %collective-permute-start.22 = (bf16[128,1024]{1,0:T(8,128)(2,1)S(1)}, bf16[128,1024]{1,0:T(8,128)(2,1)S(1)}, u32[]{:S(2)}, u32[]{:S(2)}) collective-permute-start(bf16[128,1024]{1,0:T(8,128)(2,1)S(1)} %get-tuple-element.130), channel_id=1, source_target_pairs={{0,16},{2,18},{4,20},{6,22},{8,24},{10,26},{12,28},{14,30},{16,0},... | collective-permute-start | bytes 786440 | tf_op jit(solution)/shard_map/ppermute | solution.py:1005
  90.5 18.2 %collective-permute-start.18 = (bf16[128,1024]{1,0:T(8,128)(2,1)S(1)}, bf16[128,1024]{1,0:T(8,128)(2,1)S(1)}, u32[]{:S(2)}, u32[]{:S(2)}) collective-permute-start(bf16[128,1024]{1,0:T(8,128)(2,1)S(1)} %get-tuple-element.126), channel_id=1, source_target_pairs={{0,8},{2,10},{4,12},{6,14},{8,0},{10,2},{12,4},{14,6},{16,24},{18,... | collective-permute-start | bytes 786440 | tf_op jit(solution)/shard_map/ppermute | solution.py:1005
  95.5 5.3 %collective-permute-start.27 = (bf16[704,768]{1,0:T(8,128)(2,1)S(1)}, bf16[704,768]{1,0:T(8,128)(2,1)S(1)}, u32[]{:S(2)}, u32[]{:S(2)}) collective-permute-start(bf16[704,768]{1,0:T(8,128)(2,1)S(1)} %get-tuple-element.136.refs_2_), channel_id=1, source_target_pairs={{0,1},{1,0},{2,3},{3,2},{4,5},{5,4},{6,7},{7,6},{8,9},{9,8},{10,11... | collective-permute-start | bytes 3244040 | tf_op jit(solution)/shard_map/ppermute | solution.py:1011
  96.0 15.5 %collective-permute-start.24 = (bf16[272,1024]{1,0:T(8,128)(2,1)S(1)}, bf16[272,1024]{1,0:T(8,128)(2,1)S(1)}, u32[]{:S(2)}, u32[]{:S(2)}) collective-permute-start(bf16[272,1024]{1,0:T(8,128)(2,1)S(1)} %get-tuple-element.138), channel_id=1, source_target_pairs={{0,2},{2,0},{4,6},{6,4},{8,10},{10,8},{12,14},{14,12},{16,18},{18,... | collective-permute-start | bytes 1671176 | tf_op jit(solution)/shard_map/ppermute | solution.py:1008
  99.5 24.6 %collective-permute-start.25 = (bf16[272,1024]{1,0:T(8,128)(2,1)S(1)}, bf16[272,1024]{1,0:T(8,128)(2,1)S(1)}, u32[]{:S(2)}, u32[]{:S(2)}) collective-permute-start(bf16[272,1024]{1,0:T(8,128)(2,1)S(1)} %get-tuple-element.139), channel_id=1, source_target_pairs={{0,4},{2,6},{4,0},{6,2},{8,12},{10,14},{12,8},{14,10},{16,20},{18,... | collective-permute-start | bytes 1671176 | tf_op jit(solution)/shard_map/ppermute | solution.py:1008
  100.8 25.7 %collective-permute-start.26 = (bf16[272,1024]{1,0:T(8,128)(2,1)S(1)}, bf16[272,1024]{1,0:T(8,128)(2,1)S(1)}, u32[]{:S(2)}, u32[]{:S(2)}) collective-permute-start(bf16[272,1024]{1,0:T(8,128)(2,1)S(1)} %get-tuple-element.140), channel_id=1, source_target_pairs={{0,6},{2,4},{4,2},{6,0},{8,14},{10,12},{12,10},{14,8},{16,22},{18,... | collective-permute-start | bytes 1671176 | tf_op jit(solution)/shard_map/ppermute | solution.py:1008
  104.1 24.9 %collective-permute-start.19 = (bf16[128,1024]{1,0:T(8,128)(2,1)S(1)}, bf16[128,1024]{1,0:T(8,128)(2,1)S(1)}, u32[]{:S(2)}, u32[]{:S(2)}) collective-permute-start(bf16[128,1024]{1,0:T(8,128)(2,1)S(1)} %get-tuple-element.127), channel_id=1, source_target_pairs={{0,16},{2,18},{4,20},{6,22},{8,24},{10,26},{12,28},{14,30},{16,0},... | collective-permute-start | bytes 786440 | tf_op jit(solution)/shard_map/ppermute | solution.py:1005
  108.7 20.3 %collective-permute-start.20 = (bf16[128,1024]{1,0:T(8,128)(2,1)S(1)}, bf16[128,1024]{1,0:T(8,128)(2,1)S(1)}, u32[]{:S(2)}, u32[]{:S(2)}) collective-permute-start(bf16[128,1024]{1,0:T(8,128)(2,1)S(1)} %get-tuple-element.128), channel_id=1, source_target_pairs={{0,24},{2,26},{4,28},{6,30},{8,16},{10,18},{12,20},{14,22},{16,8},... | collective-permute-start | bytes 786440 | tf_op jit(solution)/shard_map/ppermute | solution.py:1005
  111.5 19.0 %collective-permute-start.28 = (bf16[176,768]{1,0:T(8,128)(2,1)S(1)}, bf16[176,768]{1,0:T(8,128)(2,1)S(1)}, u32[]{:S(2)}, u32[]{:S(2)}) collective-permute-start(bf16[176,768]{1,0:T(8,128)(2,1)S(1)} %get-tuple-element.146), channel_id=1, source_target_pairs={{0,2},{2,0},{4,6},{6,4},{8,10},{10,8},{12,14},{14,12},{16,18},{18,... | collective-permute-start | bytes 811016 | tf_op jit(solution)/shard_map/ppermute | solution.py:1008
  124.1 13.8 %collective-permute-start.29 = (bf16[176,768]{1,0:T(8,128)(2,1)S(1)}, bf16[176,768]{1,0:T(8,128)(2,1)S(1)}, u32[]{:S(2)}, u32[]{:S(2)}) collective-permute-start(bf16[176,768]{1,0:T(8,128)(2,1)S(1)} %get-tuple-element.147), channel_id=1, source_target_pairs={{0,4},{2,6},{4,0},{6,2},{8,12},{10,14},{12,8},{14,10},{16,20},{18,... | collective-permute-start | bytes 811016 | tf_op jit(solution)/shard_map/ppermute | solution.py:1008
  126.6 11.3 %collective-permute-start.30 = (bf16[176,768]{1,0:T(8,128)(2,1)S(1)}, bf16[176,768]{1,0:T(8,128)(2,1)S(1)}, u32[]{:S(2)}, u32[]{:S(2)}) collective-permute-start(bf16[176,768]{1,0:T(8,128)(2,1)S(1)} %get-tuple-element.148), channel_id=1, source_target_pairs={{0,6},{2,4},{4,2},{6,0},{8,14},{10,12},{12,10},{14,8},{16,22},{18,... | collective-permute-start | bytes 811016 | tf_op jit(solution)/shard_map/ppermute | solution.py:1008
  129.0 11.1 %collective-permute-start.34 = (bf16[32,1024]{1,0:T(8,128)(2,1)S(1)}, bf16[32,1024]{1,0:T(8,128)(2,1)S(1)}, u32[]{:S(2)}, u32[]{:S(2)}) collective-permute-start(bf16[32,1024]{1,0:T(8,128)(2,1)S(1)} %get-tuple-element.154), channel_id=1, source_target_pairs={{0,8},{2,10},{4,12},{6,14},{8,0},{10,2},{12,4},{14,6},{16,24},{18,... | collective-permute-start | bytes 196616 | tf_op jit(solution)/shard_map/ppermute | solution.py:1005
  129.0 14.0 %collective-permute-start.35 = (bf16[32,1024]{1,0:T(8,128)(2,1)S(1)}, bf16[32,1024]{1,0:T(8,128)(2,1)S(1)}, u32[]{:S(2)}, u32[]{:S(2)}) collective-permute-start(bf16[32,1024]{1,0:T(8,128)(2,1)S(1)} %get-tuple-element.155), channel_id=1, source_target_pairs={{0,16},{2,18},{4,20},{6,22},{8,24},{10,26},{12,28},{14,30},{16,0},... | collective-permute-start | bytes 196616 | tf_op jit(solution)/shard_map/ppermute | solution.py:1005
  130.5 12.4 %collective-permute-start.36 = (bf16[32,1024]{1,0:T(8,128)(2,1)S(1)}, bf16[32,1024]{1,0:T(8,128)(2,1)S(1)}, u32[]{:S(2)}, u32[]{:S(2)}) collective-permute-start(bf16[32,1024]{1,0:T(8,128)(2,1)S(1)} %get-tuple-element.156), channel_id=1, source_target_pairs={{0,24},{2,26},{4,28},{6,30},{8,16},{10,18},{12,20},{14,22},{16,8},... | collective-permute-start | bytes 196616 | tf_op jit(solution)/shard_map/ppermute | solution.py:1005
  137.8 9.2 %copy-start.4 = (f32[32]{0:T(128)S(1)}, f32[32]{0:T(128)}, u32[]{:S(2)}) copy-start(f32[32]{0:T(128)} %get-tuple-element.187) | copy-start | bytes 388
  138.6 5.2 %collective-permute-start.31 = (bf16[48,768]{1,0:T(8,128)(2,1)S(1)}, bf16[48,768]{1,0:T(8,128)(2,1)S(1)}, u32[]{:S(2)}, u32[]{:S(2)}) collective-permute-start(bf16[48,768]{1,0:T(8,128)(2,1)S(1)} %get-tuple-element.150), channel_id=1, source_target_pairs={{0,8},{2,10},{4,12},{6,14},{8,0},{10,2},{12,4},{14,6},{16,24},{18,... | collective-permute-start | bytes 221192 | tf_op jit(solution)/shard_map/ppermute | solution.py:1005
  138.6 6.8 %collective-permute-start.32 = (bf16[48,768]{1,0:T(8,128)(2,1)S(1)}, bf16[48,768]{1,0:T(8,128)(2,1)S(1)}, u32[]{:S(2)}, u32[]{:S(2)}) collective-permute-start(bf16[48,768]{1,0:T(8,128)(2,1)S(1)} %get-tuple-element.151), channel_id=1, source_target_pairs={{0,16},{2,18},{4,20},{6,22},{8,24},{10,26},{12,28},{14,30},{16,0},... | collective-permute-start | bytes 221192 | tf_op jit(solution)/shard_map/ppermute | solution.py:1005
  140.1 6.2 %collective-permute-start.33 = (bf16[48,768]{1,0:T(8,128)(2,1)S(1)}, bf16[48,768]{1,0:T(8,128)(2,1)S(1)}, u32[]{:S(2)}, u32[]{:S(2)}) collective-permute-start(bf16[48,768]{1,0:T(8,128)(2,1)S(1)} %get-tuple-element.152), channel_id=1, source_target_pairs={{0,24},{2,26},{4,28},{6,30},{8,16},{10,18},{12,20},{14,22},{16,8},... | collective-permute-start | bytes 221192 | tf_op jit(solution)/shard_map/ppermute | solution.py:1005
